TPU v7x, 32 devices: a whole 2x2x4 slice. The times are simulated.
32 devices in a mesh: groups: 2 (over y), expert: 4 (over z), etp: 4 (over x, core).
Axes of the slice: x: 2, y: 2, z: 4, core: 2. Of those that a mesh axis runs over, the one named last changes fastest.
Arguments:
- hidden_in: bfloat16 [1024, 1024], P(('groups', 'expert'), 'etp'), parts along dimension 0, may hold values from -6 to 6
- out_grad: bfloat16 [1024, 1024], P(('groups', 'expert'), 'etp'), parts along dimension 0, may hold values from -3 to 3
- expert_ids: int32 [1024, 6], P(('groups', 'expert')), parts along dimension 0, may hold values from 0 to 63, all different within a row; in each aligned block of 128 rows (0 to 127, 128 to 255, ...) at most 16 rows name the same one
- gate_values: float32 [1024, 6], P(('groups', 'expert')), parts along dimension 0, may hold values from 0.1 to 1
- capacity_blocks: int32 [128], P('groups'), parts along dimension 0, may hold values from 1 to 4
- gate_weight: bfloat16 [64, 1024, 1408], P('expert', None, 'etp'), may hold values from -0.1875 to 0.1875
- up_weight: bfloat16 [64, 1024, 1408], P('expert', None, 'etp'), may hold values from -0.1875 to 0.1875
- down_weight: bfloat16 [64, 1408, 1024], P('expert', 'etp'), may hold values from -0.15625 to 0.15625
Outputs:
- layer_out: bfloat16 [1024, 1024], P(('groups', 'expert'), 'etp'), parts along dimension 0
- input_grad: bfloat16 [1024, 1024], P(('groups', 'expert'), 'etp'), parts along dimension 0
- gate_value_grad: float32 [1024, 6], P(('groups', 'expert')), parts along dimension 0
- gate_weight_grad: bfloat16 [128, 1024, 1408], P(('groups', 'expert'), None, 'etp'), parts along dimension 0
- up_weight_grad: bfloat16 [128, 1024, 1408], P(('groups', 'expert'), None, 'etp'), parts along dimension 0
- down_weight_grad: bfloat16 [128, 1408, 1024], P(('groups', 'expert'), 'etp'), parts along dimension 0
There are 2 independent parts, one for each index of `groups`. A program takes and returns all parts, laid end to end along the dimension named above; an argument that names none is the same for every part. Nothing has to cross between parts.
Inputs may be any that keep to these rules, and one draw needn't show every extreme that they name: `expert_ids`: each row names 6 different experts; within each aligned block of 128 rows no expert is named more than 16 times.
All inputs are finite; a program needn't handle non-finite values.
Results may differ from a plain program's by a relative error of at most 0.013.
Values may be sent and summed in bfloat16 or wider, within the bound.
No kernel may reach another device: no remote copies, remote signals or barrier semaphores. Data moves between devices by JAX's collectives and lax.ppermute only.
A program may use at most 192 MiB of HBM per device.

v0:
```python
import jax
import jax.numpy as jnp
from jax import lax
from jax.sharding import PartitionSpec as P

CAP = 16
BLK = 4


def slot_layout(expert_ids, capacity_blocks):
    tokens_here, choose = expert_ids.shape
    experts = capacity_blocks.shape[0]
    flat_ids = expert_ids.reshape(-1)
    onehot = (flat_ids[:, None] == jnp.arange(experts, dtype=jnp.int32)[None, :]).astype(jnp.int32)
    before = jnp.cumsum(onehot, axis=0) - onehot
    ranks = jnp.sum(before * onehot, axis=1)
    limits = jnp.sum(onehot * capacity_blocks[None, :], axis=1) * BLK
    kept = ranks < limits
    slots = jnp.where(kept, flat_ids * CAP + ranks, experts * CAP)
    token_index = jnp.arange(tokens_here * choose, dtype=jnp.int32) // choose
    owners = (
        jnp.full((experts * CAP,), tokens_here, jnp.int32).at[slots].set(token_index, mode="drop")
    )
    return (kept.reshape(tokens_here, choose), slots.reshape(tokens_here, choose), owners)


def outgoing(rows, owners, experts, scale):
    padded = jnp.concatenate([rows, jnp.zeros((1, rows.shape[1]), rows.dtype)], 0)
    picked = padded[owners]
    if scale is not None:
        picked = (scale[:, None] * picked.astype(jnp.float32)).astype(jnp.bfloat16)
    return picked.reshape(experts, CAP, rows.shape[1])


def local_grads(hidden_gate, hidden_up, act_grad):
    sigma = jax.nn.sigmoid(hidden_gate)
    gate_part = (act_grad * hidden_up * sigma * (1.0 + hidden_gate * (1.0 - sigma))).astype(
        jnp.bfloat16
    )
    up_part = (act_grad * jax.nn.silu(hidden_gate)).astype(jnp.bfloat16)
    return (gate_part, up_part)


def combine(back, slots, weights):
    padded = jnp.concatenate([back, jnp.zeros((1, back.shape[1]), back.dtype)], 0)
    picked = padded[slots].astype(jnp.float32)
    return (jnp.einsum("tk,tkw->tw", weights, picked), picked)


def body(
    hidden_in,
    out_grad,
    expert_ids,
    gate_values,
    capacity_blocks,
    gate_weight,
    up_weight,
    down_weight,
):
    experts = capacity_blocks.shape[0]
    sources = lax.axis_size("expert")
    local_experts = gate_weight.shape[0]
    kept, slots, owners = slot_layout(expert_ids, capacity_blocks)
    weights = jnp.where(kept, gate_values, 0.0)
    slot_gates = (
        jnp.zeros((experts * CAP,), jnp.float32)
        .at[slots.reshape(-1)]
        .set(weights.reshape(-1), mode="drop")
    )
    send_in = outgoing(hidden_in, owners, experts, None)
    send_grad = outgoing(out_grad, owners, experts, slot_gates)
    recv_in, recv_grad = (
        lax.all_to_all(send_in, "expert", split_axis=0, concat_axis=0, tiled=True),
        lax.all_to_all(send_grad, "expert", split_axis=0, concat_axis=0, tiled=True),
    )
    share = recv_in.shape[2]
    share_in = recv_in.reshape(sources, local_experts, CAP, share)
    share_grad = recv_grad.reshape(sources, local_experts, CAP, share)
    piece = lax.all_gather(share_in, "etp", axis=3, tiled=True)
    hidden_gate = jnp.einsum(
        "secn,enf->secf", piece, gate_weight, preferred_element_type=jnp.float32
    )
    hidden_up = jnp.einsum("secn,enf->secf", piece, up_weight, preferred_element_type=jnp.float32)
    activ = (jax.nn.silu(hidden_gate) * hidden_up).astype(jnp.bfloat16)
    piece = lax.all_gather(share_grad, "etp", axis=3, tiled=True)
    act_grad = jnp.einsum("secn,efn->secf", piece, down_weight, preferred_element_type=jnp.float32)
    columns = jnp.einsum("secf,secn->efn", activ, piece, preferred_element_type=jnp.float32)
    act_grad, down_grad = (act_grad, columns)
    gate_part, up_part = local_grads(hidden_gate, hidden_up, act_grad)
    stacked = jnp.stack([gate_part, up_part])
    weight_grads = jnp.einsum(
        "secn,gsecf->genf",
        lax.all_gather(share_in, "etp", axis=3, tiled=True),
        stacked,
        preferred_element_type=jnp.float32,
    )
    out_part = jnp.einsum("secf,efd->secd", activ, down_weight, preferred_element_type=jnp.float32)
    back_part = jnp.einsum(
        "secf,edf->secd", gate_part, gate_weight, preferred_element_type=jnp.float32
    )
    back_part = back_part + jnp.einsum(
        "secf,edf->secd", up_part, up_weight, preferred_element_type=jnp.float32
    )
    out_rows = lax.psum_scatter(
        out_part.astype(jnp.bfloat16), "etp", scatter_dimension=3, tiled=True
    )
    home_out = lax.all_to_all(out_rows, "expert", split_axis=0, concat_axis=0, tiled=True)
    share_width = home_out.shape[3]
    layer_sum, picked = combine(home_out.reshape(experts * CAP, share_width), slots, weights)
    dot_part = jnp.einsum("tw,tkw->tk", out_grad.astype(jnp.float32), picked) * kept.astype(
        jnp.float32
    )
    gate_value_grad = lax.psum(dot_part, "etp")
    back_rows = lax.psum_scatter(
        back_part.astype(jnp.bfloat16), "etp", scatter_dimension=3, tiled=True
    )
    home_back = lax.all_to_all(back_rows, "expert", split_axis=0, concat_axis=0, tiled=True)
    input_sum, returned = combine(home_back.reshape(experts * CAP, share_width), slots, weights)
    return (
        layer_sum.astype(jnp.bfloat16),
        input_sum.astype(jnp.bfloat16),
        gate_value_grad,
        weight_grads[0].astype(jnp.bfloat16),
        weight_grads[1].astype(jnp.bfloat16),
        down_grad.astype(jnp.bfloat16),
    )


def solution(mesh):
    in_specs = (
        P(("groups", "expert"), "etp"),
        P(("groups", "expert"), "etp"),
        P(("groups", "expert"), None),
        P(("groups", "expert"), None),
        P("groups"),
        P("expert", None, "etp"),
        P("expert", None, "etp"),
        P("expert", "etp", None),
    )
    out_specs = (
        P(("groups", "expert"), "etp"),
        P(("groups", "expert"), "etp"),
        P(("groups", "expert"), None),
        P(("groups", "expert"), None, "etp"),
        P(("groups", "expert"), None, "etp"),
        P(("groups", "expert"), "etp", None),
    )
    return jax.shard_map(body, mesh=mesh, in_specs=in_specs, out_specs=out_specs, check_vma=False)
```

profile of v0, /device:TPU:0, one launch (start us, length us, event | category | flops | bytes accessed | tf_op | source)
XLA Modules:
  0.0 219.6 jit_solution(17645093123843979847)
XLA Ops:
  11.7 3.4 %scatter_custom_fusion = s32[1024]{0:T(1024)S(1)} fusion(s32[768]{0:T(1024)S(1)} %fusion.40, s32[768]{0:T(1024)S(1)} %add_select_fusion, s32[]{:T(128)} %constant.11.clone.1), kind=kCustom, calls=%fused_computation.79 | custom fusion | bytes 4100 | tf_op jit(solution)/shard_map/scatter | solution.py:22
  16.0 3.9 %gather_fusion = bf16[1024,256]{1,0:T(8,128)(2,1)S(1)} fusion(bf16[129,256]{1,0:T(8,128)(2,1)S(1)} %concatenate.12, s32[1024]{0:T(1024)S(1)} %fusion.38), kind=kCustom, calls=%fused_computation | custom fusion | bytes 1052672 | tf_op jit(solution)/shard_map/gather | solution.py:29
  19.9 20.7 %all_to_all.20 = bf16[64,16,256]{2,1,0:T(8,128)(2,1)S(1)} all-to-all(bf16[64,16,256]{2,1,0:T(8,128)(2,1)S(1)} %bitcast.147), channel_id=1, replica_groups=mesh['groups'=2,'expert'=4,'etp'=4] {'expert'}, dimensions={0} | all-to-all | bytes 1048576 | tf_op jit(solution)/shard_map/all_to_all | solution.py:73
  41.7 3.9 %gather_fusion.2 = bf16[1024,256]{1,0:T(8,128)(2,1)S(1)} fusion(bf16[129,256]{1,0:T(8,128)(2,1)S(1)} %concatenate.14, s32[1024]{0:T(1024)S(1)} %fusion.38), kind=kCustom, calls=%fused_computation.2 | custom fusion | bytes 1052672 | tf_op jit(solution)/shard_map/gather | solution.py:29
  45.8 3.4 %scatter_custom_fusion.1 = f32[1024]{0:T(1024)S(1)} fusion(s32[768]{0:T(1024)S(1)} %fusion.40, f32[768]{0:T(1024)S(1)} %reshape.164, f32[]{:T(128)} %constant.15.clone.1), kind=kCustom, calls=%fused_computation.77 | custom fusion | bytes 4100 | tf_op jit(solution)/shard_map/scatter | solution.py:68
  49.5 16.6 %all_to_all.21 = bf16[64,16,256]{2,1,0:T(8,128)(2,1)S(1)} all-to-all(bf16[64,16,256]{2,1,0:T(8,128)(2,1)S(1)} %fusion.29), channel_id=1, replica_groups=mesh['groups'=2,'expert'=4,'etp'=4] {'expert'}, dimensions={0} | all-to-all | bytes 1048576 | tf_op jit(solution)/shard_map/all_to_all | solution.py:74
  67.2 9.5 %fusion.3 = f32[16,4,16,352]{3,2,1,0:T(8,128)} fusion(bf16[4,16,16,1024]{3,2,0,1:T(8,128)(2,1)} %all-gather.3.cloned.1.call-done, bf16[16,1024,352]{1,2,0:T(8,128)(2,1)} %param.14), kind=kOutput, calls=%fused_computation.13 | convolution fusion | flops 738197504 | bytes 15073280 | tf_op jit(solution)/shard_map/secn,enf->secf/dot_general | solution.py:83
  76.8 8.7 %fusion.7 = f32[16,4,16,352]{3,2,1,0:T(8,128)} fusion(bf16[4,16,16,1024]{3,2,0,1:T(8,128)(2,1)S(1)} %copy-done, bf16[16,1024,352]{1,2,0:T(8,128)(2,1)} %param.13), kind=kOutput, calls=%fused_computation.17 | convolution fusion | flops 738197504 | bytes 15073280 | tf_op jit(solution)/shard_map/secn,enf->secf/dot_general | solution.py:80
  85.5 3.6 %all-gather.5.cloned.1.call-done = bf16[4,16,16,1024]{3,2,0,1:T(8,128)(2,1)} async-done(((bf16[4,16,16,256]{3,2,0,1:T(8,128)(2,1)}), bf16[4,16,16,1024]{3,2,0,1:T(8,128)(2,1)}) %all-gather.5.cloned.1.call-update) | async-done | bytes 2097168 | tf_op jit(solution)/shard_map/all_gather | solution.py:85
  89.0 10.6 %fusion.21 = (bf16[4,16,16,352]{3,2,0,1:T(8,128)(2,1)}, bf16[4,16,16,352]{3,2,0,1:T(8,128)(2,1)}, bf16[4,16,16,352]{3,2,0,1:T(8,128)(2,1)}) fusion(f32[16,4,16,352]{3,2,1,0:T(8,128)} %fusion.3, f32[16,4,16,352]{3,2,1,0:T(8,128)} %fusion.7, bf16[4,16,16,1024]{3,2,0,1:T(8,128)(2,1)} %all-gather.5.cloned.1.call-done, bf16[16,352,1024]{2,1,0:T(8,128)(2,1)} %param.15), kind=kOutput, calls=%fused_computation.32 | convolution fusion | flops 743604224 | bytes 18677760 | tf_op jit(solution)/shard_map/secn,efn->secf/dot_general | solution.py:86
  99.6 6.8 %fusion.1 = f32[16,4,16,1024]{3,2,1,0:T(8,128)S(1)} fusion(bf16[4,16,16,352]{3,2,0,1:T(8,128)(2,1)} %get-tuple-element.26, bf16[16,1024,352]{1,2,0:T(8,128)(2,1)} %param.14), kind=kOutput, calls=%fused_computation.11 | convolution fusion | flops 738197504 | bytes 16449536 | tf_op jit(solution)/shard_map/secf,edf->secd/dot_general | solution.py:101
  106.5 3.9 %fusion.13 = bf16[4,16,16,1024]{3,2,0,1:T(8,128)(2,1)} fusion(f32[16,4,16,1024]{3,2,1,0:T(8,128)S(1)} %fusion.1, bf16[4,16,16,352]{3,2,0,1:T(8,128)(2,1)S(1)} %copy-done.1, bf16[16,1024,352]{1,2,0:T(8,128)(2,1)S(1)} %bitcast.141), kind=kOutput, calls=%fused_computation.24 | convolution fusion | flops 740294656 | bytes 18546688 | tf_op jit(solution)/shard_map/secf,edf->secd/dot_general | solution.py:98
  111.5 7.8 %convert_bitcast_fusion = bf16[4,16,16,1024]{3,2,0,1:T(8,128)(2,1)} fusion(bf16[4,16,16,352]{3,2,0,1:T(8,128)(2,1)S(1)} %copy-done.2, bf16[16,352,1024]{2,1,0:T(8,128)(2,1)} %param.15), kind=kOutput, calls=%fused_computation.26 | convolution fusion | flops 739246080 | bytes 14352384 | tf_op jit(solution)/shard_map/secf,efd->secd/dot_general | solution.py:97
  119.5 12.4 %fusion = bf16[2,16,1024,352]{2,3,0,1:T(8,128)(2,1)} fusion(bf16[4,16,16,1024]{3,2,0,1:T(8,128)(2,1)S(1)} %copy-done, bf16[1,4,16,16,352]{4,3,1,2,0:T(8,128)(2,1)} %bitcast.149, bf16[1,4,16,16,352]{4,3,1,2,0:T(8,128)(2,1)} %bitcast.148), kind=kOutput, calls=%fused_computation.7 | convolution fusion | flops 1488650240 | bytes 26607616 | tf_op jit(solution)/shard_map/secn,gsecf->genf/dot_general | solution.py:91
  132.0 10.0 %reduce-scatter.5.cloned.1.call-done = bf16[4,16,16,256]{3,2,0,1:T(8,128)(2,1)} async-done(((bf16[4,16,16,1024]{3,2,0,1:T(8,128)(2,1)}), bf16[4,16,16,256]{3,2,0,1:T(8,128)(2,1)}) %reduce-scatter.5.cloned.1.call-update) | async-done | bytes 524304 | tf_op jit(solution)/shard_map/reduce_scatter | solution.py:114
  143.9 4.6 %all-to-all-start.3 = ((bf16[4,16,16,256]{3,2,1,0:T(8,128)(2,1)}), bf16[4,16,16,256]{3,2,1,0:T(8,128)(2,1)S(1)}, u32[]{:S(2)}, u32[]{:S(2)}) async-start(bf16[4,16,16,256]{3,2,1,0:T(8,128)(2,1)} %copy.34), calls=%async_computation.5 | async-start | bytes 1048576 | tf_op jit(solution)/shard_map/all_to_all | solution.py:117
  148.5 17.2 %slice_bitcast_fusion = (bf16[16,1024,352]{1,2,0:T(8,128)(2,1)}, bf16[16,1024,352]{1,2,0:T(8,128)(2,1)}) fusion(bf16[2,16,1024,352]{2,3,0,1:T(8,128)(2,1)} %fusion), kind=kLoop, calls=%fused_computation.9 | loop fusion | bytes 46137344 | tf_op jit(solution)/shard_map/convert_element_type | solution.py:124
  165.7 10.4 %reduce-scatter.3.cloned.1.call-done = bf16[4,16,16,256]{3,2,0,1:T(8,128)(2,1)} async-done(((bf16[4,16,16,1024]{3,2,0,1:T(8,128)(2,1)}), bf16[4,16,16,256]{3,2,0,1:T(8,128)(2,1)}) %reduce-scatter.3.cloned.1.call-update) | async-done | bytes 524304 | tf_op jit(solution)/shard_map/reduce_scatter | solution.py:104
  177.9 4.6 %all-to-all-start.1 = ((bf16[4,16,16,256]{3,2,1,0:T(8,128)(2,1)}), bf16[4,16,16,256]{3,2,1,0:T(8,128)(2,1)S(1)}, u32[]{:S(2)}, u32[]{:S(2)}) async-start(bf16[4,16,16,256]{3,2,1,0:T(8,128)(2,1)} %copy.32), calls=%async_computation.2 | async-start | bytes 1048576 | tf_op jit(solution)/shard_map/all_to_all | solution.py:107
  182.5 9.2 %bitcast_convert_fusion.1 = bf16[16,352,1024]{2,1,0:T(8,128)(2,1)} fusion(bf16[4,16,16,352]{3,2,0,1:T(8,128)(2,1)S(1)} %copy-done.3, bf16[4,16,16,1024]{3,2,0,1:T(8,128)(2,1)} %all-gather.5.cloned.1.call-done), kind=kOutput, calls=%fused_computation.8 | convolution fusion | flops 743964672 | bytes 14352384 | tf_op jit(solution)/shard_map/secf,secn->efn/dot_general | solution.py:87
  191.8 2.7 %gather_fusion.3 = bf16[768,256]{1,0:T(8,128)(2,1)S(1)} fusion(bf16[1025,256]{1,0:T(8,128)(2,1)S(1)} %concatenate.15, s32[1024]{0:T(1024)S(1)} %pad_clamp_fusion), kind=kCustom, calls=%fused_computation.3 | custom fusion | bytes 789504 | tf_op jit(solution)/shard_map/gather | solution.py:46
  194.6 2.4 %all-to-all-done.1 = bf16[4,16,16,256]{3,2,1,0:T(8,128)(2,1)S(1)} async-done(((bf16[4,16,16,256]{3,2,1,0:T(8,128)(2,1)}), bf16[4,16,16,256]{3,2,1,0:T(8,128)(2,1)S(1)}, u32[]{:S(2)}, u32[]{:S(2)}) %all-to-all-start.1) | async-done | bytes 524320 | tf_op jit(solution)/shard_map/all_to_all | solution.py:107
  197.1 2.7 %gather_fusion.1 = bf16[768,256]{1,0:T(8,128)(2,1)S(1)} fusion(bf16[1025,256]{1,0:T(8,128)(2,1)S(1)} %concatenate.13, s32[1024]{0:T(1024)S(1)} %pad_clamp_fusion), kind=kCustom, calls=%fused_computation.1 | custom fusion | bytes 789504 | tf_op jit(solution)/shard_map/gather | solution.py:46
  200.7 11.0 %psum.7 = f32[128,6]{1,0:T(8,128)S(1)} all-reduce(f32[128,6]{1,0:T(8,128)S(1)} %broadcast_select_fusion), channel_id=1, replica_groups=mesh['groups'=2,'expert'=4,'etp'=4] {'etp'}, use_global_device_ids=true, to_apply=%region_8.9 | all-reduce | flops 768 | bytes 6144 | tf_op jit(solution)/shard_map/psum | solution.py:113
  (68 shorter events, 15.5 us)
Async XLA Ops:
  7.2 60.0 %all-gather.3.cloned.1.call-start = ((), (), s32[]{:S(2)}) async-start(), calls=%async_computation.6 | async-start | bytes 2621440 | tf_op jit(solution)/shard_map/all_gather | solution.py:79
  19.9 21.7 %copy-start.5 = (f32[128,6]{0,1:T(8,128)S(1)}, f32[128,6]{0,1:T(8,128)}, u32[]{:S(2)}) copy-start(f32[128,6]{0,1:T(8,128)} %param.11) | copy-start | bytes 9220
  19.9 21.8 %copy-start.4 = (bf16[128,256]{1,0:T(8,128)(2,1)S(1)}, bf16[128,256]{1,0:T(8,128)(2,1)}, u32[]{:S(2)}) copy-start(bf16[128,256]{1,0:T(8,128)(2,1)} %param.9) | copy-start | bytes 196612
  41.5 47.5 %all-gather.5.cloned.1.call-start = ((), (), s32[]{:S(2)}) async-start(), calls=%async_computation.8 | async-start | bytes 2621440 | tf_op jit(solution)/shard_map/all_gather | solution.py:85
  66.9 75.1 %reduce-scatter.5.cloned.1.call-start = ((), (), s32[]{:S(2)}) async-start(), calls=%async_computation.9 | async-start | bytes 2621440 | tf_op jit(solution)/shard_map/reduce_scatter | solution.py:114
  67.2 9.6 %copy-start = (bf16[4,16,16,1024]{3,2,0,1:T(8,128)(2,1)S(1)}, bf16[4,16,16,1024]{3,2,0,1:T(8,128)(2,1)}, u32[]{:S(2)}) copy-start(bf16[4,16,16,1024]{3,2,0,1:T(8,128)(2,1)} %all-gather.3.cloned.1.call-done) | copy-start | bytes 6291460
  89.0 17.4 %slice-start = ((s8[11534336]{0:T(1024)(128)(4,1)}), s8[4194304]{0:T(1024)(128)(4,1)S(1)}, s32[]{:S(2)}) async-start(s8[11534336]{0:T(1024)(128)(4,1)} %bitcast.140), calls=%async_computation.10 | async-start | bytes 8388608
  89.0 17.4 %slice-start.1 = ((s8[11534336]{0:T(1024)(128)(4,1)}), s8[3145728]{0:T(1024)(128)(4,1)S(1)}, s32[]{:S(2)}) async-start(s8[11534336]{0:T(1024)(128)(4,1)} %bitcast.140), calls=%async_computation.11 | async-start | bytes 6291456
  99.6 6.9 %slice-start.2 = ((s8[11534336]{0:T(1024)(128)(4,1)}), s8[4194304]{0:T(1024)(128)(4,1)S(1)}, s32[]{:S(2)}) async-start(s8[11534336]{0:T(1024)(128)(4,1)} %bitcast.140), calls=%async_computation.12 | async-start | bytes 8388608
  99.6 6.9 %copy-start.1 = (bf16[4,16,16,352]{3,2,0,1:T(8,128)(2,1)S(1)}, bf16[4,16,16,352]{3,2,0,1:T(8,128)(2,1)}, u32[]{:S(2)}) copy-start(bf16[4,16,16,352]{3,2,0,1:T(8,128)(2,1)} %get-tuple-element.24) | copy-start | bytes 2162692
  110.4 1.1 copy-start.2
  110.4 65.6 %reduce-scatter.3.cloned.1.call-start = ((), (), s32[]{:S(2)}) async-start(), calls=%async_computation.7 | async-start | bytes 2621440 | tf_op jit(solution)/shard_map/reduce_scatter | solution.py:104
  143.9 34.0 %all-to-all-start.3 = ((bf16[4,16,16,256]{3,2,1,0:T(8,128)(2,1)}), bf16[4,16,16,256]{3,2,1,0:T(8,128)(2,1)S(1)}, u32[]{:S(2)}, u32[]{:S(2)}) async-start(bf16[4,16,16,256]{3,2,1,0:T(8,128)(2,1)} %copy.34), calls=%async_computation.5 | async-start | bytes 1048576 | tf_op jit(solution)/shard_map/all_to_all | solution.py:117
  165.6 16.9 %copy-start.3 = (bf16[4,16,16,352]{3,2,0,1:T(8,128)(2,1)S(1)}, bf16[4,16,16,352]{3,2,0,1:T(8,128)(2,1)}, u32[]{:S(2)}) copy-start(bf16[4,16,16,352]{3,2,0,1:T(8,128)(2,1)} %get-tuple-element.25) | copy-start | bytes 2162692
  177.9 19.1 %all-to-all-start.1 = ((bf16[4,16,16,256]{3,2,1,0:T(8,128)(2,1)}), bf16[4,16,16,256]{3,2,1,0:T(8,128)(2,1)S(1)}, u32[]{:S(2)}, u32[]{:S(2)}) async-start(bf16[4,16,16,256]{3,2,1,0:T(8,128)(2,1)} %copy.32), calls=%async_computation.2 | async-start | bytes 1048576 | tf_op jit(solution)/shard_map/all_to_all | solution.py:107
Sparse Core Ops, SparseCore 0:
  41.7 21.9 all-gather.2
  67.1 21.9 all-gather.4
  110.5 31.4 reduce-scatter.4
  144.5 31.4 reduce-scatter.2
where the time goes:
time: 220 us
  matrix products  69.9 us (32%)
  blocking collectives  48.2 us (22%)
  local copies, waits for them, and re-layouts  48.1 us (22%)
  waiting for transfers between devices  26.5 us (12%)
  between operations  14.1 us (6%)
  starting transfers between devices  9.76 us (4%)
  other arithmetic  2.95 us (1%)
    all_to_all x1, blocking collectives, body(): lax.all_to_all(send_in, 'expert', split_axis=0, concat_axis=0, tiled=True)  20.7 us
    convert_element_type x1, local copies, waits for them, and re-layouts, body(): weight_grads[1].astype(jnp.bfloat16)  17.2 us
    all_to_all x1, blocking collectives, body(): lax.all_to_all(send_grad, 'expert', split_axis=0, concat_axis=0, tiled=True)  16.6 us
    dot_general x1, matrix products, body(): jnp.einsum('secn,gsecf->genf', lax.all_gather(share_in, 'etp', axis=3, ti...  12.4 us
    psum x1, blocking collectives, body(): gate_value_grad = lax.psum(dot_part, 'etp')  11 us
    dot_general x1, matrix products, body(): jnp.einsum('secn,efn->secf', piece, down_weight, preferred_element_type=j...  10.6 us
    reduce_scatter x1, waiting for transfers between devices, body(): lax.psum_scatter(out_part.astype(jnp.bfloat16), 'etp', scatter_dimension=...  10.4 us
    reduce_scatter x1, waiting for transfers between devices, body(): lax.psum_scatter(back_part.astype(jnp.bfloat16), 'etp', scatter_dimension...  10 us
  transfers between devices with their start and end apart: 6, of which 4 were waited for; matrix products, arithmetic and copies ran while one was open for 37% of the time, Pallas kernels for 0%

commit v1 on v0

--- a/solution.py
+++ b/solution.py
@@ -1,10 +1,231 @@
+import functools
+
 import jax
 import jax.numpy as jnp
 from jax import lax
+from jax.experimental import pallas as pl
+from jax.experimental.pallas import tpu as pltpu
 from jax.sharding import PartitionSpec as P
 
 CAP = 16
 BLK = 4
+EXTRA = 16
+F32 = jnp.float32
+BF16 = jnp.bfloat16
+
+
+def nn(a, b):
+    return lax.dot_general(a, b, (((1,), (0,)), ((), ())), preferred_element_type=F32)
+
+
+def nt(a, b):
+    return lax.dot_general(a, b, (((1,), (1,)), ((), ())), preferred_element_type=F32)
+
+
+def tn(a, b):
+    return lax.dot_general(a, b, (((0,), (0,)), ((), ())), preferred_element_type=F32)
+
+
+def routing_rows(expert_ids, gate_values):
+    choose = expert_ids.shape[1]
+    high = lax.reduce_precision(gate_values, exponent_bits=8, mantissa_bits=7)
+    low = lax.reduce_precision(gate_values - high, exponent_bits=8, mantissa_bits=7)
+    pad = ((0, 8 - choose), (0, 0))
+    top = jnp.concatenate([jnp.pad(expert_ids.T.astype(F32), pad), jnp.pad(high.T, pad)], axis=1)
+    bottom = jnp.concatenate([jnp.pad(low.T, pad), jnp.zeros_like(jnp.pad(low.T, pad))], axis=1)
+    return jnp.concatenate([top, bottom], axis=0).astype(BF16)
+
+
+def forward_kernel(
+    choose, block_ref, limit_ref, expert_ref, gate_ref, up_ref, down_ref,
+    home_ref, rows_ref, grads_ref, p_ref, q_ref, a_ref,
+    onehot, slot_gate, out_rows, back_rows, dots,
+):
+    step = pl.program_id(0)
+    experts = pl.num_programs(0)
+    sources, slots, tokens = onehot.shape
+    shares = block_ref.shape[0] // sources
+    width = block_ref.shape[2]
+
+    def routing(s):
+        info = block_ref[s * shares, 2 * tokens:2 * tokens + EXTRA, :].astype(F32)
+        ids = info[0:choose, 0:tokens]
+        gates = info[0:choose, tokens:2 * tokens] + info[8:8 + choose, 0:tokens]
+        return ids, gates
+
+    @pl.when(step == 0)
+    def _():
+        row = lax.broadcasted_iota(jnp.int32, (tokens, tokens), 0)
+        col = lax.broadcasted_iota(jnp.int32, (tokens, tokens), 1)
+        before = jnp.where(row < col, 1.0, 0.0).astype(BF16)
+        mine = expert_ref[...]
+        limit = limit_ref[...]
+        place = lax.broadcasted_iota(jnp.int32, (slots // CAP, CAP, tokens), 1).astype(F32)
+        for s in range(sources):
+            ids, gates = routing(s)
+            named = jnp.zeros((slots // CAP, tokens), F32)
+            gate = jnp.zeros((slots // CAP, tokens), F32)
+            for k in range(choose):
+                hit = ids[k:k + 1, :] == mine
+                named = named + jnp.where(hit, 1.0, 0.0)
+                gate = gate + jnp.where(hit, gates[k:k + 1, :], 0.0)
+            rank = nn(named.astype(BF16), before)
+            rank = jnp.where((named > 0.5) & (rank < limit), rank, -1.0)
+            chosen = jnp.where(rank[:, None, :] == place, 1.0, 0.0)
+            gate_of = jnp.sum(chosen * gate[:, None, :], axis=2, keepdims=True)
+            slot_gate[:, s * CAP:(s + 1) * CAP, :] = jnp.broadcast_to(gate_of, chosen.shape)
+            table = chosen.reshape(slots, tokens).astype(BF16)
+            onehot[s] = table
+            for q in range(shares):
+                for half, ref in ((0, rows_ref), (1, grads_ref)):
+                    part = block_ref[s * shares + q, half * tokens:(half + 1) * tokens, :]
+                    picked = nn(table, part).astype(BF16).reshape(slots // CAP, CAP, width)
+                    ref[:, s * CAP:(s + 1) * CAP, q * width:(q + 1) * width] = picked
+
+    x = rows_ref[step]
+    y = grads_ref[step]
+    gate = slot_gate[step][:, 0:1]
+    hidden_gate = nt(x, gate_ref[0])
+    hidden_up = nt(x, up_ref[0])
+    grad = nt(y, down_ref[0])
+    sigma = jax.nn.sigmoid(hidden_gate)
+    silu = hidden_gate * sigma
+    activ = (silu * hidden_up).astype(BF16).astype(F32)
+    dots[step] = jnp.broadcast_to(jnp.sum(activ * grad, axis=1, keepdims=True), dots.shape[1:])
+    scaled = (activ * gate).astype(BF16)
+    grad = grad * gate
+    gate_part = (grad * hidden_up * sigma * (1.0 + hidden_gate * (1.0 - sigma))).astype(BF16)
+    up_part = (grad * silu).astype(BF16)
+    a_ref[0] = scaled
+    p_ref[0] = gate_part
+    q_ref[0] = up_part
+    out = nn(scaled, down_ref[0]).astype(BF16)
+    back = ((nn(gate_part, gate_ref[0]) + nn(up_part, up_ref[0])) * gate).astype(BF16)
+    for s in range(sources):
+        at = pl.ds(pl.multiple_of(step * CAP, CAP), CAP)
+        out_rows[s, at, :] = out[s * CAP:(s + 1) * CAP]
+        back_rows[s, at, :] = back[s * CAP:(s + 1) * CAP]
+
+    @pl.when(step == experts - 1)
+    def _():
+        mine = expert_ref[...]
+        for s in range(sources):
+            table = onehot[s]
+            for half, ref in ((0, out_rows), (1, back_rows)):
+                total = tn(table, ref[s]).astype(BF16)
+                for q in range(shares):
+                    home_ref[s * shares + q, half * tokens:(half + 1) * tokens, :] = total[:, q * width:(q + 1) * width]
+            ids, _ = routing(s)
+            chosen = table.astype(F32).reshape(slots // CAP, CAP, tokens)
+            share = jnp.sum(chosen * dots[:, s * CAP:(s + 1) * CAP, :], axis=1)
+            rows = [jnp.sum(jnp.where(ids[k:k + 1, :] == mine, share, 0.0), axis=0, keepdims=True) for k in range(choose)]
+            rows = jnp.concatenate(rows + [jnp.zeros((8 - choose, tokens), F32)], axis=0)
+            rows = jnp.concatenate([rows, jnp.zeros_like(rows)], axis=0)
+            rows = jnp.concatenate([rows, jnp.zeros((EXTRA, width - tokens), F32)], axis=1).astype(BF16)
+            for q in range(shares):
+                home_ref[s * shares + q, 2 * tokens:2 * tokens + EXTRA, :] = rows
+
+
+def grads_kernel(rows_ref, grads_ref, p_ref, q_ref, a_ref, gate_grad, up_grad, down_grad):
+    x = rows_ref[0]
+    gate_grad[0] = tn(p_ref[0], x).astype(BF16)
+    up_grad[0] = tn(q_ref[0], x).astype(BF16)
+    down_grad[0] = tn(a_ref[0], grads_ref[0]).astype(BF16)
+
+
+def gathered_body(
+    hidden_in, out_grad, expert_ids, gate_values, capacity_blocks, gate_weight, up_weight, down_weight
+):
+    sources = lax.axis_size("expert")
+    shares = lax.axis_size("etp")
+    tokens, width = hidden_in.shape
+    choose = expert_ids.shape[1]
+    local_experts, units, model = down_weight.shape
+    slots = local_experts * CAP
+    rows = sources * CAP
+    first = lax.axis_index("expert") * local_experts
+    limit = lax.dynamic_slice(capacity_blocks, (first,), (local_experts,)).astype(F32)[:, None] * BLK
+    mine = (first + jnp.arange(local_experts, dtype=jnp.int32)).astype(F32)[:, None]
+    gate_t = jnp.swapaxes(gate_weight, 1, 2)
+    up_t = jnp.swapaxes(up_weight, 1, 2)
+    packed = jnp.concatenate([hidden_in, out_grad, routing_rows(expert_ids, gate_values)], axis=0)
+    blocks = lax.all_gather(packed, ("expert", "etp"), axis=0, tiled=False)
+
+    per_expert = lambda *shape: pl.BlockSpec((1,) + shape, lambda e: (e, 0, 0))
+    whole = lambda *shape: pl.BlockSpec(shape, lambda e: (0,) * len(shape))
+    height = 2 * tokens + EXTRA
+    home, x_rows, y_rows, gate_part, up_part, scaled = pl.pallas_call(
+        functools.partial(forward_kernel, choose),
+        grid=(local_experts,),
+        in_specs=[
+            whole(sources * shares, height, width),
+            whole(local_experts, 1),
+            whole(local_experts, 1),
+            per_expert(units, model),
+            per_expert(units, model),
+            per_expert(units, model),
+        ],
+        out_specs=[
+            whole(sources * shares, height, width),
+            whole(local_experts, rows, model),
+            whole(local_experts, rows, model),
+            per_expert(rows, units),
+            per_expert(rows, units),
+            per_expert(rows, units),
+        ],
+        out_shape=[
+            jax.ShapeDtypeStruct((sources * shares, height, width), BF16),
+            jax.ShapeDtypeStruct((local_experts, rows, model), BF16),
+            jax.ShapeDtypeStruct((local_experts, rows, model), BF16),
+            jax.ShapeDtypeStruct((local_experts, rows, units), BF16),
+            jax.ShapeDtypeStruct((local_experts, rows, units), BF16),
+            jax.ShapeDtypeStruct((local_experts, rows, units), BF16),
+        ],
+        scratch_shapes=[
+            pltpu.VMEM((sources, slots, tokens), BF16),
+            pltpu.VMEM((local_experts, rows, tokens), F32),
+            pltpu.VMEM((sources, slots, model), BF16),
+            pltpu.VMEM((sources, slots, model), BF16),
+            pltpu.VMEM((local_experts, rows, tokens), F32),
+        ],
+        compiler_params=pltpu.CompilerParams(vmem_limit_bytes=48 * 1024 * 1024),
+        cost_estimate=pl.CostEstimate(
+            flops=2 * 6 * local_experts * rows * units * model,
+            bytes_accessed=3 * 2 * local_experts * units * model,
+            transcendentals=local_experts * rows * units,
+        ),
+    )(blocks, limit, mine, gate_t, up_t, down_weight)
+
+    total = lax.psum_scatter(home, ("expert", "etp"), scatter_dimension=0, tiled=False)
+
+    gate_grad, up_grad, down_grad = pl.pallas_call(
+        grads_kernel,
+        grid=(local_experts,),
+        in_specs=[
+            per_expert(rows, model),
+            per_expert(rows, model),
+            per_expert(rows, units),
+            per_expert(rows, units),
+            per_expert(rows, units),
+        ],
+        out_specs=[per_expert(units, model)] * 3,
+        out_shape=[jax.ShapeDtypeStruct((local_experts, units, model), BF16)] * 3,
+        compiler_params=pltpu.CompilerParams(vmem_limit_bytes=32 * 1024 * 1024),
+        cost_estimate=pl.CostEstimate(
+            flops=2 * 3 * local_experts * rows * units * model,
+            bytes_accessed=3 * 2 * local_experts * units * model,
+            transcendentals=0,
+        ),
+    )(x_rows, y_rows, gate_part, up_part, scaled)
+
+    return (
+        total[0:tokens],
+        total[tokens:2 * tokens],
+        total[2 * tokens:2 * tokens + choose, 0:tokens].astype(F32).T,
+        jnp.swapaxes(gate_grad, 1, 2),
+        jnp.swapaxes(up_grad, 1, 2),
+        down_grad,
+    )
 
 
 def slot_layout(expert_ids, capacity_blocks):
@@ -47,7 +268,7 @@
     return (jnp.einsum("tk,tkw->tw", weights, picked), picked)
 
 
-def body(
+def dispatched_body(
     hidden_in,
     out_grad,
     expert_ids,
@@ -126,6 +347,13 @@
     )
 
 
+def body(*operands):
+    hidden_in, gate_weight = operands[0], operands[5]
+    if hidden_in.shape[0] <= gate_weight.shape[0] * CAP:
+        return gathered_body(*operands)
+    return dispatched_body(*operands)
+
+
 def solution(mesh):
     in_specs = (
         P(("groups", "expert"), "etp"),

time: 220 us -> 158 us (0.72)
  matrix products: 69.9 us -> 0 us
  waiting for transfers between devices: 26.5 us -> 86.5 us
  blocking collectives: 48.2 us -> 0 us
  Pallas kernels: 0 us -> 44.6 us
  local copies, waits for them, and re-layouts: 48.1 us -> 7.22 us
  starting transfers between devices: 9.76 us -> 0.08 us
    dot_general x11 -> x0, matrix products: 69.9 us -> none  [the longest x1 12.4 us: body(): jnp.einsum('secn,gsecf->genf', lax.all_gather(share_in, 'etp', axis=3, ti...]
    pallas_call x0 -> x2, Pallas kernels: none -> 44.6 us  [the longest x1 29.1 us: gathered_body(): pl.pallas_call(functools.partial(forward_kernel, choose), grid=(local_exp...]
    all_gather x2 -> x1, waiting for transfers between devices: 3.59 us -> 44.3 us  [gathered_body(): blocks = lax.all_gather(packed, ('expert', 'etp'), axis=0, tiled=False)]
    all_to_all x2 -> x0, blocking collectives: 37.3 us -> none  [the longest x1 20.7 us: body(): lax.all_to_all(send_in, 'expert', split_axis=0, concat_axis=0, tiled=True)]
    reduce_scatter x2 -> x1, waiting for transfers between devices: 20.4 us -> 42.2 us  [gathered_body(): lax.psum_scatter(home, ('expert', 'etp'), scatter_dimension=0, tiled=False)]
    convert_element_type x2 -> x0, local copies, waits for them, and re-layouts: 17.8 us -> none  [the longest x1 17.2 us: body(): weight_grads[1].astype(jnp.bfloat16)]
    gather x6 -> x0, local copies, waits for them, and re-layouts: 13.5 us -> none  [the longest x2 7.88 us: outgoing(): picked = padded[owners]]
    psum x1 -> x0, blocking collectives: 11 us -> none  [body(): gate_value_grad = lax.psum(dot_part, 'etp')]
  transfers between devices with their start and end apart: 6 -> 2, of which waited for: 4 -> 2; matrix products, arithmetic and copies ran while one was open for 37% -> 1% of each run, Pallas kernels for 0% -> 10%
where the time goes in v1:
time: 158 us; the launch traced here: 157 us
  waiting for transfers between devices  86.5 us (55%)
  Pallas kernels  44.6 us (28%)
  between operations  14.1 us (9%)
  local copies, waits for them, and re-layouts  7.22 us (5%)
  other arithmetic  4.92 us (3%)
    all_gather x1, waiting for transfers between devices, gathered_body(): blocks = lax.all_gather(packed, ('expert', 'etp'), axis=0, tiled=False)  44.3 us
    reduce_scatter x1, waiting for transfers between devices, gathered_body(): lax.psum_scatter(home, ('expert', 'etp'), scatter_dimension=0, tiled=False)  42.2 us
    pallas_call x1, Pallas kernels, gathered_body(): pl.pallas_call(functools.partial(forward_kernel, choose), grid=(local_exp...  29.1 us
    pallas_call x1, Pallas kernels, gathered_body(): pl.pallas_call(grads_kernel, grid=(local_experts,), in_specs=[per_expert(...  15.6 us
    unnamed x10, local copies, waits for them, and re-layouts  5.61 us
  transfers between devices with their start and end apart: 2, of which 2 were waited for; matrix products, arithmetic and copies ran while one was open for 1% of the time, Pallas kernels for 10%

profile of v1, /device:TPU:0, one launch (start us, length us, event | category | flops | bytes accessed | tf_op | source)
XLA Modules:
  0.0 157.4 jit_solution(15094135006916543857)
XLA Ops:
  7.2 0.0 all-gather.3.cloned.1.call-start
  7.2 0.7 fusion.13
  7.9 0.7 fusion.15
  8.6 1.5 fusion.6
  10.1 0.0 all-gather.3.cloned.1.call-update
  10.2 0.0 reduce-scatter.2.cloned.1.call-start
  10.2 0.7 multiply_bitcast_fusion
  10.9 0.1 copy.14.limit_ref
  11.0 44.3 %all-gather.3.cloned.1.call-done = bf16[4352,256]{1,0:T(8,128)(2,1)} async-done(((bf16[272,256]{1,0:T(8,128)(2,1)}), bf16[4352,256]{1,0:T(8,128)(2,1)}) %all-gather.3.cloned.1.call-update) | async-done | bytes 2228240 | tf_op jit(solution)/shard_map/all_gather | solution.py:152
  55.4 29.1 %shard_map.127 = (bf16[16,272,256]{2,1,0:T(8,128)(2,1)}, bf16[16,64,1024]{2,1,0:T(8,128)(2,1)S(1)}, bf16[16,64,1024]{2,1,0:T(8,128)(2,1)}, bf16[16,64,352]{2,1,0...) custom-call(bf16[16,272,256]{2,1,0:T(8,128)(2,1)} %bitcast.22, ...), custom_call_target="tpu_custom_call" | custom-call | flops 4429185024 | bytes 34603008 | tf_op jit(solution)/shard_map/pallas_call | solution.py:157
  84.4 0.0 copy-start.1
  84.4 0.9 copy-done.1
  85.3 0.0 copy-start.3
  85.3 0.9 copy-done.3
  86.2 0.0 reduce-scatter.2.cloned.1.call-update
  86.2 0.0 copy-start
  86.2 1.6 %copy-done = bf16[16,64,1024]{2,1,0:T(8,128)(2,1)S(1)} copy-done((bf16[16,64,1024]{2,1,0:T(8,128)(2,1)S(1)}, bf16[16,64,1024]{2,1,0:T(8,128)(2,1)}, u32[]{:S(2)}) %copy-start) | copy-done | bytes 2097176
  87.8 0.0 copy-start.2
  87.8 1.1 copy-done.2
  88.9 1.1 copy-done.4
  90.1 15.6 %shard_map.128 = (bf16[16,352,1024]{2,1,0:T(8,128)(2,1)}, bf16[16,352,1024]{2,1,0:T(8,128)(2,1)}, bf16[16,352,1024]{2,1,0:T(8,128)(2,1)}) custom-call(bf16[16,64,1024]{2,1,0:T(8,128)(2,1)S(1)} %get-tuple-element.16.rows_ref, bf16[16,64,1024]{2,1,0:T(8,128)(2,1)S(1)} %copy-done, bf16[16,64,352]{2,1,0:T(8,128)(2,1)S(1)} %get-tuple-element.18.p_ref, ...), custom_call_target="tpu_custom_call" | custom-call | flops 2214592512 | bytes 34603008 | tf_op jit(solution)/shard_map/pallas_call | solution.py:201
  105.6 42.2 %reduce-scatter.2.cloned.1.call-done = bf16[1,272,256]{2,1,0:T(8,128)(2,1)} async-done(((bf16[16,272,256]{2,1,0:T(8,128)(2,1)}), bf16[1,272,256]{2,1,0:T(8,128)(2,1)}) %reduce-scatter.2.cloned.1.call-update) | async-done | bytes 139280 | tf_op jit(solution)/shard_map/reduce_scatter | solution.py:199
  147.8 1.3 convert_bitcast_fusion
  149.1 1.5 slice_bitcast_fusion
  (2 shorter events, 0.0 us)
Async XLA Ops:
  7.2 48.2 %all-gather.3.cloned.1.call-start = ((), (), s32[]{:S(2)}) async-start(), calls=%async_computation.2 | async-start | bytes 2367488 | tf_op jit(solution)/shard_map/all_gather | solution.py:152
  10.2 137.6 %reduce-scatter.2.cloned.1.call-start = ((), (), s32[]{:S(2)}) async-start(), calls=%async_computation.1 | async-start | bytes 2367488 | tf_op jit(solution)/shard_map/reduce_scatter | solution.py:199
  84.4 0.9 copy-start.1
  85.3 0.9 copy-start.3
  86.2 1.6 %copy-start = (bf16[16,64,1024]{2,1,0:T(8,128)(2,1)S(1)}, bf16[16,64,1024]{2,1,0:T(8,128)(2,1)}, u32[]{:S(2)}) copy-start(bf16[16,64,1024]{2,1,0:T(8,128)(2,1)} %get-tuple-element.17.grads_ref) | copy-start | bytes 6291460
  87.8 1.1 copy-start.2
  88.9 1.1 copy-start.4
Sparse Core Ops, SparseCore 0:
  10.9 44.4 all-gather.2
  86.3 61.4 reduce-scatter.1

commit v2 on v1

--- a/solution.py
+++ b/solution.py
@@ -37,18 +37,24 @@
 
 
 def forward_kernel(
-    choose, block_ref, limit_ref, expert_ref, gate_ref, up_ref, down_ref,
-    home_ref, rows_ref, grads_ref, p_ref, q_ref, a_ref,
-    onehot, slot_gate, out_rows, back_rows, dots,
+    choose, sources, shares, pair, me_ref, limit_ref, expert_ref, *refs,
 ):
+    blocks, refs = refs[:sources * shares], refs[sources * shares:]
+    (
+        gate_ref, up_ref, down_ref,
+        out_keep, out_send, back_keep, back_send, rows_ref, grads_ref, p_ref, q_ref, a_ref,
+        onehot, slot_gate, out_rows, back_rows, dots,
+    ) = refs
     step = pl.program_id(0)
-    experts = pl.num_programs(0)
-    sources, slots, tokens = onehot.shape
-    shares = block_ref.shape[0] // sources
-    width = block_ref.shape[2]
+    slots, tokens = onehot.shape[1:]
+    width = blocks[0].shape[1]
+    me = me_ref[0]
+
+    def columns(mask):
+        return pl.ds(pl.multiple_of(lax.bitwise_xor(me, mask) * width, width), width)
 
     def routing(s):
-        info = block_ref[s * shares, 2 * tokens:2 * tokens + EXTRA, :].astype(F32)
+        info = blocks[s * shares][2 * tokens:2 * tokens + EXTRA, :].astype(F32)
         ids = info[0:choose, 0:tokens]
         gates = info[0:choose, tokens:2 * tokens] + info[8:8 + choose, 0:tokens]
         return ids, gates
@@ -78,59 +84,100 @@
             onehot[s] = table
             for q in range(shares):
                 for half, ref in ((0, rows_ref), (1, grads_ref)):
-                    part = block_ref[s * shares + q, half * tokens:(half + 1) * tokens, :]
+                    part = blocks[s * shares + q][half * tokens:(half + 1) * tokens, :]
                     picked = nn(table, part).astype(BF16).reshape(slots // CAP, CAP, width)
-                    ref[:, s * CAP:(s + 1) * CAP, q * width:(q + 1) * width] = picked
-
-    x = rows_ref[step]
-    y = grads_ref[step]
-    gate = slot_gate[step][:, 0:1]
-    hidden_gate = nt(x, gate_ref[0])
-    hidden_up = nt(x, up_ref[0])
-    grad = nt(y, down_ref[0])
-    sigma = jax.nn.sigmoid(hidden_gate)
-    silu = hidden_gate * sigma
-    activ = (silu * hidden_up).astype(BF16).astype(F32)
-    dots[step] = jnp.broadcast_to(jnp.sum(activ * grad, axis=1, keepdims=True), dots.shape[1:])
-    scaled = (activ * gate).astype(BF16)
-    grad = grad * gate
-    gate_part = (grad * hidden_up * sigma * (1.0 + hidden_gate * (1.0 - sigma))).astype(BF16)
-    up_part = (grad * silu).astype(BF16)
-    a_ref[0] = scaled
-    p_ref[0] = gate_part
-    q_ref[0] = up_part
-    out = nn(scaled, down_ref[0]).astype(BF16)
-    back = ((nn(gate_part, gate_ref[0]) + nn(up_part, up_ref[0])) * gate).astype(BF16)
-    for s in range(sources):
-        at = pl.ds(pl.multiple_of(step * CAP, CAP), CAP)
-        out_rows[s, at, :] = out[s * CAP:(s + 1) * CAP]
-        back_rows[s, at, :] = back[s * CAP:(s + 1) * CAP]
-
-    @pl.when(step == experts - 1)
+                    ref[:, s * CAP:(s + 1) * CAP, columns(q)] = picked
+
+    for turn in range(pair):
+        e = step * pair + turn
+        x = rows_ref[e]
+        y = grads_ref[e]
+        gate = slot_gate[e][:, 0:1]
+        hidden_gate = nt(x, gate_ref[turn])
+        hidden_up = nt(x, up_ref[turn])
+        grad = nt(y, down_ref[turn])
+        sigma = jax.nn.sigmoid(hidden_gate)
+        silu = hidden_gate * sigma
+        activ = (silu * hidden_up).astype(BF16).astype(F32)
+        dots[e] = jnp.broadcast_to(jnp.sum(activ * grad, axis=1, keepdims=True), dots.shape[1:])
+        scaled = (activ * gate).astype(BF16)
+        grad = grad * gate
+        gate_part = (grad * hidden_up * sigma * (1.0 + hidden_gate * (1.0 - sigma))).astype(BF16)
+        up_part = (grad * silu).astype(BF16)
+        a_ref[turn] = scaled
+        p_ref[turn] = gate_part
+        q_ref[turn] = up_part
+        out = nn(scaled, down_ref[turn]).astype(BF16)
+        back = ((nn(gate_part, gate_ref[turn]) + nn(up_part, up_ref[turn])) * gate).astype(BF16)
+        for s in range(sources):
+            at = pl.ds(pl.multiple_of(e * CAP, CAP), CAP)
+            out_rows[s, at, :] = out[s * CAP:(s + 1) * CAP]
+            back_rows[s, at, :] = back[s * CAP:(s + 1) * CAP]
+
+    @pl.when(step == pl.num_programs(0) - 1)
     def _():
         mine = expert_ref[...]
         for s in range(sources):
             table = onehot[s]
-            for half, ref in ((0, out_rows), (1, back_rows)):
-                total = tn(table, ref[s]).astype(BF16)
-                for q in range(shares):
-                    home_ref[s * shares + q, half * tokens:(half + 1) * tokens, :] = total[:, q * width:(q + 1) * width]
             ids, _ = routing(s)
             chosen = table.astype(F32).reshape(slots // CAP, CAP, tokens)
             share = jnp.sum(chosen * dots[:, s * CAP:(s + 1) * CAP, :], axis=1)
             rows = [jnp.sum(jnp.where(ids[k:k + 1, :] == mine, share, 0.0), axis=0, keepdims=True) for k in range(choose)]
-            rows = jnp.concatenate(rows + [jnp.zeros((8 - choose, tokens), F32)], axis=0)
-            rows = jnp.concatenate([rows, jnp.zeros_like(rows)], axis=0)
+            rows = jnp.concatenate(rows + [jnp.zeros((EXTRA - choose, tokens), F32)], axis=0)
             rows = jnp.concatenate([rows, jnp.zeros((EXTRA, width - tokens), F32)], axis=1).astype(BF16)
             for q in range(shares):
-                home_ref[s * shares + q, 2 * tokens:2 * tokens + EXTRA, :] = rows
-
-
-def grads_kernel(rows_ref, grads_ref, p_ref, q_ref, a_ref, gate_grad, up_grad, down_grad):
-    x = rows_ref[0]
-    gate_grad[0] = tn(p_ref[0], x).astype(BF16)
-    up_grad[0] = tn(q_ref[0], x).astype(BF16)
-    down_grad[0] = tn(a_ref[0], grads_ref[0]).astype(BF16)
+                out_home, back_home = (out_send, back_send) if q % 2 else (out_keep, back_keep)
+                out_home[q // 2, s, 0:tokens, :] = tn(table, out_rows[s, :, columns(q)]).astype(BF16)
+                out_home[q // 2, s, tokens:tokens + EXTRA, :] = rows
+                back_home[q // 2, s] = tn(table, back_rows[s, :, columns(q)]).astype(BF16)
+
+
+def product_kernel(left_ref, right_ref, out_ref):
+    for turn in range(out_ref.shape[0]):
+        out_ref[turn] = tn(left_ref[turn], right_ref[turn]).astype(BF16)
+
+
+def weight_grad(left, right, pair):
+    experts, rows, units = left.shape
+    model = right.shape[2]
+    block = lambda *shape: pl.BlockSpec((pair,) + shape, lambda e: (e, 0, 0))
+    return pl.pallas_call(
+        product_kernel,
+        grid=(experts // pair,),
+        in_specs=[block(rows, units), block(rows, model)],
+        out_specs=block(units, model),
+        out_shape=jax.ShapeDtypeStruct((experts, units, model), BF16),
+        compiler_params=pltpu.CompilerParams(vmem_limit_bytes=56 * 1024 * 1024),
+        cost_estimate=pl.CostEstimate(
+            flops=2 * experts * rows * units * model,
+            bytes_accessed=2 * experts * (units * model + rows * model + rows * units),
+            transcendentals=0,
+        ),
+    )(left, right)
+
+
+def swap(array, bit):
+    count = lax.axis_size("etp")
+    return lax.ppermute(array, "etp", [(i, i ^ bit) for i in range(count)])
+
+
+def shift(array, by):
+    count = lax.axis_size("expert")
+    return lax.ppermute(array, "expert", [(i, (i + by) % count) for i in range(count)])
+
+
+def gather_blocks(block):
+    sources = lax.axis_size("expert")
+    blocks = []
+    for s in range(sources):
+        held = shift(block, s) if s else block
+        across = swap(held, 2)
+        blocks = blocks + [held, swap(held, 1), across, swap(across, 1)]
+    return blocks
+
+
+def add(a, b):
+    return (a.astype(F32) + b.astype(F32)).astype(BF16)
 
 
 def gathered_body(
@@ -143,44 +190,39 @@
     local_experts, units, model = down_weight.shape
     slots = local_experts * CAP
     rows = sources * CAP
+    pair = 2 if local_experts % 2 == 0 else 1
+    me = lax.axis_index("etp").astype(jnp.int32)[None]
     first = lax.axis_index("expert") * local_experts
     limit = lax.dynamic_slice(capacity_blocks, (first,), (local_experts,)).astype(F32)[:, None] * BLK
     mine = (first + jnp.arange(local_experts, dtype=jnp.int32)).astype(F32)[:, None]
     gate_t = jnp.swapaxes(gate_weight, 1, 2)
     up_t = jnp.swapaxes(up_weight, 1, 2)
     packed = jnp.concatenate([hidden_in, out_grad, routing_rows(expert_ids, gate_values)], axis=0)
-    blocks = lax.all_gather(packed, ("expert", "etp"), axis=0, tiled=False)
-
-    per_expert = lambda *shape: pl.BlockSpec((1,) + shape, lambda e: (e, 0, 0))
+    blocks = gather_blocks(packed)
+
+    per_expert = lambda *shape: pl.BlockSpec((pair,) + shape, lambda e: (e, 0, 0))
     whole = lambda *shape: pl.BlockSpec(shape, lambda e: (0,) * len(shape))
-    height = 2 * tokens + EXTRA
-    home, x_rows, y_rows, gate_part, up_part, scaled = pl.pallas_call(
-        functools.partial(forward_kernel, choose),
-        grid=(local_experts,),
+    out_shapes = [
+        (2, sources, tokens + EXTRA, width),
+        (2, sources, tokens + EXTRA, width),
+        (2, sources, tokens, width),
+        (2, sources, tokens, width),
+        (local_experts, rows, model),
+        (local_experts, rows, model),
+    ]
+    out_keep, out_send, back_keep, back_send, x_rows, y_rows, gate_part, up_part, scaled = pl.pallas_call(
+        functools.partial(forward_kernel, choose, sources, shares, pair),
+        grid=(local_experts // pair,),
         in_specs=[
-            whole(sources * shares, height, width),
+            pl.BlockSpec(memory_space=pltpu.SMEM),
             whole(local_experts, 1),
             whole(local_experts, 1),
-            per_expert(units, model),
-            per_expert(units, model),
-            per_expert(units, model),
-        ],
-        out_specs=[
-            whole(sources * shares, height, width),
-            whole(local_experts, rows, model),
-            whole(local_experts, rows, model),
-            per_expert(rows, units),
-            per_expert(rows, units),
-            per_expert(rows, units),
-        ],
-        out_shape=[
-            jax.ShapeDtypeStruct((sources * shares, height, width), BF16),
-            jax.ShapeDtypeStruct((local_experts, rows, model), BF16),
-            jax.ShapeDtypeStruct((local_experts, rows, model), BF16),
-            jax.ShapeDtypeStruct((local_experts, rows, units), BF16),
-            jax.ShapeDtypeStruct((local_experts, rows, units), BF16),
-            jax.ShapeDtypeStruct((local_experts, rows, units), BF16),
-        ],
+        ]
+        + [whole(2 * tokens + EXTRA, width)] * (sources * shares)
+        + [per_expert(units, model)] * 3,
+        out_specs=[whole(*shape) for shape in out_shapes] + [per_expert(rows, units)] * 3,
+        out_shape=[jax.ShapeDtypeStruct(shape, BF16) for shape in out_shapes]
+        + [jax.ShapeDtypeStruct((local_experts, rows, units), BF16)] * 3,
         scratch_shapes=[
             pltpu.VMEM((sources, slots, tokens), BF16),
             pltpu.VMEM((local_experts, rows, tokens), F32),
@@ -194,34 +236,25 @@
             bytes_accessed=3 * 2 * local_experts * units * model,
             transcendentals=local_experts * rows * units,
         ),
-    )(blocks, limit, mine, gate_t, up_t, down_weight)
-
-    total = lax.psum_scatter(home, ("expert", "etp"), scatter_dimension=0, tiled=False)
-
-    gate_grad, up_grad, down_grad = pl.pallas_call(
-        grads_kernel,
-        grid=(local_experts,),
-        in_specs=[
-            per_expert(rows, model),
-            per_expert(rows, model),
-            per_expert(rows, units),
-            per_expert(rows, units),
-            per_expert(rows, units),
-        ],
-        out_specs=[per_expert(units, model)] * 3,
-        out_shape=[jax.ShapeDtypeStruct((local_experts, units, model), BF16)] * 3,
-        compiler_params=pltpu.CompilerParams(vmem_limit_bytes=32 * 1024 * 1024),
-        cost_estimate=pl.CostEstimate(
-            flops=2 * 3 * local_experts * rows * units * model,
-            bytes_accessed=3 * 2 * local_experts * units * model,
-            transcendentals=0,
-        ),
-    )(x_rows, y_rows, gate_part, up_part, scaled)
-
+    )(me, limit, mine, *blocks, gate_t, up_t, down_weight)
+
+    out_came, back_came = swap(out_send, 1), swap(back_send, 1)
+    down_grad = weight_grad(scaled, y_rows, pair)
+    out_far, back_far = add(out_keep[1], out_came[1]), add(back_keep[1], back_came[1])
+    out_far, back_far, up_part = lax.optimization_barrier((out_far, back_far, up_part))
+    out_came, back_came = add(out_keep[0], out_came[0]), add(back_keep[0], back_came[0])
+    up_grad = weight_grad(up_part, x_rows, pair)
+    out_near, back_near = add(out_came, swap(out_far, 2)), add(back_came, swap(back_far, 2))
+    out_near, back_near, gate_part = lax.optimization_barrier((out_near, back_near, gate_part))
+    gate_grad = weight_grad(gate_part, x_rows, pair)
+    out_total, back_total = out_near[0].astype(F32), back_near[0].astype(F32)
+    for s in range(1, sources):
+        out_total = out_total + shift(out_near[s], -s).astype(F32)
+        back_total = back_total + shift(back_near[s], -s).astype(F32)
     return (
-        total[0:tokens],
-        total[tokens:2 * tokens],
-        total[2 * tokens:2 * tokens + choose, 0:tokens].astype(F32).T,
+        out_total[0:tokens].astype(BF16),
+        back_total.astype(BF16),
+        out_total[tokens:tokens + choose, 0:tokens].T,
         jnp.swapaxes(gate_grad, 1, 2),
         jnp.swapaxes(up_grad, 1, 2),
         down_grad,
@@ -349,7 +382,7 @@
 
 def body(*operands):
     hidden_in, gate_weight = operands[0], operands[5]
-    if hidden_in.shape[0] <= gate_weight.shape[0] * CAP:
+    if lax.axis_size("etp") == 4 and hidden_in.shape[0] <= gate_weight.shape[0] * CAP:
         return gathered_body(*operands)
     return dispatched_body(*operands)
 

time: 158 us -> 103 us (0.65)
  waiting for transfers between devices: 86.5 us -> 19.5 us
  starting transfers between devices: 0.08 us -> 22.5 us
  between operations: 14.1 us -> 0.73 us
  Pallas kernels: 44.6 us -> 52.6 us
  local copies, waits for them, and re-layouts: 7.22 us -> 3.13 us
    all_gather x1 -> x0, waiting for transfers between devices: 44.3 us -> none  [gathered_body(): blocks = lax.all_gather(packed, ('expert', 'etp'), axis=0, tiled=False)]
    reduce_scatter x1 -> x0, waiting for transfers between devices: 42.2 us -> none  [gathered_body(): lax.psum_scatter(home, ('expert', 'etp'), scatter_dimension=0, tiled=False)]
    ppermute x0 -> x25, starting transfers between devices: none -> 22.5 us  [the longest x9 13.6 us: shift(): lax.ppermute(array, 'expert', [(i, (i + by) % count) for i in range(count)])]
    ppermute x0 -> x25, waiting for transfers between devices: none -> 19.5 us  [the longest x9 11 us: shift(): lax.ppermute(array, 'expert', [(i, (i + by) % count) for i in range(count)])]
    pallas_call x2 -> x4, Pallas kernels: 44.6 us -> 52.6 us  [the longest x3 28 us: weight_grad(): pl.pallas_call(product_kernel, grid=(experts // pair,), in_specs=[block(r...]
    unnamed x10 -> x4, local copies, waits for them, and re-layouts: 5.61 us -> 1.78 us
  transfers between devices with their start and end apart: 2 -> 25, of which waited for: 2 -> 8; matrix products, arithmetic and copies ran while one was open for 1% -> 2% of each run, Pallas kernels for 10% -> 27%
where the time goes in v2:
time: 103 us
  Pallas kernels  52.6 us (51%)
  starting transfers between devices  22.5 us (22%)
  waiting for transfers between devices  19.5 us (19%)
  other arithmetic  4.05 us (4%)
  local copies, waits for them, and re-layouts  3.13 us (3%)
    pallas_call x3, Pallas kernels, weight_grad(): pl.pallas_call(product_kernel, grid=(experts // pair,), in_specs=[block(r...  28 us
    pallas_call x1, Pallas kernels, gathered_body(): pl.pallas_call(functools.partial(forward_kernel, choose, sources, shares,...  24.6 us
    ppermute x9, starting transfers between devices, shift(): lax.ppermute(array, 'expert', [(i, (i + by) % count) for i in range(count)])  13.6 us
    ppermute x9, waiting for transfers between devices, shift(): lax.ppermute(array, 'expert', [(i, (i + by) % count) for i in range(count)])  11 us
    ppermute x16, starting transfers between devices, swap(): return lax.ppermute(array, 'etp', [(i, i ^ bit) for i in range(count)])  8.87 us
    ppermute x16, waiting for transfers between devices, swap(): return lax.ppermute(array, 'etp', [(i, i ^ bit) for i in range(count)])  8.48 us
  transfers between devices with their start and end apart: 25, of which 8 were waited for; matrix products, arithmetic and copies ran while one was open for 2% of the time, Pallas kernels for 27%

profile of v2, /device:TPU:0, one launch (start us, length us, event | category | flops | bytes accessed | tf_op | source)
XLA Modules:
  0.0 102.5 jit_solution(9822830436044204070)
XLA Ops:
  2.0 0.9 fusion.14.refs_0_
  2.9 5.1 %collective-permute-start.11 = (bf16[272,256]{1,0:T(8,128)(2,1)S(1)}, bf16[272,256]{1,0:T(8,128)(2,1)S(1)}, u32[]{:S(2)}, u32[]{:S(2)}) collective-permute-start(bf16[272,256]{1,0:T(8,128)(2,1)S(1)} %fusion.14.refs_0_), channel_id=1, source_target_pairs={{0,12},{4,0},{8,4},{12,8},{1,13},{5,1},{9,5},{13,9},{2,14},{6,2},{... | collective-permute-start | bytes 417800 | tf_op jit(solution)/shard_map/ppermute | solution.py:166
  8.0 1.0 collective-permute-start.3
  9.0 1.5 %collective-permute-start.1 = (bf16[272,256]{1,0:T(8,128)(2,1)S(1)}, bf16[272,256]{1,0:T(8,128)(2,1)S(1)}, u32[]{:S(2)}, u32[]{:S(2)}) collective-permute-start(bf16[272,256]{1,0:T(8,128)(2,1)S(1)} %fusion.14.refs_0_), channel_id=1, source_target_pairs={{0,2},{1,3},{2,0},{3,1},{4,6},{5,7},{6,4},{7,5},{8,10},{9,11},{10,... | collective-permute-start | bytes 417800 | tf_op jit(solution)/shard_map/ppermute | solution.py:161
  10.5 1.6 %collective-permute-done.11.refs_12_ = bf16[272,256]{1,0:T(8,128)(2,1)S(1)} collective-permute-done((bf16[272,256]{1,0:T(8,128)(2,1)S(1)}, bf16[272,256]{1,0:T(8,128)(2,1)S(1)}, u32[]{:S(2)}, u32[]{:S(2)}) %collective-permute-start.11) | collective-permute-done | bytes 139296 | tf_op jit(solution)/shard_map/ppermute | solution.py:166
  12.1 1.5 %collective-permute-start.13 = (bf16[272,256]{1,0:T(8,128)(2,1)S(1)}, bf16[272,256]{1,0:T(8,128)(2,1)S(1)}, u32[]{:S(2)}, u32[]{:S(2)}) collective-permute-start(bf16[272,256]{1,0:T(8,128)(2,1)S(1)} %collective-permute-done.11.refs_12_), channel_id=1, source_target_pairs={{0,2},{1,3},{2,0},{3,1},{4,6},{5,7},{6,4},{7,5},{8,10},{9,11},{10,... | collective-permute-start | bytes 417800 | tf_op jit(solution)/shard_map/ppermute | solution.py:161
  13.6 6.2 %collective-permute-done.7.refs_8_ = bf16[272,256]{1,0:T(8,128)(2,1)S(1)} collective-permute-done((bf16[272,256]{1,0:T(8,128)(2,1)S(1)}, bf16[272,256]{1,0:T(8,128)(2,1)S(1)}, u32[]{:S(2)}, u32[]{:S(2)}) %collective-permute-start.7) | collective-permute-done | bytes 139296 | tf_op jit(solution)/shard_map/ppermute | solution.py:166
  19.8 1.5 %collective-permute-start.9 = (bf16[272,256]{1,0:T(8,128)(2,1)S(1)}, bf16[272,256]{1,0:T(8,128)(2,1)S(1)}, u32[]{:S(2)}, u32[]{:S(2)}) collective-permute-start(bf16[272,256]{1,0:T(8,128)(2,1)S(1)} %collective-permute-done.7.refs_8_), channel_id=1, source_target_pairs={{0,2},{1,3},{2,0},{3,1},{4,6},{5,7},{6,4},{7,5},{8,10},{9,11},{10,... | collective-permute-start | bytes 417800 | tf_op jit(solution)/shard_map/ppermute | solution.py:161
  22.6 3.7 %collective-permute-done.9.refs_10_ = bf16[272,256]{1,0:T(8,128)(2,1)S(1)} collective-permute-done((bf16[272,256]{1,0:T(8,128)(2,1)S(1)}, bf16[272,256]{1,0:T(8,128)(2,1)S(1)}, u32[]{:S(2)}, u32[]{:S(2)}) %collective-permute-start.9) | collective-permute-done | bytes 139296 | tf_op jit(solution)/shard_map/ppermute | solution.py:161
  26.8 2.1 %collective-permute-done.5.refs_6_ = bf16[272,256]{1,0:T(8,128)(2,1)S(1)} collective-permute-done((bf16[272,256]{1,0:T(8,128)(2,1)S(1)}, bf16[272,256]{1,0:T(8,128)(2,1)S(1)}, u32[]{:S(2)}, u32[]{:S(2)}) %collective-permute-start.5) | collective-permute-done | bytes 139296 | tf_op jit(solution)/shard_map/ppermute | solution.py:161
  30.3 24.6 %shard_map.127 = (bf16[2,4,144,256]{3,2,1,0:T(8,128)(2,1)S(1)}, bf16[2,4,144,256]{3,2,1,0:T(8,128)(2,1)S(1)}, bf16[2,4,128,256]{3,2,1,0:T(8,128)(2,1)S(1)}, bf16...) custom-call(s32[1]{0:T(128)} %bitcast.me_ref, ...), custom_call_target="tpu_custom_call" | custom-call | flops 4429185024 | bytes 34603008 | tf_op jit(solution)/shard_map/pallas_call | solution.py:213
  54.9 0.9 copy-done
  55.8 0.9 copy-done.1
  57.2 1.4 %collective-permute-done.16 = bf16[2,4,128,256]{3,2,1,0:T(8,128)(2,1)S(1)} collective-permute-done((bf16[2,4,128,256]{3,2,1,0:T(8,128)(2,1)S(1)}, bf16[2,4,128,256]{3,2,1,0:T(8,128)(2,1)S(1)}, u32[]{:S(2)}, u32[]{:S(2)}) %collective-permute-start.16) | collective-permute-done | bytes 524320 | tf_op jit(solution)/shard_map/ppermute | solution.py:161
  58.6 0.8 collective-permute-done.15
  59.5 1.6 %collective-permute-start.18 = (bf16[4,128,256]{2,1,0:T(8,128)(2,1)S(1)}, bf16[4,128,256]{2,1,0:T(8,128)(2,1)S(1)}, u32[]{:S(2)}, u32[]{:S(2)}) collective-permute-start(bf16[4,128,256]{2,1,0:T(8,128)(2,1)S(1)} %fusion.10), channel_id=1, source_target_pairs={{0,2},{1,3},{2,0},{3,1},{4,6},{5,7},{6,4},{7,5},{8,10},{9,11},{10,... | collective-permute-start | bytes 786440 | tf_op jit(solution)/shard_map/ppermute | solution.py:161
  61.1 9.3 %shard_map.130 = bf16[16,352,1024]{2,1,0:T(8,128)(2,1)} custom-call(bf16[16,64,352]{2,1,0:T(8,128)(2,1)} %get-tuple-element.34.left_ref, bf16[16,64,1024]{2,1,0:T(8,128)(2,1)} %get-tuple-element.35.right_ref), custom_call_target="tpu_custom_call" | custom-call | flops 738197504 | bytes 14352384 | tf_op jit(solution)/shard_map/pallas_call | solution.py:144
  70.9 9.3 %shard_map.129 = bf16[16,352,1024]{2,1,0:T(8,128)(2,1)} custom-call(bf16[16,64,352]{2,1,0:T(8,128)(2,1)} %copy-done.1, bf16[16,64,1024]{2,1,0:T(8,128)(2,1)} %get-tuple-element.32.right_ref), custom_call_target="tpu_custom_call" | custom-call | flops 738197504 | bytes 14352384 | tf_op jit(solution)/shard_map/pallas_call | solution.py:144
  80.5 1.6 %collective-permute-start.22 = (bf16[128,256]{1,0:T(8,128)(2,1)S(1)}, bf16[128,256]{1,0:T(8,128)(2,1)S(1)}, u32[]{:S(2)}, u32[]{:S(2)}) collective-permute-start(bf16[128,256]{1,0:T(8,128)(2,1)S(1)} %get-tuple-element.39), channel_id=1, source_target_pairs={{0,12},{4,0},{8,4},{12,8},{1,13},{5,1},{9,5},{13,9},{2,14},{6,2},{... | collective-permute-start | bytes 196616 | tf_op jit(solution)/shard_map/ppermute | solution.py:166
  82.6 1.7 %collective-permute-start.23 = (bf16[128,256]{1,0:T(8,128)(2,1)S(1)}, bf16[128,256]{1,0:T(8,128)(2,1)S(1)}, u32[]{:S(2)}, u32[]{:S(2)}) collective-permute-start(bf16[128,256]{1,0:T(8,128)(2,1)S(1)} %get-tuple-element.41), channel_id=1, source_target_pairs={{0,8},{4,12},{8,0},{12,4},{1,9},{5,13},{9,1},{13,5},{2,10},{6,14},... | collective-permute-start | bytes 196616 | tf_op jit(solution)/shard_map/ppermute | solution.py:166
  84.3 1.7 %collective-permute-start.19 = (bf16[144,256]{1,0:T(8,128)(2,1)S(1)}, bf16[144,256]{1,0:T(8,128)(2,1)S(1)}, u32[]{:S(2)}, u32[]{:S(2)}) collective-permute-start(bf16[144,256]{1,0:T(8,128)(2,1)S(1)} %get-tuple-element.36), channel_id=1, source_target_pairs={{0,12},{4,0},{8,4},{12,8},{1,13},{5,1},{9,5},{13,9},{2,14},{6,2},{... | collective-permute-start | bytes 221192 | tf_op jit(solution)/shard_map/ppermute | solution.py:166
  86.6 9.3 %shard_map.128 = bf16[16,352,1024]{2,1,0:T(8,128)(2,1)} custom-call(bf16[16,64,352]{2,1,0:T(8,128)(2,1)} %copy-done, bf16[16,64,1024]{2,1,0:T(8,128)(2,1)} %get-tuple-element.32.right_ref), custom_call_target="tpu_custom_call" | custom-call | flops 738197504 | bytes 14352384 | tf_op jit(solution)/shard_map/pallas_call | solution.py:144
  96.0 1.4 %collective-permute-start.20 = (bf16[144,256]{1,0:T(8,128)(2,1)S(1)}, bf16[144,256]{1,0:T(8,128)(2,1)S(1)}, u32[]{:S(2)}, u32[]{:S(2)}) collective-permute-start(bf16[144,256]{1,0:T(8,128)(2,1)S(1)} %get-tuple-element.38), channel_id=1, source_target_pairs={{0,8},{4,12},{8,0},{12,4},{1,9},{5,13},{9,1},{13,5},{2,10},{6,14},... | collective-permute-start | bytes 221192 | tf_op jit(solution)/shard_map/ppermute | solution.py:166
  98.1 3.2 %collective-permute-done.20 = bf16[144,256]{1,0:T(8,128)(2,1)S(1)} collective-permute-done((bf16[144,256]{1,0:T(8,128)(2,1)S(1)}, bf16[144,256]{1,0:T(8,128)(2,1)S(1)}, u32[]{:S(2)}, u32[]{:S(2)}) %collective-permute-start.20) | collective-permute-done | bytes 73760 | tf_op jit(solution)/shard_map/ppermute | solution.py:166
  (50 shorter events, 9.0 us)
Async XLA Ops:
  2.9 9.2 %collective-permute-start.11 = (bf16[272,256]{1,0:T(8,128)(2,1)S(1)}, bf16[272,256]{1,0:T(8,128)(2,1)S(1)}, u32[]{:S(2)}, u32[]{:S(2)}) collective-permute-start(bf16[272,256]{1,0:T(8,128)(2,1)S(1)} %fusion.14.refs_0_), channel_id=1, source_target_pairs={{0,12},{4,0},{8,4},{12,8},{1,13},{5,1},{9,5},{13,9},{2,14},{6,2},{... | collective-permute-start | bytes 417800 | tf_op jit(solution)/shard_map/ppermute | solution.py:166
  8.0 11.8 %collective-permute-start.7 = (bf16[272,256]{1,0:T(8,128)(2,1)S(1)}, bf16[272,256]{1,0:T(8,128)(2,1)S(1)}, u32[]{:S(2)}, u32[]{:S(2)}) collective-permute-start(bf16[272,256]{1,0:T(8,128)(2,1)S(1)} %fusion.14.refs_0_), channel_id=1, source_target_pairs={{0,8},{4,12},{8,0},{12,4},{1,9},{5,13},{9,1},{13,5},{2,10},{6,14},... | collective-permute-start | bytes 417800 | tf_op jit(solution)/shard_map/ppermute | solution.py:166
  8.0 11.8 %collective-permute-start.3 = (bf16[272,256]{1,0:T(8,128)(2,1)S(1)}, bf16[272,256]{1,0:T(8,128)(2,1)S(1)}, u32[]{:S(2)}, u32[]{:S(2)}) collective-permute-start(bf16[272,256]{1,0:T(8,128)(2,1)S(1)} %fusion.14.refs_0_), channel_id=1, source_target_pairs={{0,4},{4,8},{8,12},{12,0},{1,5},{5,9},{9,13},{13,1},{2,6},{6,10},{... | collective-permute-start | bytes 417800 | tf_op jit(solution)/shard_map/ppermute | solution.py:166
  9.0 12.3 %collective-permute-start.1 = (bf16[272,256]{1,0:T(8,128)(2,1)S(1)}, bf16[272,256]{1,0:T(8,128)(2,1)S(1)}, u32[]{:S(2)}, u32[]{:S(2)}) collective-permute-start(bf16[272,256]{1,0:T(8,128)(2,1)S(1)} %fusion.14.refs_0_), channel_id=1, source_target_pairs={{0,2},{1,3},{2,0},{3,1},{4,6},{5,7},{6,4},{7,5},{8,10},{9,11},{10,... | collective-permute-start | bytes 417800 | tf_op jit(solution)/shard_map/ppermute | solution.py:161
  10.5 11.0 %collective-permute-start = (bf16[272,256]{1,0:T(8,128)(2,1)S(1)}, bf16[272,256]{1,0:T(8,128)(2,1)S(1)}, u32[]{:S(2)}, u32[]{:S(2)}) collective-permute-start(bf16[272,256]{1,0:T(8,128)(2,1)S(1)} %fusion.14.refs_0_), channel_id=1, source_target_pairs={{0,1},{1,0},{2,3},{3,2},{4,5},{5,4},{6,7},{7,6},{8,9},{9,8},{10,11... | collective-permute-start | bytes 417800 | tf_op jit(solution)/shard_map/ppermute | solution.py:161
  12.1 10.0 %collective-permute-start.13 = (bf16[272,256]{1,0:T(8,128)(2,1)S(1)}, bf16[272,256]{1,0:T(8,128)(2,1)S(1)}, u32[]{:S(2)}, u32[]{:S(2)}) collective-permute-start(bf16[272,256]{1,0:T(8,128)(2,1)S(1)} %collective-permute-done.11.refs_12_), channel_id=1, source_target_pairs={{0,2},{1,3},{2,0},{3,1},{4,6},{5,7},{6,4},{7,5},{8,10},{9,11},{10,... | collective-permute-start | bytes 417800 | tf_op jit(solution)/shard_map/ppermute | solution.py:161
  19.8 2.3 %collective-permute-start.12 = (bf16[272,256]{1,0:T(8,128)(2,1)S(1)}, bf16[272,256]{1,0:T(8,128)(2,1)S(1)}, u32[]{:S(2)}, u32[]{:S(2)}) collective-permute-start(bf16[272,256]{1,0:T(8,128)(2,1)S(1)} %collective-permute-done.11.refs_12_), channel_id=1, source_target_pairs={{0,1},{1,0},{2,3},{3,2},{4,5},{5,4},{6,7},{7,6},{8,9},{9,8},{10,11... | collective-permute-start | bytes 417800 | tf_op jit(solution)/shard_map/ppermute | solution.py:161
  19.8 6.5 %collective-permute-start.9 = (bf16[272,256]{1,0:T(8,128)(2,1)S(1)}, bf16[272,256]{1,0:T(8,128)(2,1)S(1)}, u32[]{:S(2)}, u32[]{:S(2)}) collective-permute-start(bf16[272,256]{1,0:T(8,128)(2,1)S(1)} %collective-permute-done.7.refs_8_), channel_id=1, source_target_pairs={{0,2},{1,3},{2,0},{3,1},{4,6},{5,7},{6,4},{7,5},{8,10},{9,11},{10,... | collective-permute-start | bytes 417800 | tf_op jit(solution)/shard_map/ppermute | solution.py:161
  21.3 5.0 %collective-permute-start.8 = (bf16[272,256]{1,0:T(8,128)(2,1)S(1)}, bf16[272,256]{1,0:T(8,128)(2,1)S(1)}, u32[]{:S(2)}, u32[]{:S(2)}) collective-permute-start(bf16[272,256]{1,0:T(8,128)(2,1)S(1)} %collective-permute-done.7.refs_8_), channel_id=1, source_target_pairs={{0,1},{1,0},{2,3},{3,2},{4,5},{5,4},{6,7},{7,6},{8,9},{9,8},{10,11... | collective-permute-start | bytes 417800 | tf_op jit(solution)/shard_map/ppermute | solution.py:161
  21.6 7.3 %collective-permute-start.5 = (bf16[272,256]{1,0:T(8,128)(2,1)S(1)}, bf16[272,256]{1,0:T(8,128)(2,1)S(1)}, u32[]{:S(2)}, u32[]{:S(2)}) collective-permute-start(bf16[272,256]{1,0:T(8,128)(2,1)S(1)} %collective-permute-done.3.refs_4_), channel_id=1, source_target_pairs={{0,2},{1,3},{2,0},{3,1},{4,6},{5,7},{6,4},{7,5},{8,10},{9,11},{10,... | collective-permute-start | bytes 417800 | tf_op jit(solution)/shard_map/ppermute | solution.py:161
  22.1 7.6 %collective-permute-start.4 = (bf16[272,256]{1,0:T(8,128)(2,1)S(1)}, bf16[272,256]{1,0:T(8,128)(2,1)S(1)}, u32[]{:S(2)}, u32[]{:S(2)}) collective-permute-start(bf16[272,256]{1,0:T(8,128)(2,1)S(1)} %collective-permute-done.3.refs_4_), channel_id=1, source_target_pairs={{0,1},{1,0},{2,3},{3,2},{4,5},{5,4},{6,7},{7,6},{8,9},{9,8},{10,11... | collective-permute-start | bytes 417800 | tf_op jit(solution)/shard_map/ppermute | solution.py:161
  22.1 7.6 %collective-permute-start.2 = (bf16[272,256]{1,0:T(8,128)(2,1)S(1)}, bf16[272,256]{1,0:T(8,128)(2,1)S(1)}, u32[]{:S(2)}, u32[]{:S(2)}) collective-permute-start(bf16[272,256]{1,0:T(8,128)(2,1)S(1)} %collective-permute-done.1.refs_2_), channel_id=1, source_target_pairs={{0,1},{1,0},{2,3},{3,2},{4,5},{5,4},{6,7},{7,6},{8,9},{9,8},{10,11... | collective-permute-start | bytes 417800 | tf_op jit(solution)/shard_map/ppermute | solution.py:161
  26.3 3.4 %collective-permute-start.14 = (bf16[272,256]{1,0:T(8,128)(2,1)S(1)}, bf16[272,256]{1,0:T(8,128)(2,1)S(1)}, u32[]{:S(2)}, u32[]{:S(2)}) collective-permute-start(bf16[272,256]{1,0:T(8,128)(2,1)S(1)} %collective-permute-done.13.refs_14_), channel_id=1, source_target_pairs={{0,1},{1,0},{2,3},{3,2},{4,5},{5,4},{6,7},{7,6},{8,9},{9,8},{10,11... | collective-permute-start | bytes 417800 | tf_op jit(solution)/shard_map/ppermute | solution.py:161
  26.3 3.4 %collective-permute-start.10 = (bf16[272,256]{1,0:T(8,128)(2,1)S(1)}, bf16[272,256]{1,0:T(8,128)(2,1)S(1)}, u32[]{:S(2)}, u32[]{:S(2)}) collective-permute-start(bf16[272,256]{1,0:T(8,128)(2,1)S(1)} %collective-permute-done.9.refs_10_), channel_id=1, source_target_pairs={{0,1},{1,0},{2,3},{3,2},{4,5},{5,4},{6,7},{7,6},{8,9},{9,8},{10,11... | collective-permute-start | bytes 417800 | tf_op jit(solution)/shard_map/ppermute | solution.py:161
  56.7 1.9 %collective-permute-start.16 = (bf16[2,4,128,256]{3,2,1,0:T(8,128)(2,1)S(1)}, bf16[2,4,128,256]{3,2,1,0:T(8,128)(2,1)S(1)}, u32[]{:S(2)}, u32[]{:S(2)}) collective-permute-start(bf16[2,4,128,256]{3,2,1,0:T(8,128)(2,1)S(1)} %get-tuple-element.24), channel_id=1, source_target_pairs={{0,1},{1,0},{2,3},{3,2},{4,5},{5,4},{6,7},{7,6},{8,9},{9,8},{10,11... | collective-permute-start | bytes 1572872 | tf_op jit(solution)/shard_map/ppermute | solution.py:161
  56.8 2.6 %collective-permute-start.15 = (bf16[2,4,144,256]{3,2,1,0:T(8,128)(2,1)S(1)}, bf16[2,4,144,256]{3,2,1,0:T(8,128)(2,1)S(1)}, u32[]{:S(2)}, u32[]{:S(2)}) collective-permute-start(bf16[2,4,144,256]{3,2,1,0:T(8,128)(2,1)S(1)} %get-tuple-element.22), channel_id=1, source_target_pairs={{0,1},{1,0},{2,3},{3,2},{4,5},{5,4},{6,7},{7,6},{8,9},{9,8},{10,11... | collective-permute-start | bytes 1769480 | tf_op jit(solution)/shard_map/ppermute | solution.py:161
  59.5 20.8 %collective-permute-start.18 = (bf16[4,128,256]{2,1,0:T(8,128)(2,1)S(1)}, bf16[4,128,256]{2,1,0:T(8,128)(2,1)S(1)}, u32[]{:S(2)}, u32[]{:S(2)}) collective-permute-start(bf16[4,128,256]{2,1,0:T(8,128)(2,1)S(1)} %fusion.10), channel_id=1, source_target_pairs={{0,2},{1,3},{2,0},{3,1},{4,6},{5,7},{6,4},{7,5},{8,10},{9,11},{10,... | collective-permute-start | bytes 786440 | tf_op jit(solution)/shard_map/ppermute | solution.py:161
  70.4 10.0 %collective-permute-start.17 = (bf16[4,144,256]{2,1,0:T(8,128)(2,1)S(1)}, bf16[4,144,256]{2,1,0:T(8,128)(2,1)S(1)}, u32[]{:S(2)}, u32[]{:S(2)}) collective-permute-start(bf16[4,144,256]{2,1,0:T(8,128)(2,1)S(1)} %fusion.3), channel_id=1, source_target_pairs={{0,2},{1,3},{2,0},{3,1},{4,6},{5,7},{6,4},{7,5},{8,10},{9,11},{10,... | collective-permute-start | bytes 884744 | tf_op jit(solution)/shard_map/ppermute | solution.py:161
  80.5 15.5 %collective-permute-start.22 = (bf16[128,256]{1,0:T(8,128)(2,1)S(1)}, bf16[128,256]{1,0:T(8,128)(2,1)S(1)}, u32[]{:S(2)}, u32[]{:S(2)}) collective-permute-start(bf16[128,256]{1,0:T(8,128)(2,1)S(1)} %get-tuple-element.39), channel_id=1, source_target_pairs={{0,12},{4,0},{8,4},{12,8},{1,13},{5,1},{9,5},{13,9},{2,14},{6,2},{... | collective-permute-start | bytes 196616 | tf_op jit(solution)/shard_map/ppermute | solution.py:166
  82.1 15.3 %collective-permute-start.24 = (bf16[128,256]{1,0:T(8,128)(2,1)S(1)}, bf16[128,256]{1,0:T(8,128)(2,1)S(1)}, u32[]{:S(2)}, u32[]{:S(2)}) collective-permute-start(bf16[128,256]{1,0:T(8,128)(2,1)S(1)} %get-tuple-element.40), channel_id=1, source_target_pairs={{0,4},{4,8},{8,12},{12,0},{1,5},{5,9},{9,13},{13,1},{2,6},{6,10},{... | collective-permute-start | bytes 196616 | tf_op jit(solution)/shard_map/ppermute | solution.py:166
  82.6 14.8 %collective-permute-start.23 = (bf16[128,256]{1,0:T(8,128)(2,1)S(1)}, bf16[128,256]{1,0:T(8,128)(2,1)S(1)}, u32[]{:S(2)}, u32[]{:S(2)}) collective-permute-start(bf16[128,256]{1,0:T(8,128)(2,1)S(1)} %get-tuple-element.41), channel_id=1, source_target_pairs={{0,8},{4,12},{8,0},{12,4},{1,9},{5,13},{9,1},{13,5},{2,10},{6,14},... | collective-permute-start | bytes 196616 | tf_op jit(solution)/shard_map/ppermute | solution.py:166
  84.3 13.7 %collective-permute-start.19 = (bf16[144,256]{1,0:T(8,128)(2,1)S(1)}, bf16[144,256]{1,0:T(8,128)(2,1)S(1)}, u32[]{:S(2)}, u32[]{:S(2)}) collective-permute-start(bf16[144,256]{1,0:T(8,128)(2,1)S(1)} %get-tuple-element.36), channel_id=1, source_target_pairs={{0,12},{4,0},{8,4},{12,8},{1,13},{5,1},{9,5},{13,9},{2,14},{6,2},{... | collective-permute-start | bytes 221192 | tf_op jit(solution)/shard_map/ppermute | solution.py:166
  86.0 12.1 %collective-permute-start.21 = (bf16[144,256]{1,0:T(8,128)(2,1)S(1)}, bf16[144,256]{1,0:T(8,128)(2,1)S(1)}, u32[]{:S(2)}, u32[]{:S(2)}) collective-permute-start(bf16[144,256]{1,0:T(8,128)(2,1)S(1)} %get-tuple-element.37), channel_id=1, source_target_pairs={{0,4},{4,8},{8,12},{12,0},{1,5},{5,9},{9,13},{13,1},{2,6},{6,10},{... | collective-permute-start | bytes 221192 | tf_op jit(solution)/shard_map/ppermute | solution.py:166
  96.0 5.3 %collective-permute-start.20 = (bf16[144,256]{1,0:T(8,128)(2,1)S(1)}, bf16[144,256]{1,0:T(8,128)(2,1)S(1)}, u32[]{:S(2)}, u32[]{:S(2)}) collective-permute-start(bf16[144,256]{1,0:T(8,128)(2,1)S(1)} %get-tuple-element.38), channel_id=1, source_target_pairs={{0,8},{4,12},{8,0},{12,4},{1,9},{5,13},{9,1},{13,5},{2,10},{6,14},... | collective-permute-start | bytes 221192 | tf_op jit(solution)/shard_map/ppermute | solution.py:166
  (3 other events, 3.1 us)

commit v3 on v0

--- a/solution.py
+++ b/solution.py
@@ -1,10 +1,437 @@
+import functools
+
 import jax
 import jax.numpy as jnp
 from jax import lax
+from jax.experimental import pallas as pl
+from jax.experimental.pallas import tpu as pltpu
 from jax.sharding import PartitionSpec as P
 
 CAP = 16
 BLK = 4
+EXTRA = 16
+F32 = jnp.float32
+BF16 = jnp.bfloat16
+
+
+def nn(a, b):
+    return lax.dot_general(a, b, (((1,), (0,)), ((), ())), preferred_element_type=F32)
+
+
+def nt(a, b):
+    return lax.dot_general(a, b, (((1,), (1,)), ((), ())), preferred_element_type=F32)
+
+
+def tn(a, b):
+    return lax.dot_general(a, b, (((0,), (0,)), ((), ())), preferred_element_type=F32)
+
+
+def routing_rows(expert_ids, gate_values):
+    choose = expert_ids.shape[1]
+    high = lax.reduce_precision(gate_values, exponent_bits=8, mantissa_bits=7)
+    low = lax.reduce_precision(gate_values - high, exponent_bits=8, mantissa_bits=7)
+    pad = ((0, 8 - choose), (0, 0))
+    top = jnp.concatenate([jnp.pad(expert_ids.T.astype(F32), pad), jnp.pad(high.T, pad)], axis=1)
+    bottom = jnp.concatenate([jnp.pad(low.T, pad), jnp.zeros_like(jnp.pad(low.T, pad))], axis=1)
+    return jnp.concatenate([top, bottom], axis=0).astype(BF16)
+
+
+def routing(info, choose, tokens):
+    info = info.astype(F32)
+    return info[0:choose, 0:tokens], info[0:choose, tokens:2 * tokens] + info[8:8 + choose, 0:tokens]
+
+
+def columns(me, mask, width):
+    return pl.ds(pl.multiple_of(lax.bitwise_xor(me, mask) * width, width), width)
+
+
+def send_home(home_keep, home_send, me, onehot, rows, tokens, width):
+    for s in range(onehot.shape[0]):
+        for q in range(4):
+            home = home_send if q % 2 else home_keep
+            home[q // 2, s, 0:tokens, :] = tn(onehot[s], rows[s, :, columns(me, q, width)]).astype(BF16)
+
+
+RING = 8
+
+
+def ring(weight, slots, sems):
+    def load(e):
+        slot = lax.rem(e, RING)
+        return pltpu.make_async_copy(weight.at[e], slots.at[slot], sems.at[slot])
+
+    def start(e):
+        @pl.when(e < weight.shape[0])
+        def _():
+            load(e).start()
+
+    return start, lambda e: load(e).wait()
+
+
+def forward_kernel(
+    choose, capacity_ref, o0, o1, o2, o3, b0, b1, b2, b3, gate_ref, up_ref, down_hbm, later_ref,
+    out_rows, rows_ref, act_ref, slope_ref, silu_ref, onehot, slot_gate,
+    down_ref, sems,
+):
+    sources, slots, tokens = onehot.shape
+    experts = slots // CAP
+    width = b0.shape[2]
+    me = lax.axis_index("etp")
+    first = lax.axis_index("expert") * experts
+
+    start, wait = ring(down_hbm, down_ref, sems)
+    for e in range(RING):
+        start(jnp.int32(e))
+    row = lax.broadcasted_iota(jnp.int32, (tokens, tokens), 0)
+    col = lax.broadcasted_iota(jnp.int32, (tokens, tokens), 1)
+    before = jnp.where(row < col, 1.0, 0.0).astype(BF16)
+    expert = lax.broadcasted_iota(jnp.int32, (experts, tokens), 0)
+    mine = (first + expert).astype(F32)
+    limit = jnp.zeros((experts, tokens), jnp.int32)
+    for e in range(experts):
+        limit = jnp.where(expert == e, capacity_ref[first + e] * BLK, limit)
+    limit = limit.astype(F32)
+    place = lax.broadcasted_iota(jnp.int32, (experts, CAP, tokens), 1).astype(F32)
+    for s in range(sources):
+        block = [o[...] for o in (o0, o1, o2, o3)] if s == 0 else [b[s - 1] for b in (b0, b1, b2, b3)]
+        ids, gates = routing(block[0][tokens:tokens + EXTRA, :], choose, tokens)
+        named = jnp.zeros((experts, tokens), F32)
+        gate = jnp.zeros((experts, tokens), F32)
+        for k in range(choose):
+            hit = ids[k:k + 1, :] == mine
+            named = named + jnp.where(hit, 1.0, 0.0)
+            gate = gate + jnp.where(hit, gates[k:k + 1, :], 0.0)
+        rank = nn(named.astype(BF16), before)
+        rank = jnp.where((named > 0.5) & (rank < limit), rank, -1.0)
+        chosen = jnp.where(rank[:, None, :] == place, 1.0, 0.0)
+        gate_of = jnp.sum(chosen * gate[:, None, :], axis=2, keepdims=True)
+        slot_gate[:, s * CAP:(s + 1) * CAP, :] = jnp.broadcast_to(gate_of, chosen.shape)
+        table = chosen.reshape(slots, tokens).astype(BF16)
+        onehot[s] = table
+        for q in range(4):
+            picked = nn(table, block[q][0:tokens, :]).astype(BF16).reshape(experts, CAP, width)
+            rows_ref[:, s * CAP:(s + 1) * CAP, columns(me, q, width)] = picked
+
+    def some(turn, _):
+        for e in (turn * 2, turn * 2 + 1):
+            wait(e)
+        for e in (turn * 2, turn * 2 + 1):
+            x = rows_ref[e]
+            hidden_gate = nt(x, gate_ref[e])
+            hidden_up = nt(x, up_ref[e])
+            sigma = jax.nn.sigmoid(hidden_gate)
+            silu = hidden_gate * sigma
+            activ = (silu * hidden_up).astype(BF16)
+            act_ref[e] = activ
+            slope_ref[e] = hidden_up * sigma * (1.0 + hidden_gate * (1.0 - sigma))
+            silu_ref[e] = silu
+            scaled = (activ.astype(F32) * slot_gate[e][:, 0:1]).astype(BF16)
+            out = nn(scaled, down_ref[lax.rem(e, RING)]).astype(BF16)
+            at = pl.ds(pl.multiple_of(e * CAP, CAP), CAP)
+            for s in range(sources):
+                out_rows[s, at, :] = out[s * CAP:(s + 1) * CAP]
+        for e in (turn * 2, turn * 2 + 1):
+            start(e + RING)
+        return 0
+
+    lax.fori_loop(0, experts // 2, some, 0)
+
+
+def home_kernel(onehot, rows, *refs):
+    keep, send = refs[-2:]
+    send_home(keep, send, lax.axis_index("etp"), onehot, rows, keep.shape[2], keep.shape[3])
+
+
+def slope_kernel(
+    choose, own_ref, info_ref, a0, a1, a2, a3, n0, n1, n2, n3,
+    down_hbm, act_ref, slope_ref, silu_ref, onehot, slot_gate,
+    rows_ref, p_ref, q_ref, a_ref, value_ref,
+    dots, down_ref, sems,
+):
+    sources, slots, tokens = onehot.shape
+    experts = slots // CAP
+    start, wait = ring(down_hbm, down_ref, sems)
+    for e in range(RING):
+        start(jnp.int32(e))
+    width = own_ref.shape[1]
+    me = lax.axis_index("etp")
+    for s, (here, near) in enumerate(((a0, n0), (a1, n1), (a2, n2), (a3, n3))):
+        for q in range(4):
+            block = (near if q % 2 else here)[q // 2]
+            picked = nn(onehot[s], block).astype(BF16).reshape(experts, CAP, width)
+            rows_ref[:, s * CAP:(s + 1) * CAP, columns(me, q, width)] = picked
+
+    def some(turn, _):
+        for e in (turn * 2, turn * 2 + 1):
+            wait(e)
+        for e in (turn * 2, turn * 2 + 1):
+            grad = nt(rows_ref[e], down_ref[lax.rem(e, RING)])
+            activ = act_ref[e].astype(F32)
+            gate = slot_gate[e][:, 0:1]
+            dots[e] = jnp.broadcast_to(jnp.sum(activ * grad, axis=1, keepdims=True), dots.shape[1:])
+            a_ref[e] = (activ * gate).astype(BF16)
+            grad = grad * gate
+            p_ref[e] = (grad * slope_ref[e]).astype(BF16)
+            q_ref[e] = (grad * silu_ref[e]).astype(BF16)
+        for e in (turn * 2, turn * 2 + 1):
+            start(e + RING)
+        return 0
+
+    lax.fori_loop(0, experts // 2, some, 0)
+    expert = lax.broadcasted_iota(jnp.int32, (experts, tokens), 0)
+    mine = (lax.axis_index("expert") * experts + expert).astype(F32)
+    for s in range(sources):
+        info = own_ref[tokens:tokens + EXTRA, :] if s == 0 else info_ref[s - 1, tokens:tokens + EXTRA, :]
+        ids, _ = routing(info, choose, tokens)
+        chosen = onehot[s].astype(F32).reshape(experts, CAP, tokens)
+        share = jnp.sum(chosen * dots[:, s * CAP:(s + 1) * CAP, :], axis=1)
+        rows = [jnp.sum(jnp.where(ids[k:k + 1, :] == mine, share, 0.0), axis=0, keepdims=True) for k in range(choose)]
+        rows = jnp.concatenate(rows + [jnp.zeros((EXTRA - choose, tokens), F32)], axis=0)
+        value_ref[s] = jnp.concatenate([rows, jnp.zeros((EXTRA, width - tokens), F32)], axis=1).astype(BF16)
+
+
+def back_kernel(gate_ref, up_ref, p_ref, q_ref, onehot, slot_gate, value_ref, keep, send, back_rows):
+    sources, slots, tokens = onehot.shape
+    width = keep.shape[3]
+
+    def some(turn, _):
+        for e in (turn * 2, turn * 2 + 1):
+            back = nn(p_ref[e], gate_ref[e]) + nn(q_ref[e], up_ref[e])
+            back = (back * slot_gate[e][:, 0:1]).astype(BF16)
+            at = pl.ds(pl.multiple_of(e * CAP, CAP), CAP)
+            for s in range(sources):
+                back_rows[s, at, :] = back[s * CAP:(s + 1) * CAP]
+        return 0
+
+    lax.fori_loop(0, slots // CAP // 2, some, 0)
+    send_home(keep, send, lax.axis_index("etp"), onehot, back_rows, tokens, width)
+    for s in range(sources):
+        for home in (keep, send):
+            home[0, s, tokens:tokens + EXTRA, :] = value_ref[s]
+            home[1, s, tokens:tokens + EXTRA, :] = value_ref[s]
+
+
+SLOTS = 4
+
+
+def product_kernel(left_ref, right_ref, out_ref, held, sems):
+    experts = out_ref.shape[0]
+
+    def store(e):
+        slot = lax.rem(e, SLOTS)
+        return pltpu.make_async_copy(held.at[slot], out_ref.at[e], sems.at[slot])
+
+    def one(e, _):
+        @pl.when(e >= SLOTS)
+        def _():
+            store(e - SLOTS).wait()
+
+        held[lax.rem(e, SLOTS)] = tn(left_ref[e], right_ref[e]).astype(BF16)
+        store(e).start()
+        return 0
+
+    lax.fori_loop(0, experts, one, 0)
+
+    def last(e, _):
+        store(e).wait()
+        return 0
+
+    lax.fori_loop(experts - SLOTS, experts, last, 0)
+
+
+def load_kernel(source, target, token, sems):
+    token[...] = jnp.zeros_like(token)
+    copies = [pltpu.make_async_copy(source.at[e], target.at[e], sems.at[e]) for e in range(source.shape[0])]
+    for copy in copies:
+        copy.start()
+    for copy in copies:
+        copy.wait()
+
+
+def in_vmem(weight):
+    return pl.pallas_call(
+        load_kernel,
+        in_specs=[pl.BlockSpec(memory_space=pltpu.HBM)],
+        out_specs=[pl.BlockSpec(memory_space=pltpu.VMEM)] * 2,
+        out_shape=[pltpu.VMEM(weight.shape, BF16), jax.ShapeDtypeStruct((8, 128), F32)],
+        scratch_shapes=[pltpu.SemaphoreType.DMA((weight.shape[0],))],
+        compiler_params=pltpu.CompilerParams(vmem_limit_bytes=4 * 1024 * 1024),
+        cost_estimate=pl.CostEstimate(flops=0, bytes_accessed=2 * weight.size, transcendentals=0),
+    )(pltpu.with_memory_space_constraint(weight, pltpu.HBM))
+
+
+def join_kernel(count, *refs):
+    for i in range(count):
+        refs[-1][i] = refs[i][...]
+
+
+def join(arrays, *there):
+    return kernel_call(
+        functools.partial(join_kernel, len(arrays)),
+        [jax.ShapeDtypeStruct((len(arrays),) + arrays[0].shape, arrays[0].dtype)],
+        [],
+        0,
+        limit=2,
+    )(*arrays, *there)[0]
+
+
+def kernel_call(kernel, out_shape, scratch, flops, out_specs=None, limit=4, in_hbm=()):
+    def call(*operands):
+        specs = [
+            pl.BlockSpec(memory_space=pltpu.HBM if i in in_hbm else pltpu.SMEM if x.ndim == 1 else pltpu.VMEM)
+            for i, x in enumerate(operands)
+        ]
+        operands = [
+            pltpu.with_memory_space_constraint(x, pltpu.HBM) if i in in_hbm else x for i, x in enumerate(operands)
+        ]
+        return pl.pallas_call(
+            kernel,
+            in_specs=specs,
+            out_specs=out_specs or [pl.BlockSpec(memory_space=pltpu.VMEM)] * len(out_shape),
+            out_shape=out_shape,
+            scratch_shapes=scratch,
+            compiler_params=pltpu.CompilerParams(vmem_limit_bytes=limit * 1024 * 1024),
+            cost_estimate=pl.CostEstimate(flops=flops, bytes_accessed=flops // 128, transcendentals=0),
+        )(*operands)
+
+    return call
+
+
+def weight_grad(left, right):
+    experts, rows, units = left.shape
+    model = right.shape[2]
+    return kernel_call(
+        product_kernel,
+        jax.ShapeDtypeStruct((experts, units, model), BF16),
+        [pltpu.VMEM((SLOTS, units, model), BF16), pltpu.SemaphoreType.DMA((SLOTS,))],
+        2 * experts * rows * units * model,
+        out_specs=pl.BlockSpec(memory_space=pltpu.HBM),
+        limit=6,
+    )(left, right)
+
+
+def swap(array, bit):
+    count = lax.axis_size("etp")
+    return lax.ppermute(array, "etp", [(i, i ^ bit) for i in range(count)])
+
+
+def shift(array, by):
+    count = lax.axis_size("expert")
+    return lax.ppermute(array, "expert", [(i, (i + by) % count) for i in range(count)])
+
+
+def add(a, b):
+    return (a.astype(F32) + b.astype(F32)).astype(BF16)
+
+
+def gathered_body(
+    hidden_in, out_grad, expert_ids, gate_values, capacity_blocks, gate_weight, up_weight, down_weight
+):
+    sources = lax.axis_size("expert")
+    tokens, width = hidden_in.shape
+    choose = expert_ids.shape[1]
+    local_experts, units, model = down_weight.shape
+    slots = local_experts * CAP
+    rows = sources * CAP
+    gate_t, gate_there = in_vmem(jnp.swapaxes(gate_weight, 1, 2))
+    up_t, up_there = in_vmem(jnp.swapaxes(up_weight, 1, 2))
+    product = 2 * local_experts * rows * units * model
+    held = lambda *shape, kind=BF16: pltpu.VMEM(shape, kind)
+    sent = lambda *shape: jax.ShapeDtypeStruct(shape, BF16)
+
+    own = jnp.concatenate([hidden_in, routing_rows(expert_ids, gate_values)], axis=0)
+    came = [shift(own, s) for s in range(1, sources)]
+    own_across = swap(own, 2)
+    grad_across = swap(out_grad, 2)
+    own_near = swap(own, 1)
+    came = join(came, gate_there, up_there, own_across, own_near)
+    came_across = swap(came, 2)
+    across_near = swap(own_across, 1)
+    grads = join([out_grad, grad_across], came, across_near)
+    grads = [grads] + [shift(grads, s) for s in range(1, sources)]
+
+    out_rows, x_rows, activ, slope, silu, onehot, slot_gate = kernel_call(
+        functools.partial(forward_kernel, choose),
+        [
+            held(sources, slots, model),
+            held(local_experts, rows, model),
+            held(local_experts, rows, units),
+            held(local_experts, rows, units, kind=F32),
+            held(local_experts, rows, units, kind=F32),
+            held(sources, slots, tokens),
+            held(local_experts, rows, tokens, kind=F32),
+        ],
+        [pltpu.VMEM((RING, units, model), BF16), pltpu.SemaphoreType.DMA((RING,))],
+        3 * product,
+        limit=10,
+        in_hbm=(11,),
+    )(
+        capacity_blocks,
+        own, own_near, own_across, across_near,
+        came, swap(came, 1), came_across, swap(came_across, 1),
+        gate_t, up_t, down_weight, grads[0],
+    )
+
+    keep, send = kernel_call(
+        home_kernel, [sent(2, sources, tokens, width)] * 2, [], 2 * slots * sources * tokens * model, limit=2,
+    )(onehot, out_rows, *grads)
+    out_came = swap(send, 1)
+    y_rows, gate_part, up_part, scaled, values = kernel_call(
+        functools.partial(slope_kernel, choose),
+        [
+            held(local_experts, rows, model),
+            held(local_experts, rows, units),
+            held(local_experts, rows, units),
+            held(local_experts, rows, units),
+            held(sources, EXTRA, width),
+        ],
+        [
+            pltpu.VMEM((local_experts, rows, tokens), F32),
+            pltpu.VMEM((RING, units, model), BF16),
+            pltpu.SemaphoreType.DMA((RING,)),
+        ],
+        product,
+        limit=8,
+        in_hbm=(10,),
+    )(own, came, *grads, *[swap(x, 1) for x in grads], down_weight, activ, slope, silu, onehot, slot_gate)
+
+    out_far = add(keep[1], out_came[1])
+    out_far, gate_part = lax.optimization_barrier((out_far, gate_part))
+    out_far_came = swap(out_far, 2)
+    out_near = add(keep[0], out_came[0])
+    keep, send = kernel_call(
+        back_kernel,
+        [sent(2, sources, tokens + EXTRA, width), sent(2, sources, tokens + EXTRA, width)],
+        [pltpu.VMEM((sources, slots, model), BF16)],
+        2 * product,
+    )(gate_t, up_t, gate_part, up_part, onehot, slot_gate, values)
+
+    back_came = swap(send, 1)
+    out_near = add(out_near, out_far_came)
+    out_near, scaled = lax.optimization_barrier((out_near, scaled))
+    out_total = out_near[0].astype(F32)
+    for s in range(1, sources):
+        out_total = out_total + shift(out_near[s], -s).astype(F32)
+    down_grad = weight_grad(scaled, y_rows)
+    back_far = add(keep[1], back_came[1])
+    back_far, up_part = lax.optimization_barrier((back_far, up_part))
+    back_far_came = swap(back_far, 2)
+    back_near = add(keep[0], back_came[0])
+    up_grad = weight_grad(up_part, x_rows)
+    back_near = add(back_near, back_far_came)
+    back_near, gate_part = lax.optimization_barrier((back_near, gate_part))
+    back_total = back_near[0].astype(F32)
+    for s in range(1, sources):
+        back_total = back_total + shift(back_near[s], -s).astype(F32)
+    gate_grad = weight_grad(gate_part, x_rows)
+    return (
+        out_total.astype(BF16),
+        back_total[0:tokens].astype(BF16),
+        back_total[tokens:tokens + choose, 0:tokens].T,
+        jnp.swapaxes(gate_grad, 1, 2),
+        jnp.swapaxes(up_grad, 1, 2),
+        down_grad,
+    )
 
 
 def slot_layout(expert_ids, capacity_blocks):
@@ -47,7 +474,7 @@
     return (jnp.einsum("tk,tkw->tw", weights, picked), picked)
 
 
-def body(
+def dispatched_body(
     hidden_in,
     out_grad,
     expert_ids,
@@ -126,6 +553,13 @@
     )
 
 
+def body(*operands):
+    hidden_in, gate_weight = operands[0], operands[5]
+    if lax.axis_size("etp") == 4 and hidden_in.shape[0] <= gate_weight.shape[0] * CAP:
+        return gathered_body(*operands)
+    return dispatched_body(*operands)
+
+
 def solution(mesh):
     in_specs = (
         P(("groups", "expert"), "etp"),

time: 220 us -> 103 us (0.47)
  matrix products: 69.9 us -> 0 us
  Pallas kernels: 0 us -> 57.1 us
  blocking collectives: 48.2 us -> 0 us
  local copies, waits for them, and re-layouts: 48.1 us -> 1.27 us
  starting transfers between devices: 9.76 us -> 25.6 us
  between operations: 14.1 us -> 0.92 us
  waiting for transfers between devices: 26.5 us -> 14.1 us
    dot_general x11 -> x0, matrix products: 69.9 us -> none  [the longest x1 12.4 us: body(): jnp.einsum('secn,gsecf->genf', lax.all_gather(share_in, 'etp', axis=3, ti...]
    pallas_call x0 -> x11, Pallas kernels: none -> 57.1 us  [the longest x9 48.2 us: call(): pl.pallas_call(kernel, in_specs=specs, out_specs=out_specs or [pl.BlockSp...]
    all_to_all x2 -> x0, blocking collectives: 37.3 us -> none  [the longest x1 20.7 us: body(): lax.all_to_all(send_in, 'expert', split_axis=0, concat_axis=0, tiled=True)]
    ppermute x0 -> x27, starting transfers between devices: none -> 25.6 us  [the longest x12 19.8 us: shift(): lax.ppermute(array, 'expert', [(i, (i + by) % count) for i in range(count)])]
    reduce_scatter x2 -> x0, waiting for transfers between devices: 20.4 us -> none  [the longest x1 10.4 us: body(): lax.psum_scatter(out_part.astype(jnp.bfloat16), 'etp', scatter_dimension=...]
    convert_element_type x2 -> x0, local copies, waits for them, and re-layouts: 17.8 us -> none  [the longest x1 17.2 us: body(): weight_grads[1].astype(jnp.bfloat16)]
    ppermute x0 -> x27, waiting for transfers between devices: none -> 14.1 us  [the longest x15 14.1 us: swap(): return lax.ppermute(array, 'etp', [(i, i ^ bit) for i in range(count)])]
    gather x6 -> x0, local copies, waits for them, and re-layouts: 13.5 us -> none  [the longest x2 7.88 us: outgoing(): picked = padded[owners]]
  transfers between devices with their start and end apart: 6 -> 27, of which waited for: 4 -> 7; matrix products, arithmetic and copies ran while one was open for 37% -> 1% of each run, Pallas kernels for 0% -> 55%
where the time goes in v3:
time: 103 us; the launch traced here: 102 us
  Pallas kernels  57.1 us (55%)
  starting transfers between devices  25.6 us (25%)
  waiting for transfers between devices  14.1 us (14%)
  other arithmetic  3.3 us (3%)
  local copies, waits for them, and re-layouts  1.27 us (1%)
    pallas_call x9, Pallas kernels, call(): pl.pallas_call(kernel, in_specs=specs, out_specs=out_specs or [pl.BlockSp...  48.2 us
    ppermute x12, starting transfers between devices, shift(): lax.ppermute(array, 'expert', [(i, (i + by) % count) for i in range(count)])  19.8 us
    ppermute x15, waiting for transfers between devices, swap(): return lax.ppermute(array, 'etp', [(i, i ^ bit) for i in range(count)])  14.1 us
    pallas_call x2, Pallas kernels, in_vmem(): pl.pallas_call(load_kernel, in_specs=[pl.BlockSpec(memory_space=pltpu.HBM...  8.87 us
    ppermute x15, starting transfers between devices, swap(): return lax.ppermute(array, 'etp', [(i, i ^ bit) for i in range(count)])  5.79 us
  transfers between devices with their start and end apart: 27, of which 7 were waited for; matrix products, arithmetic and copies ran while one was open for 1% of the time, Pallas kernels for 55%

profile of v3, /device:TPU:0, one launch (start us, length us, event | category | flops | bytes accessed | tf_op | source)
XLA Modules:
  0.0 102.3 jit_solution(13060791433596622755)
XLA Ops:
  0.6 0.7 fusion.24
  1.3 0.7 fusion.26
  2.0 0.8 fusion.17.o0.own_ref
  2.9 5.0 %collective-permute-start.5 = (bf16[144,256]{1,0:T(8,128)(2,1)S(1)}, bf16[144,256]{1,0:T(8,128)(2,1)S(1)}, u32[]{:S(2)}, u32[]{:S(2)}) collective-permute-start(bf16[144,256]{1,0:T(8,128)(2,1)S(1)} %fusion.17.o0.own_ref), channel_id=1, source_target_pairs={{0,12},{4,0},{8,4},{12,8},{1,13},{5,1},{9,5},{13,9},{2,14},{6,2},{... | collective-permute-start | bytes 221192 | tf_op jit(solution)/shard_map/ppermute | solution.py:320
  7.9 1.0 collective-permute-start.3
  8.9 1.5 %collective-permute-start.1 = (bf16[144,256]{1,0:T(8,128)(2,1)S(1)}, bf16[144,256]{1,0:T(8,128)(2,1)S(1)}, u32[]{:S(2)}, u32[]{:S(2)}) collective-permute-start(bf16[144,256]{1,0:T(8,128)(2,1)S(1)} %fusion.17.o0.own_ref), channel_id=1, source_target_pairs={{0,2},{1,3},{2,0},{3,1},{4,6},{5,7},{6,4},{7,5},{8,10},{9,11},{10,... | collective-permute-start | bytes 221192 | tf_op jit(solution)/shard_map/ppermute | solution.py:315
  10.4 4.4 %shard_map.127 = (bf16[16,352,1024]{2,1,0:T(8,128)(2,1)S(1)}, f32[8,128]{1,0:T(8,128)S(1)}) custom-call(bf16[16,352,1024]{2,1,0:T(8,128)(2,1)} %bitcast.44), custom_call_target="tpu_custom_call" | custom-call | bytes 11534336 | tf_op jit(solution)/shard_map/pallas_call | solution.py:252
  14.9 4.4 %shard_map.128 = (bf16[16,352,1024]{2,1,0:T(8,128)(2,1)S(1)}, f32[8,128]{1,0:T(8,128)S(1)}) custom-call(bf16[16,352,1024]{2,1,0:T(8,128)(2,1)} %bitcast.45), custom_call_target="tpu_custom_call" | custom-call | bytes 11534336 | tf_op jit(solution)/shard_map/pallas_call | solution.py:252
  20.2 7.1 %collective-permute-done.7.b2 = bf16[3,144,256]{2,1,0:T(8,128)(2,1)S(1)} collective-permute-done((bf16[3,144,256]{2,1,0:T(8,128)(2,1)S(1)}, bf16[3,144,256]{2,1,0:T(8,128)(2,1)S(1)}, u32[]{:S(2)}, u32[]{:S(2)}) %collective-permute-start.7) | collective-permute-done | bytes 221216 | tf_op jit(solution)/shard_map/ppermute | solution.py:315
  28.3 3.7 %collective-permute-done.9.refs_1_ = bf16[128,256]{1,0:T(8,128)(2,1)S(1)} collective-permute-done((bf16[128,256]{1,0:T(8,128)(2,1)S(1)}, bf16[128,256]{1,0:T(8,128)(2,1)S(1)}, u32[]{:S(2)}, u32[]{:S(2)}) %collective-permute-start.9) | collective-permute-done | bytes 65568 | tf_op jit(solution)/shard_map/ppermute | solution.py:315
  32.1 2.9 %collective-permute-start.12 = (bf16[2,128,256]{2,1,0:T(8,128)(2,1)S(1)}, bf16[2,128,256]{2,1,0:T(8,128)(2,1)S(1)}, u32[]{:S(2)}, u32[]{:S(2)}) collective-permute-start(bf16[2,128,256]{2,1,0:T(8,128)(2,1)S(1)} %shard_map.130.later_ref.refs_0_.a0), channel_id=1, source_target_pairs={{0,12},{4,0},{8,4},{12,8},{1,13},{5,1},{9,5},{13,9},{2,14},{6,2},{... | collective-permute-start | bytes 393224 | tf_op jit(solution)/shard_map/ppermute | solution.py:320
  35.0 1.1 %collective-permute-start.11 = (bf16[2,128,256]{2,1,0:T(8,128)(2,1)S(1)}, bf16[2,128,256]{2,1,0:T(8,128)(2,1)S(1)}, u32[]{:S(2)}, u32[]{:S(2)}) collective-permute-start(bf16[2,128,256]{2,1,0:T(8,128)(2,1)S(1)} %shard_map.130.later_ref.refs_0_.a0), channel_id=1, source_target_pairs={{0,8},{4,12},{8,0},{12,4},{1,9},{5,13},{9,1},{13,5},{2,10},{6,14},... | collective-permute-start | bytes 393224 | tf_op jit(solution)/shard_map/ppermute | solution.py:320
  36.1 14.0 %shard_map.131 = (bf16[4,256,1024]{2,1,0:T(8,128)(2,1)S(1)}, bf16[16,64,1024]{2,1,0:T(8,128)(2,1)S(1)}, bf16[16,64,352]{2,1,0:T(8,128)(2,1)S(1)}, f32[16,64,352]...) custom-call(s32[64]{0:T(128)S(1)} %copy-done.1, ...), custom_call_target="tpu_custom_call" | custom-call | flops 2214592512 | bytes 17301504 | tf_op jit(solution)/shard_map/pallas_call | solution.py:287
  51.8 1.0 collective-permute-done.14.n0
  53.3 7.1 %shard_map.133 = (bf16[16,64,1024]{2,1,0:T(8,128)(2,1)S(1)}, bf16[16,64,352]{2,1,0:T(8,128)(2,1)S(1)}, bf16[16,64,352]{2,1,0:T(8,128)(2,1)S(1)}, bf16[16,64,352]{2,1,0:T(8,128)(2,1)S(1)}, bf16[4,16,256]{2,1,0:T(8,128)(2,1)S(1)}) custom-call(bf16[144,256]{1,0:T(8,128)(2,1)S(1)} %fusion.17.o0.own_ref, bf16[3,144,256]{2,1,0:T(8,128)(2,1)S(1)} %shard_map.129.refs_2_.b0.info_ref, ...), custom_call_target="tpu_custom_call" | custom-call | flops 738197504 | bytes 5767168 | tf_op jit(solution)/shard_map/pallas_call | solution.py:287
  61.2 6.0 %shard_map.134 = (bf16[2,4,144,256]{3,2,1,0:T(8,128)(2,1)S(1)}, bf16[2,4,144,256]{3,2,1,0:T(8,128)(2,1)S(1)}) custom-call(bf16[16,352,1024]{2,1,0:T(8,128)(2,1)S(1)} %get-tuple-element.36.gate_ref, bf16[16,352,1024]{2,1,0:T(8,128)(2,1)S(1)} %get-tuple-element.37.up_ref, bf16[16,64,352]{2,1,0:T(8,128)(2,1)S(1)} %get-tuple-element.57.p_ref.left_ref, ...), custom_call_target="tpu_custom_call" | custom-call | flops 1476395008 | bytes 11534336 | tf_op jit(solution)/shard_map/pallas_call | solution.py:287
  67.3 1.7 %collective-permute-done.18 = bf16[4,128,256]{2,1,0:T(8,128)(2,1)S(1)} collective-permute-done((bf16[4,128,256]{2,1,0:T(8,128)(2,1)S(1)}, bf16[4,128,256]{2,1,0:T(8,128)(2,1)S(1)}, u32[]{:S(2)}, u32[]{:S(2)}) %collective-permute-start.18) | collective-permute-done | bytes 262176 | tf_op jit(solution)/shard_map/ppermute | solution.py:315
  69.1 3.9 %collective-permute-start.19 = (bf16[128,256]{1,0:T(8,128)(2,1)S(1)}, bf16[128,256]{1,0:T(8,128)(2,1)S(1)}, u32[]{:S(2)}, u32[]{:S(2)}) collective-permute-start(bf16[128,256]{1,0:T(8,128)(2,1)S(1)} %get-tuple-element.65), channel_id=1, source_target_pairs={{0,12},{4,0},{8,4},{12,8},{1,13},{5,1},{9,5},{13,9},{2,14},{6,2},{... | collective-permute-start | bytes 196616 | tf_op jit(solution)/shard_map/ppermute | solution.py:320
  74.3 6.8 %shard_map.137 = bf16[16,352,1024]{2,1,0:T(8,128)(2,1)} custom-call(bf16[16,64,352]{2,1,0:T(8,128)(2,1)S(1)} %get-tuple-element.60.left_ref, bf16[16,64,1024]{2,1,0:T(8,128)(2,1)S(1)} %get-tuple-element.61.right_ref), custom_call_target="tpu_custom_call" | custom-call | flops 738197504 | bytes 5767168 | tf_op jit(solution)/shard_map/pallas_call | solution.py:287
  81.2 0.7 fusion.16
  82.0 3.3 %collective-permute-start.24 = (bf16[144,256]{1,0:T(8,128)(2,1)S(1)}, bf16[144,256]{1,0:T(8,128)(2,1)S(1)}, u32[]{:S(2)}, u32[]{:S(2)}) collective-permute-start(bf16[144,256]{1,0:T(8,128)(2,1)S(1)} %get-tuple-element.62), channel_id=1, source_target_pairs={{0,12},{4,0},{8,4},{12,8},{1,13},{5,1},{9,5},{13,9},{2,14},{6,2},{... | collective-permute-start | bytes 221192 | tf_op jit(solution)/shard_map/ppermute | solution.py:320
  85.9 1.4 %collective-permute-start.25 = (bf16[144,256]{1,0:T(8,128)(2,1)S(1)}, bf16[144,256]{1,0:T(8,128)(2,1)S(1)}, u32[]{:S(2)}, u32[]{:S(2)}) collective-permute-start(bf16[144,256]{1,0:T(8,128)(2,1)S(1)} %get-tuple-element.64), channel_id=1, source_target_pairs={{0,8},{4,12},{8,0},{12,4},{1,9},{5,13},{9,1},{13,5},{2,10},{6,14},... | collective-permute-start | bytes 221192 | tf_op jit(solution)/shard_map/ppermute | solution.py:320
  87.3 6.9 %shard_map.136 = bf16[16,352,1024]{2,1,0:T(8,128)(2,1)} custom-call(bf16[16,64,352]{2,1,0:T(8,128)(2,1)S(1)} %get-tuple-element.59.q_ref.left_ref, bf16[16,64,1024]{2,1,0:T(8,128)(2,1)S(1)} %get-tuple-element.58.right_ref), custom_call_target="tpu_custom_call" | custom-call | flops 738197504 | bytes 5767168 | tf_op jit(solution)/shard_map/pallas_call | solution.py:287
  94.1 6.9 %shard_map.135 = bf16[16,352,1024]{2,1,0:T(8,128)(2,1)} custom-call(bf16[16,64,352]{2,1,0:T(8,128)(2,1)S(1)} %get-tuple-element.57.p_ref.left_ref, bf16[16,64,1024]{2,1,0:T(8,128)(2,1)S(1)} %get-tuple-element.58.right_ref), custom_call_target="tpu_custom_call" | custom-call | flops 738197504 | bytes 5767168 | tf_op jit(solution)/shard_map/pallas_call | solution.py:287
  (58 shorter events, 8.4 us)
Async XLA Ops:
  2.9 16.4 %collective-permute-start.5 = (bf16[144,256]{1,0:T(8,128)(2,1)S(1)}, bf16[144,256]{1,0:T(8,128)(2,1)S(1)}, u32[]{:S(2)}, u32[]{:S(2)}) collective-permute-start(bf16[144,256]{1,0:T(8,128)(2,1)S(1)} %fusion.17.o0.own_ref), channel_id=1, source_target_pairs={{0,12},{4,0},{8,4},{12,8},{1,13},{5,1},{9,5},{13,9},{2,14},{6,2},{... | collective-permute-start | bytes 221192 | tf_op jit(solution)/shard_map/ppermute | solution.py:320
  7.9 11.4 %collective-permute-start.4 = (bf16[144,256]{1,0:T(8,128)(2,1)S(1)}, bf16[144,256]{1,0:T(8,128)(2,1)S(1)}, u32[]{:S(2)}, u32[]{:S(2)}) collective-permute-start(bf16[144,256]{1,0:T(8,128)(2,1)S(1)} %fusion.17.o0.own_ref), channel_id=1, source_target_pairs={{0,8},{4,12},{8,0},{12,4},{1,9},{5,13},{9,1},{13,5},{2,10},{6,14},... | collective-permute-start | bytes 221192 | tf_op jit(solution)/shard_map/ppermute | solution.py:320
  7.9 11.4 %collective-permute-start.3 = (bf16[144,256]{1,0:T(8,128)(2,1)S(1)}, bf16[144,256]{1,0:T(8,128)(2,1)S(1)}, u32[]{:S(2)}, u32[]{:S(2)}) collective-permute-start(bf16[144,256]{1,0:T(8,128)(2,1)S(1)} %fusion.17.o0.own_ref), channel_id=1, source_target_pairs={{0,4},{4,8},{8,12},{12,0},{1,5},{5,9},{9,13},{13,1},{2,6},{6,10},{... | collective-permute-start | bytes 221192 | tf_op jit(solution)/shard_map/ppermute | solution.py:320
  8.9 10.4 %collective-permute-start.1 = (bf16[144,256]{1,0:T(8,128)(2,1)S(1)}, bf16[144,256]{1,0:T(8,128)(2,1)S(1)}, u32[]{:S(2)}, u32[]{:S(2)}) collective-permute-start(bf16[144,256]{1,0:T(8,128)(2,1)S(1)} %fusion.17.o0.own_ref), channel_id=1, source_target_pairs={{0,2},{1,3},{2,0},{3,1},{4,6},{5,7},{6,4},{7,5},{8,10},{9,11},{10,... | collective-permute-start | bytes 221192 | tf_op jit(solution)/shard_map/ppermute | solution.py:315
  10.4 8.9 %collective-permute-start = (bf16[144,256]{1,0:T(8,128)(2,1)S(1)}, bf16[144,256]{1,0:T(8,128)(2,1)S(1)}, u32[]{:S(2)}, u32[]{:S(2)}) collective-permute-start(bf16[144,256]{1,0:T(8,128)(2,1)S(1)} %fusion.17.o0.own_ref), channel_id=1, source_target_pairs={{0,1},{1,0},{2,3},{3,2},{4,5},{5,4},{6,7},{7,6},{8,9},{9,8},{10,11... | collective-permute-start | bytes 221192 | tf_op jit(solution)/shard_map/ppermute | solution.py:315
  19.4 7.9 %collective-permute-start.7 = (bf16[3,144,256]{2,1,0:T(8,128)(2,1)S(1)}, bf16[3,144,256]{2,1,0:T(8,128)(2,1)S(1)}, u32[]{:S(2)}, u32[]{:S(2)}) collective-permute-start(bf16[3,144,256]{2,1,0:T(8,128)(2,1)S(1)} %shard_map.129.refs_2_.b0.info_ref), channel_id=1, source_target_pairs={{0,2},{1,3},{2,0},{3,1},{4,6},{5,7},{6,4},{7,5},{8,10},{9,11},{10,... | collective-permute-start | bytes 663560 | tf_op jit(solution)/shard_map/ppermute | solution.py:315
  20.0 16.1 %collective-permute-start.6 = (bf16[3,144,256]{2,1,0:T(8,128)(2,1)S(1)}, bf16[3,144,256]{2,1,0:T(8,128)(2,1)S(1)}, u32[]{:S(2)}, u32[]{:S(2)}) collective-permute-start(bf16[3,144,256]{2,1,0:T(8,128)(2,1)S(1)} %shard_map.129.refs_2_.b0.info_ref), channel_id=1, source_target_pairs={{0,1},{1,0},{2,3},{3,2},{4,5},{5,4},{6,7},{7,6},{8,9},{9,8},{10,11... | collective-permute-start | bytes 663560 | tf_op jit(solution)/shard_map/ppermute | solution.py:315
  27.3 8.8 %collective-permute-start.8 = (bf16[3,144,256]{2,1,0:T(8,128)(2,1)S(1)}, bf16[3,144,256]{2,1,0:T(8,128)(2,1)S(1)}, u32[]{:S(2)}, u32[]{:S(2)}) collective-permute-start(bf16[3,144,256]{2,1,0:T(8,128)(2,1)S(1)} %collective-permute-done.7.b2), channel_id=1, source_target_pairs={{0,1},{1,0},{2,3},{3,2},{4,5},{5,4},{6,7},{7,6},{8,9},{9,8},{10,11... | collective-permute-start | bytes 663560 | tf_op jit(solution)/shard_map/ppermute | solution.py:315
  27.3 4.8 %collective-permute-start.2 = (bf16[144,256]{1,0:T(8,128)(2,1)S(1)}, bf16[144,256]{1,0:T(8,128)(2,1)S(1)}, u32[]{:S(2)}, u32[]{:S(2)}) collective-permute-start(bf16[144,256]{1,0:T(8,128)(2,1)S(1)} %collective-permute-done.1.refs_5_.o2), channel_id=1, source_target_pairs={{0,1},{1,0},{2,3},{3,2},{4,5},{5,4},{6,7},{7,6},{8,9},{9,8},{10,11... | collective-permute-start | bytes 221192 | tf_op jit(solution)/shard_map/ppermute | solution.py:315
  27.8 4.3 %collective-permute-start.9 = (bf16[128,256]{1,0:T(8,128)(2,1)S(1)}, bf16[128,256]{1,0:T(8,128)(2,1)S(1)}, u32[]{:S(2)}, u32[]{:S(2)}) collective-permute-start(bf16[128,256]{1,0:T(8,128)(2,1)S(1)} %copy-done), channel_id=1, source_target_pairs={{0,2},{1,3},{2,0},{3,1},{4,6},{5,7},{6,4},{7,5},{8,10},{9,11},{10,... | collective-permute-start | bytes 196616 | tf_op jit(solution)/shard_map/ppermute | solution.py:315
  32.1 18.0 %collective-permute-start.12 = (bf16[2,128,256]{2,1,0:T(8,128)(2,1)S(1)}, bf16[2,128,256]{2,1,0:T(8,128)(2,1)S(1)}, u32[]{:S(2)}, u32[]{:S(2)}) collective-permute-start(bf16[2,128,256]{2,1,0:T(8,128)(2,1)S(1)} %shard_map.130.later_ref.refs_0_.a0), channel_id=1, source_target_pairs={{0,12},{4,0},{8,4},{12,8},{1,13},{5,1},{9,5},{13,9},{2,14},{6,2},{... | collective-permute-start | bytes 393224 | tf_op jit(solution)/shard_map/ppermute | solution.py:320
  35.0 15.1 %collective-permute-start.11 = (bf16[2,128,256]{2,1,0:T(8,128)(2,1)S(1)}, bf16[2,128,256]{2,1,0:T(8,128)(2,1)S(1)}, u32[]{:S(2)}, u32[]{:S(2)}) collective-permute-start(bf16[2,128,256]{2,1,0:T(8,128)(2,1)S(1)} %shard_map.130.later_ref.refs_0_.a0), channel_id=1, source_target_pairs={{0,8},{4,12},{8,0},{12,4},{1,9},{5,13},{9,1},{13,5},{2,10},{6,14},... | collective-permute-start | bytes 393224 | tf_op jit(solution)/shard_map/ppermute | solution.py:320
  36.1 14.0 %collective-permute-start.10 = (bf16[2,128,256]{2,1,0:T(8,128)(2,1)S(1)}, bf16[2,128,256]{2,1,0:T(8,128)(2,1)S(1)}, u32[]{:S(2)}, u32[]{:S(2)}) collective-permute-start(bf16[2,128,256]{2,1,0:T(8,128)(2,1)S(1)} %shard_map.130.later_ref.refs_0_.a0), channel_id=1, source_target_pairs={{0,4},{4,8},{8,12},{12,0},{1,5},{5,9},{9,13},{13,1},{2,6},{6,10},{... | collective-permute-start | bytes 393224 | tf_op jit(solution)/shard_map/ppermute | solution.py:320
  50.6 9.9 %collective-permute-start.13 = (bf16[2,4,128,256]{3,2,1,0:T(8,128)(2,1)S(1)}, bf16[2,4,128,256]{3,2,1,0:T(8,128)(2,1)S(1)}, u32[]{:S(2)}, u32[]{:S(2)}) collective-permute-start(bf16[2,4,128,256]{3,2,1,0:T(8,128)(2,1)S(1)} %get-tuple-element.41), channel_id=1, source_target_pairs={{0,1},{1,0},{2,3},{3,2},{4,5},{5,4},{6,7},{7,6},{8,9},{9,8},{10,11... | collective-permute-start | bytes 1572872 | tf_op jit(solution)/shard_map/ppermute | solution.py:315
  50.7 2.1 %collective-permute-start.14 = (bf16[2,128,256]{2,1,0:T(8,128)(2,1)S(1)}, bf16[2,128,256]{2,1,0:T(8,128)(2,1)S(1)}, u32[]{:S(2)}, u32[]{:S(2)}) collective-permute-start(bf16[2,128,256]{2,1,0:T(8,128)(2,1)S(1)} %shard_map.130.later_ref.refs_0_.a0), channel_id=1, source_target_pairs={{0,1},{1,0},{2,3},{3,2},{4,5},{5,4},{6,7},{7,6},{8,9},{9,8},{10,11... | collective-permute-start | bytes 393224 | tf_op jit(solution)/shard_map/ppermute | solution.py:315
  60.6 8.4 %collective-permute-start.18 = (bf16[4,128,256]{2,1,0:T(8,128)(2,1)S(1)}, bf16[4,128,256]{2,1,0:T(8,128)(2,1)S(1)}, u32[]{:S(2)}, u32[]{:S(2)}) collective-permute-start(bf16[4,128,256]{2,1,0:T(8,128)(2,1)S(1)} %fusion.5), channel_id=1, source_target_pairs={{0,2},{1,3},{2,0},{3,1},{4,6},{5,7},{6,4},{7,5},{8,10},{9,11},{10,... | collective-permute-start | bytes 786440 | tf_op jit(solution)/shard_map/ppermute | solution.py:315
  67.2 6.4 %collective-permute-start.22 = (bf16[2,4,144,256]{3,2,1,0:T(8,128)(2,1)S(1)}, bf16[2,4,144,256]{3,2,1,0:T(8,128)(2,1)S(1)}, u32[]{:S(2)}, u32[]{:S(2)}) collective-permute-start(bf16[2,4,144,256]{3,2,1,0:T(8,128)(2,1)S(1)} %get-tuple-element.54), channel_id=1, source_target_pairs={{0,1},{1,0},{2,3},{3,2},{4,5},{5,4},{6,7},{7,6},{8,9},{9,8},{10,11... | collective-permute-start | bytes 1769480 | tf_op jit(solution)/shard_map/ppermute | solution.py:315
  69.1 12.0 %collective-permute-start.19 = (bf16[128,256]{1,0:T(8,128)(2,1)S(1)}, bf16[128,256]{1,0:T(8,128)(2,1)S(1)}, u32[]{:S(2)}, u32[]{:S(2)}) collective-permute-start(bf16[128,256]{1,0:T(8,128)(2,1)S(1)} %get-tuple-element.65), channel_id=1, source_target_pairs={{0,12},{4,0},{8,4},{12,8},{1,13},{5,1},{9,5},{13,9},{2,14},{6,2},{... | collective-permute-start | bytes 196616 | tf_op jit(solution)/shard_map/ppermute | solution.py:320
  73.0 8.2 %collective-permute-start.21 = (bf16[128,256]{1,0:T(8,128)(2,1)S(1)}, bf16[128,256]{1,0:T(8,128)(2,1)S(1)}, u32[]{:S(2)}, u32[]{:S(2)}) collective-permute-start(bf16[128,256]{1,0:T(8,128)(2,1)S(1)} %get-tuple-element.66), channel_id=1, source_target_pairs={{0,4},{4,8},{8,12},{12,0},{1,5},{5,9},{9,13},{13,1},{2,6},{6,10},{... | collective-permute-start | bytes 196616 | tf_op jit(solution)/shard_map/ppermute | solution.py:320
  73.0 8.2 %collective-permute-start.20 = (bf16[128,256]{1,0:T(8,128)(2,1)S(1)}, bf16[128,256]{1,0:T(8,128)(2,1)S(1)}, u32[]{:S(2)}, u32[]{:S(2)}) collective-permute-start(bf16[128,256]{1,0:T(8,128)(2,1)S(1)} %get-tuple-element.67), channel_id=1, source_target_pairs={{0,8},{4,12},{8,0},{12,4},{1,9},{5,13},{9,1},{13,5},{2,10},{6,14},... | collective-permute-start | bytes 196616 | tf_op jit(solution)/shard_map/ppermute | solution.py:320
  73.7 8.1 %collective-permute-start.23 = (bf16[4,144,256]{2,1,0:T(8,128)(2,1)S(1)}, bf16[4,144,256]{2,1,0:T(8,128)(2,1)S(1)}, u32[]{:S(2)}, u32[]{:S(2)}) collective-permute-start(bf16[4,144,256]{2,1,0:T(8,128)(2,1)S(1)} %fusion.3), channel_id=1, source_target_pairs={{0,2},{1,3},{2,0},{3,1},{4,6},{5,7},{6,4},{7,5},{8,10},{9,11},{10,... | collective-permute-start | bytes 884744 | tf_op jit(solution)/shard_map/ppermute | solution.py:315
  82.0 19.0 %collective-permute-start.24 = (bf16[144,256]{1,0:T(8,128)(2,1)S(1)}, bf16[144,256]{1,0:T(8,128)(2,1)S(1)}, u32[]{:S(2)}, u32[]{:S(2)}) collective-permute-start(bf16[144,256]{1,0:T(8,128)(2,1)S(1)} %get-tuple-element.62), channel_id=1, source_target_pairs={{0,12},{4,0},{8,4},{12,8},{1,13},{5,1},{9,5},{13,9},{2,14},{6,2},{... | collective-permute-start | bytes 221192 | tf_op jit(solution)/shard_map/ppermute | solution.py:320
  85.2 15.8 %collective-permute-start.26 = (bf16[144,256]{1,0:T(8,128)(2,1)S(1)}, bf16[144,256]{1,0:T(8,128)(2,1)S(1)}, u32[]{:S(2)}, u32[]{:S(2)}) collective-permute-start(bf16[144,256]{1,0:T(8,128)(2,1)S(1)} %get-tuple-element.63), channel_id=1, source_target_pairs={{0,4},{4,8},{8,12},{12,0},{1,5},{5,9},{9,13},{13,1},{2,6},{6,10},{... | collective-permute-start | bytes 221192 | tf_op jit(solution)/shard_map/ppermute | solution.py:320
  85.9 15.2 %collective-permute-start.25 = (bf16[144,256]{1,0:T(8,128)(2,1)S(1)}, bf16[144,256]{1,0:T(8,128)(2,1)S(1)}, u32[]{:S(2)}, u32[]{:S(2)}) collective-permute-start(bf16[144,256]{1,0:T(8,128)(2,1)S(1)} %get-tuple-element.64), channel_id=1, source_target_pairs={{0,8},{4,12},{8,0},{12,4},{1,9},{5,13},{9,1},{13,5},{2,10},{6,14},... | collective-permute-start | bytes 221192 | tf_op jit(solution)/shard_map/ppermute | solution.py:320
  (5 other events, 48.4 us)

commit v4 on v3

--- a/solution.py
+++ b/solution.py
@@ -26,14 +26,24 @@
     return lax.dot_general(a, b, (((0,), (0,)), ((), ())), preferred_element_type=F32)
 
 
-def routing_rows(expert_ids, gate_values):
-    choose = expert_ids.shape[1]
-    high = lax.reduce_precision(gate_values, exponent_bits=8, mantissa_bits=7)
-    low = lax.reduce_precision(gate_values - high, exponent_bits=8, mantissa_bits=7)
-    pad = ((0, 8 - choose), (0, 0))
-    top = jnp.concatenate([jnp.pad(expert_ids.T.astype(F32), pad), jnp.pad(high.T, pad)], axis=1)
-    bottom = jnp.concatenate([jnp.pad(low.T, pad), jnp.zeros_like(jnp.pad(low.T, pad))], axis=1)
-    return jnp.concatenate([top, bottom], axis=0).astype(BF16)
+def pack_kernel(hidden_hbm, ids_hbm, gates_hbm, own_ref, ids_ref, gates_ref, sems):
+    tokens, width = hidden_hbm.shape
+    choose = ids_ref.shape[0]
+    copies = [
+        pltpu.make_async_copy(hidden_hbm, own_ref.at[pl.ds(0, tokens)], sems.at[0]),
+        pltpu.make_async_copy(ids_hbm, ids_ref, sems.at[1]),
+        pltpu.make_async_copy(gates_hbm, gates_ref, sems.at[2]),
+    ]
+    for copy in copies:
+        copy.start()
+    for copy in copies:
+        copy.wait()
+    gates = gates_ref[...]
+    high = gates.astype(BF16).astype(F32)
+    fill = jnp.zeros((8 - choose, tokens), F32)
+    top = jnp.concatenate([jnp.concatenate([ids_ref[...].astype(F32), fill], axis=0), jnp.concatenate([high, fill], axis=0)], axis=1)
+    low = jnp.concatenate([jnp.concatenate([gates - high, fill], axis=0), jnp.zeros((8, width - tokens), F32)], axis=1)
+    own_ref[tokens:tokens + EXTRA, :] = jnp.concatenate([top, low], axis=0).astype(BF16)
 
 
 def routing(info, choose, tokens):
@@ -52,7 +62,7 @@
             home[q // 2, s, 0:tokens, :] = tn(onehot[s], rows[s, :, columns(me, q, width)]).astype(BF16)
 
 
-RING = 8
+RING = 4
 
 
 def ring(weight, slots, sems):
@@ -70,7 +80,7 @@
 
 def forward_kernel(
     choose, capacity_ref, o0, o1, o2, o3, b0, b1, b2, b3, gate_ref, up_ref, down_hbm, later_ref,
-    out_rows, rows_ref, act_ref, slope_ref, silu_ref, onehot, slot_gate,
+    out_rows, rows_ref, act_ref, a_ref, slope_ref, silu_ref, onehot, slot_gate,
     down_ref, sems,
 ):
     sources, slots, tokens = onehot.shape
@@ -112,29 +122,50 @@
             picked = nn(table, block[q][0:tokens, :]).astype(BF16).reshape(experts, CAP, width)
             rows_ref[:, s * CAP:(s + 1) * CAP, columns(me, q, width)] = picked
 
-    def some(turn, _):
-        for e in (turn * 2, turn * 2 + 1):
-            wait(e)
-        for e in (turn * 2, turn * 2 + 1):
-            x = rows_ref[e]
-            hidden_gate = nt(x, gate_ref[e])
-            hidden_up = nt(x, up_ref[e])
-            sigma = jax.nn.sigmoid(hidden_gate)
-            silu = hidden_gate * sigma
-            activ = (silu * hidden_up).astype(BF16)
-            act_ref[e] = activ
-            slope_ref[e] = hidden_up * sigma * (1.0 + hidden_gate * (1.0 - sigma))
-            silu_ref[e] = silu
-            scaled = (activ.astype(F32) * slot_gate[e][:, 0:1]).astype(BF16)
-            out = nn(scaled, down_ref[lax.rem(e, RING)]).astype(BF16)
-            at = pl.ds(pl.multiple_of(e * CAP, CAP), CAP)
-            for s in range(sources):
-                out_rows[s, at, :] = out[s * CAP:(s + 1) * CAP]
-        for e in (turn * 2, turn * 2 + 1):
-            start(e + RING)
+    def activate(e):
+        x = rows_ref[e]
+        hidden_gate = nt(x, gate_ref[e])
+        hidden_up = nt(x, up_ref[e])
+        sigma = jax.nn.sigmoid(hidden_gate)
+        silu = hidden_gate * sigma
+        activ = (silu * hidden_up).astype(BF16)
+        act_ref[e] = activ
+        slope_ref[e] = hidden_up * sigma * (1.0 + hidden_gate * (1.0 - sigma))
+        silu_ref[e] = silu
+        a_ref[e] = (activ.astype(F32) * slot_gate[e][:, 0:1]).astype(BF16)
+
+    def project(e):
+        out = nn(a_ref[e], down_ref[lax.rem(e, RING)]).astype(BF16)
+        at = pl.ds(pl.multiple_of(e * CAP, CAP), CAP)
+        for s in range(sources):
+            out_rows[s, at, :] = out[s * CAP:(s + 1) * CAP]
+
+    def both(e):
+        wait(e - 2)
+        wait(e - 1)
+        project(e - 2)
+        project(e - 1)
+        activate(e)
+        activate(e + 1)
+        start(e - 2 + RING)
+        start(e - 1 + RING)
+
+    skewed(experts, activate, wait, project, both)
+
+
+def skewed(experts, first, wait, second, both):
+    first(jnp.int32(0))
+    first(jnp.int32(1))
+
+    def turn(i, _):
+        both(i * 2)
         return 0
 
-    lax.fori_loop(0, experts // 2, some, 0)
+    lax.fori_loop(1, experts // 2, turn, 0)
+    for e in (experts - 2, experts - 1):
+        wait(jnp.int32(e))
+    for e in (experts - 2, experts - 1):
+        second(jnp.int32(e))
 
 
 def home_kernel(onehot, rows, *refs):
@@ -142,42 +173,12 @@
     send_home(keep, send, lax.axis_index("etp"), onehot, rows, keep.shape[2], keep.shape[3])
 
 
-def slope_kernel(
-    choose, own_ref, info_ref, a0, a1, a2, a3, n0, n1, n2, n3,
-    down_hbm, act_ref, slope_ref, silu_ref, onehot, slot_gate,
-    rows_ref, p_ref, q_ref, a_ref, value_ref,
-    dots, down_ref, sems,
-):
+def home_values_kernel(choose, onehot, rows, dots, own_ref, info_ref, *refs):
+    keep, send = refs[-2:]
     sources, slots, tokens = onehot.shape
     experts = slots // CAP
-    start, wait = ring(down_hbm, down_ref, sems)
-    for e in range(RING):
-        start(jnp.int32(e))
-    width = own_ref.shape[1]
-    me = lax.axis_index("etp")
-    for s, (here, near) in enumerate(((a0, n0), (a1, n1), (a2, n2), (a3, n3))):
-        for q in range(4):
-            block = (near if q % 2 else here)[q // 2]
-            picked = nn(onehot[s], block).astype(BF16).reshape(experts, CAP, width)
-            rows_ref[:, s * CAP:(s + 1) * CAP, columns(me, q, width)] = picked
-
-    def some(turn, _):
-        for e in (turn * 2, turn * 2 + 1):
-            wait(e)
-        for e in (turn * 2, turn * 2 + 1):
-            grad = nt(rows_ref[e], down_ref[lax.rem(e, RING)])
-            activ = act_ref[e].astype(F32)
-            gate = slot_gate[e][:, 0:1]
-            dots[e] = jnp.broadcast_to(jnp.sum(activ * grad, axis=1, keepdims=True), dots.shape[1:])
-            a_ref[e] = (activ * gate).astype(BF16)
-            grad = grad * gate
-            p_ref[e] = (grad * slope_ref[e]).astype(BF16)
-            q_ref[e] = (grad * silu_ref[e]).astype(BF16)
-        for e in (turn * 2, turn * 2 + 1):
-            start(e + RING)
-        return 0
-
-    lax.fori_loop(0, experts // 2, some, 0)
+    width = keep.shape[3]
+    send_home(keep, send, lax.axis_index("etp"), onehot, rows, tokens, width)
     expert = lax.broadcasted_iota(jnp.int32, (experts, tokens), 0)
     mine = (lax.axis_index("expert") * experts + expert).astype(F32)
     for s in range(sources):
@@ -185,58 +186,119 @@
         ids, _ = routing(info, choose, tokens)
         chosen = onehot[s].astype(F32).reshape(experts, CAP, tokens)
         share = jnp.sum(chosen * dots[:, s * CAP:(s + 1) * CAP, :], axis=1)
-        rows = [jnp.sum(jnp.where(ids[k:k + 1, :] == mine, share, 0.0), axis=0, keepdims=True) for k in range(choose)]
-        rows = jnp.concatenate(rows + [jnp.zeros((EXTRA - choose, tokens), F32)], axis=0)
-        value_ref[s] = jnp.concatenate([rows, jnp.zeros((EXTRA, width - tokens), F32)], axis=1).astype(BF16)
-
-
-def back_kernel(gate_ref, up_ref, p_ref, q_ref, onehot, slot_gate, value_ref, keep, send, back_rows):
+        values = [jnp.sum(jnp.where(ids[k:k + 1, :] == mine, share, 0.0), axis=0, keepdims=True) for k in range(choose)]
+        values = jnp.concatenate(values + [jnp.zeros((EXTRA - choose, tokens), F32)], axis=0)
+        values = jnp.concatenate([values, jnp.zeros((EXTRA, width - tokens), F32)], axis=1).astype(BF16)
+        for home in (keep, send):
+            home[0, s, tokens:tokens + EXTRA, :] = values
+            home[1, s, tokens:tokens + EXTRA, :] = values
+
+
+def backward_kernel(
+    a0, a1, a2, a3, n0, n1, n2, n3,
+    gate_ref, up_ref, down_hbm, act_ref, slope_ref, silu_ref, onehot, slot_gate, earlier_ref,
+    back_rows, dots, rows_ref, p_ref, q_ref,
+    down_ref, sems,
+):
     sources, slots, tokens = onehot.shape
-    width = keep.shape[3]
-
-    def some(turn, _):
-        for e in (turn * 2, turn * 2 + 1):
-            back = nn(p_ref[e], gate_ref[e]) + nn(q_ref[e], up_ref[e])
-            back = (back * slot_gate[e][:, 0:1]).astype(BF16)
-            at = pl.ds(pl.multiple_of(e * CAP, CAP), CAP)
-            for s in range(sources):
-                back_rows[s, at, :] = back[s * CAP:(s + 1) * CAP]
+    experts = slots // CAP
+    width = a0.shape[2]
+    me = lax.axis_index("etp")
+    start, wait = ring(down_hbm, down_ref, sems)
+    for e in range(RING):
+        start(jnp.int32(e))
+    for s, (here, near) in enumerate(((a0, n0), (a1, n1), (a2, n2), (a3, n3))):
+        for q in range(4):
+            block = (near if q % 2 else here)[q // 2]
+            picked = nn(onehot[s], block).astype(BF16).reshape(experts, CAP, width)
+            rows_ref[:, s * CAP:(s + 1) * CAP, columns(me, q, width)] = picked
+
+    def slopes(e):
+        grad = nt(rows_ref[e], down_ref[lax.rem(e, RING)])
+        activ = act_ref[e].astype(F32)
+        dots[e] = jnp.broadcast_to(jnp.sum(activ * grad, axis=1, keepdims=True), dots.shape[1:])
+        grad = grad * slot_gate[e][:, 0:1]
+        p_ref[e] = (grad * slope_ref[e]).astype(BF16)
+        q_ref[e] = (grad * silu_ref[e]).astype(BF16)
+
+    def project(e):
+        back = nn(p_ref[e], gate_ref[e]) + nn(q_ref[e], up_ref[e])
+        back = (back * slot_gate[e][:, 0:1]).astype(BF16)
+        at = pl.ds(pl.multiple_of(e * CAP, CAP), CAP)
+        for s in range(sources):
+            back_rows[s, at, :] = back[s * CAP:(s + 1) * CAP]
+
+    def first(e):
+        wait(e)
+        slopes(e)
+        start(e + RING)
+
+    def both(e):
+        wait(e)
+        wait(e + 1)
+        project(e - 2)
+        project(e - 1)
+        slopes(e)
+        slopes(e + 1)
+        start(e + RING)
+        start(e + 1 + RING)
+
+    skewed(experts, first, lambda e: None, project, both)
+
+
+def add_kernel(keep, came, *refs):
+    near, far = refs[-2:]
+    for s in range(near.shape[0]):
+        far[s] = (keep[1, s].astype(F32) + came[1, s].astype(F32)).astype(BF16)
+        near[s] = (keep[0, s].astype(F32) + came[0, s].astype(F32)).astype(BF16)
+
+
+def chips_kernel(near, came, *refs):
+    parts = refs[-near.shape[0]:]
+    for s in range(near.shape[0]):
+        parts[s][...] = (near[s].astype(F32) + came[s].astype(F32)).astype(BF16)
+
+
+def total_kernel(count, *refs):
+    total = refs[0][...].astype(F32)
+    for ref in refs[1:count]:
+        total = total + ref[...].astype(F32)
+    rows = refs[count]
+    tokens = rows.shape[0]
+    rows[...] = total[0:tokens].astype(BF16)
+    for values in refs[count + 1:]:
+        values[...] = total[tokens:tokens + values.shape[0], 0:values.shape[1]]
+
+
+TURN = 4
+
+
+def product_kernel(left_ref, right_ref, *refs):
+    out_ref, held, sems = refs[-3:]
+    turns = out_ref.shape[0] // TURN
+
+    def store(turn, i):
+        bank = lax.rem(turn, 2)
+        return pltpu.make_async_copy(held.at[bank, i], out_ref.at[turn * TURN + i], sems.at[bank, i])
+
+    def one(turn, _):
+        @pl.when(turn >= 2)
+        def _():
+            for i in range(TURN):
+                store(turn - 2, i).wait()
+
+        bank = lax.rem(turn, 2)
+        for i in range(TURN):
+            held[bank, i] = tn(left_ref[turn * TURN + i], right_ref[turn * TURN + i]).astype(BF16)
+            if i % 2:
+                store(turn, i - 1).start()
+                store(turn, i).start()
         return 0
 
-    lax.fori_loop(0, slots // CAP // 2, some, 0)
-    send_home(keep, send, lax.axis_index("etp"), onehot, back_rows, tokens, width)
-    for s in range(sources):
-        for home in (keep, send):
-            home[0, s, tokens:tokens + EXTRA, :] = value_ref[s]
-            home[1, s, tokens:tokens + EXTRA, :] = value_ref[s]
-
-
-SLOTS = 4
-
-
-def product_kernel(left_ref, right_ref, out_ref, held, sems):
-    experts = out_ref.shape[0]
-
-    def store(e):
-        slot = lax.rem(e, SLOTS)
-        return pltpu.make_async_copy(held.at[slot], out_ref.at[e], sems.at[slot])
-
-    def one(e, _):
-        @pl.when(e >= SLOTS)
-        def _():
-            store(e - SLOTS).wait()
-
-        held[lax.rem(e, SLOTS)] = tn(left_ref[e], right_ref[e]).astype(BF16)
-        store(e).start()
-        return 0
-
-    lax.fori_loop(0, experts, one, 0)
-
-    def last(e, _):
-        store(e).wait()
-        return 0
-
-    lax.fori_loop(experts - SLOTS, experts, last, 0)
+    lax.fori_loop(0, turns, one, 0)
+    for turn in (turns - 2, turns - 1):
+        for i in range(TURN):
+            store(jnp.int32(turn), i).wait()
 
 
 def load_kernel(source, target, token, sems):
@@ -291,37 +353,42 @@
             out_shape=out_shape,
             scratch_shapes=scratch,
             compiler_params=pltpu.CompilerParams(vmem_limit_bytes=limit * 1024 * 1024),
-            cost_estimate=pl.CostEstimate(flops=flops, bytes_accessed=flops // 128, transcendentals=0),
+            cost_estimate=pl.CostEstimate(flops=flops, bytes_accessed=flops // 32, transcendentals=0),
         )(*operands)
 
     return call
 
 
-def weight_grad(left, right):
+def weight_grad(left, right, *earlier):
     experts, rows, units = left.shape
     model = right.shape[2]
     return kernel_call(
         product_kernel,
         jax.ShapeDtypeStruct((experts, units, model), BF16),
-        [pltpu.VMEM((SLOTS, units, model), BF16), pltpu.SemaphoreType.DMA((SLOTS,))],
+        [pltpu.VMEM((2, TURN, units, model), BF16), pltpu.SemaphoreType.DMA((2, TURN))],
         2 * experts * rows * units * model,
         out_specs=pl.BlockSpec(memory_space=pltpu.HBM),
-        limit=6,
-    )(left, right)
-
-
-def swap(array, bit):
-    count = lax.axis_size("etp")
-    return lax.ppermute(array, "etp", [(i, i ^ bit) for i in range(count)])
-
-
-def shift(array, by):
-    count = lax.axis_size("expert")
-    return lax.ppermute(array, "expert", [(i, (i + by) % count) for i in range(count)])
-
-
-def add(a, b):
-    return (a.astype(F32) + b.astype(F32)).astype(BF16)
+        limit=8,
+    )(left, right, *earlier)
+
+
+def swap(array, bit, axis="etp"):
+    count = lax.axis_size(axis)
+    return lax.ppermute(array, axis, [(i, i ^ bit) for i in range(count)])
+
+
+def add_cores(keep, send, *earlier):
+    shape = jax.ShapeDtypeStruct(keep.shape[1:], BF16)
+    hbm = range(2, 2 + len(earlier))
+    return kernel_call(add_kernel, [shape, shape], [], 0, limit=2, in_hbm=hbm)(keep, swap(send, 1), *earlier)
+
+
+def add_chips(near, far, *earlier):
+    sources = near.shape[0]
+    shape = jax.ShapeDtypeStruct(near.shape[1:], BF16)
+    hbm = range(2, 2 + len(earlier))
+    parts = kernel_call(chips_kernel, [shape] * sources, [], 0, limit=2, in_hbm=hbm)(near, far, *earlier)
+    return parts[0], [swap(parts[s], s, "expert") for s in range(1, sources)]
 
 
 def gathered_body(
@@ -339,22 +406,28 @@
     held = lambda *shape, kind=BF16: pltpu.VMEM(shape, kind)
     sent = lambda *shape: jax.ShapeDtypeStruct(shape, BF16)
 
-    own = jnp.concatenate([hidden_in, routing_rows(expert_ids, gate_values)], axis=0)
-    came = [shift(own, s) for s in range(1, sources)]
+    own = kernel_call(
+        pack_kernel,
+        [sent(tokens + EXTRA, width)],
+        [pltpu.VMEM((choose, tokens), jnp.int32), pltpu.VMEM((choose, tokens), F32), pltpu.SemaphoreType.DMA((3,))],
+        0,
+        limit=2,
+        in_hbm=(0, 1, 2),
+    )(hidden_in, expert_ids.T, gate_values.T)[0]
+    came = [swap(own, s, "expert") for s in range(1, sources)]
     own_across = swap(own, 2)
     grad_across = swap(out_grad, 2)
-    own_near = swap(own, 1)
-    came = join(came, gate_there, up_there, own_across, own_near)
-    came_across = swap(came, 2)
-    across_near = swap(own_across, 1)
-    grads = join([out_grad, grad_across], came, across_near)
-    grads = [grads] + [shift(grads, s) for s in range(1, sources)]
-
-    out_rows, x_rows, activ, slope, silu, onehot, slot_gate = kernel_call(
+    came = join(came, gate_there, own_across, grad_across)
+    came_across = join([swap(came, 2)], up_there)[0]
+    grads = join([out_grad, grad_across], came)
+    grads = [grads] + [swap(grads, s, "expert") for s in range(1, sources)]
+
+    out_rows, x_rows, activ, scaled, slope, silu, onehot, slot_gate = kernel_call(
         functools.partial(forward_kernel, choose),
         [
             held(sources, slots, model),
             held(local_experts, rows, model),
+            held(local_experts, rows, units),
             held(local_experts, rows, units),
             held(local_experts, rows, units, kind=F32),
             held(local_experts, rows, units, kind=F32),
@@ -363,11 +436,11 @@
         ],
         [pltpu.VMEM((RING, units, model), BF16), pltpu.SemaphoreType.DMA((RING,))],
         3 * product,
-        limit=10,
+        limit=6,
         in_hbm=(11,),
     )(
         capacity_blocks,
-        own, own_near, own_across, across_near,
+        own, swap(own, 1), own_across, swap(own_across, 1),
         came, swap(came, 1), came_across, swap(came_across, 1),
         gate_t, up_t, down_weight, grads[0],
     )
@@ -375,59 +448,52 @@
     keep, send = kernel_call(
         home_kernel, [sent(2, sources, tokens, width)] * 2, [], 2 * slots * sources * tokens * model, limit=2,
     )(onehot, out_rows, *grads)
-    out_came = swap(send, 1)
-    y_rows, gate_part, up_part, scaled, values = kernel_call(
-        functools.partial(slope_kernel, choose),
+    out_near, out_far = add_cores(keep, send)
+    back_rows, dots, y_rows, gate_part, up_part = kernel_call(
+        backward_kernel,
         [
+            held(sources, slots, model),
+            held(local_experts, rows, tokens, kind=F32),
             held(local_experts, rows, model),
             held(local_experts, rows, units),
             held(local_experts, rows, units),
-            held(local_experts, rows, units),
-            held(sources, EXTRA, width),
         ],
-        [
-            pltpu.VMEM((local_experts, rows, tokens), F32),
-            pltpu.VMEM((RING, units, model), BF16),
-            pltpu.SemaphoreType.DMA((RING,)),
-        ],
-        product,
-        limit=8,
+        [pltpu.VMEM((RING, units, model), BF16), pltpu.SemaphoreType.DMA((RING,))],
+        3 * product,
+        limit=6,
         in_hbm=(10,),
-    )(own, came, *grads, *[swap(x, 1) for x in grads], down_weight, activ, slope, silu, onehot, slot_gate)
-
-    out_far = add(keep[1], out_came[1])
-    out_far, gate_part = lax.optimization_barrier((out_far, gate_part))
-    out_far_came = swap(out_far, 2)
-    out_near = add(keep[0], out_came[0])
+    )(
+        *grads, *[swap(x, 1) for x in grads],
+        gate_t, up_t, down_weight, activ, slope, silu, onehot, slot_gate, out_near,
+    )
+
+    out_own, out_parts = add_chips(out_near, swap(out_far, 2))
     keep, send = kernel_call(
-        back_kernel,
-        [sent(2, sources, tokens + EXTRA, width), sent(2, sources, tokens + EXTRA, width)],
-        [pltpu.VMEM((sources, slots, model), BF16)],
-        2 * product,
-    )(gate_t, up_t, gate_part, up_part, onehot, slot_gate, values)
-
-    back_came = swap(send, 1)
-    out_near = add(out_near, out_far_came)
-    out_near, scaled = lax.optimization_barrier((out_near, scaled))
-    out_total = out_near[0].astype(F32)
-    for s in range(1, sources):
-        out_total = out_total + shift(out_near[s], -s).astype(F32)
-    down_grad = weight_grad(scaled, y_rows)
-    back_far = add(keep[1], back_came[1])
-    back_far, up_part = lax.optimization_barrier((back_far, up_part))
-    back_far_came = swap(back_far, 2)
-    back_near = add(keep[0], back_came[0])
-    up_grad = weight_grad(up_part, x_rows)
-    back_near = add(back_near, back_far_came)
-    back_near, gate_part = lax.optimization_barrier((back_near, gate_part))
-    back_total = back_near[0].astype(F32)
-    for s in range(1, sources):
-        back_total = back_total + shift(back_near[s], -s).astype(F32)
-    gate_grad = weight_grad(gate_part, x_rows)
+        functools.partial(home_values_kernel, choose),
+        [sent(2, sources, tokens + EXTRA, width)] * 2,
+        [],
+        2 * slots * sources * tokens * model,
+        limit=2,
+    )(onehot, back_rows, dots, own, came, out_own)
+    down_grad = weight_grad(scaled, y_rows, out_own)
+    back_near, back_far = add_cores(keep, send, down_grad)
+    up_grad = weight_grad(up_part, x_rows, back_near)
+    layer_out = kernel_call(
+        functools.partial(total_kernel, sources), [sent(tokens, width)], [], 0, limit=2
+    )(out_own, *out_parts)[0]
+    back_own, back_parts = add_chips(back_near, swap(back_far, 2), up_grad)
+    gate_grad = weight_grad(gate_part, x_rows, back_own)
+    input_grad, value_grad = kernel_call(
+        functools.partial(total_kernel, sources),
+        [sent(tokens, width), jax.ShapeDtypeStruct((choose, tokens), F32)],
+        [],
+        0,
+        limit=2,
+    )(back_own, *back_parts)
     return (
-        out_total.astype(BF16),
-        back_total[0:tokens].astype(BF16),
-        back_total[tokens:tokens + choose, 0:tokens].T,
+        layer_out,
+        input_grad,
+        value_grad.T,
         jnp.swapaxes(gate_grad, 1, 2),
         jnp.swapaxes(up_grad, 1, 2),
         down_grad,

time: 103 us -> 81.8 us (0.79)
  waiting for transfers between devices: 14.1 us -> 3.09 us
  Pallas kernels: 57.1 us -> 51.8 us
  other arithmetic: 3.3 us -> 0 us
  local copies, waits for them, and re-layouts: 1.27 us -> 0.01 us
    ppermute x27, waiting for transfers between devices: 14.1 us -> 3.09 us  [swap(): return lax.ppermute(array, axis, [(i, i ^ bit) for i in range(count)])]
    pallas_call x9 -> x17, Pallas kernels: 48.2 us -> 42.9 us  [call(): pl.pallas_call(kernel, in_specs=specs, out_specs=out_specs or [pl.BlockSp...]
    convert_element_type x6 -> x0, other arithmetic: 1.73 us -> none  [the longest x1 0.69 us: routing_rows(): expert_ids.T.astype(F32)]
  transfers between devices with their start and end apart: 27 -> 27, of which waited for: 7 -> 4; matrix products, arithmetic and copies ran while one was open for 1% -> 0% of each run, Pallas kernels for 55% -> 60%
where the time goes in v4:
time: 81.8 us; the launch traced here: 81.4 us
  Pallas kernels  51.8 us (63%)
  starting transfers between devices  25.6 us (31%)
  waiting for transfers between devices  3.09 us (4%)
  between operations  0.92 us (1%)
    pallas_call x17, Pallas kernels, call(): pl.pallas_call(kernel, in_specs=specs, out_specs=out_specs or [pl.BlockSp...  42.9 us
    ppermute x27, starting transfers between devices, swap(): return lax.ppermute(array, axis, [(i, i ^ bit) for i in range(count)])  25.6 us
    pallas_call x2, Pallas kernels, in_vmem(): pl.pallas_call(load_kernel, in_specs=[pl.BlockSpec(memory_space=pltpu.HBM...  8.86 us
    ppermute x27, waiting for transfers between devices, swap(): return lax.ppermute(array, axis, [(i, i ^ bit) for i in range(count)])  3.09 us
  transfers between devices with their start and end apart: 27, of which 4 were waited for; matrix products, arithmetic and copies ran while one was open for 0% of the time, Pallas kernels for 60%

profile of v4, /device:TPU:0, one launch (start us, length us, event | category | flops | bytes accessed | tf_op | source)
XLA Modules:
  0.0 81.4 jit_solution(11882963329931530186)
XLA Ops:
  0.6 0.9 %shard_map.127.o0.own_ref = bf16[144,256]{1,0:T(8,128)(2,1)S(1)} custom-call(bf16[128,256]{1,0:T(8,128)(2,1)} %hidden_hbm.1, s32[6,128]{1,0:T(8,128)} %bitcast.14, f32[6,128]{1,0:T(8,128)} %bitcast.15), custom_call_target="tpu_custom_call" | custom-call | tf_op jit(solution)/shard_map/pallas_call | solution.py:349
  1.5 3.0 %collective-permute-start.1 = (bf16[144,256]{1,0:T(8,128)(2,1)S(1)}, bf16[144,256]{1,0:T(8,128)(2,1)S(1)}, u32[]{:S(2)}, u32[]{:S(2)}) collective-permute-start(bf16[144,256]{1,0:T(8,128)(2,1)S(1)} %shard_map.127.o0.own_ref), channel_id=1, source_target_pairs={{0,2},{1,3},{2,0},{3,1},{4,6},{5,7},{6,4},{7,5},{8,10},{9,11},{10,... | collective-permute-start | bytes 221192 | tf_op jit(solution)/shard_map/ppermute | solution.py:377
  4.5 1.6 %collective-permute-start.3 = (bf16[144,256]{1,0:T(8,128)(2,1)S(1)}, bf16[144,256]{1,0:T(8,128)(2,1)S(1)}, u32[]{:S(2)}, u32[]{:S(2)}) collective-permute-start(bf16[144,256]{1,0:T(8,128)(2,1)S(1)} %shard_map.127.o0.own_ref), channel_id=1, source_target_pairs={{0,4},{4,0},{8,12},{12,8},{1,5},{5,1},{9,13},{13,9},{2,6},{6,2},{1... | collective-permute-start | bytes 221192 | tf_op jit(solution)/shard_map/ppermute | solution.py:377
  6.1 2.6 %collective-permute-start.4 = (bf16[144,256]{1,0:T(8,128)(2,1)S(1)}, bf16[144,256]{1,0:T(8,128)(2,1)S(1)}, u32[]{:S(2)}, u32[]{:S(2)}) collective-permute-start(bf16[144,256]{1,0:T(8,128)(2,1)S(1)} %shard_map.127.o0.own_ref), channel_id=1, source_target_pairs={{0,8},{4,12},{8,0},{12,4},{1,9},{5,13},{9,1},{13,5},{2,10},{6,14},... | collective-permute-start | bytes 221192 | tf_op jit(solution)/shard_map/ppermute | solution.py:377
  9.2 4.4 %shard_map.128 = (bf16[16,352,1024]{2,1,0:T(8,128)(2,1)S(1)}, f32[8,128]{1,0:T(8,128)S(1)}) custom-call(bf16[16,352,1024]{2,1,0:T(8,128)(2,1)} %bitcast.11), custom_call_target="tpu_custom_call" | custom-call | bytes 11534336 | tf_op jit(solution)/shard_map/pallas_call | solution.py:314
  13.7 1.2 %collective-permute-done.5.refs_2_ = bf16[144,256]{1,0:T(8,128)(2,1)S(1)} collective-permute-done((bf16[144,256]{1,0:T(8,128)(2,1)S(1)}, bf16[144,256]{1,0:T(8,128)(2,1)S(1)}, u32[]{:S(2)}, u32[]{:S(2)}) %collective-permute-start.5) | collective-permute-done | bytes 73760 | tf_op jit(solution)/shard_map/ppermute | solution.py:377
  15.6 4.4 %shard_map.130 = (bf16[16,352,1024]{2,1,0:T(8,128)(2,1)S(1)}, f32[8,128]{1,0:T(8,128)S(1)}) custom-call(bf16[16,352,1024]{2,1,0:T(8,128)(2,1)} %bitcast.12), custom_call_target="tpu_custom_call" | custom-call | bytes 11534336 | tf_op jit(solution)/shard_map/pallas_call | solution.py:314
  20.1 0.9 %collective-permute-done.8.refs_0_ = bf16[3,144,256]{2,1,0:T(8,128)(2,1)S(1)} collective-permute-done((bf16[3,144,256]{2,1,0:T(8,128)(2,1)S(1)}, bf16[3,144,256]{2,1,0:T(8,128)(2,1)S(1)}, u32[]{:S(2)}, u32[]{:S(2)}) %collective-permute-start.8) | collective-permute-done | bytes 221216 | tf_op jit(solution)/shard_map/ppermute | solution.py:377
  21.6 0.9 %collective-permute-start.10 = (bf16[2,128,256]{2,1,0:T(8,128)(2,1)S(1)}, bf16[2,128,256]{2,1,0:T(8,128)(2,1)S(1)}, u32[]{:S(2)}, u32[]{:S(2)}) collective-permute-start(bf16[2,128,256]{2,1,0:T(8,128)(2,1)S(1)} %shard_map.132.later_ref.refs_0_.a0), channel_id=1, source_target_pairs={{0,4},{4,0},{8,12},{12,8},{1,5},{5,1},{9,13},{13,9},{2,6},{6,2},{1... | collective-permute-start | bytes 393224 | tf_op jit(solution)/shard_map/ppermute | solution.py:377
  22.6 2.8 %collective-permute-start.11 = (bf16[2,128,256]{2,1,0:T(8,128)(2,1)S(1)}, bf16[2,128,256]{2,1,0:T(8,128)(2,1)S(1)}, u32[]{:S(2)}, u32[]{:S(2)}) collective-permute-start(bf16[2,128,256]{2,1,0:T(8,128)(2,1)S(1)} %shard_map.132.later_ref.refs_0_.a0), channel_id=1, source_target_pairs={{0,8},{4,12},{8,0},{12,4},{1,9},{5,13},{9,1},{13,5},{2,10},{6,14},... | collective-permute-start | bytes 393224 | tf_op jit(solution)/shard_map/ppermute | solution.py:377
  25.4 0.7 collective-permute-start.12
  26.1 11.7 %shard_map.133 = (bf16[4,256,1024]{2,1,0:T(8,128)(2,1)S(1)}, bf16[16,64,1024]{2,1,0:T(8,128)(2,1)S(1)}, bf16[16,64,352]{2,1,0:T(8,128)(2,1)S(1)}, bf16[16,64,352...) custom-call(s32[64]{0:T(128)S(1)} %copy-done.1, ...), custom_call_target="tpu_custom_call" | custom-call | flops 2214592512 | bytes 69206016 | tf_op jit(solution)/shard_map/pallas_call | solution.py:349
  39.6 0.8 collective-permute-done.13.came
  40.5 1.1 %collective-permute-start.14 = (bf16[4,128,256]{2,1,0:T(8,128)(2,1)S(1)}, bf16[4,128,256]{2,1,0:T(8,128)(2,1)S(1)}, u32[]{:S(2)}, u32[]{:S(2)}) collective-permute-start(bf16[4,128,256]{2,1,0:T(8,128)(2,1)S(1)} %get-tuple-element.50), channel_id=1, source_target_pairs={{0,2},{1,3},{2,0},{3,1},{4,6},{5,7},{6,4},{7,5},{8,10},{9,11},{10,... | collective-permute-start | bytes 786440 | tf_op jit(solution)/shard_map/ppermute | solution.py:377
  41.6 11.8 %shard_map.138 = (bf16[4,256,1024]{2,1,0:T(8,128)(2,1)S(1)}, f32[16,64,128]{2,1,0:T(8,128)S(1)}, bf16[16,64,1024]{2,1,0:T(8,128)(2,1)S(1)}, bf16[16,64,352]{2,1,0:T(8,128)(2,1)S(1)}, bf16[16,64,352]{2,1,0:T(8,128)(2,1)S(1)}) custom-call(bf16[2,128,256]{2,1,0:T(8,128)(2,1)S(1)} %shard_map.132.later_ref.refs_0_.a0, ...), custom_call_target="tpu_custom_call" | custom-call | flops 2214592512 | bytes 69206016 | tf_op jit(solution)/shard_map/pallas_call | solution.py:349
  54.2 5.2 %shard_map.140.refs_0_ = bf16[16,352,1024]{2,1,0:T(8,128)(2,1)} custom-call(bf16[16,64,352]{2,1,0:T(8,128)(2,1)S(1)} %get-tuple-element.63.left_ref, bf16[16,64,1024]{2,1,0:T(8,128)(2,1)S(1)} %get-tuple-element.64.right_ref, bf16[128,256]{1,0:T(8,128)(2,1)S(1)} %get-tuple-element.51.refs_0_), custom_call_target="tpu_custom_call" | custom-call | flops 738197504 | bytes 23068672 | tf_op jit(solution)/shard_map/pallas_call | solution.py:349
  59.6 1.1 %collective-permute-start.23 = (bf16[4,144,256]{2,1,0:T(8,128)(2,1)S(1)}, bf16[4,144,256]{2,1,0:T(8,128)(2,1)S(1)}, u32[]{:S(2)}, u32[]{:S(2)}) collective-permute-start(bf16[4,144,256]{2,1,0:T(8,128)(2,1)S(1)} %get-tuple-element.66), channel_id=1, source_target_pairs={{0,2},{1,3},{2,0},{3,1},{4,6},{5,7},{6,4},{7,5},{8,10},{9,11},{10,... | collective-permute-start | bytes 884744 | tf_op jit(solution)/shard_map/ppermute | solution.py:377
  60.9 3.4 %collective-permute-start.16 = (bf16[128,256]{1,0:T(8,128)(2,1)S(1)}, bf16[128,256]{1,0:T(8,128)(2,1)S(1)}, u32[]{:S(2)}, u32[]{:S(2)}) collective-permute-start(bf16[128,256]{1,0:T(8,128)(2,1)S(1)} %get-tuple-element.53), channel_id=1, source_target_pairs={{0,8},{4,12},{8,0},{12,4},{1,9},{5,13},{9,1},{13,5},{2,10},{6,14},... | collective-permute-start | bytes 196616 | tf_op jit(solution)/shard_map/ppermute | solution.py:377
  64.4 0.7 collective-permute-start.17
  65.1 5.2 %shard_map.142.refs_0_ = bf16[16,352,1024]{2,1,0:T(8,128)(2,1)} custom-call(bf16[16,64,352]{2,1,0:T(8,128)(2,1)S(1)} %get-tuple-element.67.left_ref, bf16[16,64,1024]{2,1,0:T(8,128)(2,1)S(1)} %get-tuple-element.68.right_ref, bf16[4,144,256]{2,1,0:T(8,128)(2,1)S(1)} %get-tuple-element.65.refs_0_.near), custom_call_target="tpu_custom_call" | custom-call | flops 738197504 | bytes 23068672 | tf_op jit(solution)/shard_map/pallas_call | solution.py:349
  70.5 3.7 %collective-permute-start.25 = (bf16[144,256]{1,0:T(8,128)(2,1)S(1)}, bf16[144,256]{1,0:T(8,128)(2,1)S(1)}, u32[]{:S(2)}, u32[]{:S(2)}) collective-permute-start(bf16[144,256]{1,0:T(8,128)(2,1)S(1)} %get-tuple-element.71), channel_id=1, source_target_pairs={{0,8},{4,12},{8,0},{12,4},{1,9},{5,13},{9,1},{13,5},{2,10},{6,14},... | collective-permute-start | bytes 221192 | tf_op jit(solution)/shard_map/ppermute | solution.py:377
  74.1 0.7 collective-permute-start.26
  75.5 5.2 %shard_map.145 = bf16[16,352,1024]{2,1,0:T(8,128)(2,1)} custom-call(bf16[16,64,352]{2,1,0:T(8,128)(2,1)S(1)} %get-tuple-element.75.left_ref, bf16[16,64,1024]{2,1,0:T(8,128)(2,1)S(1)} %get-tuple-element.68.right_ref, bf16[144,256]{1,0:T(8,128)(2,1)S(1)} %get-tuple-element.69.refs_0_), custom_call_target="tpu_custom_call" | custom-call | flops 738197504 | bytes 23068672 | tf_op jit(solution)/shard_map/pallas_call | solution.py:349
  80.7 0.7 shard_map.144
  (53 shorter events, 5.8 us)
Async XLA Ops:
  1.5 12.2 %collective-permute-start.1 = (bf16[144,256]{1,0:T(8,128)(2,1)S(1)}, bf16[144,256]{1,0:T(8,128)(2,1)S(1)}, u32[]{:S(2)}, u32[]{:S(2)}) collective-permute-start(bf16[144,256]{1,0:T(8,128)(2,1)S(1)} %shard_map.127.o0.own_ref), channel_id=1, source_target_pairs={{0,2},{1,3},{2,0},{3,1},{4,6},{5,7},{6,4},{7,5},{8,10},{9,11},{10,... | collective-permute-start | bytes 221192 | tf_op jit(solution)/shard_map/ppermute | solution.py:377
  4.5 9.2 %collective-permute-start.3 = (bf16[144,256]{1,0:T(8,128)(2,1)S(1)}, bf16[144,256]{1,0:T(8,128)(2,1)S(1)}, u32[]{:S(2)}, u32[]{:S(2)}) collective-permute-start(bf16[144,256]{1,0:T(8,128)(2,1)S(1)} %shard_map.127.o0.own_ref), channel_id=1, source_target_pairs={{0,4},{4,0},{8,12},{12,8},{1,5},{5,1},{9,13},{13,9},{2,6},{6,2},{1... | collective-permute-start | bytes 221192 | tf_op jit(solution)/shard_map/ppermute | solution.py:377
  6.1 7.6 %collective-permute-start.4 = (bf16[144,256]{1,0:T(8,128)(2,1)S(1)}, bf16[144,256]{1,0:T(8,128)(2,1)S(1)}, u32[]{:S(2)}, u32[]{:S(2)}) collective-permute-start(bf16[144,256]{1,0:T(8,128)(2,1)S(1)} %shard_map.127.o0.own_ref), channel_id=1, source_target_pairs={{0,8},{4,12},{8,0},{12,4},{1,9},{5,13},{9,1},{13,5},{2,10},{6,14},... | collective-permute-start | bytes 221192 | tf_op jit(solution)/shard_map/ppermute | solution.py:377
  8.7 6.3 %collective-permute-start.5 = (bf16[144,256]{1,0:T(8,128)(2,1)S(1)}, bf16[144,256]{1,0:T(8,128)(2,1)S(1)}, u32[]{:S(2)}, u32[]{:S(2)}) collective-permute-start(bf16[144,256]{1,0:T(8,128)(2,1)S(1)} %shard_map.127.o0.own_ref), channel_id=1, source_target_pairs={{0,12},{4,8},{8,4},{12,0},{1,13},{5,9},{9,5},{13,1},{2,14},{6,10},... | collective-permute-start | bytes 221192 | tf_op jit(solution)/shard_map/ppermute | solution.py:377
  8.9 4.8 %collective-permute-start.6 = (bf16[128,256]{1,0:T(8,128)(2,1)}, bf16[128,256]{1,0:T(8,128)(2,1)S(1)}, u32[]{:S(2)}, u32[]{:S(2)}) collective-permute-start(bf16[128,256]{1,0:T(8,128)(2,1)} %refs_0_.1), channel_id=1, source_target_pairs={{0,2},{1,3},{2,0},{3,1},{4,6},{5,7},{6,4},{7,5},{8,10},{9,11},{10,... | collective-permute-start | bytes 196616 | tf_op jit(solution)/shard_map/ppermute | solution.py:377
  15.0 6.0 %collective-permute-start.8 = (bf16[3,144,256]{2,1,0:T(8,128)(2,1)S(1)}, bf16[3,144,256]{2,1,0:T(8,128)(2,1)S(1)}, u32[]{:S(2)}, u32[]{:S(2)}) collective-permute-start(bf16[3,144,256]{2,1,0:T(8,128)(2,1)S(1)} %shard_map.129.refs_2_.b0.info_ref), channel_id=1, source_target_pairs={{0,2},{1,3},{2,0},{3,1},{4,6},{5,7},{6,4},{7,5},{8,10},{9,11},{10,... | collective-permute-start | bytes 663560 | tf_op jit(solution)/shard_map/ppermute | solution.py:377
  20.0 6.1 %collective-permute-start.7 = (bf16[3,144,256]{2,1,0:T(8,128)(2,1)S(1)}, bf16[3,144,256]{2,1,0:T(8,128)(2,1)S(1)}, u32[]{:S(2)}, u32[]{:S(2)}) collective-permute-start(bf16[3,144,256]{2,1,0:T(8,128)(2,1)S(1)} %shard_map.129.refs_2_.b0.info_ref), channel_id=1, source_target_pairs={{0,1},{1,0},{2,3},{3,2},{4,5},{5,4},{6,7},{7,6},{8,9},{9,8},{10,11... | collective-permute-start | bytes 663560 | tf_op jit(solution)/shard_map/ppermute | solution.py:377
  21.0 5.1 %collective-permute-start.9 = (bf16[3,144,256]{2,1,0:T(8,128)(2,1)S(1)}, bf16[3,144,256]{2,1,0:T(8,128)(2,1)S(1)}, u32[]{:S(2)}, u32[]{:S(2)}) collective-permute-start(bf16[3,144,256]{2,1,0:T(8,128)(2,1)S(1)} %bitcast.8), channel_id=1, source_target_pairs={{0,1},{1,0},{2,3},{3,2},{4,5},{5,4},{6,7},{7,6},{8,9},{9,8},{10,11... | collective-permute-start | bytes 663560 | tf_op jit(solution)/shard_map/ppermute | solution.py:377
  21.6 3.8 %collective-permute-start.2 = (bf16[144,256]{1,0:T(8,128)(2,1)S(1)}, bf16[144,256]{1,0:T(8,128)(2,1)S(1)}, u32[]{:S(2)}, u32[]{:S(2)}) collective-permute-start(bf16[144,256]{1,0:T(8,128)(2,1)S(1)} %collective-permute-done.1.refs_4_.o2), channel_id=1, source_target_pairs={{0,1},{1,0},{2,3},{3,2},{4,5},{5,4},{6,7},{7,6},{8,9},{9,8},{10,11... | collective-permute-start | bytes 221192 | tf_op jit(solution)/shard_map/ppermute | solution.py:377
  21.6 16.2 %collective-permute-start.10 = (bf16[2,128,256]{2,1,0:T(8,128)(2,1)S(1)}, bf16[2,128,256]{2,1,0:T(8,128)(2,1)S(1)}, u32[]{:S(2)}, u32[]{:S(2)}) collective-permute-start(bf16[2,128,256]{2,1,0:T(8,128)(2,1)S(1)} %shard_map.132.later_ref.refs_0_.a0), channel_id=1, source_target_pairs={{0,4},{4,0},{8,12},{12,8},{1,5},{5,1},{9,13},{13,9},{2,6},{6,2},{1... | collective-permute-start | bytes 393224 | tf_op jit(solution)/shard_map/ppermute | solution.py:377
  22.6 15.3 %collective-permute-start.11 = (bf16[2,128,256]{2,1,0:T(8,128)(2,1)S(1)}, bf16[2,128,256]{2,1,0:T(8,128)(2,1)S(1)}, u32[]{:S(2)}, u32[]{:S(2)}) collective-permute-start(bf16[2,128,256]{2,1,0:T(8,128)(2,1)S(1)} %shard_map.132.later_ref.refs_0_.a0), channel_id=1, source_target_pairs={{0,8},{4,12},{8,0},{12,4},{1,9},{5,13},{9,1},{13,5},{2,10},{6,14},... | collective-permute-start | bytes 393224 | tf_op jit(solution)/shard_map/ppermute | solution.py:377
  25.4 12.5 %collective-permute-start.12 = (bf16[2,128,256]{2,1,0:T(8,128)(2,1)S(1)}, bf16[2,128,256]{2,1,0:T(8,128)(2,1)S(1)}, u32[]{:S(2)}, u32[]{:S(2)}) collective-permute-start(bf16[2,128,256]{2,1,0:T(8,128)(2,1)S(1)} %shard_map.132.later_ref.refs_0_.a0), channel_id=1, source_target_pairs={{0,12},{4,8},{8,4},{12,0},{1,13},{5,9},{9,5},{13,1},{2,14},{6,10},... | collective-permute-start | bytes 393224 | tf_op jit(solution)/shard_map/ppermute | solution.py:377
  38.5 3.1 %collective-permute-start.18 = (bf16[2,128,256]{2,1,0:T(8,128)(2,1)S(1)}, bf16[2,128,256]{2,1,0:T(8,128)(2,1)S(1)}, u32[]{:S(2)}, u32[]{:S(2)}) collective-permute-start(bf16[2,128,256]{2,1,0:T(8,128)(2,1)S(1)} %shard_map.132.later_ref.refs_0_.a0), channel_id=1, source_target_pairs={{0,1},{1,0},{2,3},{3,2},{4,5},{5,4},{6,7},{7,6},{8,9},{9,8},{10,11... | collective-permute-start | bytes 393224 | tf_op jit(solution)/shard_map/ppermute | solution.py:377
  39.0 2.6 %collective-permute-start.19 = (bf16[2,128,256]{2,1,0:T(8,128)(2,1)S(1)}, bf16[2,128,256]{2,1,0:T(8,128)(2,1)S(1)}, u32[]{:S(2)}, u32[]{:S(2)}) collective-permute-start(bf16[2,128,256]{2,1,0:T(8,128)(2,1)S(1)} %collective-permute-done.10.refs_1_.a1), channel_id=1, source_target_pairs={{0,1},{1,0},{2,3},{3,2},{4,5},{5,4},{6,7},{7,6},{8,9},{9,8},{10,11... | collective-permute-start | bytes 393224 | tf_op jit(solution)/shard_map/ppermute | solution.py:377
  39.1 2.5 %collective-permute-start.20 = (bf16[2,128,256]{2,1,0:T(8,128)(2,1)S(1)}, bf16[2,128,256]{2,1,0:T(8,128)(2,1)S(1)}, u32[]{:S(2)}, u32[]{:S(2)}) collective-permute-start(bf16[2,128,256]{2,1,0:T(8,128)(2,1)S(1)} %collective-permute-done.11.refs_2_.a2), channel_id=1, source_target_pairs={{0,1},{1,0},{2,3},{3,2},{4,5},{5,4},{6,7},{7,6},{8,9},{9,8},{10,11... | collective-permute-start | bytes 393224 | tf_op jit(solution)/shard_map/ppermute | solution.py:377
  40.5 13.0 %collective-permute-start.14 = (bf16[4,128,256]{2,1,0:T(8,128)(2,1)S(1)}, bf16[4,128,256]{2,1,0:T(8,128)(2,1)S(1)}, u32[]{:S(2)}, u32[]{:S(2)}) collective-permute-start(bf16[4,128,256]{2,1,0:T(8,128)(2,1)S(1)} %get-tuple-element.50), channel_id=1, source_target_pairs={{0,2},{1,3},{2,0},{3,1},{4,6},{5,7},{6,4},{7,5},{8,10},{9,11},{10,... | collective-permute-start | bytes 786440 | tf_op jit(solution)/shard_map/ppermute | solution.py:377
  54.2 5.3 %collective-permute-start.22 = (bf16[2,4,144,256]{3,2,1,0:T(8,128)(2,1)S(1)}, bf16[2,4,144,256]{3,2,1,0:T(8,128)(2,1)S(1)}, u32[]{:S(2)}, u32[]{:S(2)}) collective-permute-start(bf16[2,4,144,256]{3,2,1,0:T(8,128)(2,1)S(1)} %get-tuple-element.62), channel_id=1, source_target_pairs={{0,1},{1,0},{2,3},{3,2},{4,5},{5,4},{6,7},{7,6},{8,9},{9,8},{10,11... | collective-permute-start | bytes 1769480 | tf_op jit(solution)/shard_map/ppermute | solution.py:377
  59.6 10.7 %collective-permute-start.23 = (bf16[4,144,256]{2,1,0:T(8,128)(2,1)S(1)}, bf16[4,144,256]{2,1,0:T(8,128)(2,1)S(1)}, u32[]{:S(2)}, u32[]{:S(2)}) collective-permute-start(bf16[4,144,256]{2,1,0:T(8,128)(2,1)S(1)} %get-tuple-element.66), channel_id=1, source_target_pairs={{0,2},{1,3},{2,0},{3,1},{4,6},{5,7},{6,4},{7,5},{8,10},{9,11},{10,... | collective-permute-start | bytes 884744 | tf_op jit(solution)/shard_map/ppermute | solution.py:377
  60.7 13.4 %collective-permute-start.15 = (bf16[128,256]{1,0:T(8,128)(2,1)S(1)}, bf16[128,256]{1,0:T(8,128)(2,1)S(1)}, u32[]{:S(2)}, u32[]{:S(2)}) collective-permute-start(bf16[128,256]{1,0:T(8,128)(2,1)S(1)} %get-tuple-element.52), channel_id=1, source_target_pairs={{0,4},{4,0},{8,12},{12,8},{1,5},{5,1},{9,13},{13,9},{2,6},{6,2},{1... | collective-permute-start | bytes 196616 | tf_op jit(solution)/shard_map/ppermute | solution.py:377
  60.9 13.9 %collective-permute-start.16 = (bf16[128,256]{1,0:T(8,128)(2,1)S(1)}, bf16[128,256]{1,0:T(8,128)(2,1)S(1)}, u32[]{:S(2)}, u32[]{:S(2)}) collective-permute-start(bf16[128,256]{1,0:T(8,128)(2,1)S(1)} %get-tuple-element.53), channel_id=1, source_target_pairs={{0,8},{4,12},{8,0},{12,4},{1,9},{5,13},{9,1},{13,5},{2,10},{6,14},... | collective-permute-start | bytes 196616 | tf_op jit(solution)/shard_map/ppermute | solution.py:377
  64.4 10.5 %collective-permute-start.17 = (bf16[128,256]{1,0:T(8,128)(2,1)S(1)}, bf16[128,256]{1,0:T(8,128)(2,1)S(1)}, u32[]{:S(2)}, u32[]{:S(2)}) collective-permute-start(bf16[128,256]{1,0:T(8,128)(2,1)S(1)} %get-tuple-element.54), channel_id=1, source_target_pairs={{0,12},{4,8},{8,4},{12,0},{1,13},{5,9},{9,5},{13,1},{2,14},{6,10},... | collective-permute-start | bytes 196616 | tf_op jit(solution)/shard_map/ppermute | solution.py:377
  70.4 10.3 %collective-permute-start.24 = (bf16[144,256]{1,0:T(8,128)(2,1)S(1)}, bf16[144,256]{1,0:T(8,128)(2,1)S(1)}, u32[]{:S(2)}, u32[]{:S(2)}) collective-permute-start(bf16[144,256]{1,0:T(8,128)(2,1)S(1)} %get-tuple-element.70), channel_id=1, source_target_pairs={{0,4},{4,0},{8,12},{12,8},{1,5},{5,1},{9,13},{13,9},{2,6},{6,2},{1... | collective-permute-start | bytes 221192 | tf_op jit(solution)/shard_map/ppermute | solution.py:377
  70.5 10.3 %collective-permute-start.25 = (bf16[144,256]{1,0:T(8,128)(2,1)S(1)}, bf16[144,256]{1,0:T(8,128)(2,1)S(1)}, u32[]{:S(2)}, u32[]{:S(2)}) collective-permute-start(bf16[144,256]{1,0:T(8,128)(2,1)S(1)} %get-tuple-element.71), channel_id=1, source_target_pairs={{0,8},{4,12},{8,0},{12,4},{1,9},{5,13},{9,1},{13,5},{2,10},{6,14},... | collective-permute-start | bytes 221192 | tf_op jit(solution)/shard_map/ppermute | solution.py:377
  74.1 6.6 %collective-permute-start.26 = (bf16[144,256]{1,0:T(8,128)(2,1)S(1)}, bf16[144,256]{1,0:T(8,128)(2,1)S(1)}, u32[]{:S(2)}, u32[]{:S(2)}) collective-permute-start(bf16[144,256]{1,0:T(8,128)(2,1)S(1)} %get-tuple-element.72), channel_id=1, source_target_pairs={{0,12},{4,8},{8,4},{12,0},{1,13},{5,9},{9,5},{13,1},{2,14},{6,10},... | collective-permute-start | bytes 221192 | tf_op jit(solution)/shard_map/ppermute | solution.py:377
  (5 other events, 35.0 us)

commit v5 on v4

--- a/solution.py
+++ b/solution.py
@@ -65,23 +65,37 @@
 RING = 4
 
 
-def ring(weight, slots, sems):
+def ring(weight, slots, sems, columns=None):
     def load(e):
         slot = lax.rem(e, RING)
-        return pltpu.make_async_copy(weight.at[e], slots.at[slot], sems.at[slot])
+        source = weight.at[e] if columns is None else weight.at[e, :, columns]
+        return pltpu.make_async_copy(source, slots.at[slot], sems.at[slot])
 
     def start(e):
         @pl.when(e < weight.shape[0])
         def _():
             load(e).start()
 
+    for e in range(RING):
+        load(jnp.int32(e)).start()
     return start, lambda e: load(e).wait()
 
 
-def forward_kernel(
-    choose, capacity_ref, o0, o1, o2, o3, b0, b1, b2, b3, gate_ref, up_ref, down_hbm, later_ref,
-    out_rows, rows_ref, act_ref, a_ref, slope_ref, silu_ref, onehot, slot_gate,
-    down_ref, sems,
+def half(me, other, size):
+    return pl.ds(pl.multiple_of(lax.bitwise_xor(me // 2, other) * size, size), size)
+
+
+def gather_half(me, onehot, blocks, rows_ref, experts, width, tokens, start):
+    for q, block in enumerate(blocks):
+        picked = nn(onehot, block).astype(BF16).reshape(experts, CAP, width)
+        at = pl.multiple_of(lax.rem(lax.bitwise_xor(me, q), 2) * width, width)
+        rows_ref[:, start:start + CAP, pl.ds(at, width)] = picked
+
+
+def early_kernel(
+    choose, capacity_ref, o0, o1, b0, b1, gate_ref, up_hbm,
+    rows_ref, part_ref, onehot, slot_gate,
+    up_ref, sems,
 ):
     sources, slots, tokens = onehot.shape
     experts = slots // CAP
@@ -89,9 +103,8 @@
     me = lax.axis_index("etp")
     first = lax.axis_index("expert") * experts
 
-    start, wait = ring(down_hbm, down_ref, sems)
-    for e in range(RING):
-        start(jnp.int32(e))
+    here = half(me, 0, 2 * width)
+    start, wait = ring(up_hbm, up_ref, sems, here)
     row = lax.broadcasted_iota(jnp.int32, (tokens, tokens), 0)
     col = lax.broadcasted_iota(jnp.int32, (tokens, tokens), 1)
     before = jnp.where(row < col, 1.0, 0.0).astype(BF16)
@@ -103,7 +116,7 @@
     limit = limit.astype(F32)
     place = lax.broadcasted_iota(jnp.int32, (experts, CAP, tokens), 1).astype(F32)
     for s in range(sources):
-        block = [o[...] for o in (o0, o1, o2, o3)] if s == 0 else [b[s - 1] for b in (b0, b1, b2, b3)]
+        block = [o[...] for o in (o0, o1)] if s == 0 else [b[s - 1] for b in (b0, b1)]
         ids, gates = routing(block[0][tokens:tokens + EXTRA, :], choose, tokens)
         named = jnp.zeros((experts, tokens), F32)
         gate = jnp.zeros((experts, tokens), F32)
@@ -118,14 +131,43 @@
         slot_gate[:, s * CAP:(s + 1) * CAP, :] = jnp.broadcast_to(gate_of, chosen.shape)
         table = chosen.reshape(slots, tokens).astype(BF16)
         onehot[s] = table
-        for q in range(4):
-            picked = nn(table, block[q][0:tokens, :]).astype(BF16).reshape(experts, CAP, width)
-            rows_ref[:, s * CAP:(s + 1) * CAP, columns(me, q, width)] = picked
+        gather_half(me, table, [x[0:tokens, :] for x in block], rows_ref, experts, width, tokens, s * CAP)
+
+    def some(turn, _):
+        for e in (turn * 2, turn * 2 + 1):
+            wait(e)
+        for e in (turn * 2, turn * 2 + 1):
+            part_ref[0, e] = nt(rows_ref[e], gate_ref[e, :, here])
+            part_ref[1, e] = nt(rows_ref[e], up_ref[lax.rem(e, RING)])
+        for e in (turn * 2, turn * 2 + 1):
+            start(e + RING)
+        return 0
+
+    lax.fori_loop(0, experts // 2, some, 0)
+
+
+def forward_kernel(
+    o2, o3, b2, b3, gate_ref, up_hbm, down_hbm, half_ref, part_ref, onehot, slot_gate, later_ref,
+    out_rows, rows_ref, act_ref, a_ref, slope_ref, silu_ref,
+    there_ref, up_ref, down_ref, up_sems, down_sems,
+):
+    sources, slots, tokens = onehot.shape
+    experts = slots // CAP
+    width = b2.shape[2]
+    me = lax.axis_index("etp")
+    here, there = half(me, 0, 2 * width), half(me, 1, 2 * width)
+    start_up, wait_up = ring(up_hbm, up_ref, up_sems, there)
+    start_down, wait_down = ring(down_hbm, down_ref, down_sems)
+    for s in range(sources):
+        block = [o[0:tokens, :] for o in (o2, o3)] if s == 0 else [b[s - 1, 0:tokens, :] for b in (b2, b3)]
+        gather_half(me, onehot[s], block, there_ref, experts, width, tokens, s * CAP)
 
     def activate(e):
-        x = rows_ref[e]
-        hidden_gate = nt(x, gate_ref[e])
-        hidden_up = nt(x, up_ref[e])
+        rows_ref[e, :, here] = half_ref[e]
+        x = there_ref[e]
+        rows_ref[e, :, there] = x
+        hidden_gate = part_ref[0, e] + nt(x, gate_ref[e, :, there])
+        hidden_up = part_ref[1, e] + nt(x, up_ref[lax.rem(e, RING)])
         sigma = jax.nn.sigmoid(hidden_gate)
         silu = hidden_gate * sigma
         activ = (silu * hidden_up).astype(BF16)
@@ -140,17 +182,26 @@
         for s in range(sources):
             out_rows[s, at, :] = out[s * CAP:(s + 1) * CAP]
 
+    def first(e):
+        wait_up(e)
+        activate(e)
+        start_up(e + RING)
+
     def both(e):
-        wait(e - 2)
-        wait(e - 1)
+        for i in (e - 2, e - 1):
+            wait_down(i)
+        for i in (e, e + 1):
+            wait_up(i)
         project(e - 2)
         project(e - 1)
         activate(e)
         activate(e + 1)
-        start(e - 2 + RING)
-        start(e - 1 + RING)
-
-    skewed(experts, activate, wait, project, both)
+        for i in (e - 2, e - 1):
+            start_down(i + RING)
+        for i in (e, e + 1):
+            start_up(i + RING)
+
+    skewed(experts, first, wait_down, project, both)
 
 
 def skewed(experts, first, wait, second, both):
@@ -169,8 +220,11 @@
 
 
 def home_kernel(onehot, rows, *refs):
-    keep, send = refs[-2:]
+    grads, (keep, send) = refs[:-2], refs[-2:]
     send_home(keep, send, lax.axis_index("etp"), onehot, rows, keep.shape[2], keep.shape[3])
+    for s, grad in enumerate(grads):
+        for q in range(2):
+            send[2 + q, s] = grad[q]
 
 
 def home_values_kernel(choose, onehot, rows, dots, own_ref, info_ref, *refs):
@@ -195,21 +249,20 @@
 
 
 def backward_kernel(
-    a0, a1, a2, a3, n0, n1, n2, n3,
-    gate_ref, up_ref, down_hbm, act_ref, slope_ref, silu_ref, onehot, slot_gate, earlier_ref,
+    a0, a1, a2, a3, near_ref,
+    gate_ref, up_hbm, down_hbm, act_ref, slope_ref, silu_ref, onehot, slot_gate, earlier_ref,
     back_rows, dots, rows_ref, p_ref, q_ref,
-    down_ref, sems,
+    up_ref, down_ref, up_sems, down_sems,
 ):
     sources, slots, tokens = onehot.shape
     experts = slots // CAP
     width = a0.shape[2]
     me = lax.axis_index("etp")
-    start, wait = ring(down_hbm, down_ref, sems)
-    for e in range(RING):
-        start(jnp.int32(e))
-    for s, (here, near) in enumerate(((a0, n0), (a1, n1), (a2, n2), (a3, n3))):
+    start_down, wait_down = ring(down_hbm, down_ref, down_sems)
+    start_up, wait_up = ring(up_hbm, up_ref, up_sems)
+    for s, here in enumerate((a0, a1, a2, a3)):
         for q in range(4):
-            block = (near if q % 2 else here)[q // 2]
+            block = near_ref[2 + q // 2, s] if q % 2 else here[q // 2]
             picked = nn(onehot[s], block).astype(BF16).reshape(experts, CAP, width)
             rows_ref[:, s * CAP:(s + 1) * CAP, columns(me, q, width)] = picked
 
@@ -222,28 +275,32 @@
         q_ref[e] = (grad * silu_ref[e]).astype(BF16)
 
     def project(e):
-        back = nn(p_ref[e], gate_ref[e]) + nn(q_ref[e], up_ref[e])
+        back = nn(p_ref[e], gate_ref[e]) + nn(q_ref[e], up_ref[lax.rem(e, RING)])
         back = (back * slot_gate[e][:, 0:1]).astype(BF16)
         at = pl.ds(pl.multiple_of(e * CAP, CAP), CAP)
         for s in range(sources):
             back_rows[s, at, :] = back[s * CAP:(s + 1) * CAP]
 
     def first(e):
-        wait(e)
+        wait_down(e)
         slopes(e)
-        start(e + RING)
+        start_down(e + RING)
 
     def both(e):
-        wait(e)
-        wait(e + 1)
+        for i in (e, e + 1):
+            wait_down(i)
+        for i in (e - 2, e - 1):
+            wait_up(i)
         project(e - 2)
         project(e - 1)
         slopes(e)
         slopes(e + 1)
-        start(e + RING)
-        start(e + 1 + RING)
-
-    skewed(experts, first, lambda e: None, project, both)
+        for i in (e, e + 1):
+            start_down(i + RING)
+        for i in (e - 2, e - 1):
+            start_up(i + RING)
+
+    skewed(experts, first, wait_up, project, both)
 
 
 def add_kernel(keep, came, *refs):
@@ -257,6 +314,20 @@
     parts = refs[-near.shape[0]:]
     for s in range(near.shape[0]):
         parts[s][...] = (near[s].astype(F32) + came[s].astype(F32)).astype(BF16)
+
+
+def pairs_kernel(near, came, *refs):
+    lower, upper = refs[-2:]
+    count = lower.shape[0]
+    for s in range(count):
+        lower[s] = (near[s].astype(F32) + came[s].astype(F32)).astype(BF16)
+        upper[s] = (near[count + s].astype(F32) + came[count + s].astype(F32)).astype(BF16)
+
+
+def step_kernel(lower, came, *refs):
+    own, other = refs[-2:]
+    own[...] = (lower[0].astype(F32) + came[0].astype(F32)).astype(BF16)
+    other[...] = (lower[1].astype(F32) + came[1].astype(F32)).astype(BF16)
 
 
 def total_kernel(count, *refs):
@@ -290,9 +361,8 @@
         bank = lax.rem(turn, 2)
         for i in range(TURN):
             held[bank, i] = tn(left_ref[turn * TURN + i], right_ref[turn * TURN + i]).astype(BF16)
-            if i % 2:
-                store(turn, i - 1).start()
-                store(turn, i).start()
+        for i in range(TURN):
+            store(turn, i).start()
         return 0
 
     lax.fori_loop(0, turns, one, 0)
@@ -377,10 +447,10 @@
     return lax.ppermute(array, axis, [(i, i ^ bit) for i in range(count)])
 
 
-def add_cores(keep, send, *earlier):
+def add_cores(keep, came, *earlier):
     shape = jax.ShapeDtypeStruct(keep.shape[1:], BF16)
-    hbm = range(2, 2 + len(earlier))
-    return kernel_call(add_kernel, [shape, shape], [], 0, limit=2, in_hbm=hbm)(keep, swap(send, 1), *earlier)
+    hbm = [2] if earlier else []
+    return kernel_call(add_kernel, [shape, shape], [], 0, limit=2, in_hbm=hbm)(keep, came, *earlier)
 
 
 def add_chips(near, far, *earlier):
@@ -401,7 +471,7 @@
     slots = local_experts * CAP
     rows = sources * CAP
     gate_t, gate_there = in_vmem(jnp.swapaxes(gate_weight, 1, 2))
-    up_t, up_there = in_vmem(jnp.swapaxes(up_weight, 1, 2))
+    up_t = jnp.swapaxes(up_weight, 1, 2)
     product = 2 * local_experts * rows * units * model
     held = lambda *shape, kind=BF16: pltpu.VMEM(shape, kind)
     sent = lambda *shape: jax.ShapeDtypeStruct(shape, BF16)
@@ -418,12 +488,25 @@
     own_across = swap(own, 2)
     grad_across = swap(out_grad, 2)
     came = join(came, gate_there, own_across, grad_across)
-    came_across = join([swap(came, 2)], up_there)[0]
+    came_across_there = swap(came, 2)
     grads = join([out_grad, grad_across], came)
     grads = [grads] + [swap(grads, s, "expert") for s in range(1, sources)]
 
-    out_rows, x_rows, activ, scaled, slope, silu, onehot, slot_gate = kernel_call(
-        functools.partial(forward_kernel, choose),
+    half_rows, partial, onehot, slot_gate = kernel_call(
+        functools.partial(early_kernel, choose),
+        [
+            held(local_experts, rows, model // 2),
+            held(2, local_experts, rows, units, kind=F32),
+            held(sources, slots, tokens),
+            held(local_experts, rows, tokens, kind=F32),
+        ],
+        [pltpu.VMEM((RING, units, model // 2), BF16), pltpu.SemaphoreType.DMA((RING,))],
+        product,
+        in_hbm=(6,),
+    )(capacity_blocks, own, swap(own, 1), came, swap(came, 1), gate_t, up_t)
+    came_across = join([came_across_there], onehot)[0]
+    out_rows, x_rows, activ, scaled, slope, silu = kernel_call(
+        forward_kernel,
         [
             held(sources, slots, model),
             held(local_experts, rows, model),
@@ -431,24 +514,31 @@
             held(local_experts, rows, units),
             held(local_experts, rows, units, kind=F32),
             held(local_experts, rows, units, kind=F32),
-            held(sources, slots, tokens),
-            held(local_experts, rows, tokens, kind=F32),
         ],
-        [pltpu.VMEM((RING, units, model), BF16), pltpu.SemaphoreType.DMA((RING,))],
-        3 * product,
-        limit=6,
-        in_hbm=(11,),
+        [
+            pltpu.VMEM((local_experts, rows, model // 2), BF16),
+            pltpu.VMEM((RING, units, model // 2), BF16),
+            pltpu.VMEM((RING, units, model), BF16),
+            pltpu.SemaphoreType.DMA((RING,)),
+            pltpu.SemaphoreType.DMA((RING,)),
+        ],
+        2 * product,
+        limit=9,
+        in_hbm=(5, 6),
     )(
-        capacity_blocks,
-        own, swap(own, 1), own_across, swap(own_across, 1),
-        came, swap(came, 1), came_across, swap(came_across, 1),
-        gate_t, up_t, down_weight, grads[0],
+        own_across, swap(own_across, 1), came_across, swap(came_across, 1),
+        gate_t, up_t, down_weight, half_rows, partial, onehot, slot_gate, grads[0],
     )
 
     keep, send = kernel_call(
-        home_kernel, [sent(2, sources, tokens, width)] * 2, [], 2 * slots * sources * tokens * model, limit=2,
+        home_kernel,
+        [sent(2, sources, tokens, width), sent(4, sources, tokens, width)],
+        [],
+        2 * slots * sources * tokens * model,
+        limit=2,
     )(onehot, out_rows, *grads)
-    out_near, out_far = add_cores(keep, send)
+    near = swap(send, 1)
+    out_near, out_far = add_cores(keep, near)
     back_rows, dots, y_rows, gate_part, up_part = kernel_call(
         backward_kernel,
         [
@@ -458,34 +548,38 @@
             held(local_experts, rows, units),
             held(local_experts, rows, units),
         ],
-        [pltpu.VMEM((RING, units, model), BF16), pltpu.SemaphoreType.DMA((RING,))],
+        [pltpu.VMEM((RING, units, model), BF16)] * 2 + [pltpu.SemaphoreType.DMA((RING,))] * 2,
         3 * product,
-        limit=6,
-        in_hbm=(10,),
+        limit=9,
+        in_hbm=(6, 7),
     )(
-        *grads, *[swap(x, 1) for x in grads],
+        *grads, near,
         gate_t, up_t, down_weight, activ, slope, silu, onehot, slot_gate, out_near,
     )
 
-    out_own, out_parts = add_chips(out_near, swap(out_far, 2))
+    part = sent(tokens, width)
+    pair = sent(2, tokens, width)
+    out_lower, out_upper = kernel_call(pairs_kernel, [pair, pair], [], 0, limit=2)(out_near, swap(out_far, 2))
     keep, send = kernel_call(
         functools.partial(home_values_kernel, choose),
         [sent(2, sources, tokens + EXTRA, width)] * 2,
         [],
         2 * slots * sources * tokens * model,
         limit=2,
-    )(onehot, back_rows, dots, own, came, out_own)
-    down_grad = weight_grad(scaled, y_rows, out_own)
-    back_near, back_far = add_cores(keep, send, down_grad)
-    up_grad = weight_grad(up_part, x_rows, back_near)
-    layer_out = kernel_call(
-        functools.partial(total_kernel, sources), [sent(tokens, width)], [], 0, limit=2
-    )(out_own, *out_parts)[0]
+    )(onehot, back_rows, dots, own, came, out_lower)
+    out_came = swap(out_upper, 2, "expert")
+    down_grad = weight_grad(scaled, y_rows, out_lower)
+    back_near, back_far = add_cores(keep, swap(send, 1), down_grad, out_came)
+    out_own, out_other = kernel_call(step_kernel, [part, part], [], 0, limit=2)(out_lower, out_came, back_near)
+    up_grad = weight_grad(up_part, x_rows, back_near, out_own)
     back_own, back_parts = add_chips(back_near, swap(back_far, 2), up_grad)
+    layer_out = kernel_call(functools.partial(total_kernel, 2), [part], [], 0, limit=2)(
+        out_own, swap(out_other, 1, "expert")
+    )[0]
     gate_grad = weight_grad(gate_part, x_rows, back_own)
     input_grad, value_grad = kernel_call(
         functools.partial(total_kernel, sources),
-        [sent(tokens, width), jax.ShapeDtypeStruct((choose, tokens), F32)],
+        [part, jax.ShapeDtypeStruct((choose, tokens), F32)],
         [],
         0,
         limit=2,
@@ -621,7 +715,7 @@
 
 def body(*operands):
     hidden_in, gate_weight = operands[0], operands[5]
-    if lax.axis_size("etp") == 4 and hidden_in.shape[0] <= gate_weight.shape[0] * CAP:
+    if lax.axis_size("expert") == 4 and lax.axis_size("etp") == 4 and hidden_in.shape[0] <= gate_weight.shape[0] * CAP:
         return gathered_body(*operands)
     return dispatched_body(*operands)
 

time: 81.8 us -> 89.5 us (1.094)
  Pallas kernels: 51.8 us -> 58 us
  waiting for transfers between devices: 3.09 us -> 6.14 us
  starting transfers between devices: 25.6 us -> 23.9 us
    pallas_call x17 -> x19, Pallas kernels: 42.9 us -> 53.6 us  [call(): pl.pallas_call(kernel, in_specs=specs, out_specs=out_specs or [pl.BlockSp...]
    pallas_call x2 -> x1, Pallas kernels: 8.86 us -> 4.42 us  [in_vmem(): pl.pallas_call(load_kernel, in_specs=[pl.BlockSpec(memory_space=pltpu.HBM...]
    ppermute x27 -> x22, waiting for transfers between devices: 3.09 us -> 6.14 us  [swap(): return lax.ppermute(array, axis, [(i, i ^ bit) for i in range(count)])]
    ppermute x27 -> x22, starting transfers between devices: 25.6 us -> 23.9 us  [swap(): return lax.ppermute(array, axis, [(i, i ^ bit) for i in range(count)])]
  transfers between devices with their start and end apart: 27 -> 22, of which waited for: 4 -> 5; matrix products, arithmetic and copies ran while one was open for 0% -> 0% of each run, Pallas kernels for 60% -> 62%
where the time goes in v5:
time: 89.5 us; the launch traced here: 88.9 us
  Pallas kernels  58 us (65%)
  starting transfers between devices  23.9 us (27%)
  waiting for transfers between devices  6.14 us (7%)
    pallas_call x19, Pallas kernels, call(): pl.pallas_call(kernel, in_specs=specs, out_specs=out_specs or [pl.BlockSp...  53.6 us
    ppermute x22, starting transfers between devices, swap(): return lax.ppermute(array, axis, [(i, i ^ bit) for i in range(count)])  23.9 us
    ppermute x22, waiting for transfers between devices, swap(): return lax.ppermute(array, axis, [(i, i ^ bit) for i in range(count)])  6.14 us
    pallas_call x1, Pallas kernels, in_vmem(): pl.pallas_call(load_kernel, in_specs=[pl.BlockSpec(memory_space=pltpu.HBM...  4.42 us
  transfers between devices with their start and end apart: 22, of which 5 were waited for; matrix products, arithmetic and copies ran while one was open for 0% of the time, Pallas kernels for 62%

profile of v5, /device:TPU:0, one launch (start us, length us, event | category | flops | bytes accessed | tf_op | source)
XLA Modules:
  0.0 88.9 jit_solution(2849085396243161900)
XLA Ops:
  0.6 0.9 shard_map.127.o0.own_ref
  1.5 3.0 %collective-permute-start.4 = (bf16[144,256]{1,0:T(8,128)(2,1)S(1)}, bf16[144,256]{1,0:T(8,128)(2,1)S(1)}, u32[]{:S(2)}, u32[]{:S(2)}) collective-permute-start(bf16[144,256]{1,0:T(8,128)(2,1)S(1)} %shard_map.127.o0.own_ref), channel_id=1, source_target_pairs={{0,2},{1,3},{2,0},{3,1},{4,6},{5,7},{6,4},{7,5},{8,10},{9,11},{10,... | collective-permute-start | bytes 221192 | tf_op jit(solution)/shard_map/ppermute | solution.py:447
  4.5 3.6 %collective-permute-start.3 = (bf16[144,256]{1,0:T(8,128)(2,1)S(1)}, bf16[144,256]{1,0:T(8,128)(2,1)S(1)}, u32[]{:S(2)}, u32[]{:S(2)}) collective-permute-start(bf16[144,256]{1,0:T(8,128)(2,1)S(1)} %shard_map.127.o0.own_ref), channel_id=1, source_target_pairs={{0,12},{4,8},{8,4},{12,0},{1,13},{5,9},{9,5},{13,1},{2,14},{6,10},... | collective-permute-start | bytes 221192 | tf_op jit(solution)/shard_map/ppermute | solution.py:447
  8.1 0.8 collective-permute-start.1
  9.2 4.4 %shard_map.128 = (bf16[16,352,1024]{2,1,0:T(8,128)(2,1)S(1)}, f32[8,128]{1,0:T(8,128)S(1)}) custom-call(bf16[16,352,1024]{2,1,0:T(8,128)(2,1)} %bitcast.14), custom_call_target="tpu_custom_call" | custom-call | bytes 11534336 | tf_op jit(solution)/shard_map/pallas_call | solution.py:384
  14.2 1.4 %collective-permute-start.8 = (bf16[3,144,256]{2,1,0:T(8,128)(2,1)S(1)}, bf16[3,144,256]{2,1,0:T(8,128)(2,1)S(1)}, u32[]{:S(2)}, u32[]{:S(2)}) collective-permute-start(bf16[3,144,256]{2,1,0:T(8,128)(2,1)S(1)} %shard_map.129.b0.refs_2_.info_ref), channel_id=1, source_target_pairs={{0,2},{1,3},{2,0},{3,1},{4,6},{5,7},{6,4},{7,5},{8,10},{9,11},{10,... | collective-permute-start | bytes 663560 | tf_op jit(solution)/shard_map/ppermute | solution.py:447
  15.8 1.1 %collective-permute-done.o1 = bf16[144,256]{1,0:T(8,128)(2,1)S(1)} collective-permute-done((bf16[144,256]{1,0:T(8,128)(2,1)S(1)}, bf16[144,256]{1,0:T(8,128)(2,1)S(1)}, u32[]{:S(2)}, u32[]{:S(2)}) %collective-permute-start) | collective-permute-done | bytes 73760 | tf_op jit(solution)/shard_map/ppermute | solution.py:447
  16.9 8.2 %shard_map.130 = (bf16[16,64,512]{2,1,0:T(8,128)(2,1)S(1)}, f32[2,16,64,352]{3,2,1,0:T(8,128)S(1)}, bf16[4,256,128]{2,1,0:T(8,128)(2,1)S(1)}, f32[16,64,128]{2,1,0:T(8,128)S(1)}) custom-call(s32[64]{0:T(128)S(1)} %copy-done.1, bf16[144,256]{1,0:T(8,128)(2,1)S(1)} %shard_map.127.o0.own_ref, bf16[144,256]{1,0:T(8,128)(2,1)S(1)} %collective-permute-done.o1, ...), custom_call_target="tpu_custom_call" | custom-call | flops 738197504 | bytes 23068672 | tf_op jit(solution)/shard_map/pallas_call | solution.py:419
  25.7 3.7 %collective-permute-start.12 = (bf16[2,128,256]{2,1,0:T(8,128)(2,1)S(1)}, bf16[2,128,256]{2,1,0:T(8,128)(2,1)S(1)}, u32[]{:S(2)}, u32[]{:S(2)}) collective-permute-start(bf16[2,128,256]{2,1,0:T(8,128)(2,1)S(1)} %shard_map.132.later_ref.refs_0_.a0), channel_id=1, source_target_pairs={{0,12},{4,8},{8,4},{12,0},{1,13},{5,9},{9,5},{13,1},{2,14},{6,10},... | collective-permute-start | bytes 393224 | tf_op jit(solution)/shard_map/ppermute | solution.py:447
  29.4 0.8 collective-permute-start.10
  30.2 10.4 %shard_map.133 = (bf16[4,256,1024]{2,1,0:T(8,128)(2,1)S(1)}, bf16[16,64,1024]{2,1,0:T(8,128)(2,1)S(1)}, bf16[16,64,352]{2,1,0:T(8,128)(2,1)S(1)}, bf16[16,64,352...) custom-call(bf16[144,256]{1,0:T(8,128)(2,1)S(1)} %collective-permute-done.4.refs_4_.o2, ...), custom_call_target="tpu_custom_call" | custom-call | flops 1476395008 | bytes 46137344 | tf_op jit(solution)/shard_map/pallas_call | solution.py:419
  41.2 2.6 %collective-permute-done.13.came.near_ref = bf16[4,4,128,256]{3,2,1,0:T(8,128)(2,1)S(1)} collective-permute-done((bf16[4,4,128,256]{3,2,1,0:T(8,128)(2,1)S(1)}, bf16[4,4,128,256]{3,2,1,0:T(8,128)(2,1)S(1)}, u32[]{:S(2)}, u32[]{:S(2)}) %collective-permute-start.13) | collective-permute-done | bytes 1048608 | tf_op jit(solution)/shard_map/ppermute | solution.py:447
  44.0 0.7 collective-permute-start.14
  44.7 13.2 %shard_map.137 = (bf16[4,256,1024]{2,1,0:T(8,128)(2,1)S(1)}, f32[16,64,128]{2,1,0:T(8,128)S(1)}, bf16[16,64,1024]{2,1,0:T(8,128)(2,1)S(1)}, bf16[16,64,352]{2,1,0:T(8,128)(2,1)S(1)}, bf16[16,64,352]{2,1,0:T(8,128)(2,1)S(1)}) custom-call(bf16[2,128,256]{2,1,0:T(8,128)(2,1)S(1)} %shard_map.132.later_ref.refs_0_.a0, ...), custom_call_target="tpu_custom_call" | custom-call | flops 2214592512 | bytes 69206016 | tf_op jit(solution)/shard_map/pallas_call | solution.py:419
  58.6 2.1 %collective-permute-start.15 = (bf16[2,128,256]{2,1,0:T(8,128)(2,1)S(1)}, bf16[2,128,256]{2,1,0:T(8,128)(2,1)S(1)}, u32[]{:S(2)}, u32[]{:S(2)}) collective-permute-start(bf16[2,128,256]{2,1,0:T(8,128)(2,1)S(1)} %get-tuple-element.53), channel_id=1, source_target_pairs={{0,8},{4,12},{8,0},{12,4},{1,9},{5,13},{9,1},{13,5},{2,10},{6,14},... | collective-permute-start | bytes 393224 | tf_op jit(solution)/shard_map/ppermute | solution.py:447
  60.7 6.0 %shard_map.139.refs_0_ = bf16[16,352,1024]{2,1,0:T(8,128)(2,1)} custom-call(bf16[16,64,352]{2,1,0:T(8,128)(2,1)S(1)} %get-tuple-element.61.left_ref, bf16[16,64,1024]{2,1,0:T(8,128)(2,1)S(1)} %get-tuple-element.62.right_ref, bf16[2,128,256]{2,1,0:T(8,128)(2,1)S(1)} %get-tuple-element.52.refs_0_.lower), custom_call_target="tpu_custom_call" | custom-call | flops 738197504 | bytes 23068672 | tf_op jit(solution)/shard_map/pallas_call | solution.py:419
  66.7 1.5 %collective-permute-done.15.refs_1_.came = bf16[2,128,256]{2,1,0:T(8,128)(2,1)S(1)} collective-permute-done((bf16[2,128,256]{2,1,0:T(8,128)(2,1)S(1)}, bf16[2,128,256]{2,1,0:T(8,128)(2,1)S(1)}, u32[]{:S(2)}, u32[]{:S(2)}) %collective-permute-start.15) | collective-permute-done | bytes 131104 | tf_op jit(solution)/shard_map/ppermute | solution.py:447
  68.4 1.4 %collective-permute-start.18 = (bf16[4,144,256]{2,1,0:T(8,128)(2,1)S(1)}, bf16[4,144,256]{2,1,0:T(8,128)(2,1)S(1)}, u32[]{:S(2)}, u32[]{:S(2)}) collective-permute-start(bf16[4,144,256]{2,1,0:T(8,128)(2,1)S(1)} %get-tuple-element.66), channel_id=1, source_target_pairs={{0,2},{1,3},{2,0},{3,1},{4,6},{5,7},{6,4},{7,5},{8,10},{9,11},{10,... | collective-permute-start | bytes 884744 | tf_op jit(solution)/shard_map/ppermute | solution.py:447
  69.9 0.7 collective-permute-start.17
  70.6 6.0 %shard_map.143.refs_0_ = bf16[16,352,1024]{2,1,0:T(8,128)(2,1)} custom-call(bf16[16,64,352]{2,1,0:T(8,128)(2,1)S(1)} %get-tuple-element.67.left_ref, bf16[16,64,1024]{2,1,0:T(8,128)(2,1)S(1)} %get-tuple-element.68.right_ref, bf16[4,144,256]{2,1,0:T(8,128)(2,1)S(1)} %get-tuple-element.63.refs_0_.near, bf16[128,256]{1,0:T(8,128)(2,1)S(1)} %get-tuple-element.64.refs_0_.refs_1_), custom_call_target="tpu_custom_call" | custom-call | flops 738197504 | bytes 23068672 | tf_op jit(solution)/shard_map/pallas_call | solution.py:419
  77.1 1.1 %collective-permute-start.19 = (bf16[144,256]{1,0:T(8,128)(2,1)S(1)}, bf16[144,256]{1,0:T(8,128)(2,1)S(1)}, u32[]{:S(2)}, u32[]{:S(2)}) collective-permute-start(bf16[144,256]{1,0:T(8,128)(2,1)S(1)} %get-tuple-element.70), channel_id=1, source_target_pairs={{0,4},{4,0},{8,12},{12,8},{1,5},{5,1},{9,13},{13,9},{2,6},{6,2},{1... | collective-permute-start | bytes 221192 | tf_op jit(solution)/shard_map/ppermute | solution.py:447
  78.2 2.9 %collective-permute-start.20 = (bf16[144,256]{1,0:T(8,128)(2,1)S(1)}, bf16[144,256]{1,0:T(8,128)(2,1)S(1)}, u32[]{:S(2)}, u32[]{:S(2)}) collective-permute-start(bf16[144,256]{1,0:T(8,128)(2,1)S(1)} %get-tuple-element.71), channel_id=1, source_target_pairs={{0,8},{4,12},{8,0},{12,4},{1,9},{5,13},{9,1},{13,5},{2,10},{6,14},... | collective-permute-start | bytes 221192 | tf_op jit(solution)/shard_map/ppermute | solution.py:447
  82.2 6.0 %shard_map.146 = bf16[16,352,1024]{2,1,0:T(8,128)(2,1)} custom-call(bf16[16,64,352]{2,1,0:T(8,128)(2,1)S(1)} %get-tuple-element.75.left_ref, bf16[16,64,1024]{2,1,0:T(8,128)(2,1)S(1)} %get-tuple-element.68.right_ref, bf16[144,256]{1,0:T(8,128)(2,1)S(1)} %get-tuple-element.69.refs_0_), custom_call_target="tpu_custom_call" | custom-call | flops 738197504 | bytes 23068672 | tf_op jit(solution)/shard_map/pallas_call | solution.py:419
  88.3 0.7 shard_map.145
  (44 shorter events, 4.9 us)
Async XLA Ops:
  0.6 16.2 %copy-start.1 = (s32[64]{0:T(128)S(1)}, s32[64]{0:T(128)}, u32[]{:S(2)}) copy-start(s32[64]{0:T(128)} %capacity_ref.1) | copy-start | bytes 772
  1.5 12.1 %collective-permute-start.4 = (bf16[144,256]{1,0:T(8,128)(2,1)S(1)}, bf16[144,256]{1,0:T(8,128)(2,1)S(1)}, u32[]{:S(2)}, u32[]{:S(2)}) collective-permute-start(bf16[144,256]{1,0:T(8,128)(2,1)S(1)} %shard_map.127.o0.own_ref), channel_id=1, source_target_pairs={{0,2},{1,3},{2,0},{3,1},{4,6},{5,7},{6,4},{7,5},{8,10},{9,11},{10,... | collective-permute-start | bytes 221192 | tf_op jit(solution)/shard_map/ppermute | solution.py:447
  4.5 9.2 %collective-permute-start.3 = (bf16[144,256]{1,0:T(8,128)(2,1)S(1)}, bf16[144,256]{1,0:T(8,128)(2,1)S(1)}, u32[]{:S(2)}, u32[]{:S(2)}) collective-permute-start(bf16[144,256]{1,0:T(8,128)(2,1)S(1)} %shard_map.127.o0.own_ref), channel_id=1, source_target_pairs={{0,12},{4,8},{8,4},{12,0},{1,13},{5,9},{9,5},{13,1},{2,14},{6,10},... | collective-permute-start | bytes 221192 | tf_op jit(solution)/shard_map/ppermute | solution.py:447
  8.1 5.9 %collective-permute-start.2 = (bf16[144,256]{1,0:T(8,128)(2,1)S(1)}, bf16[144,256]{1,0:T(8,128)(2,1)S(1)}, u32[]{:S(2)}, u32[]{:S(2)}) collective-permute-start(bf16[144,256]{1,0:T(8,128)(2,1)S(1)} %shard_map.127.o0.own_ref), channel_id=1, source_target_pairs={{0,8},{4,12},{8,0},{12,4},{1,9},{5,13},{9,1},{13,5},{2,10},{6,14},... | collective-permute-start | bytes 221192 | tf_op jit(solution)/shard_map/ppermute | solution.py:447
  8.1 5.9 %collective-permute-start.1 = (bf16[144,256]{1,0:T(8,128)(2,1)S(1)}, bf16[144,256]{1,0:T(8,128)(2,1)S(1)}, u32[]{:S(2)}, u32[]{:S(2)}) collective-permute-start(bf16[144,256]{1,0:T(8,128)(2,1)S(1)} %shard_map.127.o0.own_ref), channel_id=1, source_target_pairs={{0,4},{4,0},{8,12},{12,8},{1,5},{5,1},{9,13},{13,9},{2,6},{6,2},{1... | collective-permute-start | bytes 221192 | tf_op jit(solution)/shard_map/ppermute | solution.py:447
  8.9 4.7 %collective-permute-start.5 = (bf16[128,256]{1,0:T(8,128)(2,1)}, bf16[128,256]{1,0:T(8,128)(2,1)S(1)}, u32[]{:S(2)}, u32[]{:S(2)}) collective-permute-start(bf16[128,256]{1,0:T(8,128)(2,1)} %refs_0_.1), channel_id=1, source_target_pairs={{0,2},{1,3},{2,0},{3,1},{4,6},{5,7},{6,4},{7,5},{8,10},{9,11},{10,... | collective-permute-start | bytes 196616 | tf_op jit(solution)/shard_map/ppermute | solution.py:447
  14.1 2.8 %collective-permute-start.6 = (bf16[3,144,256]{2,1,0:T(8,128)(2,1)S(1)}, bf16[3,144,256]{2,1,0:T(8,128)(2,1)S(1)}, u32[]{:S(2)}, u32[]{:S(2)}) collective-permute-start(bf16[3,144,256]{2,1,0:T(8,128)(2,1)S(1)} %shard_map.129.b0.refs_2_.info_ref), channel_id=1, source_target_pairs={{0,1},{1,0},{2,3},{3,2},{4,5},{5,4},{6,7},{7,6},{8,9},{9,8},{10,11... | collective-permute-start | bytes 663560 | tf_op jit(solution)/shard_map/ppermute | solution.py:447
  14.2 10.9 %collective-permute-start.8 = (bf16[3,144,256]{2,1,0:T(8,128)(2,1)S(1)}, bf16[3,144,256]{2,1,0:T(8,128)(2,1)S(1)}, u32[]{:S(2)}, u32[]{:S(2)}) collective-permute-start(bf16[3,144,256]{2,1,0:T(8,128)(2,1)S(1)} %shard_map.129.b0.refs_2_.info_ref), channel_id=1, source_target_pairs={{0,2},{1,3},{2,0},{3,1},{4,6},{5,7},{6,4},{7,5},{8,10},{9,11},{10,... | collective-permute-start | bytes 663560 | tf_op jit(solution)/shard_map/ppermute | solution.py:447
  15.6 1.3 %collective-permute-start = (bf16[144,256]{1,0:T(8,128)(2,1)S(1)}, bf16[144,256]{1,0:T(8,128)(2,1)S(1)}, u32[]{:S(2)}, u32[]{:S(2)}) collective-permute-start(bf16[144,256]{1,0:T(8,128)(2,1)S(1)} %shard_map.127.o0.own_ref), channel_id=1, source_target_pairs={{0,1},{1,0},{2,3},{3,2},{4,5},{5,4},{6,7},{7,6},{8,9},{9,8},{10,11... | collective-permute-start | bytes 221192 | tf_op jit(solution)/shard_map/ppermute | solution.py:447
  16.9 8.8 %copy-start = (bf16[128,256]{1,0:T(8,128)(2,1)S(1)}, bf16[128,256]{1,0:T(8,128)(2,1)}, u32[]{:S(2)}) copy-start(bf16[128,256]{1,0:T(8,128)(2,1)} %refs_0_.1) | copy-start | bytes 196612
  25.1 5.1 %collective-permute-start.9 = (bf16[3,144,256]{2,1,0:T(8,128)(2,1)S(1)}, bf16[3,144,256]{2,1,0:T(8,128)(2,1)S(1)}, u32[]{:S(2)}, u32[]{:S(2)}) collective-permute-start(bf16[3,144,256]{2,1,0:T(8,128)(2,1)S(1)} %bitcast.8), channel_id=1, source_target_pairs={{0,1},{1,0},{2,3},{3,2},{4,5},{5,4},{6,7},{7,6},{8,9},{9,8},{10,11... | collective-permute-start | bytes 663560 | tf_op jit(solution)/shard_map/ppermute | solution.py:447
  25.3 4.8 %collective-permute-start.7 = (bf16[144,256]{1,0:T(8,128)(2,1)S(1)}, bf16[144,256]{1,0:T(8,128)(2,1)S(1)}, u32[]{:S(2)}, u32[]{:S(2)}) collective-permute-start(bf16[144,256]{1,0:T(8,128)(2,1)S(1)} %collective-permute-done.4.refs_4_.o2), channel_id=1, source_target_pairs={{0,1},{1,0},{2,3},{3,2},{4,5},{5,4},{6,7},{7,6},{8,9},{9,8},{10,11... | collective-permute-start | bytes 221192 | tf_op jit(solution)/shard_map/ppermute | solution.py:447
  25.7 14.9 %collective-permute-start.12 = (bf16[2,128,256]{2,1,0:T(8,128)(2,1)S(1)}, bf16[2,128,256]{2,1,0:T(8,128)(2,1)S(1)}, u32[]{:S(2)}, u32[]{:S(2)}) collective-permute-start(bf16[2,128,256]{2,1,0:T(8,128)(2,1)S(1)} %shard_map.132.later_ref.refs_0_.a0), channel_id=1, source_target_pairs={{0,12},{4,8},{8,4},{12,0},{1,13},{5,9},{9,5},{13,1},{2,14},{6,10},... | collective-permute-start | bytes 393224 | tf_op jit(solution)/shard_map/ppermute | solution.py:447
  29.4 11.2 %collective-permute-start.11 = (bf16[2,128,256]{2,1,0:T(8,128)(2,1)S(1)}, bf16[2,128,256]{2,1,0:T(8,128)(2,1)S(1)}, u32[]{:S(2)}, u32[]{:S(2)}) collective-permute-start(bf16[2,128,256]{2,1,0:T(8,128)(2,1)S(1)} %shard_map.132.later_ref.refs_0_.a0), channel_id=1, source_target_pairs={{0,8},{4,12},{8,0},{12,4},{1,9},{5,13},{9,1},{13,5},{2,10},{6,14},... | collective-permute-start | bytes 393224 | tf_op jit(solution)/shard_map/ppermute | solution.py:447
  29.4 11.2 %collective-permute-start.10 = (bf16[2,128,256]{2,1,0:T(8,128)(2,1)S(1)}, bf16[2,128,256]{2,1,0:T(8,128)(2,1)S(1)}, u32[]{:S(2)}, u32[]{:S(2)}) collective-permute-start(bf16[2,128,256]{2,1,0:T(8,128)(2,1)S(1)} %shard_map.132.later_ref.refs_0_.a0), channel_id=1, source_target_pairs={{0,4},{4,0},{8,12},{12,8},{1,5},{5,1},{9,13},{13,9},{2,6},{6,2},{1... | collective-permute-start | bytes 393224 | tf_op jit(solution)/shard_map/ppermute | solution.py:447
  41.1 2.7 %collective-permute-start.13 = (bf16[4,4,128,256]{3,2,1,0:T(8,128)(2,1)S(1)}, bf16[4,4,128,256]{3,2,1,0:T(8,128)(2,1)S(1)}, u32[]{:S(2)}, u32[]{:S(2)}) collective-permute-start(bf16[4,4,128,256]{3,2,1,0:T(8,128)(2,1)S(1)} %get-tuple-element.49), channel_id=1, source_target_pairs={{0,1},{1,0},{2,3},{3,2},{4,5},{5,4},{6,7},{7,6},{8,9},{9,8},{10,11... | collective-permute-start | bytes 3145736 | tf_op jit(solution)/shard_map/ppermute | solution.py:447
  44.0 13.9 %collective-permute-start.14 = (bf16[4,128,256]{2,1,0:T(8,128)(2,1)S(1)}, bf16[4,128,256]{2,1,0:T(8,128)(2,1)S(1)}, u32[]{:S(2)}, u32[]{:S(2)}) collective-permute-start(bf16[4,128,256]{2,1,0:T(8,128)(2,1)S(1)} %get-tuple-element.51), channel_id=1, source_target_pairs={{0,2},{1,3},{2,0},{3,1},{4,6},{5,7},{6,4},{7,5},{8,10},{9,11},{10,... | collective-permute-start | bytes 786440 | tf_op jit(solution)/shard_map/ppermute | solution.py:447
  58.6 9.7 %collective-permute-start.16 = (bf16[2,4,144,256]{3,2,1,0:T(8,128)(2,1)S(1)}, bf16[2,4,144,256]{3,2,1,0:T(8,128)(2,1)S(1)}, u32[]{:S(2)}, u32[]{:S(2)}) collective-permute-start(bf16[2,4,144,256]{3,2,1,0:T(8,128)(2,1)S(1)} %get-tuple-element.60), channel_id=1, source_target_pairs={{0,1},{1,0},{2,3},{3,2},{4,5},{5,4},{6,7},{7,6},{8,9},{9,8},{10,11... | collective-permute-start | bytes 1769480 | tf_op jit(solution)/shard_map/ppermute | solution.py:447
  58.6 9.6 %collective-permute-start.15 = (bf16[2,128,256]{2,1,0:T(8,128)(2,1)S(1)}, bf16[2,128,256]{2,1,0:T(8,128)(2,1)S(1)}, u32[]{:S(2)}, u32[]{:S(2)}) collective-permute-start(bf16[2,128,256]{2,1,0:T(8,128)(2,1)S(1)} %get-tuple-element.53), channel_id=1, source_target_pairs={{0,8},{4,12},{8,0},{12,4},{1,9},{5,13},{9,1},{13,5},{2,10},{6,14},... | collective-permute-start | bytes 393224 | tf_op jit(solution)/shard_map/ppermute | solution.py:447
  68.4 8.6 %collective-permute-start.18 = (bf16[4,144,256]{2,1,0:T(8,128)(2,1)S(1)}, bf16[4,144,256]{2,1,0:T(8,128)(2,1)S(1)}, u32[]{:S(2)}, u32[]{:S(2)}) collective-permute-start(bf16[4,144,256]{2,1,0:T(8,128)(2,1)S(1)} %get-tuple-element.66), channel_id=1, source_target_pairs={{0,2},{1,3},{2,0},{3,1},{4,6},{5,7},{6,4},{7,5},{8,10},{9,11},{10,... | collective-permute-start | bytes 884744 | tf_op jit(solution)/shard_map/ppermute | solution.py:447
  69.9 11.7 %collective-permute-start.17 = (bf16[128,256]{1,0:T(8,128)(2,1)S(1)}, bf16[128,256]{1,0:T(8,128)(2,1)S(1)}, u32[]{:S(2)}, u32[]{:S(2)}) collective-permute-start(bf16[128,256]{1,0:T(8,128)(2,1)S(1)} %get-tuple-element.65), channel_id=1, source_target_pairs={{0,4},{4,0},{8,12},{12,8},{1,5},{5,1},{9,13},{13,9},{2,6},{6,2},{1... | collective-permute-start | bytes 196616 | tf_op jit(solution)/shard_map/ppermute | solution.py:447
  77.1 11.1 %collective-permute-start.19 = (bf16[144,256]{1,0:T(8,128)(2,1)S(1)}, bf16[144,256]{1,0:T(8,128)(2,1)S(1)}, u32[]{:S(2)}, u32[]{:S(2)}) collective-permute-start(bf16[144,256]{1,0:T(8,128)(2,1)S(1)} %get-tuple-element.70), channel_id=1, source_target_pairs={{0,4},{4,0},{8,12},{12,8},{1,5},{5,1},{9,13},{13,9},{2,6},{6,2},{1... | collective-permute-start | bytes 221192 | tf_op jit(solution)/shard_map/ppermute | solution.py:447
  78.2 10.0 %collective-permute-start.20 = (bf16[144,256]{1,0:T(8,128)(2,1)S(1)}, bf16[144,256]{1,0:T(8,128)(2,1)S(1)}, u32[]{:S(2)}, u32[]{:S(2)}) collective-permute-start(bf16[144,256]{1,0:T(8,128)(2,1)S(1)} %get-tuple-element.71), channel_id=1, source_target_pairs={{0,8},{4,12},{8,0},{12,4},{1,9},{5,13},{9,1},{13,5},{2,10},{6,14},... | collective-permute-start | bytes 221192 | tf_op jit(solution)/shard_map/ppermute | solution.py:447
  81.1 7.2 %collective-permute-start.21 = (bf16[144,256]{1,0:T(8,128)(2,1)S(1)}, bf16[144,256]{1,0:T(8,128)(2,1)S(1)}, u32[]{:S(2)}, u32[]{:S(2)}) collective-permute-start(bf16[144,256]{1,0:T(8,128)(2,1)S(1)} %get-tuple-element.72), channel_id=1, source_target_pairs={{0,12},{4,8},{8,4},{12,0},{1,13},{5,9},{9,5},{13,1},{2,14},{6,10},... | collective-permute-start | bytes 221192 | tf_op jit(solution)/shard_map/ppermute | solution.py:447

commit v6 on v5

--- a/solution.py
+++ b/solution.py
@@ -62,12 +62,14 @@
             home[q // 2, s, 0:tokens, :] = tn(onehot[s], rows[s, :, columns(me, q, width)]).astype(BF16)
 
 
-RING = 4
+RING = 8
 
 
 def ring(weight, slots, sems, columns=None):
+    depth = slots.shape[0]
+
     def load(e):
-        slot = lax.rem(e, RING)
+        slot = lax.rem(e, depth)
         source = weight.at[e] if columns is None else weight.at[e, :, columns]
         return pltpu.make_async_copy(source, slots.at[slot], sems.at[slot])
 
@@ -76,9 +78,15 @@
         def _():
             load(e).start()
 
-    for e in range(RING):
+    for e in range(min(depth, weight.shape[0])):
         load(jnp.int32(e)).start()
-    return start, lambda e: load(e).wait()
+    if depth >= weight.shape[0]:
+        return lambda e: None, lambda e: load(e).wait()
+    return lambda e: start(e + depth), lambda e: load(e).wait()
+
+
+def slot_of(slots, e):
+    return slots[lax.rem(e, slots.shape[0])]
 
 
 def half(me, other, size):
@@ -138,9 +146,9 @@
             wait(e)
         for e in (turn * 2, turn * 2 + 1):
             part_ref[0, e] = nt(rows_ref[e], gate_ref[e, :, here])
-            part_ref[1, e] = nt(rows_ref[e], up_ref[lax.rem(e, RING)])
+            part_ref[1, e] = nt(rows_ref[e], slot_of(up_ref, e))
         for e in (turn * 2, turn * 2 + 1):
-            start(e + RING)
+            start(e)
         return 0
 
     lax.fori_loop(0, experts // 2, some, 0)
@@ -167,7 +175,7 @@
         x = there_ref[e]
         rows_ref[e, :, there] = x
         hidden_gate = part_ref[0, e] + nt(x, gate_ref[e, :, there])
-        hidden_up = part_ref[1, e] + nt(x, up_ref[lax.rem(e, RING)])
+        hidden_up = part_ref[1, e] + nt(x, slot_of(up_ref, e))
         sigma = jax.nn.sigmoid(hidden_gate)
         silu = hidden_gate * sigma
         activ = (silu * hidden_up).astype(BF16)
@@ -177,7 +185,7 @@
         a_ref[e] = (activ.astype(F32) * slot_gate[e][:, 0:1]).astype(BF16)
 
     def project(e):
-        out = nn(a_ref[e], down_ref[lax.rem(e, RING)]).astype(BF16)
+        out = nn(a_ref[e], slot_of(down_ref, e)).astype(BF16)
         at = pl.ds(pl.multiple_of(e * CAP, CAP), CAP)
         for s in range(sources):
             out_rows[s, at, :] = out[s * CAP:(s + 1) * CAP]
@@ -185,7 +193,7 @@
     def first(e):
         wait_up(e)
         activate(e)
-        start_up(e + RING)
+        start_up(e)
 
     def both(e):
         for i in (e - 2, e - 1):
@@ -197,9 +205,9 @@
         activate(e)
         activate(e + 1)
         for i in (e - 2, e - 1):
-            start_down(i + RING)
+            start_down(i)
         for i in (e, e + 1):
-            start_up(i + RING)
+            start_up(i)
 
     skewed(experts, first, wait_down, project, both)
 
@@ -267,7 +275,7 @@
             rows_ref[:, s * CAP:(s + 1) * CAP, columns(me, q, width)] = picked
 
     def slopes(e):
-        grad = nt(rows_ref[e], down_ref[lax.rem(e, RING)])
+        grad = nt(rows_ref[e], slot_of(down_ref, e))
         activ = act_ref[e].astype(F32)
         dots[e] = jnp.broadcast_to(jnp.sum(activ * grad, axis=1, keepdims=True), dots.shape[1:])
         grad = grad * slot_gate[e][:, 0:1]
@@ -275,7 +283,7 @@
         q_ref[e] = (grad * silu_ref[e]).astype(BF16)
 
     def project(e):
-        back = nn(p_ref[e], gate_ref[e]) + nn(q_ref[e], up_ref[lax.rem(e, RING)])
+        back = nn(p_ref[e], gate_ref[e]) + nn(q_ref[e], slot_of(up_ref, e))
         back = (back * slot_gate[e][:, 0:1]).astype(BF16)
         at = pl.ds(pl.multiple_of(e * CAP, CAP), CAP)
         for s in range(sources):
@@ -284,7 +292,7 @@
     def first(e):
         wait_down(e)
         slopes(e)
-        start_down(e + RING)
+        start_down(e)
 
     def both(e):
         for i in (e, e + 1):
@@ -296,9 +304,9 @@
         slopes(e)
         slopes(e + 1)
         for i in (e, e + 1):
-            start_down(i + RING)
+            start_down(i)
         for i in (e - 2, e - 1):
-            start_up(i + RING)
+            start_up(i)
 
     skewed(experts, first, wait_up, project, both)
 
@@ -310,65 +318,62 @@
         near[s] = (keep[0, s].astype(F32) + came[0, s].astype(F32)).astype(BF16)
 
 
-def chips_kernel(near, came, *refs):
-    parts = refs[-near.shape[0]:]
-    for s in range(near.shape[0]):
-        parts[s][...] = (near[s].astype(F32) + came[s].astype(F32)).astype(BF16)
-
-
-def pairs_kernel(near, came, *refs):
-    lower, upper = refs[-2:]
-    count = lower.shape[0]
-    for s in range(count):
-        lower[s] = (near[s].astype(F32) + came[s].astype(F32)).astype(BF16)
-        upper[s] = (near[count + s].astype(F32) + came[count + s].astype(F32)).astype(BF16)
-
-
-def step_kernel(lower, came, *refs):
-    own, other = refs[-2:]
-    own[...] = (lower[0].astype(F32) + came[0].astype(F32)).astype(BF16)
-    other[...] = (lower[1].astype(F32) + came[1].astype(F32)).astype(BF16)
+def chips_kernel(out_near, out_came, back_near, back_came, *refs):
+    sources, tokens = out_near.shape[:2]
+    parts = refs[-sources:]
+    for s in range(sources):
+        parts[s][0:tokens, :] = (out_near[s].astype(F32) + out_came[s].astype(F32)).astype(BF16)
+        parts[s][tokens:, :] = (back_near[s].astype(F32) + back_came[s].astype(F32)).astype(BF16)
 
 
 def total_kernel(count, *refs):
+    out_ref, back_ref, value_ref = refs[count:]
+    tokens = out_ref.shape[0]
     total = refs[0][...].astype(F32)
     for ref in refs[1:count]:
         total = total + ref[...].astype(F32)
-    rows = refs[count]
-    tokens = rows.shape[0]
-    rows[...] = total[0:tokens].astype(BF16)
-    for values in refs[count + 1:]:
-        values[...] = total[tokens:tokens + values.shape[0], 0:values.shape[1]]
-
-
+    out_ref[...] = total[0:tokens].astype(BF16)
+    back_ref[...] = total[tokens:2 * tokens].astype(BF16)
+    value_ref[...] = total[2 * tokens:2 * tokens + value_ref.shape[0], 0:value_ref.shape[1]]
+
+
+BANKS = 8
 TURN = 4
 
 
-def product_kernel(left_ref, right_ref, *refs):
-    out_ref, held, sems = refs[-3:]
-    turns = out_ref.shape[0] // TURN
-
-    def store(turn, i):
-        bank = lax.rem(turn, 2)
-        return pltpu.make_async_copy(held.at[bank, i], out_ref.at[turn * TURN + i], sems.at[bank, i])
-
-    def one(turn, _):
-        @pl.when(turn >= 2)
-        def _():
-            for i in range(TURN):
-                store(turn - 2, i).wait()
-
-        bank = lax.rem(turn, 2)
-        for i in range(TURN):
-            held[bank, i] = tn(left_ref[turn * TURN + i], right_ref[turn * TURN + i]).astype(BF16)
-        for i in range(TURN):
-            store(turn, i).start()
-        return 0
-
-    lax.fori_loop(0, turns, one, 0)
-    for turn in (turns - 2, turns - 1):
-        for i in range(TURN):
-            store(jnp.int32(turn), i).wait()
+def product_kernel(jobs, *refs):
+    lefts, rights, outs = (refs[i * len(jobs):(i + 1) * len(jobs)] for i in range(3))
+    held, sems = refs[-2:]
+    outs = refs[-2 - len(jobs):-2]
+
+    def store(job, e, slot):
+        return pltpu.make_async_copy(held.at[slot], outs[job].at[e], sems.at[slot])
+
+    def turn(job, first, done, i, full):
+        for pair in range(0, TURN, 2):
+            places = [(first + i * TURN + j, lax.rem(done + i * TURN + j, BANKS)) for j in (pair, pair + 1)]
+            if full:
+                for e, slot in places:
+                    store(job, e, slot).wait()
+            for e, slot in places:
+                held[slot] = tn(lefts[job][e], rights[job][e]).astype(BF16)
+            for e, slot in places:
+                store(job, e, slot).start()
+
+    done = 0
+    for job, (first, last) in enumerate(jobs):
+        fresh = max(0, min(BANKS - done, last - first) // TURN)
+        for i in range(fresh):
+            turn(job, first, done, jnp.int32(i), False)
+
+        def later(i, _, job=job, first=first, done=done):
+            turn(job, first, done, i, True)
+            return 0
+
+        lax.fori_loop(fresh, (last - first) // TURN, later, 0)
+        done = done + last - first
+    for slot in range(min(done, BANKS)):
+        store(0, jobs[0][0], slot).wait()
 
 
 def load_kernel(source, target, token, sems):
@@ -407,7 +412,7 @@
     )(*arrays, *there)[0]
 
 
-def kernel_call(kernel, out_shape, scratch, flops, out_specs=None, limit=4, in_hbm=()):
+def kernel_call(kernel, out_shape, scratch, flops, out_specs=None, limit=4, in_hbm=(), aliases={}):
     def call(*operands):
         specs = [
             pl.BlockSpec(memory_space=pltpu.HBM if i in in_hbm else pltpu.SMEM if x.ndim == 1 else pltpu.VMEM)
@@ -422,6 +427,7 @@
             out_specs=out_specs or [pl.BlockSpec(memory_space=pltpu.VMEM)] * len(out_shape),
             out_shape=out_shape,
             scratch_shapes=scratch,
+            input_output_aliases=aliases,
             compiler_params=pltpu.CompilerParams(vmem_limit_bytes=limit * 1024 * 1024),
             cost_estimate=pl.CostEstimate(flops=flops, bytes_accessed=flops // 32, transcendentals=0),
         )(*operands)
@@ -429,17 +435,24 @@
     return call
 
 
-def weight_grad(left, right, *earlier):
-    experts, rows, units = left.shape
-    model = right.shape[2]
+def weight_grads(jobs, begun=None, *earlier):
+    count = len(jobs)
+    lefts, rights = [job[0] for job in jobs], [job[1] for job in jobs]
+    experts, rows, units = lefts[0].shape
+    model = rights[0].shape[2]
+    shape = jax.ShapeDtypeStruct((experts, units, model), BF16)
+    work = sum(job[3] - job[2] for job in jobs)
+    more = [] if begun is None else [begun]
     return kernel_call(
-        product_kernel,
-        jax.ShapeDtypeStruct((experts, units, model), BF16),
-        [pltpu.VMEM((2, TURN, units, model), BF16), pltpu.SemaphoreType.DMA((2, TURN))],
-        2 * experts * rows * units * model,
-        out_specs=pl.BlockSpec(memory_space=pltpu.HBM),
+        functools.partial(product_kernel, [job[2:] for job in jobs]),
+        [shape] * count,
+        [pltpu.VMEM((BANKS, units, model), BF16), pltpu.SemaphoreType.DMA((BANKS,))],
+        2 * work * rows * units * model,
+        out_specs=[pl.BlockSpec(memory_space=pltpu.HBM)] * count,
         limit=8,
-    )(left, right, *earlier)
+        in_hbm=(2 * count,) if more else (),
+        aliases={2 * count: 0} if more else {},
+    )(*lefts, *rights, *more, *earlier)
 
 
 def swap(array, bit, axis="etp"):
@@ -451,14 +464,6 @@
     shape = jax.ShapeDtypeStruct(keep.shape[1:], BF16)
     hbm = [2] if earlier else []
     return kernel_call(add_kernel, [shape, shape], [], 0, limit=2, in_hbm=hbm)(keep, came, *earlier)
-
-
-def add_chips(near, far, *earlier):
-    sources = near.shape[0]
-    shape = jax.ShapeDtypeStruct(near.shape[1:], BF16)
-    hbm = range(2, 2 + len(earlier))
-    parts = kernel_call(chips_kernel, [shape] * sources, [], 0, limit=2, in_hbm=hbm)(near, far, *earlier)
-    return parts[0], [swap(parts[s], s, "expert") for s in range(1, sources)]
 
 
 def gathered_body(
@@ -500,8 +505,9 @@
             held(sources, slots, tokens),
             held(local_experts, rows, tokens, kind=F32),
         ],
-        [pltpu.VMEM((RING, units, model // 2), BF16), pltpu.SemaphoreType.DMA((RING,))],
+        [pltpu.VMEM((local_experts, units, model // 2), BF16), pltpu.SemaphoreType.DMA((local_experts,))],
         product,
+        limit=8,
         in_hbm=(6,),
     )(capacity_blocks, own, swap(own, 1), came, swap(came, 1), gate_t, up_t)
     came_across = join([came_across_there], onehot)[0]
@@ -517,13 +523,13 @@
         ],
         [
             pltpu.VMEM((local_experts, rows, model // 2), BF16),
-            pltpu.VMEM((RING, units, model // 2), BF16),
+            pltpu.VMEM((local_experts, units, model // 2), BF16),
             pltpu.VMEM((RING, units, model), BF16),
-            pltpu.SemaphoreType.DMA((RING,)),
+            pltpu.SemaphoreType.DMA((local_experts,)),
             pltpu.SemaphoreType.DMA((RING,)),
         ],
         2 * product,
-        limit=9,
+        limit=14,
         in_hbm=(5, 6),
     )(
         own_across, swap(own_across, 1), came_across, swap(came_across, 1),
@@ -550,40 +556,39 @@
         ],
         [pltpu.VMEM((RING, units, model), BF16)] * 2 + [pltpu.SemaphoreType.DMA((RING,))] * 2,
         3 * product,
-        limit=9,
+        limit=14,
         in_hbm=(6, 7),
     )(
         *grads, near,
         gate_t, up_t, down_weight, activ, slope, silu, onehot, slot_gate, out_near,
     )
 
-    part = sent(tokens, width)
-    pair = sent(2, tokens, width)
-    out_lower, out_upper = kernel_call(pairs_kernel, [pair, pair], [], 0, limit=2)(out_near, swap(out_far, 2))
+    out_came = swap(out_far, 2)
     keep, send = kernel_call(
         functools.partial(home_values_kernel, choose),
         [sent(2, sources, tokens + EXTRA, width)] * 2,
         [],
         2 * slots * sources * tokens * model,
         limit=2,
-    )(onehot, back_rows, dots, own, came, out_lower)
-    out_came = swap(out_upper, 2, "expert")
-    down_grad = weight_grad(scaled, y_rows, out_lower)
-    back_near, back_far = add_cores(keep, swap(send, 1), down_grad, out_came)
-    out_own, out_other = kernel_call(step_kernel, [part, part], [], 0, limit=2)(out_lower, out_came, back_near)
-    up_grad = weight_grad(up_part, x_rows, back_near, out_own)
-    back_own, back_parts = add_chips(back_near, swap(back_far, 2), up_grad)
-    layer_out = kernel_call(functools.partial(total_kernel, 2), [part], [], 0, limit=2)(
-        out_own, swap(out_other, 1, "expert")
-    )[0]
-    gate_grad = weight_grad(gate_part, x_rows, back_own)
-    input_grad, value_grad = kernel_call(
+    )(onehot, back_rows, dots, own, came, out_came)
+    some = local_experts // 2
+    (down_grad,) = weight_grads([(scaled, y_rows, 0, some)])
+    back_near, back_far = add_cores(keep, swap(send, 1), down_grad)
+    (up_grad,) = weight_grads([(up_part, x_rows, 0, local_experts)], None, back_near)
+    height = 2 * tokens + EXTRA
+    parts = kernel_call(chips_kernel, [sent(height, width)] * sources, [], 0, limit=2, in_hbm=(4,))(
+        out_near, out_came, back_near, swap(back_far, 2), up_grad
+    )
+    down_grad, gate_grad = weight_grads(
+        [(scaled, y_rows, some, local_experts), (gate_part, x_rows, 0, local_experts)], down_grad, parts[0]
+    )
+    layer_out, input_grad, value_grad = kernel_call(
         functools.partial(total_kernel, sources),
-        [part, jax.ShapeDtypeStruct((choose, tokens), F32)],
+        [sent(tokens, width), sent(tokens, width), jax.ShapeDtypeStruct((choose, tokens), F32)],
         [],
         0,
         limit=2,
-    )(back_own, *back_parts)
+    )(parts[0], *[swap(parts[s], s, "expert") for s in range(1, sources)])
     return (
         layer_out,
         input_grad,

time: 89.5 us -> 83.6 us (0.934)
  Pallas kernels: 58 us -> 51.5 us
  waiting for transfers between devices: 6.14 us -> 9.67 us
  starting transfers between devices: 23.9 us -> 21.4 us
    pallas_call x19 -> x16, Pallas kernels: 53.6 us -> 47.1 us  [call(): pl.pallas_call(kernel, in_specs=specs, out_specs=out_specs or [pl.BlockSp...]
    ppermute x22 -> x20, waiting for transfers between devices: 6.14 us -> 9.67 us  [swap(): return lax.ppermute(array, axis, [(i, i ^ bit) for i in range(count)])]
    ppermute x22 -> x20, starting transfers between devices: 23.9 us -> 21.4 us  [swap(): return lax.ppermute(array, axis, [(i, i ^ bit) for i in range(count)])]
  transfers between devices with their start and end apart: 22 -> 20, of which waited for: 5 -> 6; matrix products, arithmetic and copies ran while one was open for 0% -> 0% of each run, Pallas kernels for 62% -> 58%
where the time goes in v6:
time: 83.6 us; the launch traced here: 83.4 us
  Pallas kernels  51.5 us (62%)
  starting transfers between devices  21.4 us (26%)
  waiting for transfers between devices  9.67 us (12%)
  between operations  0.85 us (1%)
    pallas_call x16, Pallas kernels, call(): pl.pallas_call(kernel, in_specs=specs, out_specs=out_specs or [pl.BlockSp...  47.1 us
    ppermute x20, starting transfers between devices, swap(): return lax.ppermute(array, axis, [(i, i ^ bit) for i in range(count)])  21.4 us
    ppermute x20, waiting for transfers between devices, swap(): return lax.ppermute(array, axis, [(i, i ^ bit) for i in range(count)])  9.67 us
    pallas_call x1, Pallas kernels, in_vmem(): pl.pallas_call(load_kernel, in_specs=[pl.BlockSpec(memory_space=pltpu.HBM...  4.42 us
  transfers between devices with their start and end apart: 20, of which 6 were waited for; matrix products, arithmetic and copies ran while one was open for 0% of the time, Pallas kernels for 58%

profile of v6, /device:TPU:0, one launch (start us, length us, event | category | flops | bytes accessed | tf_op | source)
XLA Modules:
  0.0 83.4 jit_solution(8152779955371307101)
XLA Ops:
  0.6 0.9 %shard_map.127.o0.own_ref = bf16[144,256]{1,0:T(8,128)(2,1)S(1)} custom-call(bf16[128,256]{1,0:T(8,128)(2,1)} %hidden_hbm.1, s32[6,128]{1,0:T(8,128)} %bitcast.15, f32[6,128]{1,0:T(8,128)} %bitcast.16), custom_call_target="tpu_custom_call" | custom-call | tf_op jit(solution)/shard_map/pallas_call | solution.py:424
  1.5 3.0 %collective-permute-start.4 = (bf16[144,256]{1,0:T(8,128)(2,1)S(1)}, bf16[144,256]{1,0:T(8,128)(2,1)S(1)}, u32[]{:S(2)}, u32[]{:S(2)}) collective-permute-start(bf16[144,256]{1,0:T(8,128)(2,1)S(1)} %shard_map.127.o0.own_ref), channel_id=1, source_target_pairs={{0,2},{1,3},{2,0},{3,1},{4,6},{5,7},{6,4},{7,5},{8,10},{9,11},{10,... | collective-permute-start | bytes 221192 | tf_op jit(solution)/shard_map/ppermute | solution.py:460
  4.5 3.6 %collective-permute-start.3 = (bf16[144,256]{1,0:T(8,128)(2,1)S(1)}, bf16[144,256]{1,0:T(8,128)(2,1)S(1)}, u32[]{:S(2)}, u32[]{:S(2)}) collective-permute-start(bf16[144,256]{1,0:T(8,128)(2,1)S(1)} %shard_map.127.o0.own_ref), channel_id=1, source_target_pairs={{0,12},{4,8},{8,4},{12,0},{1,13},{5,9},{9,5},{13,1},{2,14},{6,10},... | collective-permute-start | bytes 221192 | tf_op jit(solution)/shard_map/ppermute | solution.py:460
  8.1 0.8 collective-permute-start.1
  9.2 4.4 %shard_map.128 = (bf16[16,352,1024]{2,1,0:T(8,128)(2,1)S(1)}, f32[8,128]{1,0:T(8,128)S(1)}) custom-call(bf16[16,352,1024]{2,1,0:T(8,128)(2,1)} %bitcast.14), custom_call_target="tpu_custom_call" | custom-call | bytes 11534336 | tf_op jit(solution)/shard_map/pallas_call | solution.py:389
  14.2 1.4 %collective-permute-start.8 = (bf16[3,144,256]{2,1,0:T(8,128)(2,1)S(1)}, bf16[3,144,256]{2,1,0:T(8,128)(2,1)S(1)}, u32[]{:S(2)}, u32[]{:S(2)}) collective-permute-start(bf16[3,144,256]{2,1,0:T(8,128)(2,1)S(1)} %shard_map.129.b0.refs_2_.info_ref), channel_id=1, source_target_pairs={{0,2},{1,3},{2,0},{3,1},{4,6},{5,7},{6,4},{7,5},{8,10},{9,11},{10,... | collective-permute-start | bytes 663560 | tf_op jit(solution)/shard_map/ppermute | solution.py:460
  15.8 1.1 %collective-permute-done.o1 = bf16[144,256]{1,0:T(8,128)(2,1)S(1)} collective-permute-done((bf16[144,256]{1,0:T(8,128)(2,1)S(1)}, bf16[144,256]{1,0:T(8,128)(2,1)S(1)}, u32[]{:S(2)}, u32[]{:S(2)}) %collective-permute-start) | collective-permute-done | bytes 73760 | tf_op jit(solution)/shard_map/ppermute | solution.py:460
  16.9 6.9 %shard_map.130 = (bf16[16,64,512]{2,1,0:T(8,128)(2,1)S(1)}, f32[2,16,64,352]{3,2,1,0:T(8,128)S(1)}, bf16[4,256,128]{2,1,0:T(8,128)(2,1)S(1)}, f32[16,64,128]{2,1,0:T(8,128)S(1)}) custom-call(s32[64]{0:T(128)S(1)} %copy-done.1, bf16[144,256]{1,0:T(8,128)(2,1)S(1)} %shard_map.127.o0.own_ref, bf16[144,256]{1,0:T(8,128)(2,1)S(1)} %collective-permute-done.o1, ...), custom_call_target="tpu_custom_call" | custom-call | flops 738197504 | bytes 23068672 | tf_op jit(solution)/shard_map/pallas_call | solution.py:424
  24.4 3.7 %collective-permute-start.12 = (bf16[2,128,256]{2,1,0:T(8,128)(2,1)S(1)}, bf16[2,128,256]{2,1,0:T(8,128)(2,1)S(1)}, u32[]{:S(2)}, u32[]{:S(2)}) collective-permute-start(bf16[2,128,256]{2,1,0:T(8,128)(2,1)S(1)} %shard_map.132.later_ref.refs_0_.a0), channel_id=1, source_target_pairs={{0,12},{4,8},{8,4},{12,0},{1,13},{5,9},{9,5},{13,1},{2,14},{6,10},... | collective-permute-start | bytes 393224 | tf_op jit(solution)/shard_map/ppermute | solution.py:460
  28.1 0.8 collective-permute-start.10
  28.9 9.3 %shard_map.133 = (bf16[4,256,1024]{2,1,0:T(8,128)(2,1)S(1)}, bf16[16,64,1024]{2,1,0:T(8,128)(2,1)S(1)}, bf16[16,64,352]{2,1,0:T(8,128)(2,1)S(1)}, bf16[16,64,352...) custom-call(bf16[144,256]{1,0:T(8,128)(2,1)S(1)} %collective-permute-done.4.refs_4_.o2, ...), custom_call_target="tpu_custom_call" | custom-call | flops 1476395008 | bytes 46137344 | tf_op jit(solution)/shard_map/pallas_call | solution.py:424
  38.2 0.9 %collective-permute-done.11.refs_2_.a2 = bf16[2,128,256]{2,1,0:T(8,128)(2,1)S(1)} collective-permute-done((bf16[2,128,256]{2,1,0:T(8,128)(2,1)S(1)}, bf16[2,128,256]{2,1,0:T(8,128)(2,1)S(1)}, u32[]{:S(2)}, u32[]{:S(2)}) %collective-permute-start.11) | collective-permute-done | bytes 131104 | tf_op jit(solution)/shard_map/ppermute | solution.py:460
  39.7 2.6 %collective-permute-done.13.came.near_ref = bf16[4,4,128,256]{3,2,1,0:T(8,128)(2,1)S(1)} collective-permute-done((bf16[4,4,128,256]{3,2,1,0:T(8,128)(2,1)S(1)}, bf16[4,4,128,256]{3,2,1,0:T(8,128)(2,1)S(1)}, u32[]{:S(2)}, u32[]{:S(2)}) %collective-permute-start.13) | collective-permute-done | bytes 1048608 | tf_op jit(solution)/shard_map/ppermute | solution.py:460
  43.1 12.2 %shard_map.136 = (bf16[4,256,1024]{2,1,0:T(8,128)(2,1)S(1)}, f32[16,64,128]{2,1,0:T(8,128)S(1)}, bf16[16,64,1024]{2,1,0:T(8,128)(2,1)S(1)}, bf16[16,64,352]{2,1,0:T(8,128)(2,1)S(1)}, bf16[16,64,352]{2,1,0:T(8,128)(2,1)S(1)}) custom-call(bf16[2,128,256]{2,1,0:T(8,128)(2,1)S(1)} %shard_map.132.later_ref.refs_0_.a0, ...), custom_call_target="tpu_custom_call" | custom-call | flops 2214592512 | bytes 69206016 | tf_op jit(solution)/shard_map/pallas_call | solution.py:424
  55.3 0.6 shard_map.137
  56.0 3.1 %shard_map.138.refs_0_.refs_4_ = bf16[16,352,1024]{2,1,0:T(8,128)(2,1)} custom-call(bf16[16,64,352]{2,1,0:T(8,128)(2,1)S(1)} %get-tuple-element.58.refs_0_, bf16[16,64,1024]{2,1,0:T(8,128)(2,1)S(1)} %get-tuple-element.59.refs_1_.refs_2_), custom_call_target="tpu_custom_call" | custom-call | flops 369098752 | bytes 11534336 | tf_op jit(solution)/shard_map/pallas_call | solution.py:424
  59.3 1.8 %collective-permute-start.16 = (bf16[4,144,256]{2,1,0:T(8,128)(2,1)S(1)}, bf16[4,144,256]{2,1,0:T(8,128)(2,1)S(1)}, u32[]{:S(2)}, u32[]{:S(2)}) collective-permute-start(bf16[4,144,256]{2,1,0:T(8,128)(2,1)S(1)} %get-tuple-element.61), channel_id=1, source_target_pairs={{0,2},{1,3},{2,0},{3,1},{4,6},{5,7},{6,4},{7,5},{8,10},{9,11},{10,... | collective-permute-start | bytes 884744 | tf_op jit(solution)/shard_map/ppermute | solution.py:460
  61.1 5.1 %shard_map.140.refs_0_ = bf16[16,352,1024]{2,1,0:T(8,128)(2,1)} custom-call(bf16[16,64,352]{2,1,0:T(8,128)(2,1)S(1)} %get-tuple-element.62.refs_0_, bf16[16,64,1024]{2,1,0:T(8,128)(2,1)S(1)} %get-tuple-element.63.refs_1_.refs_3_, bf16[4,144,256]{2,1,0:T(8,128)(2,1)S(1)} %get-tuple-element.60.refs_2_.back_near), custom_call_target="tpu_custom_call" | custom-call | flops 738197504 | bytes 23068672 | tf_op jit(solution)/shard_map/pallas_call | solution.py:424
  66.2 2.6 %collective-permute-done.16.back_came = bf16[4,144,256]{2,1,0:T(8,128)(2,1)S(1)} collective-permute-done((bf16[4,144,256]{2,1,0:T(8,128)(2,1)S(1)}, bf16[4,144,256]{2,1,0:T(8,128)(2,1)S(1)}, u32[]{:S(2)}, u32[]{:S(2)}) %collective-permute-start.16) | collective-permute-done | bytes 294944 | tf_op jit(solution)/shard_map/ppermute | solution.py:460
  69.2 2.9 %collective-permute-start.18 = (bf16[272,256]{1,0:T(8,128)(2,1)S(1)}, bf16[272,256]{1,0:T(8,128)(2,1)S(1)}, u32[]{:S(2)}, u32[]{:S(2)}) collective-permute-start(bf16[272,256]{1,0:T(8,128)(2,1)S(1)} %get-tuple-element.66), channel_id=1, source_target_pairs={{0,8},{4,12},{8,0},{12,4},{1,9},{5,13},{9,1},{13,5},{2,10},{6,14},... | collective-permute-start | bytes 417800 | tf_op jit(solution)/shard_map/ppermute | solution.py:460
  72.2 1.2 %collective-permute-start.19 = (bf16[272,256]{1,0:T(8,128)(2,1)S(1)}, bf16[272,256]{1,0:T(8,128)(2,1)S(1)}, u32[]{:S(2)}, u32[]{:S(2)}) collective-permute-start(bf16[272,256]{1,0:T(8,128)(2,1)S(1)} %get-tuple-element.67), channel_id=1, source_target_pairs={{0,12},{4,8},{8,4},{12,0},{1,13},{5,9},{9,5},{13,1},{2,14},{6,10},... | collective-permute-start | bytes 417800 | tf_op jit(solution)/shard_map/ppermute | solution.py:460
  73.4 7.3 %shard_map.143 = (bf16[16,352,1024]{2,1,0:T(8,128)(2,1)}, bf16[16,352,1024]{2,1,0:T(8,128)(2,1)}) custom-call(bf16[16,64,352]{2,1,0:T(8,128)(2,1)S(1)} %get-tuple-element.58.refs_0_, bf16[16,64,352]{2,1,0:T(8,128)(2,1)S(1)} %get-tuple-element.71.refs_1_, ...), custom_call_target="tpu_custom_call", output_to_operand_aliasing={{0}: (4, {})} | custom-call | flops 1107296256 | bytes 34603008 | tf_op jit(solution)/shard_map/pallas_call | solution.py:424
  80.7 2.0 %collective-permute-done.18.refs_2_ = bf16[272,256]{1,0:T(8,128)(2,1)S(1)} collective-permute-done((bf16[272,256]{1,0:T(8,128)(2,1)S(1)}, bf16[272,256]{1,0:T(8,128)(2,1)S(1)}, u32[]{:S(2)}, u32[]{:S(2)}) %collective-permute-start.18) | collective-permute-done | bytes 139296 | tf_op jit(solution)/shard_map/ppermute | solution.py:460
  82.7 0.7 shard_map.142
  (37 shorter events, 3.6 us)
Async XLA Ops:
  0.6 16.2 %copy-start.1 = (s32[64]{0:T(128)S(1)}, s32[64]{0:T(128)}, u32[]{:S(2)}) copy-start(s32[64]{0:T(128)} %capacity_ref.1) | copy-start | bytes 772
  1.5 12.1 %collective-permute-start.4 = (bf16[144,256]{1,0:T(8,128)(2,1)S(1)}, bf16[144,256]{1,0:T(8,128)(2,1)S(1)}, u32[]{:S(2)}, u32[]{:S(2)}) collective-permute-start(bf16[144,256]{1,0:T(8,128)(2,1)S(1)} %shard_map.127.o0.own_ref), channel_id=1, source_target_pairs={{0,2},{1,3},{2,0},{3,1},{4,6},{5,7},{6,4},{7,5},{8,10},{9,11},{10,... | collective-permute-start | bytes 221192 | tf_op jit(solution)/shard_map/ppermute | solution.py:460
  4.5 9.2 %collective-permute-start.3 = (bf16[144,256]{1,0:T(8,128)(2,1)S(1)}, bf16[144,256]{1,0:T(8,128)(2,1)S(1)}, u32[]{:S(2)}, u32[]{:S(2)}) collective-permute-start(bf16[144,256]{1,0:T(8,128)(2,1)S(1)} %shard_map.127.o0.own_ref), channel_id=1, source_target_pairs={{0,12},{4,8},{8,4},{12,0},{1,13},{5,9},{9,5},{13,1},{2,14},{6,10},... | collective-permute-start | bytes 221192 | tf_op jit(solution)/shard_map/ppermute | solution.py:460
  8.1 5.9 %collective-permute-start.2 = (bf16[144,256]{1,0:T(8,128)(2,1)S(1)}, bf16[144,256]{1,0:T(8,128)(2,1)S(1)}, u32[]{:S(2)}, u32[]{:S(2)}) collective-permute-start(bf16[144,256]{1,0:T(8,128)(2,1)S(1)} %shard_map.127.o0.own_ref), channel_id=1, source_target_pairs={{0,8},{4,12},{8,0},{12,4},{1,9},{5,13},{9,1},{13,5},{2,10},{6,14},... | collective-permute-start | bytes 221192 | tf_op jit(solution)/shard_map/ppermute | solution.py:460
  8.1 5.9 %collective-permute-start.1 = (bf16[144,256]{1,0:T(8,128)(2,1)S(1)}, bf16[144,256]{1,0:T(8,128)(2,1)S(1)}, u32[]{:S(2)}, u32[]{:S(2)}) collective-permute-start(bf16[144,256]{1,0:T(8,128)(2,1)S(1)} %shard_map.127.o0.own_ref), channel_id=1, source_target_pairs={{0,4},{4,0},{8,12},{12,8},{1,5},{5,1},{9,13},{13,9},{2,6},{6,2},{1... | collective-permute-start | bytes 221192 | tf_op jit(solution)/shard_map/ppermute | solution.py:460
  8.9 4.7 %collective-permute-start.5 = (bf16[128,256]{1,0:T(8,128)(2,1)}, bf16[128,256]{1,0:T(8,128)(2,1)S(1)}, u32[]{:S(2)}, u32[]{:S(2)}) collective-permute-start(bf16[128,256]{1,0:T(8,128)(2,1)} %refs_0_.1), channel_id=1, source_target_pairs={{0,2},{1,3},{2,0},{3,1},{4,6},{5,7},{6,4},{7,5},{8,10},{9,11},{10,... | collective-permute-start | bytes 196616 | tf_op jit(solution)/shard_map/ppermute | solution.py:460
  14.1 2.8 %collective-permute-start.6 = (bf16[3,144,256]{2,1,0:T(8,128)(2,1)S(1)}, bf16[3,144,256]{2,1,0:T(8,128)(2,1)S(1)}, u32[]{:S(2)}, u32[]{:S(2)}) collective-permute-start(bf16[3,144,256]{2,1,0:T(8,128)(2,1)S(1)} %shard_map.129.b0.refs_2_.info_ref), channel_id=1, source_target_pairs={{0,1},{1,0},{2,3},{3,2},{4,5},{5,4},{6,7},{7,6},{8,9},{9,8},{10,11... | collective-permute-start | bytes 663560 | tf_op jit(solution)/shard_map/ppermute | solution.py:460
  14.2 9.6 %collective-permute-start.8 = (bf16[3,144,256]{2,1,0:T(8,128)(2,1)S(1)}, bf16[3,144,256]{2,1,0:T(8,128)(2,1)S(1)}, u32[]{:S(2)}, u32[]{:S(2)}) collective-permute-start(bf16[3,144,256]{2,1,0:T(8,128)(2,1)S(1)} %shard_map.129.b0.refs_2_.info_ref), channel_id=1, source_target_pairs={{0,2},{1,3},{2,0},{3,1},{4,6},{5,7},{6,4},{7,5},{8,10},{9,11},{10,... | collective-permute-start | bytes 663560 | tf_op jit(solution)/shard_map/ppermute | solution.py:460
  15.6 1.3 %collective-permute-start = (bf16[144,256]{1,0:T(8,128)(2,1)S(1)}, bf16[144,256]{1,0:T(8,128)(2,1)S(1)}, u32[]{:S(2)}, u32[]{:S(2)}) collective-permute-start(bf16[144,256]{1,0:T(8,128)(2,1)S(1)} %shard_map.127.o0.own_ref), channel_id=1, source_target_pairs={{0,1},{1,0},{2,3},{3,2},{4,5},{5,4},{6,7},{7,6},{8,9},{9,8},{10,11... | collective-permute-start | bytes 221192 | tf_op jit(solution)/shard_map/ppermute | solution.py:460
  16.9 7.5 %copy-start = (bf16[128,256]{1,0:T(8,128)(2,1)S(1)}, bf16[128,256]{1,0:T(8,128)(2,1)}, u32[]{:S(2)}) copy-start(bf16[128,256]{1,0:T(8,128)(2,1)} %refs_0_.1) | copy-start | bytes 196612
  23.8 5.1 %collective-permute-start.9 = (bf16[3,144,256]{2,1,0:T(8,128)(2,1)S(1)}, bf16[3,144,256]{2,1,0:T(8,128)(2,1)S(1)}, u32[]{:S(2)}, u32[]{:S(2)}) collective-permute-start(bf16[3,144,256]{2,1,0:T(8,128)(2,1)S(1)} %bitcast.8), channel_id=1, source_target_pairs={{0,1},{1,0},{2,3},{3,2},{4,5},{5,4},{6,7},{7,6},{8,9},{9,8},{10,11... | collective-permute-start | bytes 663560 | tf_op jit(solution)/shard_map/ppermute | solution.py:460
  24.1 4.8 %collective-permute-start.7 = (bf16[144,256]{1,0:T(8,128)(2,1)S(1)}, bf16[144,256]{1,0:T(8,128)(2,1)S(1)}, u32[]{:S(2)}, u32[]{:S(2)}) collective-permute-start(bf16[144,256]{1,0:T(8,128)(2,1)S(1)} %collective-permute-done.4.refs_4_.o2), channel_id=1, source_target_pairs={{0,1},{1,0},{2,3},{3,2},{4,5},{5,4},{6,7},{7,6},{8,9},{9,8},{10,11... | collective-permute-start | bytes 221192 | tf_op jit(solution)/shard_map/ppermute | solution.py:460
  24.4 13.8 %collective-permute-start.12 = (bf16[2,128,256]{2,1,0:T(8,128)(2,1)S(1)}, bf16[2,128,256]{2,1,0:T(8,128)(2,1)S(1)}, u32[]{:S(2)}, u32[]{:S(2)}) collective-permute-start(bf16[2,128,256]{2,1,0:T(8,128)(2,1)S(1)} %shard_map.132.later_ref.refs_0_.a0), channel_id=1, source_target_pairs={{0,12},{4,8},{8,4},{12,0},{1,13},{5,9},{9,5},{13,1},{2,14},{6,10},... | collective-permute-start | bytes 393224 | tf_op jit(solution)/shard_map/ppermute | solution.py:460
  28.1 11.1 %collective-permute-start.11 = (bf16[2,128,256]{2,1,0:T(8,128)(2,1)S(1)}, bf16[2,128,256]{2,1,0:T(8,128)(2,1)S(1)}, u32[]{:S(2)}, u32[]{:S(2)}) collective-permute-start(bf16[2,128,256]{2,1,0:T(8,128)(2,1)S(1)} %shard_map.132.later_ref.refs_0_.a0), channel_id=1, source_target_pairs={{0,8},{4,12},{8,0},{12,4},{1,9},{5,13},{9,1},{13,5},{2,10},{6,14},... | collective-permute-start | bytes 393224 | tf_op jit(solution)/shard_map/ppermute | solution.py:460
  28.1 11.1 %collective-permute-start.10 = (bf16[2,128,256]{2,1,0:T(8,128)(2,1)S(1)}, bf16[2,128,256]{2,1,0:T(8,128)(2,1)S(1)}, u32[]{:S(2)}, u32[]{:S(2)}) collective-permute-start(bf16[2,128,256]{2,1,0:T(8,128)(2,1)S(1)} %shard_map.132.later_ref.refs_0_.a0), channel_id=1, source_target_pairs={{0,4},{4,0},{8,12},{12,8},{1,5},{5,1},{9,13},{13,9},{2,6},{6,2},{1... | collective-permute-start | bytes 393224 | tf_op jit(solution)/shard_map/ppermute | solution.py:460
  39.7 2.7 %collective-permute-start.13 = (bf16[4,4,128,256]{3,2,1,0:T(8,128)(2,1)S(1)}, bf16[4,4,128,256]{3,2,1,0:T(8,128)(2,1)S(1)}, u32[]{:S(2)}, u32[]{:S(2)}) collective-permute-start(bf16[4,4,128,256]{3,2,1,0:T(8,128)(2,1)S(1)} %get-tuple-element.48), channel_id=1, source_target_pairs={{0,1},{1,0},{2,3},{3,2},{4,5},{5,4},{6,7},{7,6},{8,9},{9,8},{10,11... | collective-permute-start | bytes 3145736 | tf_op jit(solution)/shard_map/ppermute | solution.py:460
  42.5 12.8 %collective-permute-start.14 = (bf16[4,128,256]{2,1,0:T(8,128)(2,1)S(1)}, bf16[4,128,256]{2,1,0:T(8,128)(2,1)S(1)}, u32[]{:S(2)}, u32[]{:S(2)}) collective-permute-start(bf16[4,128,256]{2,1,0:T(8,128)(2,1)S(1)} %get-tuple-element.50), channel_id=1, source_target_pairs={{0,2},{1,3},{2,0},{3,1},{4,6},{5,7},{6,4},{7,5},{8,10},{9,11},{10,... | collective-permute-start | bytes 786440 | tf_op jit(solution)/shard_map/ppermute | solution.py:460
  55.9 3.2 %collective-permute-start.15 = (bf16[2,4,144,256]{3,2,1,0:T(8,128)(2,1)S(1)}, bf16[2,4,144,256]{3,2,1,0:T(8,128)(2,1)S(1)}, u32[]{:S(2)}, u32[]{:S(2)}) collective-permute-start(bf16[2,4,144,256]{3,2,1,0:T(8,128)(2,1)S(1)} %get-tuple-element.57), channel_id=1, source_target_pairs={{0,1},{1,0},{2,3},{3,2},{4,5},{5,4},{6,7},{7,6},{8,9},{9,8},{10,11... | collective-permute-start | bytes 1769480 | tf_op jit(solution)/shard_map/ppermute | solution.py:460
  59.3 9.5 %collective-permute-start.16 = (bf16[4,144,256]{2,1,0:T(8,128)(2,1)S(1)}, bf16[4,144,256]{2,1,0:T(8,128)(2,1)S(1)}, u32[]{:S(2)}, u32[]{:S(2)}) collective-permute-start(bf16[4,144,256]{2,1,0:T(8,128)(2,1)S(1)} %get-tuple-element.61), channel_id=1, source_target_pairs={{0,2},{1,3},{2,0},{3,1},{4,6},{5,7},{6,4},{7,5},{8,10},{9,11},{10,... | collective-permute-start | bytes 884744 | tf_op jit(solution)/shard_map/ppermute | solution.py:460
  68.9 11.8 %collective-permute-start.17 = (bf16[272,256]{1,0:T(8,128)(2,1)S(1)}, bf16[272,256]{1,0:T(8,128)(2,1)S(1)}, u32[]{:S(2)}, u32[]{:S(2)}) collective-permute-start(bf16[272,256]{1,0:T(8,128)(2,1)S(1)} %get-tuple-element.65), channel_id=1, source_target_pairs={{0,4},{4,0},{8,12},{12,8},{1,5},{5,1},{9,13},{13,9},{2,6},{6,2},{1... | collective-permute-start | bytes 417800 | tf_op jit(solution)/shard_map/ppermute | solution.py:460
  69.2 13.5 %collective-permute-start.18 = (bf16[272,256]{1,0:T(8,128)(2,1)S(1)}, bf16[272,256]{1,0:T(8,128)(2,1)S(1)}, u32[]{:S(2)}, u32[]{:S(2)}) collective-permute-start(bf16[272,256]{1,0:T(8,128)(2,1)S(1)} %get-tuple-element.66), channel_id=1, source_target_pairs={{0,8},{4,12},{8,0},{12,4},{1,9},{5,13},{9,1},{13,5},{2,10},{6,14},... | collective-permute-start | bytes 417800 | tf_op jit(solution)/shard_map/ppermute | solution.py:460
  72.2 10.5 %collective-permute-start.19 = (bf16[272,256]{1,0:T(8,128)(2,1)S(1)}, bf16[272,256]{1,0:T(8,128)(2,1)S(1)}, u32[]{:S(2)}, u32[]{:S(2)}) collective-permute-start(bf16[272,256]{1,0:T(8,128)(2,1)S(1)} %get-tuple-element.67), channel_id=1, source_target_pairs={{0,12},{4,8},{8,4},{12,0},{1,13},{5,9},{9,5},{13,1},{2,14},{6,10},... | collective-permute-start | bytes 417800 | tf_op jit(solution)/shard_map/ppermute | solution.py:460

commit v7 on v6

--- a/solution.py
+++ b/solution.py
@@ -48,7 +48,7 @@
 
 def routing(info, choose, tokens):
     info = info.astype(F32)
-    return info[0:choose, 0:tokens], info[0:choose, tokens:2 * tokens] + info[8:8 + choose, 0:tokens]
+    return info[0:choose, 0:tokens], info[0:choose, tokens:2 * tokens], info[8:8 + choose, 0:tokens]
 
 
 def columns(me, mask, width):
@@ -93,29 +93,25 @@
     return pl.ds(pl.multiple_of(lax.bitwise_xor(me // 2, other) * size, size), size)
 
 
-def gather_half(me, onehot, blocks, rows_ref, experts, width, tokens, start):
+def gather_half(me, onehot, blocks, rows_ref, experts, width, tokens, start, offset):
     for q, block in enumerate(blocks):
         picked = nn(onehot, block).astype(BF16).reshape(experts, CAP, width)
-        at = pl.multiple_of(lax.rem(lax.bitwise_xor(me, q), 2) * width, width)
+        at = pl.multiple_of(lax.rem(lax.bitwise_xor(me, q), 2) * width + offset, width)
         rows_ref[:, start:start + CAP, pl.ds(at, width)] = picked
 
 
-def early_kernel(
-    choose, capacity_ref, o0, o1, b0, b1, gate_ref, up_hbm,
-    rows_ref, part_ref, onehot, slot_gate,
-    up_ref, sems,
+def routing_kernel(
+    choose, capacity_ref, o0, o1, b0, b1, earlier_ref, rows_ref, onehot, slot_gate
 ):
     sources, slots, tokens = onehot.shape
     experts = slots // CAP
     width = b0.shape[2]
     me = lax.axis_index("etp")
     first = lax.axis_index("expert") * experts
-
-    here = half(me, 0, 2 * width)
-    start, wait = ring(up_hbm, up_ref, sems, here)
     row = lax.broadcasted_iota(jnp.int32, (tokens, tokens), 0)
     col = lax.broadcasted_iota(jnp.int32, (tokens, tokens), 1)
     before = jnp.where(row < col, 1.0, 0.0).astype(BF16)
+    ones = jnp.ones((tokens, tokens), BF16)
     expert = lax.broadcasted_iota(jnp.int32, (experts, tokens), 0)
     mine = (first + expert).astype(F32)
     limit = jnp.zeros((experts, tokens), jnp.int32)
@@ -125,57 +121,46 @@
     place = lax.broadcasted_iota(jnp.int32, (experts, CAP, tokens), 1).astype(F32)
     for s in range(sources):
         block = [o[...] for o in (o0, o1)] if s == 0 else [b[s - 1] for b in (b0, b1)]
-        ids, gates = routing(block[0][tokens:tokens + EXTRA, :], choose, tokens)
+        ids, highs, lows = routing(block[0][tokens:tokens + EXTRA, :], choose, tokens)
         named = jnp.zeros((experts, tokens), F32)
-        gate = jnp.zeros((experts, tokens), F32)
+        high, low = named, named
         for k in range(choose):
             hit = ids[k:k + 1, :] == mine
             named = named + jnp.where(hit, 1.0, 0.0)
-            gate = gate + jnp.where(hit, gates[k:k + 1, :], 0.0)
+            high = high + jnp.where(hit, highs[k:k + 1, :], 0.0)
+            low = low + jnp.where(hit, lows[k:k + 1, :], 0.0)
         rank = nn(named.astype(BF16), before)
         rank = jnp.where((named > 0.5) & (rank < limit), rank, -1.0)
-        chosen = jnp.where(rank[:, None, :] == place, 1.0, 0.0)
-        gate_of = jnp.sum(chosen * gate[:, None, :], axis=2, keepdims=True)
-        slot_gate[:, s * CAP:(s + 1) * CAP, :] = jnp.broadcast_to(gate_of, chosen.shape)
-        table = chosen.reshape(slots, tokens).astype(BF16)
+        taken = rank[:, None, :] == place
+        spread = lambda x: jnp.where(taken, x[:, None, :], 0.0).reshape(slots, tokens).astype(BF16)
+        gates = nn(spread(high), ones) + nn(spread(low), ones)
+        slot_gate[:, s * CAP:(s + 1) * CAP, :] = gates.reshape(experts, CAP, tokens)
+        table = jnp.where(taken, 1.0, 0.0).reshape(slots, tokens).astype(BF16)
         onehot[s] = table
-        gather_half(me, table, [x[0:tokens, :] for x in block], rows_ref, experts, width, tokens, s * CAP)
-
-    def some(turn, _):
-        for e in (turn * 2, turn * 2 + 1):
-            wait(e)
-        for e in (turn * 2, turn * 2 + 1):
-            part_ref[0, e] = nt(rows_ref[e], gate_ref[e, :, here])
-            part_ref[1, e] = nt(rows_ref[e], slot_of(up_ref, e))
-        for e in (turn * 2, turn * 2 + 1):
-            start(e)
-        return 0
-
-    lax.fori_loop(0, experts // 2, some, 0)
+        gather_half(me, table, [x[0:tokens, :] for x in block], rows_ref, experts, width, tokens, s * CAP, 0)
 
 
 def forward_kernel(
-    o2, o3, b2, b3, gate_ref, up_hbm, down_hbm, half_ref, part_ref, onehot, slot_gate, later_ref,
+    o2, o3, b2, b3, gate_ref, up_hbm, down_hbm, half_ref, onehot, slot_gate, later_ref,
     out_rows, rows_ref, act_ref, a_ref, slope_ref, silu_ref,
-    there_ref, up_ref, down_ref, up_sems, down_sems,
+    up_ref, down_ref, up_sems, down_sems,
 ):
     sources, slots, tokens = onehot.shape
     experts = slots // CAP
     width = b2.shape[2]
     me = lax.axis_index("etp")
-    here, there = half(me, 0, 2 * width), half(me, 1, 2 * width)
-    start_up, wait_up = ring(up_hbm, up_ref, up_sems, there)
+    start_up, wait_up = ring(up_hbm, up_ref, up_sems)
     start_down, wait_down = ring(down_hbm, down_ref, down_sems)
+    rows_ref[:, :, half(me, 0, 2 * width)] = half_ref[...]
+    other = lax.bitwise_xor(me // 2, 1) * 2 * width
     for s in range(sources):
         block = [o[0:tokens, :] for o in (o2, o3)] if s == 0 else [b[s - 1, 0:tokens, :] for b in (b2, b3)]
-        gather_half(me, onehot[s], block, there_ref, experts, width, tokens, s * CAP)
+        gather_half(me, onehot[s], block, rows_ref, experts, width, tokens, s * CAP, other)
 
     def activate(e):
-        rows_ref[e, :, here] = half_ref[e]
-        x = there_ref[e]
-        rows_ref[e, :, there] = x
-        hidden_gate = part_ref[0, e] + nt(x, gate_ref[e, :, there])
-        hidden_up = part_ref[1, e] + nt(x, slot_of(up_ref, e))
+        x = rows_ref[e]
+        hidden_gate = nt(x, gate_ref[e])
+        hidden_up = nt(x, slot_of(up_ref, e))
         sigma = jax.nn.sigmoid(hidden_gate)
         silu = hidden_gate * sigma
         activ = (silu * hidden_up).astype(BF16)
@@ -245,7 +230,7 @@
     mine = (lax.axis_index("expert") * experts + expert).astype(F32)
     for s in range(sources):
         info = own_ref[tokens:tokens + EXTRA, :] if s == 0 else info_ref[s - 1, tokens:tokens + EXTRA, :]
-        ids, _ = routing(info, choose, tokens)
+        ids, _, _ = routing(info, choose, tokens)
         chosen = onehot[s].astype(F32).reshape(experts, CAP, tokens)
         share = jnp.sum(chosen * dots[:, s * CAP:(s + 1) * CAP, :], axis=1)
         values = [jnp.sum(jnp.where(ids[k:k + 1, :] == mine, share, 0.0), axis=0, keepdims=True) for k in range(choose)]
@@ -258,9 +243,9 @@
 
 def backward_kernel(
     a0, a1, a2, a3, near_ref,
-    gate_ref, up_hbm, down_hbm, act_ref, slope_ref, silu_ref, onehot, slot_gate, earlier_ref,
-    back_rows, dots, rows_ref, p_ref, q_ref,
-    up_ref, down_ref, up_sems, down_sems,
+    gate_ref, up_hbm, down_hbm, act_ref, a_ref, slope_ref, silu_ref, onehot, slot_gate, earlier_ref,
+    back_rows, dots, rows_ref, p_ref, q_ref, down_grad,
+    up_ref, down_ref, held, up_sems, down_sems, held_sems,
 ):
     sources, slots, tokens = onehot.shape
     experts = slots // CAP
@@ -282,7 +267,12 @@
         p_ref[e] = (grad * slope_ref[e]).astype(BF16)
         q_ref[e] = (grad * silu_ref[e]).astype(BF16)
 
+    def store(e):
+        slot = lax.rem(e, BANKS)
+        return pltpu.make_async_copy(held.at[slot], down_grad.at[e], held_sems.at[slot])
+
     def project(e):
+        held[lax.rem(e, BANKS)] = tn(a_ref[e], rows_ref[e]).astype(BF16)
         back = nn(p_ref[e], gate_ref[e]) + nn(q_ref[e], slot_of(up_ref, e))
         back = (back * slot_gate[e][:, 0:1]).astype(BF16)
         at = pl.ds(pl.multiple_of(e * CAP, CAP), CAP)
@@ -299,16 +289,32 @@
             wait_down(i)
         for i in (e - 2, e - 1):
             wait_up(i)
+
+        @pl.when(e - 2 >= BANKS)
+        def _():
+            for i in (e - 2, e - 1):
+                store(i - BANKS).wait()
+
         project(e - 2)
         project(e - 1)
         slopes(e)
         slopes(e + 1)
+        for i in (e - 2, e - 1):
+            store(i).start()
         for i in (e, e + 1):
             start_down(i)
         for i in (e - 2, e - 1):
             start_up(i)
 
-    skewed(experts, first, wait_up, project, both)
+    def last(e):
+        wait_up(e)
+        store(e - BANKS).wait()
+
+    skewed(experts, first, last, project, both)
+    for e in (experts - 2, experts - 1):
+        store(jnp.int32(e)).start()
+    for e in range(experts - BANKS, experts):
+        store(jnp.int32(e)).wait()
 
 
 def add_kernel(keep, came, *refs):
@@ -318,23 +324,21 @@
         near[s] = (keep[0, s].astype(F32) + came[0, s].astype(F32)).astype(BF16)
 
 
-def chips_kernel(out_near, out_came, back_near, back_came, *refs):
-    sources, tokens = out_near.shape[:2]
-    parts = refs[-sources:]
-    for s in range(sources):
-        parts[s][0:tokens, :] = (out_near[s].astype(F32) + out_came[s].astype(F32)).astype(BF16)
-        parts[s][tokens:, :] = (back_near[s].astype(F32) + back_came[s].astype(F32)).astype(BF16)
+def chips_kernel(near, came, *refs):
+    parts = refs[-near.shape[0]:]
+    for s in range(near.shape[0]):
+        parts[s][...] = (near[s].astype(F32) + came[s].astype(F32)).astype(BF16)
 
 
 def total_kernel(count, *refs):
-    out_ref, back_ref, value_ref = refs[count:]
-    tokens = out_ref.shape[0]
     total = refs[0][...].astype(F32)
     for ref in refs[1:count]:
         total = total + ref[...].astype(F32)
-    out_ref[...] = total[0:tokens].astype(BF16)
-    back_ref[...] = total[tokens:2 * tokens].astype(BF16)
-    value_ref[...] = total[2 * tokens:2 * tokens + value_ref.shape[0], 0:value_ref.shape[1]]
+    rows = refs[count]
+    tokens = rows.shape[0]
+    rows[...] = total[0:tokens].astype(BF16)
+    for values in refs[count + 1:]:
+        values[...] = total[tokens:tokens + values.shape[0], 0:values.shape[1]]
 
 
 BANKS = 8
@@ -466,6 +470,14 @@
     return kernel_call(add_kernel, [shape, shape], [], 0, limit=2, in_hbm=hbm)(keep, came, *earlier)
 
 
+def add_chips(near, far, *earlier):
+    sources = near.shape[0]
+    shape = jax.ShapeDtypeStruct(near.shape[1:], BF16)
+    hbm = [2] if earlier else []
+    parts = kernel_call(chips_kernel, [shape] * sources, [], 0, limit=2, in_hbm=hbm)(near, far, *earlier)
+    return parts[0], [swap(parts[s], s, "expert") for s in range(1, sources)]
+
+
 def gathered_body(
     hidden_in, out_grad, expert_ids, gate_values, capacity_blocks, gate_weight, up_weight, down_weight
 ):
@@ -494,23 +506,21 @@
     grad_across = swap(out_grad, 2)
     came = join(came, gate_there, own_across, grad_across)
     came_across_there = swap(came, 2)
+    across_near = swap(own_across, 1)
     grads = join([out_grad, grad_across], came)
     grads = [grads] + [swap(grads, s, "expert") for s in range(1, sources)]
 
-    half_rows, partial, onehot, slot_gate = kernel_call(
-        functools.partial(early_kernel, choose),
+    half_rows, onehot, slot_gate = kernel_call(
+        functools.partial(routing_kernel, choose),
         [
             held(local_experts, rows, model // 2),
-            held(2, local_experts, rows, units, kind=F32),
             held(sources, slots, tokens),
             held(local_experts, rows, tokens, kind=F32),
         ],
-        [pltpu.VMEM((local_experts, units, model // 2), BF16), pltpu.SemaphoreType.DMA((local_experts,))],
-        product,
-        limit=8,
-        in_hbm=(6,),
-    )(capacity_blocks, own, swap(own, 1), came, swap(came, 1), gate_t, up_t)
-    came_across = join([came_across_there], onehot)[0]
+        [],
+        product // 4,
+    )(capacity_blocks, own, swap(own, 1), came, swap(came, 1), across_near)
+    came_across = join([came_across_there], onehot, grads[1])[0]
     out_rows, x_rows, activ, scaled, slope, silu = kernel_call(
         forward_kernel,
         [
@@ -521,19 +531,13 @@
             held(local_experts, rows, units, kind=F32),
             held(local_experts, rows, units, kind=F32),
         ],
-        [
-            pltpu.VMEM((local_experts, rows, model // 2), BF16),
-            pltpu.VMEM((local_experts, units, model // 2), BF16),
-            pltpu.VMEM((RING, units, model), BF16),
-            pltpu.SemaphoreType.DMA((local_experts,)),
-            pltpu.SemaphoreType.DMA((RING,)),
-        ],
-        2 * product,
+        [pltpu.VMEM((RING, units, model), BF16)] * 2 + [pltpu.SemaphoreType.DMA((RING,))] * 2,
+        3 * product,
         limit=14,
         in_hbm=(5, 6),
     )(
-        own_across, swap(own_across, 1), came_across, swap(came_across, 1),
-        gate_t, up_t, down_weight, half_rows, partial, onehot, slot_gate, grads[0],
+        own_across, across_near, came_across, swap(came_across, 1),
+        gate_t, up_t, down_weight, half_rows, onehot, slot_gate, grads[0],
     )
 
     keep, send = kernel_call(
@@ -545,7 +549,7 @@
     )(onehot, out_rows, *grads)
     near = swap(send, 1)
     out_near, out_far = add_cores(keep, near)
-    back_rows, dots, y_rows, gate_part, up_part = kernel_call(
+    back_rows, dots, y_rows, gate_part, up_part, down_grad = kernel_call(
         backward_kernel,
         [
             held(sources, slots, model),
@@ -553,42 +557,49 @@
             held(local_experts, rows, model),
             held(local_experts, rows, units),
             held(local_experts, rows, units),
+            sent(local_experts, units, model),
         ],
-        [pltpu.VMEM((RING, units, model), BF16)] * 2 + [pltpu.SemaphoreType.DMA((RING,))] * 2,
-        3 * product,
-        limit=14,
+        [
+            pltpu.VMEM((RING, units, model), BF16),
+            pltpu.VMEM((RING, units, model), BF16),
+            pltpu.VMEM((BANKS, units, model), BF16),
+            pltpu.SemaphoreType.DMA((RING,)),
+            pltpu.SemaphoreType.DMA((RING,)),
+            pltpu.SemaphoreType.DMA((BANKS,)),
+        ],
+        4 * product,
+        out_specs=[pl.BlockSpec(memory_space=pltpu.VMEM)] * 5 + [pl.BlockSpec(memory_space=pltpu.HBM)],
+        limit=20,
         in_hbm=(6, 7),
     )(
         *grads, near,
-        gate_t, up_t, down_weight, activ, slope, silu, onehot, slot_gate, out_near,
-    )
-
-    out_came = swap(out_far, 2)
+        gate_t, up_t, down_weight, activ, scaled, slope, silu, onehot, slot_gate, out_near,
+    )
+
+    out_own, out_parts = add_chips(out_near, swap(out_far, 2))
     keep, send = kernel_call(
         functools.partial(home_values_kernel, choose),
         [sent(2, sources, tokens + EXTRA, width)] * 2,
         [],
         2 * slots * sources * tokens * model,
         limit=2,
-    )(onehot, back_rows, dots, own, came, out_came)
+    )(onehot, back_rows, dots, own, came, out_own)
     some = local_experts // 2
-    (down_grad,) = weight_grads([(scaled, y_rows, 0, some)])
-    back_near, back_far = add_cores(keep, swap(send, 1), down_grad)
-    (up_grad,) = weight_grads([(up_part, x_rows, 0, local_experts)], None, back_near)
-    height = 2 * tokens + EXTRA
-    parts = kernel_call(chips_kernel, [sent(height, width)] * sources, [], 0, limit=2, in_hbm=(4,))(
-        out_near, out_came, back_near, swap(back_far, 2), up_grad
-    )
-    down_grad, gate_grad = weight_grads(
-        [(scaled, y_rows, some, local_experts), (gate_part, x_rows, 0, local_experts)], down_grad, parts[0]
-    )
-    layer_out, input_grad, value_grad = kernel_call(
+    (up_grad,) = weight_grads([(up_part, x_rows, 0, some)])
+    back_near, back_far = add_cores(keep, swap(send, 1), up_grad)
+    (up_grad,) = weight_grads([(up_part, x_rows, some, local_experts)], up_grad, back_near)
+    (layer_out,) = kernel_call(functools.partial(total_kernel, sources), [sent(tokens, width)], [], 0, limit=2)(
+        out_own, *out_parts
+    )
+    back_own, back_parts = add_chips(back_near, swap(back_far, 2), up_grad)
+    (gate_grad,) = weight_grads([(gate_part, x_rows, 0, local_experts)], None, back_own)
+    input_grad, value_grad = kernel_call(
         functools.partial(total_kernel, sources),
-        [sent(tokens, width), sent(tokens, width), jax.ShapeDtypeStruct((choose, tokens), F32)],
+        [sent(tokens, width), jax.ShapeDtypeStruct((choose, tokens), F32)],
         [],
         0,
         limit=2,
-    )(parts[0], *[swap(parts[s], s, "expert") for s in range(1, sources)])
+    )(back_own, *back_parts)
     return (
         layer_out,
         input_grad,

time: 83.6 us -> 85.2 us (1.019)
  starting transfers between devices: 21.4 us -> 26.1 us
  waiting for transfers between devices: 9.67 us -> 7.18 us
    ppermute x20 -> x23, starting transfers between devices: 21.4 us -> 26.1 us  [swap(): return lax.ppermute(array, axis, [(i, i ^ bit) for i in range(count)])]
    ppermute x20 -> x23, waiting for transfers between devices: 9.67 us -> 7.18 us  [swap(): return lax.ppermute(array, axis, [(i, i ^ bit) for i in range(count)])]
    pallas_call x16 -> x18, Pallas kernels: 47.1 us -> 46.5 us  [call(): pl.pallas_call(kernel, in_specs=specs, out_specs=out_specs or [pl.BlockSp...]
  transfers between devices with their start and end apart: 20 -> 23, of which waited for: 6 -> 6; matrix products, arithmetic and copies ran while one was open for 0% -> 0% of each run, Pallas kernels for 58% -> 56%
where the time goes in v7:
time: 85.2 us; the launch traced here: 85.1 us
  Pallas kernels  50.9 us (60%)
  starting transfers between devices  26.1 us (31%)
  waiting for transfers between devices  7.18 us (8%)
  between operations  0.9 us (1%)
    pallas_call x18, Pallas kernels, call(): pl.pallas_call(kernel, in_specs=specs, out_specs=out_specs or [pl.BlockSp...  46.5 us
    ppermute x23, starting transfers between devices, swap(): return lax.ppermute(array, axis, [(i, i ^ bit) for i in range(count)])  26.1 us
    ppermute x23, waiting for transfers between devices, swap(): return lax.ppermute(array, axis, [(i, i ^ bit) for i in range(count)])  7.18 us
    pallas_call x1, Pallas kernels, in_vmem(): pl.pallas_call(load_kernel, in_specs=[pl.BlockSpec(memory_space=pltpu.HBM...  4.42 us
  transfers between devices with their start and end apart: 23, of which 6 were waited for; matrix products, arithmetic and copies ran while one was open for 0% of the time, Pallas kernels for 56%

profile of v7, /device:TPU:0, one launch (start us, length us, event | category | flops | bytes accessed | tf_op | source)
XLA Modules:
  0.0 85.1 jit_solution(11765211309567604611)
XLA Ops:
  0.7 0.9 %shard_map.127.o0.own_ref = bf16[144,256]{1,0:T(8,128)(2,1)S(1)} custom-call(bf16[128,256]{1,0:T(8,128)(2,1)} %hidden_hbm.1, s32[6,128]{1,0:T(8,128)} %bitcast.15, f32[6,128]{1,0:T(8,128)} %bitcast.16), custom_call_target="tpu_custom_call" | custom-call | tf_op jit(solution)/shard_map/pallas_call | solution.py:428
  1.6 3.1 %collective-permute-start.1 = (bf16[144,256]{1,0:T(8,128)(2,1)S(1)}, bf16[144,256]{1,0:T(8,128)(2,1)S(1)}, u32[]{:S(2)}, u32[]{:S(2)}) collective-permute-start(bf16[144,256]{1,0:T(8,128)(2,1)S(1)} %shard_map.127.o0.own_ref), channel_id=1, source_target_pairs={{0,4},{4,0},{8,12},{12,8},{1,5},{5,1},{9,13},{13,9},{2,6},{6,2},{1... | collective-permute-start | bytes 221192 | tf_op jit(solution)/shard_map/ppermute | solution.py:464
  4.7 2.6 %collective-permute-start.2 = (bf16[144,256]{1,0:T(8,128)(2,1)S(1)}, bf16[144,256]{1,0:T(8,128)(2,1)S(1)}, u32[]{:S(2)}, u32[]{:S(2)}) collective-permute-start(bf16[144,256]{1,0:T(8,128)(2,1)S(1)} %shard_map.127.o0.own_ref), channel_id=1, source_target_pairs={{0,8},{4,12},{8,0},{12,4},{1,9},{5,13},{9,1},{13,5},{2,10},{6,14},... | collective-permute-start | bytes 221192 | tf_op jit(solution)/shard_map/ppermute | solution.py:464
  7.2 1.7 %collective-permute-start.4 = (bf16[144,256]{1,0:T(8,128)(2,1)S(1)}, bf16[144,256]{1,0:T(8,128)(2,1)S(1)}, u32[]{:S(2)}, u32[]{:S(2)}) collective-permute-start(bf16[144,256]{1,0:T(8,128)(2,1)S(1)} %shard_map.127.o0.own_ref), channel_id=1, source_target_pairs={{0,2},{1,3},{2,0},{3,1},{4,6},{5,7},{6,4},{7,5},{8,10},{9,11},{10,... | collective-permute-start | bytes 221192 | tf_op jit(solution)/shard_map/ppermute | solution.py:464
  9.3 4.4 %shard_map.128 = (bf16[16,352,1024]{2,1,0:T(8,128)(2,1)S(1)}, f32[8,128]{1,0:T(8,128)S(1)}) custom-call(bf16[16,352,1024]{2,1,0:T(8,128)(2,1)} %bitcast.13), custom_call_target="tpu_custom_call" | custom-call | bytes 11534336 | tf_op jit(solution)/shard_map/pallas_call | solution.py:393
  13.9 1.8 %collective-permute-start.8 = (bf16[3,144,256]{2,1,0:T(8,128)(2,1)S(1)}, bf16[3,144,256]{2,1,0:T(8,128)(2,1)S(1)}, u32[]{:S(2)}, u32[]{:S(2)}) collective-permute-start(bf16[3,144,256]{2,1,0:T(8,128)(2,1)S(1)} %shard_map.129.b0.refs_2_.info_ref), channel_id=1, source_target_pairs={{0,2},{1,3},{2,0},{3,1},{4,6},{5,7},{6,4},{7,5},{8,10},{9,11},{10,... | collective-permute-start | bytes 663560 | tf_op jit(solution)/shard_map/ppermute | solution.py:464
  15.6 0.7 collective-permute-start.9
  16.9 0.8 collective-permute-done.o1
  17.8 1.6 %shard_map.130 = (bf16[16,64,512]{2,1,0:T(8,128)(2,1)S(1)}, bf16[4,256,128]{2,1,0:T(8,128)(2,1)S(1)}, f32[16,64,128]{2,1,0:T(8,128)S(1)}) custom-call(s32[64]{0:T(128)S(1)} %copy-done.1, bf16[144,256]{1,0:T(8,128)(2,1)S(1)} %shard_map.127.o0.own_ref, bf16[144,256]{1,0:T(8,128)(2,1)S(1)} %collective-permute-done.o1, ...), custom_call_target="tpu_custom_call" | custom-call | flops 184549376 | bytes 5767168 | tf_op jit(solution)/shard_map/pallas_call | solution.py:428
  19.4 1.9 %collective-permute-done.9.refs_2_.refs_1_.a1 = bf16[2,128,256]{2,1,0:T(8,128)(2,1)S(1)} collective-permute-done((bf16[2,128,256]{2,1,0:T(8,128)(2,1)S(1)}, bf16[2,128,256]{2,1,0:T(8,128)(2,1)S(1)}, u32[]{:S(2)}, u32[]{:S(2)}) %collective-permute-start.9) | collective-permute-done | bytes 131104 | tf_op jit(solution)/shard_map/ppermute | solution.py:464
  21.8 2.1 %collective-permute-start.11 = (bf16[2,128,256]{2,1,0:T(8,128)(2,1)S(1)}, bf16[2,128,256]{2,1,0:T(8,128)(2,1)S(1)}, u32[]{:S(2)}, u32[]{:S(2)}) collective-permute-start(bf16[2,128,256]{2,1,0:T(8,128)(2,1)S(1)} %shard_map.131.later_ref.refs_0_.a0), channel_id=1, source_target_pairs={{0,8},{4,12},{8,0},{12,4},{1,9},{5,13},{9,1},{13,5},{2,10},{6,14},... | collective-permute-start | bytes 393224 | tf_op jit(solution)/shard_map/ppermute | solution.py:464
  23.9 1.9 %collective-permute-start.12 = (bf16[2,128,256]{2,1,0:T(8,128)(2,1)S(1)}, bf16[2,128,256]{2,1,0:T(8,128)(2,1)S(1)}, u32[]{:S(2)}, u32[]{:S(2)}) collective-permute-start(bf16[2,128,256]{2,1,0:T(8,128)(2,1)S(1)} %shard_map.131.later_ref.refs_0_.a0), channel_id=1, source_target_pairs={{0,12},{4,8},{8,4},{12,0},{1,13},{5,9},{9,5},{13,1},{2,14},{6,10},... | collective-permute-start | bytes 393224 | tf_op jit(solution)/shard_map/ppermute | solution.py:464
  25.8 12.4 %shard_map.133 = (bf16[4,256,1024]{2,1,0:T(8,128)(2,1)S(1)}, bf16[16,64,1024]{2,1,0:T(8,128)(2,1)S(1)}, bf16[16,64,352]{2,1,0:T(8,128)(2,1)S(1)}, bf16[16,64,352...) custom-call(bf16[144,256]{1,0:T(8,128)(2,1)S(1)} %collective-permute-done.4.refs_4_.o2, ...), custom_call_target="tpu_custom_call" | custom-call | flops 2214592512 | bytes 69206016 | tf_op jit(solution)/shard_map/pallas_call | solution.py:428
  38.8 2.6 %collective-permute-done.13.came.near_ref = bf16[4,4,128,256]{3,2,1,0:T(8,128)(2,1)S(1)} collective-permute-done((bf16[4,4,128,256]{3,2,1,0:T(8,128)(2,1)S(1)}, bf16[4,4,128,256]{3,2,1,0:T(8,128)(2,1)S(1)}, u32[]{:S(2)}, u32[]{:S(2)}) %collective-permute-start.13) | collective-permute-done | bytes 1048608 | tf_op jit(solution)/shard_map/ppermute | solution.py:464
  41.5 1.6 %collective-permute-start.14 = (bf16[4,128,256]{2,1,0:T(8,128)(2,1)S(1)}, bf16[4,128,256]{2,1,0:T(8,128)(2,1)S(1)}, u32[]{:S(2)}, u32[]{:S(2)}) collective-permute-start(bf16[4,128,256]{2,1,0:T(8,128)(2,1)S(1)} %get-tuple-element.49), channel_id=1, source_target_pairs={{0,2},{1,3},{2,0},{3,1},{4,6},{5,7},{6,4},{7,5},{8,10},{9,11},{10,... | collective-permute-start | bytes 786440 | tf_op jit(solution)/shard_map/ppermute | solution.py:464
  43.1 17.4 %shard_map.138 = (bf16[4,256,1024]{2,1,0:T(8,128)(2,1)S(1)}, f32[16,64,128]{2,1,0:T(8,128)S(1)}, bf16[16,64,1024]{2,1,0:T(8,128)(2,1)}, bf16[16,64,352]{2,1,0:T(...) custom-call(bf16[2,128,256]{2,1,0:T(8,128)(2,1)S(1)} %shard_map.131.later_ref.refs_0_.a0, ...), custom_call_target="tpu_custom_call" | custom-call | flops 2952790016 | bytes 92274688 | tf_op jit(solution)/shard_map/pallas_call | solution.py:428
  61.3 3.1 %shard_map.140.refs_0_.refs_2_ = bf16[16,352,1024]{2,1,0:T(8,128)(2,1)} custom-call(bf16[16,64,352]{2,1,0:T(8,128)(2,1)S(1)} %get-tuple-element.62.refs_0_, bf16[16,64,1024]{2,1,0:T(8,128)(2,1)S(1)} %get-tuple-element.63.refs_1_), custom_call_target="tpu_custom_call" | custom-call | flops 369098752 | bytes 11534336 | tf_op jit(solution)/shard_map/pallas_call | solution.py:428
  65.7 2.0 %collective-permute-start.16 = (bf16[128,256]{1,0:T(8,128)(2,1)S(1)}, bf16[128,256]{1,0:T(8,128)(2,1)S(1)}, u32[]{:S(2)}, u32[]{:S(2)}) collective-permute-start(bf16[128,256]{1,0:T(8,128)(2,1)S(1)} %get-tuple-element.52), channel_id=1, source_target_pairs={{0,8},{4,12},{8,0},{12,4},{1,9},{5,13},{9,1},{13,5},{2,10},{6,14},... | collective-permute-start | bytes 196616 | tf_op jit(solution)/shard_map/ppermute | solution.py:464
  67.7 1.9 %collective-permute-start.17 = (bf16[128,256]{1,0:T(8,128)(2,1)S(1)}, bf16[128,256]{1,0:T(8,128)(2,1)S(1)}, u32[]{:S(2)}, u32[]{:S(2)}) collective-permute-start(bf16[128,256]{1,0:T(8,128)(2,1)S(1)} %get-tuple-element.53), channel_id=1, source_target_pairs={{0,12},{4,8},{8,4},{12,0},{1,13},{5,9},{9,5},{13,1},{2,14},{6,10},... | collective-permute-start | bytes 196616 | tf_op jit(solution)/shard_map/ppermute | solution.py:464
  69.6 3.1 %shard_map.142.refs_0_ = bf16[16,352,1024]{2,1,0:T(8,128)(2,1)} custom-call(bf16[16,64,352]{2,1,0:T(8,128)(2,1)S(1)} %get-tuple-element.62.refs_0_, bf16[16,64,1024]{2,1,0:T(8,128)(2,1)S(1)} %get-tuple-element.63.refs_1_, bf16[16,352,1024]{2,1,0:T(8,128)(2,1)} %shard_map.140.refs_0_.refs_2_, ...), custom_call_target="tpu_custom_call", output_to_operand_aliasing={{}: (2, {})} | custom-call | flops 369098752 | bytes 11534336 | tf_op jit(solution)/shard_map/pallas_call | solution.py:428
  72.7 1.4 %collective-permute-done.19.came = bf16[4,144,256]{2,1,0:T(8,128)(2,1)S(1)} collective-permute-done((bf16[4,144,256]{2,1,0:T(8,128)(2,1)S(1)}, bf16[4,144,256]{2,1,0:T(8,128)(2,1)S(1)}, u32[]{:S(2)}, u32[]{:S(2)}) %collective-permute-start.19) | collective-permute-done | bytes 294944 | tf_op jit(solution)/shard_map/ppermute | solution.py:464
  74.7 1.9 %collective-permute-start.21 = (bf16[144,256]{1,0:T(8,128)(2,1)S(1)}, bf16[144,256]{1,0:T(8,128)(2,1)S(1)}, u32[]{:S(2)}, u32[]{:S(2)}) collective-permute-start(bf16[144,256]{1,0:T(8,128)(2,1)S(1)} %get-tuple-element.68), channel_id=1, source_target_pairs={{0,8},{4,12},{8,0},{12,4},{1,9},{5,13},{9,1},{13,5},{2,10},{6,14},... | collective-permute-start | bytes 221192 | tf_op jit(solution)/shard_map/ppermute | solution.py:464
  76.6 2.0 %collective-permute-start.22 = (bf16[144,256]{1,0:T(8,128)(2,1)S(1)}, bf16[144,256]{1,0:T(8,128)(2,1)S(1)}, u32[]{:S(2)}, u32[]{:S(2)}) collective-permute-start(bf16[144,256]{1,0:T(8,128)(2,1)S(1)} %get-tuple-element.69), channel_id=1, source_target_pairs={{0,12},{4,8},{8,4},{12,0},{1,13},{5,9},{9,5},{13,1},{2,14},{6,10},... | collective-permute-start | bytes 221192 | tf_op jit(solution)/shard_map/ppermute | solution.py:464
  79.3 5.1 %shard_map.145 = bf16[16,352,1024]{2,1,0:T(8,128)(2,1)} custom-call(bf16[16,64,352]{2,1,0:T(8,128)(2,1)S(1)} %get-tuple-element.72.refs_0_, bf16[16,64,1024]{2,1,0:T(8,128)(2,1)S(1)} %get-tuple-element.63.refs_1_, bf16[144,256]{1,0:T(8,128)(2,1)S(1)} %get-tuple-element.66.refs_0_.refs_2_), custom_call_target="tpu_custom_call" | custom-call | flops 738197504 | bytes 23068672 | tf_op jit(solution)/shard_map/pallas_call | solution.py:428
  (45 shorter events, 6.3 us)
Async XLA Ops:
  0.6 17.2 %copy-start.1 = (s32[64]{0:T(128)S(1)}, s32[64]{0:T(128)}, u32[]{:S(2)}) copy-start(s32[64]{0:T(128)} %capacity_ref.1) | copy-start | bytes 772
  1.6 12.1 %collective-permute-start.1 = (bf16[144,256]{1,0:T(8,128)(2,1)S(1)}, bf16[144,256]{1,0:T(8,128)(2,1)S(1)}, u32[]{:S(2)}, u32[]{:S(2)}) collective-permute-start(bf16[144,256]{1,0:T(8,128)(2,1)S(1)} %shard_map.127.o0.own_ref), channel_id=1, source_target_pairs={{0,4},{4,0},{8,12},{12,8},{1,5},{5,1},{9,13},{13,9},{2,6},{6,2},{1... | collective-permute-start | bytes 221192 | tf_op jit(solution)/shard_map/ppermute | solution.py:464
  4.7 9.1 %collective-permute-start.2 = (bf16[144,256]{1,0:T(8,128)(2,1)S(1)}, bf16[144,256]{1,0:T(8,128)(2,1)S(1)}, u32[]{:S(2)}, u32[]{:S(2)}) collective-permute-start(bf16[144,256]{1,0:T(8,128)(2,1)S(1)} %shard_map.127.o0.own_ref), channel_id=1, source_target_pairs={{0,8},{4,12},{8,0},{12,4},{1,9},{5,13},{9,1},{13,5},{2,10},{6,14},... | collective-permute-start | bytes 221192 | tf_op jit(solution)/shard_map/ppermute | solution.py:464
  7.2 6.5 %collective-permute-start.3 = (bf16[144,256]{1,0:T(8,128)(2,1)S(1)}, bf16[144,256]{1,0:T(8,128)(2,1)S(1)}, u32[]{:S(2)}, u32[]{:S(2)}) collective-permute-start(bf16[144,256]{1,0:T(8,128)(2,1)S(1)} %shard_map.127.o0.own_ref), channel_id=1, source_target_pairs={{0,12},{4,8},{8,4},{12,0},{1,13},{5,9},{9,5},{13,1},{2,14},{6,10},... | collective-permute-start | bytes 221192 | tf_op jit(solution)/shard_map/ppermute | solution.py:464
  7.2 6.5 %collective-permute-start.4 = (bf16[144,256]{1,0:T(8,128)(2,1)S(1)}, bf16[144,256]{1,0:T(8,128)(2,1)S(1)}, u32[]{:S(2)}, u32[]{:S(2)}) collective-permute-start(bf16[144,256]{1,0:T(8,128)(2,1)S(1)} %shard_map.127.o0.own_ref), channel_id=1, source_target_pairs={{0,2},{1,3},{2,0},{3,1},{4,6},{5,7},{6,4},{7,5},{8,10},{9,11},{10,... | collective-permute-start | bytes 221192 | tf_op jit(solution)/shard_map/ppermute | solution.py:464
  9.0 4.7 %collective-permute-start.5 = (bf16[128,256]{1,0:T(8,128)(2,1)}, bf16[128,256]{1,0:T(8,128)(2,1)S(1)}, u32[]{:S(2)}, u32[]{:S(2)}) collective-permute-start(bf16[128,256]{1,0:T(8,128)(2,1)} %refs_0_.1), channel_id=1, source_target_pairs={{0,2},{1,3},{2,0},{3,1},{4,6},{5,7},{6,4},{7,5},{8,10},{9,11},{10,... | collective-permute-start | bytes 196616 | tf_op jit(solution)/shard_map/ppermute | solution.py:464
  13.8 4.0 %collective-permute-start.6 = (bf16[3,144,256]{2,1,0:T(8,128)(2,1)S(1)}, bf16[3,144,256]{2,1,0:T(8,128)(2,1)S(1)}, u32[]{:S(2)}, u32[]{:S(2)}) collective-permute-start(bf16[3,144,256]{2,1,0:T(8,128)(2,1)S(1)} %shard_map.129.b0.refs_2_.info_ref), channel_id=1, source_target_pairs={{0,1},{1,0},{2,3},{3,2},{4,5},{5,4},{6,7},{7,6},{8,9},{9,8},{10,11... | collective-permute-start | bytes 663560 | tf_op jit(solution)/shard_map/ppermute | solution.py:464
  13.9 7.8 %collective-permute-start.8 = (bf16[3,144,256]{2,1,0:T(8,128)(2,1)S(1)}, bf16[3,144,256]{2,1,0:T(8,128)(2,1)S(1)}, u32[]{:S(2)}, u32[]{:S(2)}) collective-permute-start(bf16[3,144,256]{2,1,0:T(8,128)(2,1)S(1)} %shard_map.129.b0.refs_2_.info_ref), channel_id=1, source_target_pairs={{0,2},{1,3},{2,0},{3,1},{4,6},{5,7},{6,4},{7,5},{8,10},{9,11},{10,... | collective-permute-start | bytes 663560 | tf_op jit(solution)/shard_map/ppermute | solution.py:464
  15.6 5.6 %collective-permute-start.9 = (bf16[2,128,256]{2,1,0:T(8,128)(2,1)S(1)}, bf16[2,128,256]{2,1,0:T(8,128)(2,1)S(1)}, u32[]{:S(2)}, u32[]{:S(2)}) collective-permute-start(bf16[2,128,256]{2,1,0:T(8,128)(2,1)S(1)} %shard_map.131.later_ref.refs_0_.a0), channel_id=1, source_target_pairs={{0,4},{4,0},{8,12},{12,8},{1,5},{5,1},{9,13},{13,9},{2,6},{6,2},{1... | collective-permute-start | bytes 393224 | tf_op jit(solution)/shard_map/ppermute | solution.py:464
  16.4 1.3 %collective-permute-start = (bf16[144,256]{1,0:T(8,128)(2,1)S(1)}, bf16[144,256]{1,0:T(8,128)(2,1)S(1)}, u32[]{:S(2)}, u32[]{:S(2)}) collective-permute-start(bf16[144,256]{1,0:T(8,128)(2,1)S(1)} %shard_map.127.o0.own_ref), channel_id=1, source_target_pairs={{0,1},{1,0},{2,3},{3,2},{4,5},{5,4},{6,7},{7,6},{8,9},{9,8},{10,11... | collective-permute-start | bytes 221192 | tf_op jit(solution)/shard_map/ppermute | solution.py:464
  16.4 1.4 %collective-permute-start.7 = (bf16[144,256]{1,0:T(8,128)(2,1)S(1)}, bf16[144,256]{1,0:T(8,128)(2,1)S(1)}, u32[]{:S(2)}, u32[]{:S(2)}) collective-permute-start(bf16[144,256]{1,0:T(8,128)(2,1)S(1)} %collective-permute-done.4.refs_4_.o2), channel_id=1, source_target_pairs={{0,1},{1,0},{2,3},{3,2},{4,5},{5,4},{6,7},{7,6},{8,9},{9,8},{10,11... | collective-permute-start | bytes 221192 | tf_op jit(solution)/shard_map/ppermute | solution.py:464
  21.7 4.0 %collective-permute-start.10 = (bf16[3,144,256]{2,1,0:T(8,128)(2,1)S(1)}, bf16[3,144,256]{2,1,0:T(8,128)(2,1)S(1)}, u32[]{:S(2)}, u32[]{:S(2)}) collective-permute-start(bf16[3,144,256]{2,1,0:T(8,128)(2,1)S(1)} %bitcast.8), channel_id=1, source_target_pairs={{0,1},{1,0},{2,3},{3,2},{4,5},{5,4},{6,7},{7,6},{8,9},{9,8},{10,11... | collective-permute-start | bytes 663560 | tf_op jit(solution)/shard_map/ppermute | solution.py:464
  21.8 16.4 %collective-permute-start.11 = (bf16[2,128,256]{2,1,0:T(8,128)(2,1)S(1)}, bf16[2,128,256]{2,1,0:T(8,128)(2,1)S(1)}, u32[]{:S(2)}, u32[]{:S(2)}) collective-permute-start(bf16[2,128,256]{2,1,0:T(8,128)(2,1)S(1)} %shard_map.131.later_ref.refs_0_.a0), channel_id=1, source_target_pairs={{0,8},{4,12},{8,0},{12,4},{1,9},{5,13},{9,1},{13,5},{2,10},{6,14},... | collective-permute-start | bytes 393224 | tf_op jit(solution)/shard_map/ppermute | solution.py:464
  23.9 14.3 %collective-permute-start.12 = (bf16[2,128,256]{2,1,0:T(8,128)(2,1)S(1)}, bf16[2,128,256]{2,1,0:T(8,128)(2,1)S(1)}, u32[]{:S(2)}, u32[]{:S(2)}) collective-permute-start(bf16[2,128,256]{2,1,0:T(8,128)(2,1)S(1)} %shard_map.131.later_ref.refs_0_.a0), channel_id=1, source_target_pairs={{0,12},{4,8},{8,4},{12,0},{1,13},{5,9},{9,5},{13,1},{2,14},{6,10},... | collective-permute-start | bytes 393224 | tf_op jit(solution)/shard_map/ppermute | solution.py:464
  38.7 2.7 %collective-permute-start.13 = (bf16[4,4,128,256]{3,2,1,0:T(8,128)(2,1)S(1)}, bf16[4,4,128,256]{3,2,1,0:T(8,128)(2,1)S(1)}, u32[]{:S(2)}, u32[]{:S(2)}) collective-permute-start(bf16[4,4,128,256]{3,2,1,0:T(8,128)(2,1)S(1)} %get-tuple-element.47), channel_id=1, source_target_pairs={{0,1},{1,0},{2,3},{3,2},{4,5},{5,4},{6,7},{7,6},{8,9},{9,8},{10,11... | collective-permute-start | bytes 3145736 | tf_op jit(solution)/shard_map/ppermute | solution.py:464
  41.5 19.0 %collective-permute-start.14 = (bf16[4,128,256]{2,1,0:T(8,128)(2,1)S(1)}, bf16[4,128,256]{2,1,0:T(8,128)(2,1)S(1)}, u32[]{:S(2)}, u32[]{:S(2)}) collective-permute-start(bf16[4,128,256]{2,1,0:T(8,128)(2,1)S(1)} %get-tuple-element.49), channel_id=1, source_target_pairs={{0,2},{1,3},{2,0},{3,1},{4,6},{5,7},{6,4},{7,5},{8,10},{9,11},{10,... | collective-permute-start | bytes 786440 | tf_op jit(solution)/shard_map/ppermute | solution.py:464
  61.2 3.2 %collective-permute-start.18 = (bf16[2,4,144,256]{3,2,1,0:T(8,128)(2,1)S(1)}, bf16[2,4,144,256]{3,2,1,0:T(8,128)(2,1)S(1)}, u32[]{:S(2)}, u32[]{:S(2)}) collective-permute-start(bf16[2,4,144,256]{3,2,1,0:T(8,128)(2,1)S(1)} %get-tuple-element.61), channel_id=1, source_target_pairs={{0,1},{1,0},{2,3},{3,2},{4,5},{5,4},{6,7},{7,6},{8,9},{9,8},{10,11... | collective-permute-start | bytes 1769480 | tf_op jit(solution)/shard_map/ppermute | solution.py:464
  64.6 9.5 %collective-permute-start.19 = (bf16[4,144,256]{2,1,0:T(8,128)(2,1)S(1)}, bf16[4,144,256]{2,1,0:T(8,128)(2,1)S(1)}, u32[]{:S(2)}, u32[]{:S(2)}) collective-permute-start(bf16[4,144,256]{2,1,0:T(8,128)(2,1)S(1)} %get-tuple-element.65), channel_id=1, source_target_pairs={{0,2},{1,3},{2,0},{3,1},{4,6},{5,7},{6,4},{7,5},{8,10},{9,11},{10,... | collective-permute-start | bytes 884744 | tf_op jit(solution)/shard_map/ppermute | solution.py:464
  65.2 11.4 %collective-permute-start.15 = (bf16[128,256]{1,0:T(8,128)(2,1)S(1)}, bf16[128,256]{1,0:T(8,128)(2,1)S(1)}, u32[]{:S(2)}, u32[]{:S(2)}) collective-permute-start(bf16[128,256]{1,0:T(8,128)(2,1)S(1)} %get-tuple-element.51), channel_id=1, source_target_pairs={{0,4},{4,0},{8,12},{12,8},{1,5},{5,1},{9,13},{13,9},{2,6},{6,2},{1... | collective-permute-start | bytes 196616 | tf_op jit(solution)/shard_map/ppermute | solution.py:464
  65.7 12.9 %collective-permute-start.16 = (bf16[128,256]{1,0:T(8,128)(2,1)S(1)}, bf16[128,256]{1,0:T(8,128)(2,1)S(1)}, u32[]{:S(2)}, u32[]{:S(2)}) collective-permute-start(bf16[128,256]{1,0:T(8,128)(2,1)S(1)} %get-tuple-element.52), channel_id=1, source_target_pairs={{0,8},{4,12},{8,0},{12,4},{1,9},{5,13},{9,1},{13,5},{2,10},{6,14},... | collective-permute-start | bytes 196616 | tf_op jit(solution)/shard_map/ppermute | solution.py:464
  67.7 10.9 %collective-permute-start.17 = (bf16[128,256]{1,0:T(8,128)(2,1)S(1)}, bf16[128,256]{1,0:T(8,128)(2,1)S(1)}, u32[]{:S(2)}, u32[]{:S(2)}) collective-permute-start(bf16[128,256]{1,0:T(8,128)(2,1)S(1)} %get-tuple-element.53), channel_id=1, source_target_pairs={{0,12},{4,8},{8,4},{12,0},{1,13},{5,9},{9,5},{13,1},{2,14},{6,10},... | collective-permute-start | bytes 196616 | tf_op jit(solution)/shard_map/ppermute | solution.py:464
  74.2 10.2 %collective-permute-start.20 = (bf16[144,256]{1,0:T(8,128)(2,1)S(1)}, bf16[144,256]{1,0:T(8,128)(2,1)S(1)}, u32[]{:S(2)}, u32[]{:S(2)}) collective-permute-start(bf16[144,256]{1,0:T(8,128)(2,1)S(1)} %get-tuple-element.67), channel_id=1, source_target_pairs={{0,4},{4,0},{8,12},{12,8},{1,5},{5,1},{9,13},{13,9},{2,6},{6,2},{1... | collective-permute-start | bytes 221192 | tf_op jit(solution)/shard_map/ppermute | solution.py:464
  74.7 9.7 %collective-permute-start.21 = (bf16[144,256]{1,0:T(8,128)(2,1)S(1)}, bf16[144,256]{1,0:T(8,128)(2,1)S(1)}, u32[]{:S(2)}, u32[]{:S(2)}) collective-permute-start(bf16[144,256]{1,0:T(8,128)(2,1)S(1)} %get-tuple-element.68), channel_id=1, source_target_pairs={{0,8},{4,12},{8,0},{12,4},{1,9},{5,13},{9,1},{13,5},{2,10},{6,14},... | collective-permute-start | bytes 221192 | tf_op jit(solution)/shard_map/ppermute | solution.py:464
  76.6 7.8 %collective-permute-start.22 = (bf16[144,256]{1,0:T(8,128)(2,1)S(1)}, bf16[144,256]{1,0:T(8,128)(2,1)S(1)}, u32[]{:S(2)}, u32[]{:S(2)}) collective-permute-start(bf16[144,256]{1,0:T(8,128)(2,1)S(1)} %get-tuple-element.69), channel_id=1, source_target_pairs={{0,12},{4,8},{8,4},{12,0},{1,13},{5,9},{9,5},{13,1},{2,14},{6,10},... | collective-permute-start | bytes 221192 | tf_op jit(solution)/shard_map/ppermute | solution.py:464
  (1 other events, 15.0 us)

commit v8 on v7

--- a/solution.py
+++ b/solution.py
@@ -141,15 +141,14 @@
 
 
 def forward_kernel(
-    o2, o3, b2, b3, gate_ref, up_hbm, down_hbm, half_ref, onehot, slot_gate, later_ref,
+    o2, o3, b2, b3, gate_ref, up_ref, down_hbm, half_ref, onehot, slot_gate, later_ref,
     out_rows, rows_ref, act_ref, a_ref, slope_ref, silu_ref,
-    up_ref, down_ref, up_sems, down_sems,
+    down_ref, down_sems,
 ):
     sources, slots, tokens = onehot.shape
     experts = slots // CAP
     width = b2.shape[2]
     me = lax.axis_index("etp")
-    start_up, wait_up = ring(up_hbm, up_ref, up_sems)
     start_down, wait_down = ring(down_hbm, down_ref, down_sems)
     rows_ref[:, :, half(me, 0, 2 * width)] = half_ref[...]
     other = lax.bitwise_xor(me // 2, 1) * 2 * width
@@ -160,7 +159,7 @@
     def activate(e):
         x = rows_ref[e]
         hidden_gate = nt(x, gate_ref[e])
-        hidden_up = nt(x, slot_of(up_ref, e))
+        hidden_up = nt(x, up_ref[e])
         sigma = jax.nn.sigmoid(hidden_gate)
         silu = hidden_gate * sigma
         activ = (silu * hidden_up).astype(BF16)
@@ -175,26 +174,17 @@
         for s in range(sources):
             out_rows[s, at, :] = out[s * CAP:(s + 1) * CAP]
 
-    def first(e):
-        wait_up(e)
-        activate(e)
-        start_up(e)
-
     def both(e):
         for i in (e - 2, e - 1):
             wait_down(i)
-        for i in (e, e + 1):
-            wait_up(i)
         project(e - 2)
         project(e - 1)
         activate(e)
         activate(e + 1)
         for i in (e - 2, e - 1):
             start_down(i)
-        for i in (e, e + 1):
-            start_up(i)
-
-    skewed(experts, first, wait_down, project, both)
+
+    skewed(experts, activate, wait_down, project, both)
 
 
 def skewed(experts, first, wait, second, both):
@@ -243,9 +233,9 @@
 
 def backward_kernel(
     a0, a1, a2, a3, near_ref,
-    gate_ref, up_hbm, down_hbm, act_ref, a_ref, slope_ref, silu_ref, onehot, slot_gate, earlier_ref,
-    back_rows, dots, rows_ref, p_ref, q_ref, down_grad,
-    up_ref, down_ref, held, up_sems, down_sems, held_sems,
+    gate_ref, up_hbm, down_hbm, act_ref, slope_ref, silu_ref, onehot, slot_gate, earlier_ref,
+    back_rows, dots, rows_ref, p_ref, q_ref,
+    up_ref, down_ref, up_sems, down_sems,
 ):
     sources, slots, tokens = onehot.shape
     experts = slots // CAP
@@ -267,12 +257,7 @@
         p_ref[e] = (grad * slope_ref[e]).astype(BF16)
         q_ref[e] = (grad * silu_ref[e]).astype(BF16)
 
-    def store(e):
-        slot = lax.rem(e, BANKS)
-        return pltpu.make_async_copy(held.at[slot], down_grad.at[e], held_sems.at[slot])
-
     def project(e):
-        held[lax.rem(e, BANKS)] = tn(a_ref[e], rows_ref[e]).astype(BF16)
         back = nn(p_ref[e], gate_ref[e]) + nn(q_ref[e], slot_of(up_ref, e))
         back = (back * slot_gate[e][:, 0:1]).astype(BF16)
         at = pl.ds(pl.multiple_of(e * CAP, CAP), CAP)
@@ -289,32 +274,16 @@
             wait_down(i)
         for i in (e - 2, e - 1):
             wait_up(i)
-
-        @pl.when(e - 2 >= BANKS)
-        def _():
-            for i in (e - 2, e - 1):
-                store(i - BANKS).wait()
-
         project(e - 2)
         project(e - 1)
         slopes(e)
         slopes(e + 1)
-        for i in (e - 2, e - 1):
-            store(i).start()
         for i in (e, e + 1):
             start_down(i)
         for i in (e - 2, e - 1):
             start_up(i)
 
-    def last(e):
-        wait_up(e)
-        store(e - BANKS).wait()
-
-    skewed(experts, first, last, project, both)
-    for e in (experts - 2, experts - 1):
-        store(jnp.int32(e)).start()
-    for e in range(experts - BANKS, experts):
-        store(jnp.int32(e)).wait()
+    skewed(experts, first, wait_up, project, both)
 
 
 def add_kernel(keep, came, *refs):
@@ -328,6 +297,16 @@
     parts = refs[-near.shape[0]:]
     for s in range(near.shape[0]):
         parts[s][...] = (near[s].astype(F32) + came[s].astype(F32)).astype(BF16)
+
+
+def pairs_kernel(near, came, *refs):
+    for s in range(near.shape[0]):
+        refs[-2 + s % 2][s // 2] = (near[s].astype(F32) + came[s].astype(F32)).astype(BF16)
+
+
+def step_kernel(even, came, *refs):
+    for s in range(2):
+        refs[-2 + s][...] = (even[s].astype(F32) + came[s].astype(F32)).astype(BF16)
 
 
 def total_kernel(count, *refs):
@@ -488,7 +467,7 @@
     slots = local_experts * CAP
     rows = sources * CAP
     gate_t, gate_there = in_vmem(jnp.swapaxes(gate_weight, 1, 2))
-    up_t = jnp.swapaxes(up_weight, 1, 2)
+    up_t, up_there = in_vmem(jnp.swapaxes(up_weight, 1, 2))
     product = 2 * local_experts * rows * units * model
     held = lambda *shape, kind=BF16: pltpu.VMEM(shape, kind)
     sent = lambda *shape: jax.ShapeDtypeStruct(shape, BF16)
@@ -520,7 +499,7 @@
         [],
         product // 4,
     )(capacity_blocks, own, swap(own, 1), came, swap(came, 1), across_near)
-    came_across = join([came_across_there], onehot, grads[1])[0]
+    came_across = join([came_across_there], onehot, up_there, grads[1])[0]
     out_rows, x_rows, activ, scaled, slope, silu = kernel_call(
         forward_kernel,
         [
@@ -531,10 +510,10 @@
             held(local_experts, rows, units, kind=F32),
             held(local_experts, rows, units, kind=F32),
         ],
-        [pltpu.VMEM((RING, units, model), BF16)] * 2 + [pltpu.SemaphoreType.DMA((RING,))] * 2,
+        [pltpu.VMEM((RING, units, model), BF16), pltpu.SemaphoreType.DMA((RING,))],
         3 * product,
-        limit=14,
-        in_hbm=(5, 6),
+        limit=8,
+        in_hbm=(6,),
     )(
         own_across, across_near, came_across, swap(came_across, 1),
         gate_t, up_t, down_weight, half_rows, onehot, slot_gate, grads[0],
@@ -549,7 +528,7 @@
     )(onehot, out_rows, *grads)
     near = swap(send, 1)
     out_near, out_far = add_cores(keep, near)
-    back_rows, dots, y_rows, gate_part, up_part, down_grad = kernel_call(
+    back_rows, dots, y_rows, gate_part, up_part = kernel_call(
         backward_kernel,
         [
             held(sources, slots, model),
@@ -557,45 +536,41 @@
             held(local_experts, rows, model),
             held(local_experts, rows, units),
             held(local_experts, rows, units),
-            sent(local_experts, units, model),
         ],
-        [
-            pltpu.VMEM((RING, units, model), BF16),
-            pltpu.VMEM((RING, units, model), BF16),
-            pltpu.VMEM((BANKS, units, model), BF16),
-            pltpu.SemaphoreType.DMA((RING,)),
-            pltpu.SemaphoreType.DMA((RING,)),
-            pltpu.SemaphoreType.DMA((BANKS,)),
-        ],
-        4 * product,
-        out_specs=[pl.BlockSpec(memory_space=pltpu.VMEM)] * 5 + [pl.BlockSpec(memory_space=pltpu.HBM)],
-        limit=20,
+        [pltpu.VMEM((RING, units, model), BF16)] * 2 + [pltpu.SemaphoreType.DMA((RING,))] * 2,
+        3 * product,
+        limit=14,
         in_hbm=(6, 7),
     )(
         *grads, near,
-        gate_t, up_t, down_weight, activ, scaled, slope, silu, onehot, slot_gate, out_near,
-    )
-
-    out_own, out_parts = add_chips(out_near, swap(out_far, 2))
+        gate_t, jnp.swapaxes(up_weight, 1, 2), down_weight, activ, slope, silu, onehot, slot_gate, out_near,
+    )
+
+    part, pair = sent(tokens, width), sent(2, tokens, width)
+    out_even, out_odd = kernel_call(pairs_kernel, [pair, pair], [], 0, limit=2)(out_near, swap(out_far, 2))
     keep, send = kernel_call(
         functools.partial(home_values_kernel, choose),
         [sent(2, sources, tokens + EXTRA, width)] * 2,
         [],
         2 * slots * sources * tokens * model,
         limit=2,
-    )(onehot, back_rows, dots, own, came, out_own)
+    )(onehot, back_rows, dots, own, came, out_even)
     some = local_experts // 2
-    (up_grad,) = weight_grads([(up_part, x_rows, 0, some)])
-    back_near, back_far = add_cores(keep, swap(send, 1), up_grad)
-    (up_grad,) = weight_grads([(up_part, x_rows, some, local_experts)], up_grad, back_near)
-    (layer_out,) = kernel_call(functools.partial(total_kernel, sources), [sent(tokens, width)], [], 0, limit=2)(
-        out_own, *out_parts
+    out_came = swap(out_odd, 1, "expert")
+    (down_grad,) = weight_grads([(scaled, y_rows, 0, some)])
+    back_near, back_far = add_cores(keep, swap(send, 1), down_grad, out_came)
+    out_own, out_other = kernel_call(step_kernel, [part, part], [], 0, limit=2)(out_even, out_came, back_near)
+    (up_grad,) = weight_grads([(up_part, x_rows, 0, local_experts)], None, back_near)
+    (layer_out,) = kernel_call(functools.partial(total_kernel, 2), [part], [], 0, limit=2)(
+        out_own, swap(out_other, 2, "expert")
     )
     back_own, back_parts = add_chips(back_near, swap(back_far, 2), up_grad)
-    (gate_grad,) = weight_grads([(gate_part, x_rows, 0, local_experts)], None, back_own)
+    down_grad, gate_grad = weight_grads(
+        [(scaled, y_rows, some, local_experts), (gate_part, x_rows, 0, local_experts)], down_grad, back_own
+    )
     input_grad, value_grad = kernel_call(
         functools.partial(total_kernel, sources),
-        [sent(tokens, width), jax.ShapeDtypeStruct((choose, tokens), F32)],
+        [part, jax.ShapeDtypeStruct((choose, tokens), F32)],
         [],
         0,
         limit=2,

time: 85.2 us -> 84 us (0.986)
  starting transfers between devices: 26.1 us -> 22.5 us
  Pallas kernels: 50.9 us -> 52.8 us
    pallas_call x1 -> x2, Pallas kernels: 4.42 us -> 8.84 us  [in_vmem(): pl.pallas_call(load_kernel, in_specs=[pl.BlockSpec(memory_space=pltpu.HBM...]
    ppermute x23 -> x22, starting transfers between devices: 26.1 us -> 22.5 us  [swap(): return lax.ppermute(array, axis, [(i, i ^ bit) for i in range(count)])]
    pallas_call x18 -> x19, Pallas kernels: 46.5 us -> 44 us  [call(): pl.pallas_call(kernel, in_specs=specs, out_specs=out_specs or [pl.BlockSp...]
    ppermute x23 -> x22, waiting for transfers between devices: 7.18 us -> 7.55 us  [swap(): return lax.ppermute(array, axis, [(i, i ^ bit) for i in range(count)])]
  transfers between devices with their start and end apart: 23 -> 22, of which waited for: 6 -> 4; matrix products, arithmetic and copies ran while one was open for 0% -> 0% of each run, Pallas kernels for 56% -> 59%
where the time goes in v8:
time: 84 us; the launch traced here: 83.8 us
  Pallas kernels  52.8 us (63%)
  starting transfers between devices  22.5 us (27%)
  waiting for transfers between devices  7.55 us (9%)
  between operations  0.93 us (1%)
    pallas_call x19, Pallas kernels, call(): pl.pallas_call(kernel, in_specs=specs, out_specs=out_specs or [pl.BlockSp...  44 us
    ppermute x22, starting transfers between devices, swap(): return lax.ppermute(array, axis, [(i, i ^ bit) for i in range(count)])  22.5 us
    pallas_call x2, Pallas kernels, in_vmem(): pl.pallas_call(load_kernel, in_specs=[pl.BlockSpec(memory_space=pltpu.HBM...  8.84 us
    ppermute x22, waiting for transfers between devices, swap(): return lax.ppermute(array, axis, [(i, i ^ bit) for i in range(count)])  7.55 us
  transfers between devices with their start and end apart: 22, of which 4 were waited for; matrix products, arithmetic and copies ran while one was open for 0% of the time, Pallas kernels for 59%

profile of v8, /device:TPU:0, one launch (start us, length us, event | category | flops | bytes accessed | tf_op | source)
XLA Modules:
  0.0 83.8 jit_solution(9086684803094991596)
XLA Ops:
  0.6 0.9 %shard_map.127.o0.own_ref = bf16[144,256]{1,0:T(8,128)(2,1)S(1)} custom-call(bf16[128,256]{1,0:T(8,128)(2,1)} %hidden_hbm.1, s32[6,128]{1,0:T(8,128)} %bitcast.14, f32[6,128]{1,0:T(8,128)} %bitcast.15), custom_call_target="tpu_custom_call" | custom-call | tf_op jit(solution)/shard_map/pallas_call | solution.py:407
  1.6 3.0 %collective-permute-start.4 = (bf16[144,256]{1,0:T(8,128)(2,1)S(1)}, bf16[144,256]{1,0:T(8,128)(2,1)S(1)}, u32[]{:S(2)}, u32[]{:S(2)}) collective-permute-start(bf16[144,256]{1,0:T(8,128)(2,1)S(1)} %shard_map.127.o0.own_ref), channel_id=1, source_target_pairs={{0,2},{1,3},{2,0},{3,1},{4,6},{5,7},{6,4},{7,5},{8,10},{9,11},{10,... | collective-permute-start | bytes 221192 | tf_op jit(solution)/shard_map/ppermute | solution.py:443
  4.6 3.6 %collective-permute-start.3 = (bf16[144,256]{1,0:T(8,128)(2,1)S(1)}, bf16[144,256]{1,0:T(8,128)(2,1)S(1)}, u32[]{:S(2)}, u32[]{:S(2)}) collective-permute-start(bf16[144,256]{1,0:T(8,128)(2,1)S(1)} %shard_map.127.o0.own_ref), channel_id=1, source_target_pairs={{0,12},{4,8},{8,4},{12,0},{1,13},{5,9},{9,5},{13,1},{2,14},{6,10},... | collective-permute-start | bytes 221192 | tf_op jit(solution)/shard_map/ppermute | solution.py:443
  8.2 0.8 collective-permute-start.1
  9.3 4.4 %shard_map.128 = (bf16[16,352,1024]{2,1,0:T(8,128)(2,1)S(1)}, f32[8,128]{1,0:T(8,128)S(1)}) custom-call(bf16[16,352,1024]{2,1,0:T(8,128)(2,1)} %bitcast.13), custom_call_target="tpu_custom_call" | custom-call | bytes 11534336 | tf_op jit(solution)/shard_map/pallas_call | solution.py:372
  14.2 1.4 %collective-permute-start.8 = (bf16[3,144,256]{2,1,0:T(8,128)(2,1)S(1)}, bf16[3,144,256]{2,1,0:T(8,128)(2,1)S(1)}, u32[]{:S(2)}, u32[]{:S(2)}) collective-permute-start(bf16[3,144,256]{2,1,0:T(8,128)(2,1)S(1)} %shard_map.129.b0.refs_2_.info_ref), channel_id=1, source_target_pairs={{0,2},{1,3},{2,0},{3,1},{4,6},{5,7},{6,4},{7,5},{8,10},{9,11},{10,... | collective-permute-start | bytes 663560 | tf_op jit(solution)/shard_map/ppermute | solution.py:443
  15.7 1.3 %collective-permute-start.9 = (bf16[2,128,256]{2,1,0:T(8,128)(2,1)S(1)}, bf16[2,128,256]{2,1,0:T(8,128)(2,1)S(1)}, u32[]{:S(2)}, u32[]{:S(2)}) collective-permute-start(bf16[2,128,256]{2,1,0:T(8,128)(2,1)S(1)} %shard_map.132.later_ref.refs_0_.a0), channel_id=1, source_target_pairs={{0,4},{4,0},{8,12},{12,8},{1,5},{5,1},{9,13},{13,9},{2,6},{6,2},{1... | collective-permute-start | bytes 393224 | tf_op jit(solution)/shard_map/ppermute | solution.py:443
  17.5 4.4 %shard_map.131 = (bf16[16,352,1024]{2,1,0:T(8,128)(2,1)S(1)}, f32[8,128]{1,0:T(8,128)S(1)}) custom-call(bf16[16,352,1024]{2,1,0:T(8,128)(2,1)} %bitcast.11), custom_call_target="tpu_custom_call" | custom-call | bytes 11534336 | tf_op jit(solution)/shard_map/pallas_call | solution.py:372
  21.9 1.6 %shard_map.130 = (bf16[16,64,512]{2,1,0:T(8,128)(2,1)S(1)}, bf16[4,256,128]{2,1,0:T(8,128)(2,1)S(1)}, f32[16,64,128]{2,1,0:T(8,128)S(1)}) custom-call(s32[64]{0:T(128)S(1)} %copy-done.1, bf16[144,256]{1,0:T(8,128)(2,1)S(1)} %shard_map.127.o0.own_ref, bf16[144,256]{1,0:T(8,128)(2,1)S(1)} %collective-permute-done.o1, ...), custom_call_target="tpu_custom_call" | custom-call | flops 184549376 | bytes 5767168 | tf_op jit(solution)/shard_map/pallas_call | solution.py:407
  23.7 2.6 %collective-permute-start.12 = (bf16[2,128,256]{2,1,0:T(8,128)(2,1)S(1)}, bf16[2,128,256]{2,1,0:T(8,128)(2,1)S(1)}, u32[]{:S(2)}, u32[]{:S(2)}) collective-permute-start(bf16[2,128,256]{2,1,0:T(8,128)(2,1)S(1)} %shard_map.132.later_ref.refs_0_.a0), channel_id=1, source_target_pairs={{0,12},{4,8},{8,4},{12,0},{1,13},{5,9},{9,5},{13,1},{2,14},{6,10},... | collective-permute-start | bytes 393224 | tf_op jit(solution)/shard_map/ppermute | solution.py:443
  26.7 10.6 %shard_map.134 = (bf16[4,256,1024]{2,1,0:T(8,128)(2,1)S(1)}, bf16[16,64,1024]{2,1,0:T(8,128)(2,1)S(1)}, bf16[16,64,352]{2,1,0:T(8,128)(2,1)S(1)}, bf16[16,64,352...) custom-call(bf16[144,256]{1,0:T(8,128)(2,1)S(1)} %collective-permute-done.4.refs_4_.o2, ...), custom_call_target="tpu_custom_call" | custom-call | flops 2214592512 | bytes 69206016 | tf_op jit(solution)/shard_map/pallas_call | solution.py:407
  37.4 1.8 %collective-permute-done.11.refs_2_.a2 = bf16[2,128,256]{2,1,0:T(8,128)(2,1)S(1)} collective-permute-done((bf16[2,128,256]{2,1,0:T(8,128)(2,1)S(1)}, bf16[2,128,256]{2,1,0:T(8,128)(2,1)S(1)}, u32[]{:S(2)}, u32[]{:S(2)}) %collective-permute-start.11) | collective-permute-done | bytes 131104 | tf_op jit(solution)/shard_map/ppermute | solution.py:443
  39.7 2.6 %collective-permute-done.13.came.near_ref = bf16[4,4,128,256]{3,2,1,0:T(8,128)(2,1)S(1)} collective-permute-done((bf16[4,4,128,256]{3,2,1,0:T(8,128)(2,1)S(1)}, bf16[4,4,128,256]{3,2,1,0:T(8,128)(2,1)S(1)}, u32[]{:S(2)}, u32[]{:S(2)}) %collective-permute-start.13) | collective-permute-done | bytes 1048608 | tf_op jit(solution)/shard_map/ppermute | solution.py:443
  43.1 12.4 %shard_map.138 = (bf16[4,256,1024]{2,1,0:T(8,128)(2,1)S(1)}, f32[16,64,128]{2,1,0:T(8,128)S(1)}, bf16[16,64,1024]{2,1,0:T(8,128)(2,1)S(1)}, bf16[16,64,352]{2,1,0:T(8,128)(2,1)S(1)}, bf16[16,64,352]{2,1,0:T(8,128)(2,1)S(1)}) custom-call(bf16[2,128,256]{2,1,0:T(8,128)(2,1)S(1)} %shard_map.132.later_ref.refs_0_.a0, ...), custom_call_target="tpu_custom_call" | custom-call | flops 2214592512 | bytes 69206016 | tf_op jit(solution)/shard_map/pallas_call | solution.py:407
  56.4 3.1 %shard_map.140.refs_0_.refs_4_ = bf16[16,352,1024]{2,1,0:T(8,128)(2,1)} custom-call(bf16[16,64,352]{2,1,0:T(8,128)(2,1)S(1)} %get-tuple-element.65.refs_0_, bf16[16,64,1024]{2,1,0:T(8,128)(2,1)S(1)} %get-tuple-element.66.refs_1_.refs_2_), custom_call_target="tpu_custom_call" | custom-call | flops 369098752 | bytes 11534336 | tf_op jit(solution)/shard_map/pallas_call | solution.py:407
  59.5 2.7 %collective-permute-done.15.refs_1_.came = bf16[2,128,256]{2,1,0:T(8,128)(2,1)S(1)} collective-permute-done((bf16[2,128,256]{2,1,0:T(8,128)(2,1)S(1)}, bf16[2,128,256]{2,1,0:T(8,128)(2,1)S(1)}, u32[]{:S(2)}, u32[]{:S(2)}) %collective-permute-start.15) | collective-permute-done | bytes 131104 | tf_op jit(solution)/shard_map/ppermute | solution.py:443
  62.4 1.6 %collective-permute-start.18 = (bf16[4,144,256]{2,1,0:T(8,128)(2,1)S(1)}, bf16[4,144,256]{2,1,0:T(8,128)(2,1)S(1)}, u32[]{:S(2)}, u32[]{:S(2)}) collective-permute-start(bf16[4,144,256]{2,1,0:T(8,128)(2,1)S(1)} %get-tuple-element.70), channel_id=1, source_target_pairs={{0,2},{1,3},{2,0},{3,1},{4,6},{5,7},{6,4},{7,5},{8,10},{9,11},{10,... | collective-permute-start | bytes 884744 | tf_op jit(solution)/shard_map/ppermute | solution.py:443
  64.0 1.5 %collective-permute-start.17 = (bf16[128,256]{1,0:T(8,128)(2,1)S(1)}, bf16[128,256]{1,0:T(8,128)(2,1)S(1)}, u32[]{:S(2)}, u32[]{:S(2)}) collective-permute-start(bf16[128,256]{1,0:T(8,128)(2,1)S(1)} %get-tuple-element.69), channel_id=1, source_target_pairs={{0,8},{4,12},{8,0},{12,4},{1,9},{5,13},{9,1},{13,5},{2,10},{6,14},... | collective-permute-start | bytes 196616 | tf_op jit(solution)/shard_map/ppermute | solution.py:443
  65.5 5.1 %shard_map.144.refs_0_ = bf16[16,352,1024]{2,1,0:T(8,128)(2,1)} custom-call(bf16[16,64,352]{2,1,0:T(8,128)(2,1)S(1)} %get-tuple-element.71.refs_0_, bf16[16,64,1024]{2,1,0:T(8,128)(2,1)S(1)} %get-tuple-element.72.refs_1_.refs_3_, bf16[4,144,256]{2,1,0:T(8,128)(2,1)S(1)} %get-tuple-element.67.refs_0_.refs_2_.near), custom_call_target="tpu_custom_call" | custom-call | flops 738197504 | bytes 23068672 | tf_op jit(solution)/shard_map/pallas_call | solution.py:407
  71.3 1.8 %collective-permute-start.19 = (bf16[144,256]{1,0:T(8,128)(2,1)S(1)}, bf16[144,256]{1,0:T(8,128)(2,1)S(1)}, u32[]{:S(2)}, u32[]{:S(2)}) collective-permute-start(bf16[144,256]{1,0:T(8,128)(2,1)S(1)} %get-tuple-element.74), channel_id=1, source_target_pairs={{0,4},{4,0},{8,12},{12,8},{1,5},{5,1},{9,13},{13,9},{2,6},{6,2},{1... | collective-permute-start | bytes 221192 | tf_op jit(solution)/shard_map/ppermute | solution.py:443
  73.1 1.2 %collective-permute-start.20 = (bf16[144,256]{1,0:T(8,128)(2,1)S(1)}, bf16[144,256]{1,0:T(8,128)(2,1)S(1)}, u32[]{:S(2)}, u32[]{:S(2)}) collective-permute-start(bf16[144,256]{1,0:T(8,128)(2,1)S(1)} %get-tuple-element.75), channel_id=1, source_target_pairs={{0,8},{4,12},{8,0},{12,4},{1,9},{5,13},{9,1},{13,5},{2,10},{6,14},... | collective-permute-start | bytes 221192 | tf_op jit(solution)/shard_map/ppermute | solution.py:443
  74.4 1.4 %collective-permute-start.21 = (bf16[144,256]{1,0:T(8,128)(2,1)S(1)}, bf16[144,256]{1,0:T(8,128)(2,1)S(1)}, u32[]{:S(2)}, u32[]{:S(2)}) collective-permute-start(bf16[144,256]{1,0:T(8,128)(2,1)S(1)} %get-tuple-element.76), channel_id=1, source_target_pairs={{0,12},{4,8},{8,4},{12,0},{1,13},{5,9},{9,5},{13,1},{2,14},{6,10},... | collective-permute-start | bytes 221192 | tf_op jit(solution)/shard_map/ppermute | solution.py:443
  75.8 7.3 %shard_map.147 = (bf16[16,352,1024]{2,1,0:T(8,128)(2,1)}, bf16[16,352,1024]{2,1,0:T(8,128)(2,1)}) custom-call(bf16[16,64,352]{2,1,0:T(8,128)(2,1)S(1)} %get-tuple-element.65.refs_0_, bf16[16,64,352]{2,1,0:T(8,128)(2,1)S(1)} %get-tuple-element.79.refs_1_, ...), custom_call_target="tpu_custom_call", output_to_operand_aliasing={{0}: (4, {})} | custom-call | flops 1107296256 | bytes 34603008 | tf_op jit(solution)/shard_map/pallas_call | solution.py:407
  83.2 0.7 shard_map.146
  (45 shorter events, 4.9 us)
Async XLA Ops:
  0.6 15.0 %copy-start = (bf16[128,256]{1,0:T(8,128)(2,1)S(1)}, bf16[128,256]{1,0:T(8,128)(2,1)}, u32[]{:S(2)}) copy-start(bf16[128,256]{1,0:T(8,128)(2,1)} %refs_0_.1) | copy-start | bytes 196612
  1.6 12.2 %collective-permute-start.4 = (bf16[144,256]{1,0:T(8,128)(2,1)S(1)}, bf16[144,256]{1,0:T(8,128)(2,1)S(1)}, u32[]{:S(2)}, u32[]{:S(2)}) collective-permute-start(bf16[144,256]{1,0:T(8,128)(2,1)S(1)} %shard_map.127.o0.own_ref), channel_id=1, source_target_pairs={{0,2},{1,3},{2,0},{3,1},{4,6},{5,7},{6,4},{7,5},{8,10},{9,11},{10,... | collective-permute-start | bytes 221192 | tf_op jit(solution)/shard_map/ppermute | solution.py:443
  4.6 9.2 %collective-permute-start.3 = (bf16[144,256]{1,0:T(8,128)(2,1)S(1)}, bf16[144,256]{1,0:T(8,128)(2,1)S(1)}, u32[]{:S(2)}, u32[]{:S(2)}) collective-permute-start(bf16[144,256]{1,0:T(8,128)(2,1)S(1)} %shard_map.127.o0.own_ref), channel_id=1, source_target_pairs={{0,12},{4,8},{8,4},{12,0},{1,13},{5,9},{9,5},{13,1},{2,14},{6,10},... | collective-permute-start | bytes 221192 | tf_op jit(solution)/shard_map/ppermute | solution.py:443
  8.2 5.9 %collective-permute-start.2 = (bf16[144,256]{1,0:T(8,128)(2,1)S(1)}, bf16[144,256]{1,0:T(8,128)(2,1)S(1)}, u32[]{:S(2)}, u32[]{:S(2)}) collective-permute-start(bf16[144,256]{1,0:T(8,128)(2,1)S(1)} %shard_map.127.o0.own_ref), channel_id=1, source_target_pairs={{0,8},{4,12},{8,0},{12,4},{1,9},{5,13},{9,1},{13,5},{2,10},{6,14},... | collective-permute-start | bytes 221192 | tf_op jit(solution)/shard_map/ppermute | solution.py:443
  8.2 5.9 %collective-permute-start.1 = (bf16[144,256]{1,0:T(8,128)(2,1)S(1)}, bf16[144,256]{1,0:T(8,128)(2,1)S(1)}, u32[]{:S(2)}, u32[]{:S(2)}) collective-permute-start(bf16[144,256]{1,0:T(8,128)(2,1)S(1)} %shard_map.127.o0.own_ref), channel_id=1, source_target_pairs={{0,4},{4,0},{8,12},{12,8},{1,5},{5,1},{9,13},{13,9},{2,6},{6,2},{1... | collective-permute-start | bytes 221192 | tf_op jit(solution)/shard_map/ppermute | solution.py:443
  9.0 4.8 %collective-permute-start.5 = (bf16[128,256]{1,0:T(8,128)(2,1)}, bf16[128,256]{1,0:T(8,128)(2,1)S(1)}, u32[]{:S(2)}, u32[]{:S(2)}) collective-permute-start(bf16[128,256]{1,0:T(8,128)(2,1)} %refs_0_.1), channel_id=1, source_target_pairs={{0,2},{1,3},{2,0},{3,1},{4,6},{5,7},{6,4},{7,5},{8,10},{9,11},{10,... | collective-permute-start | bytes 196616 | tf_op jit(solution)/shard_map/ppermute | solution.py:443
  9.3 12.7 %copy-start.1 = (s32[64]{0:T(128)S(1)}, s32[64]{0:T(128)}, u32[]{:S(2)}) copy-start(s32[64]{0:T(128)} %capacity_ref.1) | copy-start | bytes 772
  14.1 7.8 %collective-permute-start.6 = (bf16[3,144,256]{2,1,0:T(8,128)(2,1)S(1)}, bf16[3,144,256]{2,1,0:T(8,128)(2,1)S(1)}, u32[]{:S(2)}, u32[]{:S(2)}) collective-permute-start(bf16[3,144,256]{2,1,0:T(8,128)(2,1)S(1)} %shard_map.129.b0.refs_2_.info_ref), channel_id=1, source_target_pairs={{0,1},{1,0},{2,3},{3,2},{4,5},{5,4},{6,7},{7,6},{8,9},{9,8},{10,11... | collective-permute-start | bytes 663560 | tf_op jit(solution)/shard_map/ppermute | solution.py:443
  14.2 9.3 %collective-permute-start.8 = (bf16[3,144,256]{2,1,0:T(8,128)(2,1)S(1)}, bf16[3,144,256]{2,1,0:T(8,128)(2,1)S(1)}, u32[]{:S(2)}, u32[]{:S(2)}) collective-permute-start(bf16[3,144,256]{2,1,0:T(8,128)(2,1)S(1)} %shard_map.129.b0.refs_2_.info_ref), channel_id=1, source_target_pairs={{0,2},{1,3},{2,0},{3,1},{4,6},{5,7},{6,4},{7,5},{8,10},{9,11},{10,... | collective-permute-start | bytes 663560 | tf_op jit(solution)/shard_map/ppermute | solution.py:443
  15.7 7.9 %collective-permute-start.9 = (bf16[2,128,256]{2,1,0:T(8,128)(2,1)S(1)}, bf16[2,128,256]{2,1,0:T(8,128)(2,1)S(1)}, u32[]{:S(2)}, u32[]{:S(2)}) collective-permute-start(bf16[2,128,256]{2,1,0:T(8,128)(2,1)S(1)} %shard_map.132.later_ref.refs_0_.a0), channel_id=1, source_target_pairs={{0,4},{4,0},{8,12},{12,8},{1,5},{5,1},{9,13},{13,9},{2,6},{6,2},{1... | collective-permute-start | bytes 393224 | tf_op jit(solution)/shard_map/ppermute | solution.py:443
  17.0 4.9 %collective-permute-start = (bf16[144,256]{1,0:T(8,128)(2,1)S(1)}, bf16[144,256]{1,0:T(8,128)(2,1)S(1)}, u32[]{:S(2)}, u32[]{:S(2)}) collective-permute-start(bf16[144,256]{1,0:T(8,128)(2,1)S(1)} %shard_map.127.o0.own_ref), channel_id=1, source_target_pairs={{0,1},{1,0},{2,3},{3,2},{4,5},{5,4},{6,7},{7,6},{8,9},{9,8},{10,11... | collective-permute-start | bytes 221192 | tf_op jit(solution)/shard_map/ppermute | solution.py:443
  17.0 4.9 %collective-permute-start.7 = (bf16[144,256]{1,0:T(8,128)(2,1)S(1)}, bf16[144,256]{1,0:T(8,128)(2,1)S(1)}, u32[]{:S(2)}, u32[]{:S(2)}) collective-permute-start(bf16[144,256]{1,0:T(8,128)(2,1)S(1)} %collective-permute-done.4.refs_4_.o2), channel_id=1, source_target_pairs={{0,1},{1,0},{2,3},{3,2},{4,5},{5,4},{6,7},{7,6},{8,9},{9,8},{10,11... | collective-permute-start | bytes 221192 | tf_op jit(solution)/shard_map/ppermute | solution.py:443
  23.6 3.1 %collective-permute-start.10 = (bf16[3,144,256]{2,1,0:T(8,128)(2,1)S(1)}, bf16[3,144,256]{2,1,0:T(8,128)(2,1)S(1)}, u32[]{:S(2)}, u32[]{:S(2)}) collective-permute-start(bf16[3,144,256]{2,1,0:T(8,128)(2,1)S(1)} %bitcast.8), channel_id=1, source_target_pairs={{0,1},{1,0},{2,3},{3,2},{4,5},{5,4},{6,7},{7,6},{8,9},{9,8},{10,11... | collective-permute-start | bytes 663560 | tf_op jit(solution)/shard_map/ppermute | solution.py:443
  23.7 13.7 %collective-permute-start.12 = (bf16[2,128,256]{2,1,0:T(8,128)(2,1)S(1)}, bf16[2,128,256]{2,1,0:T(8,128)(2,1)S(1)}, u32[]{:S(2)}, u32[]{:S(2)}) collective-permute-start(bf16[2,128,256]{2,1,0:T(8,128)(2,1)S(1)} %shard_map.132.later_ref.refs_0_.a0), channel_id=1, source_target_pairs={{0,12},{4,8},{8,4},{12,0},{1,13},{5,9},{9,5},{13,1},{2,14},{6,10},... | collective-permute-start | bytes 393224 | tf_op jit(solution)/shard_map/ppermute | solution.py:443
  26.3 12.9 %collective-permute-start.11 = (bf16[2,128,256]{2,1,0:T(8,128)(2,1)S(1)}, bf16[2,128,256]{2,1,0:T(8,128)(2,1)S(1)}, u32[]{:S(2)}, u32[]{:S(2)}) collective-permute-start(bf16[2,128,256]{2,1,0:T(8,128)(2,1)S(1)} %shard_map.132.later_ref.refs_0_.a0), channel_id=1, source_target_pairs={{0,8},{4,12},{8,0},{12,4},{1,9},{5,13},{9,1},{13,5},{2,10},{6,14},... | collective-permute-start | bytes 393224 | tf_op jit(solution)/shard_map/ppermute | solution.py:443
  39.7 2.7 %collective-permute-start.13 = (bf16[4,4,128,256]{3,2,1,0:T(8,128)(2,1)S(1)}, bf16[4,4,128,256]{3,2,1,0:T(8,128)(2,1)S(1)}, u32[]{:S(2)}, u32[]{:S(2)}) collective-permute-start(bf16[4,4,128,256]{3,2,1,0:T(8,128)(2,1)S(1)} %get-tuple-element.53), channel_id=1, source_target_pairs={{0,1},{1,0},{2,3},{3,2},{4,5},{5,4},{6,7},{7,6},{8,9},{9,8},{10,11... | collective-permute-start | bytes 3145736 | tf_op jit(solution)/shard_map/ppermute | solution.py:443
  42.5 13.0 %collective-permute-start.14 = (bf16[4,128,256]{2,1,0:T(8,128)(2,1)S(1)}, bf16[4,128,256]{2,1,0:T(8,128)(2,1)S(1)}, u32[]{:S(2)}, u32[]{:S(2)}) collective-permute-start(bf16[4,128,256]{2,1,0:T(8,128)(2,1)S(1)} %get-tuple-element.55), channel_id=1, source_target_pairs={{0,2},{1,3},{2,0},{3,1},{4,6},{5,7},{6,4},{7,5},{8,10},{9,11},{10,... | collective-permute-start | bytes 786440 | tf_op jit(solution)/shard_map/ppermute | solution.py:443
  56.2 6.0 %collective-permute-start.16 = (bf16[2,4,144,256]{3,2,1,0:T(8,128)(2,1)S(1)}, bf16[2,4,144,256]{3,2,1,0:T(8,128)(2,1)S(1)}, u32[]{:S(2)}, u32[]{:S(2)}) collective-permute-start(bf16[2,4,144,256]{3,2,1,0:T(8,128)(2,1)S(1)} %get-tuple-element.64), channel_id=1, source_target_pairs={{0,1},{1,0},{2,3},{3,2},{4,5},{5,4},{6,7},{7,6},{8,9},{9,8},{10,11... | collective-permute-start | bytes 1769480 | tf_op jit(solution)/shard_map/ppermute | solution.py:443
  56.3 5.9 %collective-permute-start.15 = (bf16[2,128,256]{2,1,0:T(8,128)(2,1)S(1)}, bf16[2,128,256]{2,1,0:T(8,128)(2,1)S(1)}, u32[]{:S(2)}, u32[]{:S(2)}) collective-permute-start(bf16[2,128,256]{2,1,0:T(8,128)(2,1)S(1)} %get-tuple-element.57), channel_id=1, source_target_pairs={{0,4},{4,0},{8,12},{12,8},{1,5},{5,1},{9,13},{13,9},{2,6},{6,2},{1... | collective-permute-start | bytes 393224 | tf_op jit(solution)/shard_map/ppermute | solution.py:443
  62.4 8.9 %collective-permute-start.18 = (bf16[4,144,256]{2,1,0:T(8,128)(2,1)S(1)}, bf16[4,144,256]{2,1,0:T(8,128)(2,1)S(1)}, u32[]{:S(2)}, u32[]{:S(2)}) collective-permute-start(bf16[4,144,256]{2,1,0:T(8,128)(2,1)S(1)} %get-tuple-element.70), channel_id=1, source_target_pairs={{0,2},{1,3},{2,0},{3,1},{4,6},{5,7},{6,4},{7,5},{8,10},{9,11},{10,... | collective-permute-start | bytes 884744 | tf_op jit(solution)/shard_map/ppermute | solution.py:443
  64.0 6.6 %collective-permute-start.17 = (bf16[128,256]{1,0:T(8,128)(2,1)S(1)}, bf16[128,256]{1,0:T(8,128)(2,1)S(1)}, u32[]{:S(2)}, u32[]{:S(2)}) collective-permute-start(bf16[128,256]{1,0:T(8,128)(2,1)S(1)} %get-tuple-element.69), channel_id=1, source_target_pairs={{0,8},{4,12},{8,0},{12,4},{1,9},{5,13},{9,1},{13,5},{2,10},{6,14},... | collective-permute-start | bytes 196616 | tf_op jit(solution)/shard_map/ppermute | solution.py:443
  71.3 11.8 %collective-permute-start.19 = (bf16[144,256]{1,0:T(8,128)(2,1)S(1)}, bf16[144,256]{1,0:T(8,128)(2,1)S(1)}, u32[]{:S(2)}, u32[]{:S(2)}) collective-permute-start(bf16[144,256]{1,0:T(8,128)(2,1)S(1)} %get-tuple-element.74), channel_id=1, source_target_pairs={{0,4},{4,0},{8,12},{12,8},{1,5},{5,1},{9,13},{13,9},{2,6},{6,2},{1... | collective-permute-start | bytes 221192 | tf_op jit(solution)/shard_map/ppermute | solution.py:443
  73.1 10.0 %collective-permute-start.20 = (bf16[144,256]{1,0:T(8,128)(2,1)S(1)}, bf16[144,256]{1,0:T(8,128)(2,1)S(1)}, u32[]{:S(2)}, u32[]{:S(2)}) collective-permute-start(bf16[144,256]{1,0:T(8,128)(2,1)S(1)} %get-tuple-element.75), channel_id=1, source_target_pairs={{0,8},{4,12},{8,0},{12,4},{1,9},{5,13},{9,1},{13,5},{2,10},{6,14},... | collective-permute-start | bytes 221192 | tf_op jit(solution)/shard_map/ppermute | solution.py:443
  74.4 8.8 %collective-permute-start.21 = (bf16[144,256]{1,0:T(8,128)(2,1)S(1)}, bf16[144,256]{1,0:T(8,128)(2,1)S(1)}, u32[]{:S(2)}, u32[]{:S(2)}) collective-permute-start(bf16[144,256]{1,0:T(8,128)(2,1)S(1)} %get-tuple-element.76), channel_id=1, source_target_pairs={{0,12},{4,8},{8,4},{12,0},{1,13},{5,9},{9,5},{13,1},{2,14},{6,10},... | collective-permute-start | bytes 221192 | tf_op jit(solution)/shard_map/ppermute | solution.py:443

commit v9 on v7

--- a/solution.py
+++ b/solution.py
@@ -62,7 +62,8 @@
             home[q // 2, s, 0:tokens, :] = tn(onehot[s], rows[s, :, columns(me, q, width)]).astype(BF16)
 
 
-RING = 8
+RING = 6
+HELD = 4
 
 
 def ring(weight, slots, sems, columns=None):
@@ -89,25 +90,17 @@
     return slots[lax.rem(e, slots.shape[0])]
 
 
-def half(me, other, size):
-    return pl.ds(pl.multiple_of(lax.bitwise_xor(me // 2, other) * size, size), size)
-
-
-def gather_half(me, onehot, blocks, rows_ref, experts, width, tokens, start, offset):
-    for q, block in enumerate(blocks):
-        picked = nn(onehot, block).astype(BF16).reshape(experts, CAP, width)
-        at = pl.multiple_of(lax.rem(lax.bitwise_xor(me, q), 2) * width + offset, width)
-        rows_ref[:, start:start + CAP, pl.ds(at, width)] = picked
-
-
-def routing_kernel(
-    choose, capacity_ref, o0, o1, b0, b1, earlier_ref, rows_ref, onehot, slot_gate
+def forward_kernel(
+    choose, capacity_ref, o0, o1, o2, o3, b0, b1, b2, b3, gate_ref, up_ref, down_hbm, later_ref,
+    out_rows, rows_ref, act_ref, a_ref, slope_ref, silu_ref, onehot, slot_gate,
+    down_ref, down_sems,
 ):
     sources, slots, tokens = onehot.shape
     experts = slots // CAP
     width = b0.shape[2]
     me = lax.axis_index("etp")
     first = lax.axis_index("expert") * experts
+    start_down, wait_down = ring(down_hbm, down_ref, down_sems)
     row = lax.broadcasted_iota(jnp.int32, (tokens, tokens), 0)
     col = lax.broadcasted_iota(jnp.int32, (tokens, tokens), 1)
     before = jnp.where(row < col, 1.0, 0.0).astype(BF16)
@@ -120,7 +113,7 @@
     limit = limit.astype(F32)
     place = lax.broadcasted_iota(jnp.int32, (experts, CAP, tokens), 1).astype(F32)
     for s in range(sources):
-        block = [o[...] for o in (o0, o1)] if s == 0 else [b[s - 1] for b in (b0, b1)]
+        block = [o[...] for o in (o0, o1, o2, o3)] if s == 0 else [b[s - 1] for b in (b0, b1, b2, b3)]
         ids, highs, lows = routing(block[0][tokens:tokens + EXTRA, :], choose, tokens)
         named = jnp.zeros((experts, tokens), F32)
         high, low = named, named
@@ -137,30 +130,14 @@
         slot_gate[:, s * CAP:(s + 1) * CAP, :] = gates.reshape(experts, CAP, tokens)
         table = jnp.where(taken, 1.0, 0.0).reshape(slots, tokens).astype(BF16)
         onehot[s] = table
-        gather_half(me, table, [x[0:tokens, :] for x in block], rows_ref, experts, width, tokens, s * CAP, 0)
-
-
-def forward_kernel(
-    o2, o3, b2, b3, gate_ref, up_hbm, down_hbm, half_ref, onehot, slot_gate, later_ref,
-    out_rows, rows_ref, act_ref, a_ref, slope_ref, silu_ref,
-    up_ref, down_ref, up_sems, down_sems,
-):
-    sources, slots, tokens = onehot.shape
-    experts = slots // CAP
-    width = b2.shape[2]
-    me = lax.axis_index("etp")
-    start_up, wait_up = ring(up_hbm, up_ref, up_sems)
-    start_down, wait_down = ring(down_hbm, down_ref, down_sems)
-    rows_ref[:, :, half(me, 0, 2 * width)] = half_ref[...]
-    other = lax.bitwise_xor(me // 2, 1) * 2 * width
-    for s in range(sources):
-        block = [o[0:tokens, :] for o in (o2, o3)] if s == 0 else [b[s - 1, 0:tokens, :] for b in (b2, b3)]
-        gather_half(me, onehot[s], block, rows_ref, experts, width, tokens, s * CAP, other)
+        for q in range(4):
+            picked = nn(table, block[q][0:tokens, :]).astype(BF16).reshape(experts, CAP, width)
+            rows_ref[:, s * CAP:(s + 1) * CAP, columns(me, q, width)] = picked
 
     def activate(e):
         x = rows_ref[e]
         hidden_gate = nt(x, gate_ref[e])
-        hidden_up = nt(x, slot_of(up_ref, e))
+        hidden_up = nt(x, up_ref[e])
         sigma = jax.nn.sigmoid(hidden_gate)
         silu = hidden_gate * sigma
         activ = (silu * hidden_up).astype(BF16)
@@ -175,26 +152,17 @@
         for s in range(sources):
             out_rows[s, at, :] = out[s * CAP:(s + 1) * CAP]
 
-    def first(e):
-        wait_up(e)
-        activate(e)
-        start_up(e)
-
     def both(e):
         for i in (e - 2, e - 1):
             wait_down(i)
-        for i in (e, e + 1):
-            wait_up(i)
         project(e - 2)
         project(e - 1)
         activate(e)
         activate(e + 1)
         for i in (e - 2, e - 1):
             start_down(i)
-        for i in (e, e + 1):
-            start_up(i)
-
-    skewed(experts, first, wait_down, project, both)
+
+    skewed(experts, activate, wait_down, project, both)
 
 
 def skewed(experts, first, wait, second, both):
@@ -243,16 +211,15 @@
 
 def backward_kernel(
     a0, a1, a2, a3, near_ref,
-    gate_ref, up_hbm, down_hbm, act_ref, a_ref, slope_ref, silu_ref, onehot, slot_gate, earlier_ref,
+    gate_ref, up_ref, down_hbm, act_ref, a_ref, slope_ref, silu_ref, onehot, slot_gate, earlier_ref,
     back_rows, dots, rows_ref, p_ref, q_ref, down_grad,
-    up_ref, down_ref, held, up_sems, down_sems, held_sems,
+    down_ref, held, down_sems, held_sems,
 ):
     sources, slots, tokens = onehot.shape
     experts = slots // CAP
     width = a0.shape[2]
     me = lax.axis_index("etp")
     start_down, wait_down = ring(down_hbm, down_ref, down_sems)
-    start_up, wait_up = ring(up_hbm, up_ref, up_sems)
     for s, here in enumerate((a0, a1, a2, a3)):
         for q in range(4):
             block = near_ref[2 + q // 2, s] if q % 2 else here[q // 2]
@@ -268,12 +235,12 @@
         q_ref[e] = (grad * silu_ref[e]).astype(BF16)
 
     def store(e):
-        slot = lax.rem(e, BANKS)
+        slot = lax.rem(e, HELD)
         return pltpu.make_async_copy(held.at[slot], down_grad.at[e], held_sems.at[slot])
 
     def project(e):
-        held[lax.rem(e, BANKS)] = tn(a_ref[e], rows_ref[e]).astype(BF16)
-        back = nn(p_ref[e], gate_ref[e]) + nn(q_ref[e], slot_of(up_ref, e))
+        held[lax.rem(e, HELD)] = tn(a_ref[e], rows_ref[e]).astype(BF16)
+        back = nn(p_ref[e], gate_ref[e]) + nn(q_ref[e], up_ref[e])
         back = (back * slot_gate[e][:, 0:1]).astype(BF16)
         at = pl.ds(pl.multiple_of(e * CAP, CAP), CAP)
         for s in range(sources):
@@ -287,13 +254,11 @@
     def both(e):
         for i in (e, e + 1):
             wait_down(i)
-        for i in (e - 2, e - 1):
-            wait_up(i)
-
-        @pl.when(e - 2 >= BANKS)
+
+        @pl.when(e - 2 >= HELD)
         def _():
             for i in (e - 2, e - 1):
-                store(i - BANKS).wait()
+                store(i - HELD).wait()
 
         project(e - 2)
         project(e - 1)
@@ -303,17 +268,11 @@
             store(i).start()
         for i in (e, e + 1):
             start_down(i)
-        for i in (e - 2, e - 1):
-            start_up(i)
-
-    def last(e):
-        wait_up(e)
-        store(e - BANKS).wait()
-
-    skewed(experts, first, last, project, both)
+
+    skewed(experts, first, lambda e: store(e - HELD).wait(), project, both)
     for e in (experts - 2, experts - 1):
         store(jnp.int32(e)).start()
-    for e in range(experts - BANKS, experts):
+    for e in range(experts - HELD, experts):
         store(jnp.int32(e)).wait()
 
 
@@ -488,7 +447,7 @@
     slots = local_experts * CAP
     rows = sources * CAP
     gate_t, gate_there = in_vmem(jnp.swapaxes(gate_weight, 1, 2))
-    up_t = jnp.swapaxes(up_weight, 1, 2)
+    up_t, up_there = in_vmem(jnp.swapaxes(up_weight, 1, 2))
     product = 2 * local_experts * rows * units * model
     held = lambda *shape, kind=BF16: pltpu.VMEM(shape, kind)
     sent = lambda *shape: jax.ShapeDtypeStruct(shape, BF16)
@@ -510,19 +469,9 @@
     grads = join([out_grad, grad_across], came)
     grads = [grads] + [swap(grads, s, "expert") for s in range(1, sources)]
 
-    half_rows, onehot, slot_gate = kernel_call(
-        functools.partial(routing_kernel, choose),
-        [
-            held(local_experts, rows, model // 2),
-            held(sources, slots, tokens),
-            held(local_experts, rows, tokens, kind=F32),
-        ],
-        [],
-        product // 4,
-    )(capacity_blocks, own, swap(own, 1), came, swap(came, 1), across_near)
-    came_across = join([came_across_there], onehot, grads[1])[0]
-    out_rows, x_rows, activ, scaled, slope, silu = kernel_call(
-        forward_kernel,
+    came_across = join([came_across_there], up_there, grads[1])[0]
+    out_rows, x_rows, activ, scaled, slope, silu, onehot, slot_gate = kernel_call(
+        functools.partial(forward_kernel, choose),
         [
             held(sources, slots, model),
             held(local_experts, rows, model),
@@ -530,14 +479,18 @@
             held(local_experts, rows, units),
             held(local_experts, rows, units, kind=F32),
             held(local_experts, rows, units, kind=F32),
+            held(sources, slots, tokens),
+            held(local_experts, rows, tokens, kind=F32),
         ],
-        [pltpu.VMEM((RING, units, model), BF16)] * 2 + [pltpu.SemaphoreType.DMA((RING,))] * 2,
+        [pltpu.VMEM((RING, units, model), BF16), pltpu.SemaphoreType.DMA((RING,))],
         3 * product,
-        limit=14,
-        in_hbm=(5, 6),
+        limit=9,
+        in_hbm=(11,),
     )(
-        own_across, across_near, came_across, swap(came_across, 1),
-        gate_t, up_t, down_weight, half_rows, onehot, slot_gate, grads[0],
+        capacity_blocks,
+        own, swap(own, 1), own_across, across_near,
+        came, swap(came, 1), came_across, swap(came_across, 1),
+        gate_t, up_t, down_weight, grads[0],
     )
 
     keep, send = kernel_call(
@@ -561,16 +514,14 @@
         ],
         [
             pltpu.VMEM((RING, units, model), BF16),
-            pltpu.VMEM((RING, units, model), BF16),
-            pltpu.VMEM((BANKS, units, model), BF16),
+            pltpu.VMEM((HELD, units, model), BF16),
             pltpu.SemaphoreType.DMA((RING,)),
-            pltpu.SemaphoreType.DMA((RING,)),
-            pltpu.SemaphoreType.DMA((BANKS,)),
+            pltpu.SemaphoreType.DMA((HELD,)),
         ],
         4 * product,
         out_specs=[pl.BlockSpec(memory_space=pltpu.VMEM)] * 5 + [pl.BlockSpec(memory_space=pltpu.HBM)],
-        limit=20,
-        in_hbm=(6, 7),
+        limit=13,
+        in_hbm=(7,),
     )(
         *grads, near,
         gate_t, up_t, down_weight, activ, scaled, slope, silu, onehot, slot_gate, out_near,

time: 85.2 us -> 84.8 us (level)
  Pallas kernels: 50.9 us -> 53.4 us
  waiting for transfers between devices: 7.18 us -> 5.09 us
  starting transfers between devices: 26.1 us -> 25.2 us
    pallas_call x1 -> x2, Pallas kernels: 4.42 us -> 8.84 us  [in_vmem(): pl.pallas_call(load_kernel, in_specs=[pl.BlockSpec(memory_space=pltpu.HBM...]
    ppermute x23, waiting for transfers between devices: 7.18 us -> 5.09 us  [swap(): return lax.ppermute(array, axis, [(i, i ^ bit) for i in range(count)])]
    pallas_call x18 -> x17, Pallas kernels: 46.5 us -> 44.6 us  [call(): pl.pallas_call(kernel, in_specs=specs, out_specs=out_specs or [pl.BlockSp...]
  transfers between devices with their start and end apart: 23 -> 23, of which waited for: 6 -> 3; matrix products, arithmetic and copies ran while one was open for 0% -> 0% of each run, Pallas kernels for 56% -> 60%
where the time goes in v9:
time: 84.8 us; the launch traced here: 84.6 us
  Pallas kernels  53.4 us (63%)
  starting transfers between devices  25.2 us (30%)
  waiting for transfers between devices  5.09 us (6%)
  between operations  0.91 us (1%)
    pallas_call x17, Pallas kernels, call(): pl.pallas_call(kernel, in_specs=specs, out_specs=out_specs or [pl.BlockSp...  44.6 us
    ppermute x23, starting transfers between devices, swap(): return lax.ppermute(array, axis, [(i, i ^ bit) for i in range(count)])  25.2 us
    pallas_call x2, Pallas kernels, in_vmem(): pl.pallas_call(load_kernel, in_specs=[pl.BlockSpec(memory_space=pltpu.HBM...  8.84 us
    ppermute x23, waiting for transfers between devices, swap(): return lax.ppermute(array, axis, [(i, i ^ bit) for i in range(count)])  5.09 us
  transfers between devices with their start and end apart: 23, of which 3 were waited for; matrix products, arithmetic and copies ran while one was open for 0% of the time, Pallas kernels for 60%

profile of v9, /device:TPU:0, one launch (start us, length us, event | category | flops | bytes accessed | tf_op | source)
XLA Modules:
  0.0 84.6 jit_solution(1162919396936538503)
XLA Ops:
  0.6 0.9 %shard_map.127.o0.own_ref = bf16[144,256]{1,0:T(8,128)(2,1)S(1)} custom-call(bf16[128,256]{1,0:T(8,128)(2,1)} %hidden_hbm.1, s32[6,128]{1,0:T(8,128)} %bitcast.14, f32[6,128]{1,0:T(8,128)} %bitcast.15), custom_call_target="tpu_custom_call" | custom-call | tf_op jit(solution)/shard_map/pallas_call | solution.py:387
  1.6 3.0 %collective-permute-start.1 = (bf16[144,256]{1,0:T(8,128)(2,1)S(1)}, bf16[144,256]{1,0:T(8,128)(2,1)S(1)}, u32[]{:S(2)}, u32[]{:S(2)}) collective-permute-start(bf16[144,256]{1,0:T(8,128)(2,1)S(1)} %shard_map.127.o0.own_ref), channel_id=1, source_target_pairs={{0,2},{1,3},{2,0},{3,1},{4,6},{5,7},{6,4},{7,5},{8,10},{9,11},{10,... | collective-permute-start | bytes 221192 | tf_op jit(solution)/shard_map/ppermute | solution.py:423
  4.6 1.6 %collective-permute-start.3 = (bf16[144,256]{1,0:T(8,128)(2,1)S(1)}, bf16[144,256]{1,0:T(8,128)(2,1)S(1)}, u32[]{:S(2)}, u32[]{:S(2)}) collective-permute-start(bf16[144,256]{1,0:T(8,128)(2,1)S(1)} %shard_map.127.o0.own_ref), channel_id=1, source_target_pairs={{0,4},{4,0},{8,12},{12,8},{1,5},{5,1},{9,13},{13,9},{2,6},{6,2},{1... | collective-permute-start | bytes 221192 | tf_op jit(solution)/shard_map/ppermute | solution.py:423
  6.1 2.6 %collective-permute-start.4 = (bf16[144,256]{1,0:T(8,128)(2,1)S(1)}, bf16[144,256]{1,0:T(8,128)(2,1)S(1)}, u32[]{:S(2)}, u32[]{:S(2)}) collective-permute-start(bf16[144,256]{1,0:T(8,128)(2,1)S(1)} %shard_map.127.o0.own_ref), channel_id=1, source_target_pairs={{0,8},{4,12},{8,0},{12,4},{1,9},{5,13},{9,1},{13,5},{2,10},{6,14},... | collective-permute-start | bytes 221192 | tf_op jit(solution)/shard_map/ppermute | solution.py:423
  9.3 4.4 %shard_map.128 = (bf16[16,352,1024]{2,1,0:T(8,128)(2,1)S(1)}, f32[8,128]{1,0:T(8,128)S(1)}) custom-call(bf16[16,352,1024]{2,1,0:T(8,128)(2,1)} %bitcast.11), custom_call_target="tpu_custom_call" | custom-call | bytes 11534336 | tf_op jit(solution)/shard_map/pallas_call | solution.py:352
  13.7 1.2 %collective-permute-done.5.refs_2_ = bf16[144,256]{1,0:T(8,128)(2,1)S(1)} collective-permute-done((bf16[144,256]{1,0:T(8,128)(2,1)S(1)}, bf16[144,256]{1,0:T(8,128)(2,1)S(1)}, u32[]{:S(2)}, u32[]{:S(2)}) %collective-permute-start.5) | collective-permute-done | bytes 73760 | tf_op jit(solution)/shard_map/ppermute | solution.py:423
  15.6 0.9 %collective-permute-start.9 = (bf16[2,128,256]{2,1,0:T(8,128)(2,1)S(1)}, bf16[2,128,256]{2,1,0:T(8,128)(2,1)S(1)}, u32[]{:S(2)}, u32[]{:S(2)}) collective-permute-start(bf16[2,128,256]{2,1,0:T(8,128)(2,1)S(1)} %shard_map.131.later_ref.refs_0_.a0), channel_id=1, source_target_pairs={{0,4},{4,0},{8,12},{12,8},{1,5},{5,1},{9,13},{13,9},{2,6},{6,2},{1... | collective-permute-start | bytes 393224 | tf_op jit(solution)/shard_map/ppermute | solution.py:423
  16.5 4.4 %shard_map.130 = (bf16[16,352,1024]{2,1,0:T(8,128)(2,1)S(1)}, f32[8,128]{1,0:T(8,128)S(1)}) custom-call(bf16[16,352,1024]{2,1,0:T(8,128)(2,1)} %bitcast.12), custom_call_target="tpu_custom_call" | custom-call | bytes 11534336 | tf_op jit(solution)/shard_map/pallas_call | solution.py:352
  22.1 3.3 %collective-permute-start.11 = (bf16[2,128,256]{2,1,0:T(8,128)(2,1)S(1)}, bf16[2,128,256]{2,1,0:T(8,128)(2,1)S(1)}, u32[]{:S(2)}, u32[]{:S(2)}) collective-permute-start(bf16[2,128,256]{2,1,0:T(8,128)(2,1)S(1)} %shard_map.131.later_ref.refs_0_.a0), channel_id=1, source_target_pairs={{0,8},{4,12},{8,0},{12,4},{1,9},{5,13},{9,1},{13,5},{2,10},{6,14},... | collective-permute-start | bytes 393224 | tf_op jit(solution)/shard_map/ppermute | solution.py:423
  25.9 12.3 %shard_map.133 = (bf16[4,256,1024]{2,1,0:T(8,128)(2,1)S(1)}, bf16[16,64,1024]{2,1,0:T(8,128)(2,1)S(1)}, bf16[16,64,352]{2,1,0:T(8,128)(2,1)S(1)}, bf16[16,64,352...) custom-call(s32[64]{0:T(128)S(1)} %copy-done.1, ...), custom_call_target="tpu_custom_call" | custom-call | flops 2214592512 | bytes 69206016 | tf_op jit(solution)/shard_map/pallas_call | solution.py:387
  38.8 2.6 %collective-permute-done.13.came.near_ref = bf16[4,4,128,256]{3,2,1,0:T(8,128)(2,1)S(1)} collective-permute-done((bf16[4,4,128,256]{3,2,1,0:T(8,128)(2,1)S(1)}, bf16[4,4,128,256]{3,2,1,0:T(8,128)(2,1)S(1)}, u32[]{:S(2)}, u32[]{:S(2)}) %collective-permute-start.13) | collective-permute-done | bytes 1048608 | tf_op jit(solution)/shard_map/ppermute | solution.py:423
  41.6 1.4 %collective-permute-start.14 = (bf16[4,128,256]{2,1,0:T(8,128)(2,1)S(1)}, bf16[4,128,256]{2,1,0:T(8,128)(2,1)S(1)}, u32[]{:S(2)}, u32[]{:S(2)}) collective-permute-start(bf16[4,128,256]{2,1,0:T(8,128)(2,1)S(1)} %get-tuple-element.50), channel_id=1, source_target_pairs={{0,2},{1,3},{2,0},{3,1},{4,6},{5,7},{6,4},{7,5},{8,10},{9,11},{10,... | collective-permute-start | bytes 786440 | tf_op jit(solution)/shard_map/ppermute | solution.py:423
  43.0 17.1 %shard_map.138 = (bf16[4,256,1024]{2,1,0:T(8,128)(2,1)S(1)}, f32[16,64,128]{2,1,0:T(8,128)S(1)}, bf16[16,64,1024]{2,1,0:T(8,128)(2,1)}, bf16[16,64,352]{2,1,0:T(...) custom-call(bf16[2,128,256]{2,1,0:T(8,128)(2,1)S(1)} %shard_map.131.later_ref.refs_0_.a0, ...), custom_call_target="tpu_custom_call" | custom-call | flops 2952790016 | bytes 92274688 | tf_op jit(solution)/shard_map/pallas_call | solution.py:387
  60.9 3.1 %shard_map.140.refs_0_.refs_2_ = bf16[16,352,1024]{2,1,0:T(8,128)(2,1)} custom-call(bf16[16,64,352]{2,1,0:T(8,128)(2,1)S(1)} %get-tuple-element.64.refs_0_, bf16[16,64,1024]{2,1,0:T(8,128)(2,1)S(1)} %get-tuple-element.65.refs_1_), custom_call_target="tpu_custom_call" | custom-call | flops 369098752 | bytes 11534336 | tf_op jit(solution)/shard_map/pallas_call | solution.py:387
  64.2 0.8 collective-permute-start.19
  65.0 0.9 %collective-permute-start.15 = (bf16[128,256]{1,0:T(8,128)(2,1)S(1)}, bf16[128,256]{1,0:T(8,128)(2,1)S(1)}, u32[]{:S(2)}, u32[]{:S(2)}) collective-permute-start(bf16[128,256]{1,0:T(8,128)(2,1)S(1)} %get-tuple-element.52), channel_id=1, source_target_pairs={{0,4},{4,0},{8,12},{12,8},{1,5},{5,1},{9,13},{13,9},{2,6},{6,2},{1... | collective-permute-start | bytes 196616 | tf_op jit(solution)/shard_map/ppermute | solution.py:423
  65.9 3.0 %collective-permute-start.16 = (bf16[128,256]{1,0:T(8,128)(2,1)S(1)}, bf16[128,256]{1,0:T(8,128)(2,1)S(1)}, u32[]{:S(2)}, u32[]{:S(2)}) collective-permute-start(bf16[128,256]{1,0:T(8,128)(2,1)S(1)} %get-tuple-element.53), channel_id=1, source_target_pairs={{0,8},{4,12},{8,0},{12,4},{1,9},{5,13},{9,1},{13,5},{2,10},{6,14},... | collective-permute-start | bytes 196616 | tf_op jit(solution)/shard_map/ppermute | solution.py:423
  69.4 3.1 %shard_map.142.refs_0_ = bf16[16,352,1024]{2,1,0:T(8,128)(2,1)} custom-call(bf16[16,64,352]{2,1,0:T(8,128)(2,1)S(1)} %get-tuple-element.64.refs_0_, bf16[16,64,1024]{2,1,0:T(8,128)(2,1)S(1)} %get-tuple-element.65.refs_1_, bf16[16,352,1024]{2,1,0:T(8,128)(2,1)} %shard_map.140.refs_0_.refs_2_, ...), custom_call_target="tpu_custom_call", output_to_operand_aliasing={{}: (2, {})} | custom-call | flops 369098752 | bytes 11534336 | tf_op jit(solution)/shard_map/pallas_call | solution.py:387
  72.5 1.2 %collective-permute-done.19.came = bf16[4,144,256]{2,1,0:T(8,128)(2,1)S(1)} collective-permute-done((bf16[4,144,256]{2,1,0:T(8,128)(2,1)S(1)}, bf16[4,144,256]{2,1,0:T(8,128)(2,1)S(1)}, u32[]{:S(2)}, u32[]{:S(2)}) %collective-permute-start.19) | collective-permute-done | bytes 294944 | tf_op jit(solution)/shard_map/ppermute | solution.py:423
  73.9 3.0 %collective-permute-start.21 = (bf16[144,256]{1,0:T(8,128)(2,1)S(1)}, bf16[144,256]{1,0:T(8,128)(2,1)S(1)}, u32[]{:S(2)}, u32[]{:S(2)}) collective-permute-start(bf16[144,256]{1,0:T(8,128)(2,1)S(1)} %get-tuple-element.70), channel_id=1, source_target_pairs={{0,8},{4,12},{8,0},{12,4},{1,9},{5,13},{9,1},{13,5},{2,10},{6,14},... | collective-permute-start | bytes 221192 | tf_op jit(solution)/shard_map/ppermute | solution.py:423
  76.9 1.2 %collective-permute-start.22 = (bf16[144,256]{1,0:T(8,128)(2,1)S(1)}, bf16[144,256]{1,0:T(8,128)(2,1)S(1)}, u32[]{:S(2)}, u32[]{:S(2)}) collective-permute-start(bf16[144,256]{1,0:T(8,128)(2,1)S(1)} %get-tuple-element.71), channel_id=1, source_target_pairs={{0,12},{4,8},{8,4},{12,0},{1,13},{5,9},{9,5},{13,1},{2,14},{6,10},... | collective-permute-start | bytes 221192 | tf_op jit(solution)/shard_map/ppermute | solution.py:423
  78.2 0.7 shard_map.137
  78.9 5.1 %shard_map.145 = bf16[16,352,1024]{2,1,0:T(8,128)(2,1)} custom-call(bf16[16,64,352]{2,1,0:T(8,128)(2,1)S(1)} %get-tuple-element.74.refs_0_, bf16[16,64,1024]{2,1,0:T(8,128)(2,1)S(1)} %get-tuple-element.65.refs_1_, bf16[144,256]{1,0:T(8,128)(2,1)S(1)} %get-tuple-element.68.refs_0_.refs_2_), custom_call_target="tpu_custom_call" | custom-call | flops 738197504 | bytes 23068672 | tf_op jit(solution)/shard_map/pallas_call | solution.py:387
  84.0 0.7 shard_map.144
  (45 shorter events, 5.1 us)
Async XLA Ops:
  1.6 12.2 %collective-permute-start.1 = (bf16[144,256]{1,0:T(8,128)(2,1)S(1)}, bf16[144,256]{1,0:T(8,128)(2,1)S(1)}, u32[]{:S(2)}, u32[]{:S(2)}) collective-permute-start(bf16[144,256]{1,0:T(8,128)(2,1)S(1)} %shard_map.127.o0.own_ref), channel_id=1, source_target_pairs={{0,2},{1,3},{2,0},{3,1},{4,6},{5,7},{6,4},{7,5},{8,10},{9,11},{10,... | collective-permute-start | bytes 221192 | tf_op jit(solution)/shard_map/ppermute | solution.py:423
  4.6 9.2 %collective-permute-start.3 = (bf16[144,256]{1,0:T(8,128)(2,1)S(1)}, bf16[144,256]{1,0:T(8,128)(2,1)S(1)}, u32[]{:S(2)}, u32[]{:S(2)}) collective-permute-start(bf16[144,256]{1,0:T(8,128)(2,1)S(1)} %shard_map.127.o0.own_ref), channel_id=1, source_target_pairs={{0,4},{4,0},{8,12},{12,8},{1,5},{5,1},{9,13},{13,9},{2,6},{6,2},{1... | collective-permute-start | bytes 221192 | tf_op jit(solution)/shard_map/ppermute | solution.py:423
  6.1 7.6 %collective-permute-start.4 = (bf16[144,256]{1,0:T(8,128)(2,1)S(1)}, bf16[144,256]{1,0:T(8,128)(2,1)S(1)}, u32[]{:S(2)}, u32[]{:S(2)}) collective-permute-start(bf16[144,256]{1,0:T(8,128)(2,1)S(1)} %shard_map.127.o0.own_ref), channel_id=1, source_target_pairs={{0,8},{4,12},{8,0},{12,4},{1,9},{5,13},{9,1},{13,5},{2,10},{6,14},... | collective-permute-start | bytes 221192 | tf_op jit(solution)/shard_map/ppermute | solution.py:423
  8.7 6.3 %collective-permute-start.5 = (bf16[144,256]{1,0:T(8,128)(2,1)S(1)}, bf16[144,256]{1,0:T(8,128)(2,1)S(1)}, u32[]{:S(2)}, u32[]{:S(2)}) collective-permute-start(bf16[144,256]{1,0:T(8,128)(2,1)S(1)} %shard_map.127.o0.own_ref), channel_id=1, source_target_pairs={{0,12},{4,8},{8,4},{12,0},{1,13},{5,9},{9,5},{13,1},{2,14},{6,10},... | collective-permute-start | bytes 221192 | tf_op jit(solution)/shard_map/ppermute | solution.py:423
  9.0 4.8 %collective-permute-start.6 = (bf16[128,256]{1,0:T(8,128)(2,1)}, bf16[128,256]{1,0:T(8,128)(2,1)S(1)}, u32[]{:S(2)}, u32[]{:S(2)}) collective-permute-start(bf16[128,256]{1,0:T(8,128)(2,1)} %refs_0_.1), channel_id=1, source_target_pairs={{0,2},{1,3},{2,0},{3,1},{4,6},{5,7},{6,4},{7,5},{8,10},{9,11},{10,... | collective-permute-start | bytes 196616 | tf_op jit(solution)/shard_map/ppermute | solution.py:423
  9.3 16.6 %copy-start.1 = (s32[64]{0:T(128)S(1)}, s32[64]{0:T(128)}, u32[]{:S(2)}) copy-start(s32[64]{0:T(128)} %capacity_ref.1) | copy-start | bytes 772
  15.0 6.0 %collective-permute-start.8 = (bf16[3,144,256]{2,1,0:T(8,128)(2,1)S(1)}, bf16[3,144,256]{2,1,0:T(8,128)(2,1)S(1)}, u32[]{:S(2)}, u32[]{:S(2)}) collective-permute-start(bf16[3,144,256]{2,1,0:T(8,128)(2,1)S(1)} %shard_map.129.refs_2_.b0.info_ref), channel_id=1, source_target_pairs={{0,2},{1,3},{2,0},{3,1},{4,6},{5,7},{6,4},{7,5},{8,10},{9,11},{10,... | collective-permute-start | bytes 663560 | tf_op jit(solution)/shard_map/ppermute | solution.py:423
  15.6 5.4 %collective-permute-start.9 = (bf16[2,128,256]{2,1,0:T(8,128)(2,1)S(1)}, bf16[2,128,256]{2,1,0:T(8,128)(2,1)S(1)}, u32[]{:S(2)}, u32[]{:S(2)}) collective-permute-start(bf16[2,128,256]{2,1,0:T(8,128)(2,1)S(1)} %shard_map.131.later_ref.refs_0_.a0), channel_id=1, source_target_pairs={{0,4},{4,0},{8,12},{12,8},{1,5},{5,1},{9,13},{13,9},{2,6},{6,2},{1... | collective-permute-start | bytes 393224 | tf_op jit(solution)/shard_map/ppermute | solution.py:423
  20.9 5.0 %collective-permute-start.7 = (bf16[3,144,256]{2,1,0:T(8,128)(2,1)S(1)}, bf16[3,144,256]{2,1,0:T(8,128)(2,1)S(1)}, u32[]{:S(2)}, u32[]{:S(2)}) collective-permute-start(bf16[3,144,256]{2,1,0:T(8,128)(2,1)S(1)} %shard_map.129.refs_2_.b0.info_ref), channel_id=1, source_target_pairs={{0,1},{1,0},{2,3},{3,2},{4,5},{5,4},{6,7},{7,6},{8,9},{9,8},{10,11... | collective-permute-start | bytes 663560 | tf_op jit(solution)/shard_map/ppermute | solution.py:423
  21.0 4.8 %collective-permute-start.10 = (bf16[3,144,256]{2,1,0:T(8,128)(2,1)S(1)}, bf16[3,144,256]{2,1,0:T(8,128)(2,1)S(1)}, u32[]{:S(2)}, u32[]{:S(2)}) collective-permute-start(bf16[3,144,256]{2,1,0:T(8,128)(2,1)S(1)} %bitcast.8), channel_id=1, source_target_pairs={{0,1},{1,0},{2,3},{3,2},{4,5},{5,4},{6,7},{7,6},{8,9},{9,8},{10,11... | collective-permute-start | bytes 663560 | tf_op jit(solution)/shard_map/ppermute | solution.py:423
  21.6 3.8 %collective-permute-start = (bf16[144,256]{1,0:T(8,128)(2,1)S(1)}, bf16[144,256]{1,0:T(8,128)(2,1)S(1)}, u32[]{:S(2)}, u32[]{:S(2)}) collective-permute-start(bf16[144,256]{1,0:T(8,128)(2,1)S(1)} %shard_map.127.o0.own_ref), channel_id=1, source_target_pairs={{0,1},{1,0},{2,3},{3,2},{4,5},{5,4},{6,7},{7,6},{8,9},{9,8},{10,11... | collective-permute-start | bytes 221192 | tf_op jit(solution)/shard_map/ppermute | solution.py:423
  21.7 4.2 %collective-permute-start.2 = (bf16[144,256]{1,0:T(8,128)(2,1)S(1)}, bf16[144,256]{1,0:T(8,128)(2,1)S(1)}, u32[]{:S(2)}, u32[]{:S(2)}) collective-permute-start(bf16[144,256]{1,0:T(8,128)(2,1)S(1)} %collective-permute-done.1.refs_4_.o2), channel_id=1, source_target_pairs={{0,1},{1,0},{2,3},{3,2},{4,5},{5,4},{6,7},{7,6},{8,9},{9,8},{10,11... | collective-permute-start | bytes 221192 | tf_op jit(solution)/shard_map/ppermute | solution.py:423
  22.1 16.1 %collective-permute-start.11 = (bf16[2,128,256]{2,1,0:T(8,128)(2,1)S(1)}, bf16[2,128,256]{2,1,0:T(8,128)(2,1)S(1)}, u32[]{:S(2)}, u32[]{:S(2)}) collective-permute-start(bf16[2,128,256]{2,1,0:T(8,128)(2,1)S(1)} %shard_map.131.later_ref.refs_0_.a0), channel_id=1, source_target_pairs={{0,8},{4,12},{8,0},{12,4},{1,9},{5,13},{9,1},{13,5},{2,10},{6,14},... | collective-permute-start | bytes 393224 | tf_op jit(solution)/shard_map/ppermute | solution.py:423
  25.4 12.8 %collective-permute-start.12 = (bf16[2,128,256]{2,1,0:T(8,128)(2,1)S(1)}, bf16[2,128,256]{2,1,0:T(8,128)(2,1)S(1)}, u32[]{:S(2)}, u32[]{:S(2)}) collective-permute-start(bf16[2,128,256]{2,1,0:T(8,128)(2,1)S(1)} %shard_map.131.later_ref.refs_0_.a0), channel_id=1, source_target_pairs={{0,12},{4,8},{8,4},{12,0},{1,13},{5,9},{9,5},{13,1},{2,14},{6,10},... | collective-permute-start | bytes 393224 | tf_op jit(solution)/shard_map/ppermute | solution.py:423
  38.7 2.7 %collective-permute-start.13 = (bf16[4,4,128,256]{3,2,1,0:T(8,128)(2,1)S(1)}, bf16[4,4,128,256]{3,2,1,0:T(8,128)(2,1)S(1)}, u32[]{:S(2)}, u32[]{:S(2)}) collective-permute-start(bf16[4,4,128,256]{3,2,1,0:T(8,128)(2,1)S(1)} %get-tuple-element.48), channel_id=1, source_target_pairs={{0,1},{1,0},{2,3},{3,2},{4,5},{5,4},{6,7},{7,6},{8,9},{9,8},{10,11... | collective-permute-start | bytes 3145736 | tf_op jit(solution)/shard_map/ppermute | solution.py:423
  41.6 18.5 %collective-permute-start.14 = (bf16[4,128,256]{2,1,0:T(8,128)(2,1)S(1)}, bf16[4,128,256]{2,1,0:T(8,128)(2,1)S(1)}, u32[]{:S(2)}, u32[]{:S(2)}) collective-permute-start(bf16[4,128,256]{2,1,0:T(8,128)(2,1)S(1)} %get-tuple-element.50), channel_id=1, source_target_pairs={{0,2},{1,3},{2,0},{3,1},{4,6},{5,7},{6,4},{7,5},{8,10},{9,11},{10,... | collective-permute-start | bytes 786440 | tf_op jit(solution)/shard_map/ppermute | solution.py:423
  60.8 3.2 %collective-permute-start.18 = (bf16[2,4,144,256]{3,2,1,0:T(8,128)(2,1)S(1)}, bf16[2,4,144,256]{3,2,1,0:T(8,128)(2,1)S(1)}, u32[]{:S(2)}, u32[]{:S(2)}) collective-permute-start(bf16[2,4,144,256]{3,2,1,0:T(8,128)(2,1)S(1)} %get-tuple-element.63), channel_id=1, source_target_pairs={{0,1},{1,0},{2,3},{3,2},{4,5},{5,4},{6,7},{7,6},{8,9},{9,8},{10,11... | collective-permute-start | bytes 1769480 | tf_op jit(solution)/shard_map/ppermute | solution.py:423
  64.2 9.5 %collective-permute-start.19 = (bf16[4,144,256]{2,1,0:T(8,128)(2,1)S(1)}, bf16[4,144,256]{2,1,0:T(8,128)(2,1)S(1)}, u32[]{:S(2)}, u32[]{:S(2)}) collective-permute-start(bf16[4,144,256]{2,1,0:T(8,128)(2,1)S(1)} %get-tuple-element.67), channel_id=1, source_target_pairs={{0,2},{1,3},{2,0},{3,1},{4,6},{5,7},{6,4},{7,5},{8,10},{9,11},{10,... | collective-permute-start | bytes 884744 | tf_op jit(solution)/shard_map/ppermute | solution.py:423
  65.0 12.0 %collective-permute-start.15 = (bf16[128,256]{1,0:T(8,128)(2,1)S(1)}, bf16[128,256]{1,0:T(8,128)(2,1)S(1)}, u32[]{:S(2)}, u32[]{:S(2)}) collective-permute-start(bf16[128,256]{1,0:T(8,128)(2,1)S(1)} %get-tuple-element.52), channel_id=1, source_target_pairs={{0,4},{4,0},{8,12},{12,8},{1,5},{5,1},{9,13},{13,9},{2,6},{6,2},{1... | collective-permute-start | bytes 196616 | tf_op jit(solution)/shard_map/ppermute | solution.py:423
  65.9 12.3 %collective-permute-start.16 = (bf16[128,256]{1,0:T(8,128)(2,1)S(1)}, bf16[128,256]{1,0:T(8,128)(2,1)S(1)}, u32[]{:S(2)}, u32[]{:S(2)}) collective-permute-start(bf16[128,256]{1,0:T(8,128)(2,1)S(1)} %get-tuple-element.53), channel_id=1, source_target_pairs={{0,8},{4,12},{8,0},{12,4},{1,9},{5,13},{9,1},{13,5},{2,10},{6,14},... | collective-permute-start | bytes 196616 | tf_op jit(solution)/shard_map/ppermute | solution.py:423
  68.9 9.3 %collective-permute-start.17 = (bf16[128,256]{1,0:T(8,128)(2,1)S(1)}, bf16[128,256]{1,0:T(8,128)(2,1)S(1)}, u32[]{:S(2)}, u32[]{:S(2)}) collective-permute-start(bf16[128,256]{1,0:T(8,128)(2,1)S(1)} %get-tuple-element.54), channel_id=1, source_target_pairs={{0,12},{4,8},{8,4},{12,0},{1,13},{5,9},{9,5},{13,1},{2,14},{6,10},... | collective-permute-start | bytes 196616 | tf_op jit(solution)/shard_map/ppermute | solution.py:423
  73.7 10.2 %collective-permute-start.20 = (bf16[144,256]{1,0:T(8,128)(2,1)S(1)}, bf16[144,256]{1,0:T(8,128)(2,1)S(1)}, u32[]{:S(2)}, u32[]{:S(2)}) collective-permute-start(bf16[144,256]{1,0:T(8,128)(2,1)S(1)} %get-tuple-element.69), channel_id=1, source_target_pairs={{0,4},{4,0},{8,12},{12,8},{1,5},{5,1},{9,13},{13,9},{2,6},{6,2},{1... | collective-permute-start | bytes 221192 | tf_op jit(solution)/shard_map/ppermute | solution.py:423
  73.9 10.0 %collective-permute-start.21 = (bf16[144,256]{1,0:T(8,128)(2,1)S(1)}, bf16[144,256]{1,0:T(8,128)(2,1)S(1)}, u32[]{:S(2)}, u32[]{:S(2)}) collective-permute-start(bf16[144,256]{1,0:T(8,128)(2,1)S(1)} %get-tuple-element.70), channel_id=1, source_target_pairs={{0,8},{4,12},{8,0},{12,4},{1,9},{5,13},{9,1},{13,5},{2,10},{6,14},... | collective-permute-start | bytes 221192 | tf_op jit(solution)/shard_map/ppermute | solution.py:423
  76.9 7.0 %collective-permute-start.22 = (bf16[144,256]{1,0:T(8,128)(2,1)S(1)}, bf16[144,256]{1,0:T(8,128)(2,1)S(1)}, u32[]{:S(2)}, u32[]{:S(2)}) collective-permute-start(bf16[144,256]{1,0:T(8,128)(2,1)S(1)} %get-tuple-element.71), channel_id=1, source_target_pairs={{0,12},{4,8},{8,4},{12,0},{1,13},{5,9},{9,5},{13,1},{2,14},{6,10},... | collective-permute-start | bytes 221192 | tf_op jit(solution)/shard_map/ppermute | solution.py:423
  (1 other events, 15.0 us)

commit v10 on v9

--- a/solution.py
+++ b/solution.py
@@ -48,7 +48,7 @@
 
 def routing(info, choose, tokens):
     info = info.astype(F32)
-    return info[0:choose, 0:tokens], info[0:choose, tokens:2 * tokens], info[8:8 + choose, 0:tokens]
+    return info[0:choose, 0:tokens], info[0:choose, tokens:2 * tokens] + info[8:8 + choose, 0:tokens]
 
 
 def columns(me, mask, width):
@@ -62,8 +62,8 @@
             home[q // 2, s, 0:tokens, :] = tn(onehot[s], rows[s, :, columns(me, q, width)]).astype(BF16)
 
 
-RING = 6
-HELD = 4
+RING = 8
+GROUP = 4
 
 
 def ring(weight, slots, sems, columns=None):
@@ -104,7 +104,6 @@
     row = lax.broadcasted_iota(jnp.int32, (tokens, tokens), 0)
     col = lax.broadcasted_iota(jnp.int32, (tokens, tokens), 1)
     before = jnp.where(row < col, 1.0, 0.0).astype(BF16)
-    ones = jnp.ones((tokens, tokens), BF16)
     expert = lax.broadcasted_iota(jnp.int32, (experts, tokens), 0)
     mine = (first + expert).astype(F32)
     limit = jnp.zeros((experts, tokens), jnp.int32)
@@ -114,21 +113,19 @@
     place = lax.broadcasted_iota(jnp.int32, (experts, CAP, tokens), 1).astype(F32)
     for s in range(sources):
         block = [o[...] for o in (o0, o1, o2, o3)] if s == 0 else [b[s - 1] for b in (b0, b1, b2, b3)]
-        ids, highs, lows = routing(block[0][tokens:tokens + EXTRA, :], choose, tokens)
+        ids, gates = routing(block[0][tokens:tokens + EXTRA, :], choose, tokens)
         named = jnp.zeros((experts, tokens), F32)
-        high, low = named, named
+        gate = jnp.zeros((experts, tokens), F32)
         for k in range(choose):
             hit = ids[k:k + 1, :] == mine
             named = named + jnp.where(hit, 1.0, 0.0)
-            high = high + jnp.where(hit, highs[k:k + 1, :], 0.0)
-            low = low + jnp.where(hit, lows[k:k + 1, :], 0.0)
+            gate = gate + jnp.where(hit, gates[k:k + 1, :], 0.0)
         rank = nn(named.astype(BF16), before)
         rank = jnp.where((named > 0.5) & (rank < limit), rank, -1.0)
-        taken = rank[:, None, :] == place
-        spread = lambda x: jnp.where(taken, x[:, None, :], 0.0).reshape(slots, tokens).astype(BF16)
-        gates = nn(spread(high), ones) + nn(spread(low), ones)
-        slot_gate[:, s * CAP:(s + 1) * CAP, :] = gates.reshape(experts, CAP, tokens)
-        table = jnp.where(taken, 1.0, 0.0).reshape(slots, tokens).astype(BF16)
+        chosen = jnp.where(rank[:, None, :] == place, 1.0, 0.0)
+        gate_of = jnp.sum(chosen * gate[:, None, :], axis=2, keepdims=True)
+        slot_gate[:, s * CAP:(s + 1) * CAP, :] = jnp.broadcast_to(gate_of, chosen.shape)
+        table = chosen.reshape(slots, tokens).astype(BF16)
         onehot[s] = table
         for q in range(4):
             picked = nn(table, block[q][0:tokens, :]).astype(BF16).reshape(experts, CAP, width)
@@ -153,30 +150,30 @@
             out_rows[s, at, :] = out[s * CAP:(s + 1) * CAP]
 
     def both(e):
-        for i in (e - 2, e - 1):
+        before, now = [e - GROUP + i for i in range(GROUP)], [e + i for i in range(GROUP)]
+        for i in before:
             wait_down(i)
-        project(e - 2)
-        project(e - 1)
-        activate(e)
-        activate(e + 1)
-        for i in (e - 2, e - 1):
+        for i, j in zip(before, now):
+            activate(j)
+            project(i)
+        for i in before:
             start_down(i)
 
     skewed(experts, activate, wait_down, project, both)
 
 
 def skewed(experts, first, wait, second, both):
-    first(jnp.int32(0))
-    first(jnp.int32(1))
+    for e in range(GROUP):
+        first(jnp.int32(e))
 
     def turn(i, _):
-        both(i * 2)
+        both(i * GROUP)
         return 0
 
-    lax.fori_loop(1, experts // 2, turn, 0)
-    for e in (experts - 2, experts - 1):
+    lax.fori_loop(1, experts // GROUP, turn, 0)
+    for e in range(experts - GROUP, experts):
         wait(jnp.int32(e))
-    for e in (experts - 2, experts - 1):
+    for e in range(experts - GROUP, experts):
         second(jnp.int32(e))
 
 
@@ -198,7 +195,7 @@
     mine = (lax.axis_index("expert") * experts + expert).astype(F32)
     for s in range(sources):
         info = own_ref[tokens:tokens + EXTRA, :] if s == 0 else info_ref[s - 1, tokens:tokens + EXTRA, :]
-        ids, _, _ = routing(info, choose, tokens)
+        ids, _ = routing(info, choose, tokens)
         chosen = onehot[s].astype(F32).reshape(experts, CAP, tokens)
         share = jnp.sum(chosen * dots[:, s * CAP:(s + 1) * CAP, :], axis=1)
         values = [jnp.sum(jnp.where(ids[k:k + 1, :] == mine, share, 0.0), axis=0, keepdims=True) for k in range(choose)]
@@ -211,9 +208,9 @@
 
 def backward_kernel(
     a0, a1, a2, a3, near_ref,
-    gate_ref, up_ref, down_hbm, act_ref, a_ref, slope_ref, silu_ref, onehot, slot_gate, earlier_ref,
-    back_rows, dots, rows_ref, p_ref, q_ref, down_grad,
-    down_ref, held, down_sems, held_sems,
+    gate_ref, up_ref, down_hbm, act_ref, slope_ref, silu_ref, onehot, slot_gate, earlier_ref,
+    back_rows, dots, rows_ref, p_ref, q_ref,
+    down_ref, down_sems,
 ):
     sources, slots, tokens = onehot.shape
     experts = slots // CAP
@@ -234,12 +231,7 @@
         p_ref[e] = (grad * slope_ref[e]).astype(BF16)
         q_ref[e] = (grad * silu_ref[e]).astype(BF16)
 
-    def store(e):
-        slot = lax.rem(e, HELD)
-        return pltpu.make_async_copy(held.at[slot], down_grad.at[e], held_sems.at[slot])
-
     def project(e):
-        held[lax.rem(e, HELD)] = tn(a_ref[e], rows_ref[e]).astype(BF16)
         back = nn(p_ref[e], gate_ref[e]) + nn(q_ref[e], up_ref[e])
         back = (back * slot_gate[e][:, 0:1]).astype(BF16)
         at = pl.ds(pl.multiple_of(e * CAP, CAP), CAP)
@@ -252,28 +244,16 @@
         start_down(e)
 
     def both(e):
-        for i in (e, e + 1):
+        before, now = [e - GROUP + i for i in range(GROUP)], [e + i for i in range(GROUP)]
+        for i in now:
             wait_down(i)
-
-        @pl.when(e - 2 >= HELD)
-        def _():
-            for i in (e - 2, e - 1):
-                store(i - HELD).wait()
-
-        project(e - 2)
-        project(e - 1)
-        slopes(e)
-        slopes(e + 1)
-        for i in (e - 2, e - 1):
-            store(i).start()
-        for i in (e, e + 1):
+        for i, j in zip(before, now):
+            slopes(j)
+            project(i)
+        for i in now:
             start_down(i)
 
-    skewed(experts, first, lambda e: store(e - HELD).wait(), project, both)
-    for e in (experts - 2, experts - 1):
-        store(jnp.int32(e)).start()
-    for e in range(experts - HELD, experts):
-        store(jnp.int32(e)).wait()
+    skewed(experts, first, lambda e: None, project, both)
 
 
 def add_kernel(keep, came, *refs):
@@ -484,7 +464,7 @@
         ],
         [pltpu.VMEM((RING, units, model), BF16), pltpu.SemaphoreType.DMA((RING,))],
         3 * product,
-        limit=9,
+        limit=10,
         in_hbm=(11,),
     )(
         capacity_blocks,
@@ -502,7 +482,7 @@
     )(onehot, out_rows, *grads)
     near = swap(send, 1)
     out_near, out_far = add_cores(keep, near)
-    back_rows, dots, y_rows, gate_part, up_part, down_grad = kernel_call(
+    back_rows, dots, y_rows, gate_part, up_part = kernel_call(
         backward_kernel,
         [
             held(sources, slots, model),
@@ -510,21 +490,14 @@
             held(local_experts, rows, model),
             held(local_experts, rows, units),
             held(local_experts, rows, units),
-            sent(local_experts, units, model),
         ],
-        [
-            pltpu.VMEM((RING, units, model), BF16),
-            pltpu.VMEM((HELD, units, model), BF16),
-            pltpu.SemaphoreType.DMA((RING,)),
-            pltpu.SemaphoreType.DMA((HELD,)),
-        ],
-        4 * product,
-        out_specs=[pl.BlockSpec(memory_space=pltpu.VMEM)] * 5 + [pl.BlockSpec(memory_space=pltpu.HBM)],
+        [pltpu.VMEM((RING, units, model), BF16), pltpu.SemaphoreType.DMA((RING,))],
+        3 * product,
         limit=13,
         in_hbm=(7,),
     )(
         *grads, near,
-        gate_t, up_t, down_weight, activ, scaled, slope, silu, onehot, slot_gate, out_near,
+        gate_t, up_t, down_weight, activ, slope, silu, onehot, slot_gate, out_near,
     )
 
     out_own, out_parts = add_chips(out_near, swap(out_far, 2))
@@ -535,10 +508,9 @@
         2 * slots * sources * tokens * model,
         limit=2,
     )(onehot, back_rows, dots, own, came, out_own)
-    some = local_experts // 2
-    (up_grad,) = weight_grads([(up_part, x_rows, 0, some)])
-    back_near, back_far = add_cores(keep, swap(send, 1), up_grad)
-    (up_grad,) = weight_grads([(up_part, x_rows, some, local_experts)], up_grad, back_near)
+    (down_grad,) = weight_grads([(scaled, y_rows, 0, local_experts)])
+    back_near, back_far = add_cores(keep, swap(send, 1), down_grad)
+    (up_grad,) = weight_grads([(up_part, x_rows, 0, local_experts)], None, back_near)
     (layer_out,) = kernel_call(functools.partial(total_kernel, sources), [sent(tokens, width)], [], 0, limit=2)(
         out_own, *out_parts
     )

time: 84.8 us -> 81.9 us (0.966)
  Pallas kernels: 53.4 us -> 51.6 us
  waiting for transfers between devices: 5.09 us -> 3.95 us
    pallas_call x17, Pallas kernels: 44.6 us -> 42.8 us  [call(): pl.pallas_call(kernel, in_specs=specs, out_specs=out_specs or [pl.BlockSp...]
    ppermute x23, waiting for transfers between devices: 5.09 us -> 3.95 us  [swap(): return lax.ppermute(array, axis, [(i, i ^ bit) for i in range(count)])]
  transfers between devices with their start and end apart: 23 -> 23, of which waited for: 3 -> 2; matrix products, arithmetic and copies ran while one was open for 0% -> 0% of each run, Pallas kernels for 60% -> 59%
where the time goes in v10:
time: 81.9 us; the launch traced here: 81.7 us
  Pallas kernels  51.6 us (63%)
  starting transfers between devices  25.2 us (31%)
  waiting for transfers between devices  3.95 us (5%)
  between operations  0.91 us (1%)
    pallas_call x17, Pallas kernels, call(): pl.pallas_call(kernel, in_specs=specs, out_specs=out_specs or [pl.BlockSp...  42.8 us
    ppermute x23, starting transfers between devices, swap(): return lax.ppermute(array, axis, [(i, i ^ bit) for i in range(count)])  25.2 us
    pallas_call x2, Pallas kernels, in_vmem(): pl.pallas_call(load_kernel, in_specs=[pl.BlockSpec(memory_space=pltpu.HBM...  8.84 us
    ppermute x23, waiting for transfers between devices, swap(): return lax.ppermute(array, axis, [(i, i ^ bit) for i in range(count)])  3.95 us
  transfers between devices with their start and end apart: 23, of which 2 were waited for; matrix products, arithmetic and copies ran while one was open for 0% of the time, Pallas kernels for 59%

profile of v10, /device:TPU:0, one launch (start us, length us, event | category | flops | bytes accessed | tf_op | source)
XLA Modules:
  0.0 81.7 jit_solution(17411179899581988064)
XLA Ops:
  0.6 0.9 %shard_map.127.o0.own_ref = bf16[144,256]{1,0:T(8,128)(2,1)S(1)} custom-call(bf16[128,256]{1,0:T(8,128)(2,1)} %hidden_hbm.1, s32[6,128]{1,0:T(8,128)} %bitcast.14, f32[6,128]{1,0:T(8,128)} %bitcast.15), custom_call_target="tpu_custom_call" | custom-call | tf_op jit(solution)/shard_map/pallas_call | solution.py:367
  1.6 3.0 %collective-permute-start.1 = (bf16[144,256]{1,0:T(8,128)(2,1)S(1)}, bf16[144,256]{1,0:T(8,128)(2,1)S(1)}, u32[]{:S(2)}, u32[]{:S(2)}) collective-permute-start(bf16[144,256]{1,0:T(8,128)(2,1)S(1)} %shard_map.127.o0.own_ref), channel_id=1, source_target_pairs={{0,2},{1,3},{2,0},{3,1},{4,6},{5,7},{6,4},{7,5},{8,10},{9,11},{10,... | collective-permute-start | bytes 221192 | tf_op jit(solution)/shard_map/ppermute | solution.py:403
  4.6 1.6 %collective-permute-start.3 = (bf16[144,256]{1,0:T(8,128)(2,1)S(1)}, bf16[144,256]{1,0:T(8,128)(2,1)S(1)}, u32[]{:S(2)}, u32[]{:S(2)}) collective-permute-start(bf16[144,256]{1,0:T(8,128)(2,1)S(1)} %shard_map.127.o0.own_ref), channel_id=1, source_target_pairs={{0,4},{4,0},{8,12},{12,8},{1,5},{5,1},{9,13},{13,9},{2,6},{6,2},{1... | collective-permute-start | bytes 221192 | tf_op jit(solution)/shard_map/ppermute | solution.py:403
  6.1 2.6 %collective-permute-start.4 = (bf16[144,256]{1,0:T(8,128)(2,1)S(1)}, bf16[144,256]{1,0:T(8,128)(2,1)S(1)}, u32[]{:S(2)}, u32[]{:S(2)}) collective-permute-start(bf16[144,256]{1,0:T(8,128)(2,1)S(1)} %shard_map.127.o0.own_ref), channel_id=1, source_target_pairs={{0,8},{4,12},{8,0},{12,4},{1,9},{5,13},{9,1},{13,5},{2,10},{6,14},... | collective-permute-start | bytes 221192 | tf_op jit(solution)/shard_map/ppermute | solution.py:403
  9.3 4.4 %shard_map.128 = (bf16[16,352,1024]{2,1,0:T(8,128)(2,1)S(1)}, f32[8,128]{1,0:T(8,128)S(1)}) custom-call(bf16[16,352,1024]{2,1,0:T(8,128)(2,1)} %bitcast.11), custom_call_target="tpu_custom_call" | custom-call | bytes 11534336 | tf_op jit(solution)/shard_map/pallas_call | solution.py:332
  13.7 1.2 %collective-permute-done.5.refs_2_ = bf16[144,256]{1,0:T(8,128)(2,1)S(1)} collective-permute-done((bf16[144,256]{1,0:T(8,128)(2,1)S(1)}, bf16[144,256]{1,0:T(8,128)(2,1)S(1)}, u32[]{:S(2)}, u32[]{:S(2)}) %collective-permute-start.5) | collective-permute-done | bytes 73760 | tf_op jit(solution)/shard_map/ppermute | solution.py:403
  15.0 0.6 collective-permute-start.8
  15.6 0.9 %collective-permute-start.9 = (bf16[2,128,256]{2,1,0:T(8,128)(2,1)S(1)}, bf16[2,128,256]{2,1,0:T(8,128)(2,1)S(1)}, u32[]{:S(2)}, u32[]{:S(2)}) collective-permute-start(bf16[2,128,256]{2,1,0:T(8,128)(2,1)S(1)} %shard_map.131.later_ref.refs_0_.a0), channel_id=1, source_target_pairs={{0,4},{4,0},{8,12},{12,8},{1,5},{5,1},{9,13},{13,9},{2,6},{6,2},{1... | collective-permute-start | bytes 393224 | tf_op jit(solution)/shard_map/ppermute | solution.py:403
  16.5 4.4 %shard_map.130 = (bf16[16,352,1024]{2,1,0:T(8,128)(2,1)S(1)}, f32[8,128]{1,0:T(8,128)S(1)}) custom-call(bf16[16,352,1024]{2,1,0:T(8,128)(2,1)} %bitcast.12), custom_call_target="tpu_custom_call" | custom-call | bytes 11534336 | tf_op jit(solution)/shard_map/pallas_call | solution.py:332
  22.1 3.3 %collective-permute-start.11 = (bf16[2,128,256]{2,1,0:T(8,128)(2,1)S(1)}, bf16[2,128,256]{2,1,0:T(8,128)(2,1)S(1)}, u32[]{:S(2)}, u32[]{:S(2)}) collective-permute-start(bf16[2,128,256]{2,1,0:T(8,128)(2,1)S(1)} %shard_map.131.later_ref.refs_0_.a0), channel_id=1, source_target_pairs={{0,8},{4,12},{8,0},{12,4},{1,9},{5,13},{9,1},{13,5},{2,10},{6,14},... | collective-permute-start | bytes 393224 | tf_op jit(solution)/shard_map/ppermute | solution.py:403
  25.9 11.8 %shard_map.133 = (bf16[4,256,1024]{2,1,0:T(8,128)(2,1)S(1)}, bf16[16,64,1024]{2,1,0:T(8,128)(2,1)S(1)}, bf16[16,64,352]{2,1,0:T(8,128)(2,1)S(1)}, bf16[16,64,352...) custom-call(s32[64]{0:T(128)S(1)} %copy-done.1, ...), custom_call_target="tpu_custom_call" | custom-call | flops 2214592512 | bytes 69206016 | tf_op jit(solution)/shard_map/pallas_call | solution.py:367
  38.3 2.6 %collective-permute-done.13.came.near_ref = bf16[4,4,128,256]{3,2,1,0:T(8,128)(2,1)S(1)} collective-permute-done((bf16[4,4,128,256]{3,2,1,0:T(8,128)(2,1)S(1)}, bf16[4,4,128,256]{3,2,1,0:T(8,128)(2,1)S(1)}, u32[]{:S(2)}, u32[]{:S(2)}) %collective-permute-start.13) | collective-permute-done | bytes 1048608 | tf_op jit(solution)/shard_map/ppermute | solution.py:403
  41.1 1.4 %collective-permute-start.14 = (bf16[4,128,256]{2,1,0:T(8,128)(2,1)S(1)}, bf16[4,128,256]{2,1,0:T(8,128)(2,1)S(1)}, u32[]{:S(2)}, u32[]{:S(2)}) collective-permute-start(bf16[4,128,256]{2,1,0:T(8,128)(2,1)S(1)} %get-tuple-element.50), channel_id=1, source_target_pairs={{0,2},{1,3},{2,0},{3,1},{4,6},{5,7},{6,4},{7,5},{8,10},{9,11},{10,... | collective-permute-start | bytes 786440 | tf_op jit(solution)/shard_map/ppermute | solution.py:403
  42.4 11.8 %shard_map.138 = (bf16[4,256,1024]{2,1,0:T(8,128)(2,1)S(1)}, f32[16,64,128]{2,1,0:T(8,128)S(1)}, bf16[16,64,1024]{2,1,0:T(8,128)(2,1)S(1)}, bf16[16,64,352]{2,1,0:T(8,128)(2,1)S(1)}, bf16[16,64,352]{2,1,0:T(8,128)(2,1)S(1)}) custom-call(bf16[2,128,256]{2,1,0:T(8,128)(2,1)S(1)} %shard_map.131.later_ref.refs_0_.a0, ...), custom_call_target="tpu_custom_call" | custom-call | flops 2214592512 | bytes 69206016 | tf_op jit(solution)/shard_map/pallas_call | solution.py:367
  54.3 0.6 shard_map.139
  55.0 5.1 %shard_map.140.refs_0_ = bf16[16,352,1024]{2,1,0:T(8,128)(2,1)} custom-call(bf16[16,64,352]{2,1,0:T(8,128)(2,1)S(1)} %get-tuple-element.63.refs_0_, bf16[16,64,1024]{2,1,0:T(8,128)(2,1)S(1)} %get-tuple-element.64.refs_1_), custom_call_target="tpu_custom_call" | custom-call | flops 738197504 | bytes 23068672 | tf_op jit(solution)/shard_map/pallas_call | solution.py:367
  60.2 0.8 collective-permute-start.19
  61.0 0.9 %collective-permute-start.15 = (bf16[128,256]{1,0:T(8,128)(2,1)S(1)}, bf16[128,256]{1,0:T(8,128)(2,1)S(1)}, u32[]{:S(2)}, u32[]{:S(2)}) collective-permute-start(bf16[128,256]{1,0:T(8,128)(2,1)S(1)} %get-tuple-element.52), channel_id=1, source_target_pairs={{0,4},{4,0},{8,12},{12,8},{1,5},{5,1},{9,13},{13,9},{2,6},{6,2},{1... | collective-permute-start | bytes 196616 | tf_op jit(solution)/shard_map/ppermute | solution.py:403
  61.9 3.0 %collective-permute-start.16 = (bf16[128,256]{1,0:T(8,128)(2,1)S(1)}, bf16[128,256]{1,0:T(8,128)(2,1)S(1)}, u32[]{:S(2)}, u32[]{:S(2)}) collective-permute-start(bf16[128,256]{1,0:T(8,128)(2,1)S(1)} %get-tuple-element.53), channel_id=1, source_target_pairs={{0,8},{4,12},{8,0},{12,4},{1,9},{5,13},{9,1},{13,5},{2,10},{6,14},... | collective-permute-start | bytes 196616 | tf_op jit(solution)/shard_map/ppermute | solution.py:403
  65.4 5.3 %shard_map.142.refs_0_ = bf16[16,352,1024]{2,1,0:T(8,128)(2,1)} custom-call(bf16[16,64,352]{2,1,0:T(8,128)(2,1)S(1)} %get-tuple-element.67.refs_0_, bf16[16,64,1024]{2,1,0:T(8,128)(2,1)S(1)} %get-tuple-element.68.refs_1_, bf16[4,144,256]{2,1,0:T(8,128)(2,1)S(1)} %get-tuple-element.65.refs_2_.near), custom_call_target="tpu_custom_call" | custom-call | flops 738197504 | bytes 23068672 | tf_op jit(solution)/shard_map/pallas_call | solution.py:367
  71.0 3.8 %collective-permute-start.21 = (bf16[144,256]{1,0:T(8,128)(2,1)S(1)}, bf16[144,256]{1,0:T(8,128)(2,1)S(1)}, u32[]{:S(2)}, u32[]{:S(2)}) collective-permute-start(bf16[144,256]{1,0:T(8,128)(2,1)S(1)} %get-tuple-element.71), channel_id=1, source_target_pairs={{0,8},{4,12},{8,0},{12,4},{1,9},{5,13},{9,1},{13,5},{2,10},{6,14},... | collective-permute-start | bytes 221192 | tf_op jit(solution)/shard_map/ppermute | solution.py:403
  75.3 0.7 shard_map.137
  75.9 5.1 %shard_map.145 = bf16[16,352,1024]{2,1,0:T(8,128)(2,1)} custom-call(bf16[16,64,352]{2,1,0:T(8,128)(2,1)S(1)} %get-tuple-element.75.refs_0_, bf16[16,64,1024]{2,1,0:T(8,128)(2,1)S(1)} %get-tuple-element.68.refs_1_, bf16[144,256]{1,0:T(8,128)(2,1)S(1)} %get-tuple-element.69.refs_0_.refs_2_), custom_call_target="tpu_custom_call" | custom-call | flops 738197504 | bytes 23068672 | tf_op jit(solution)/shard_map/pallas_call | solution.py:367
  81.0 0.7 shard_map.144
  (45 shorter events, 4.4 us)
Async XLA Ops:
  1.6 12.2 %collective-permute-start.1 = (bf16[144,256]{1,0:T(8,128)(2,1)S(1)}, bf16[144,256]{1,0:T(8,128)(2,1)S(1)}, u32[]{:S(2)}, u32[]{:S(2)}) collective-permute-start(bf16[144,256]{1,0:T(8,128)(2,1)S(1)} %shard_map.127.o0.own_ref), channel_id=1, source_target_pairs={{0,2},{1,3},{2,0},{3,1},{4,6},{5,7},{6,4},{7,5},{8,10},{9,11},{10,... | collective-permute-start | bytes 221192 | tf_op jit(solution)/shard_map/ppermute | solution.py:403
  4.6 9.2 %collective-permute-start.3 = (bf16[144,256]{1,0:T(8,128)(2,1)S(1)}, bf16[144,256]{1,0:T(8,128)(2,1)S(1)}, u32[]{:S(2)}, u32[]{:S(2)}) collective-permute-start(bf16[144,256]{1,0:T(8,128)(2,1)S(1)} %shard_map.127.o0.own_ref), channel_id=1, source_target_pairs={{0,4},{4,0},{8,12},{12,8},{1,5},{5,1},{9,13},{13,9},{2,6},{6,2},{1... | collective-permute-start | bytes 221192 | tf_op jit(solution)/shard_map/ppermute | solution.py:403
  6.1 7.6 %collective-permute-start.4 = (bf16[144,256]{1,0:T(8,128)(2,1)S(1)}, bf16[144,256]{1,0:T(8,128)(2,1)S(1)}, u32[]{:S(2)}, u32[]{:S(2)}) collective-permute-start(bf16[144,256]{1,0:T(8,128)(2,1)S(1)} %shard_map.127.o0.own_ref), channel_id=1, source_target_pairs={{0,8},{4,12},{8,0},{12,4},{1,9},{5,13},{9,1},{13,5},{2,10},{6,14},... | collective-permute-start | bytes 221192 | tf_op jit(solution)/shard_map/ppermute | solution.py:403
  8.7 6.3 %collective-permute-start.5 = (bf16[144,256]{1,0:T(8,128)(2,1)S(1)}, bf16[144,256]{1,0:T(8,128)(2,1)S(1)}, u32[]{:S(2)}, u32[]{:S(2)}) collective-permute-start(bf16[144,256]{1,0:T(8,128)(2,1)S(1)} %shard_map.127.o0.own_ref), channel_id=1, source_target_pairs={{0,12},{4,8},{8,4},{12,0},{1,13},{5,9},{9,5},{13,1},{2,14},{6,10},... | collective-permute-start | bytes 221192 | tf_op jit(solution)/shard_map/ppermute | solution.py:403
  9.0 4.8 %collective-permute-start.6 = (bf16[128,256]{1,0:T(8,128)(2,1)}, bf16[128,256]{1,0:T(8,128)(2,1)S(1)}, u32[]{:S(2)}, u32[]{:S(2)}) collective-permute-start(bf16[128,256]{1,0:T(8,128)(2,1)} %refs_0_.1), channel_id=1, source_target_pairs={{0,2},{1,3},{2,0},{3,1},{4,6},{5,7},{6,4},{7,5},{8,10},{9,11},{10,... | collective-permute-start | bytes 196616 | tf_op jit(solution)/shard_map/ppermute | solution.py:403
  9.3 16.6 %copy-start.1 = (s32[64]{0:T(128)S(1)}, s32[64]{0:T(128)}, u32[]{:S(2)}) copy-start(s32[64]{0:T(128)} %capacity_ref.1) | copy-start | bytes 772
  15.0 6.0 %collective-permute-start.8 = (bf16[3,144,256]{2,1,0:T(8,128)(2,1)S(1)}, bf16[3,144,256]{2,1,0:T(8,128)(2,1)S(1)}, u32[]{:S(2)}, u32[]{:S(2)}) collective-permute-start(bf16[3,144,256]{2,1,0:T(8,128)(2,1)S(1)} %shard_map.129.refs_2_.b0.info_ref), channel_id=1, source_target_pairs={{0,2},{1,3},{2,0},{3,1},{4,6},{5,7},{6,4},{7,5},{8,10},{9,11},{10,... | collective-permute-start | bytes 663560 | tf_op jit(solution)/shard_map/ppermute | solution.py:403
  15.6 5.4 %collective-permute-start.9 = (bf16[2,128,256]{2,1,0:T(8,128)(2,1)S(1)}, bf16[2,128,256]{2,1,0:T(8,128)(2,1)S(1)}, u32[]{:S(2)}, u32[]{:S(2)}) collective-permute-start(bf16[2,128,256]{2,1,0:T(8,128)(2,1)S(1)} %shard_map.131.later_ref.refs_0_.a0), channel_id=1, source_target_pairs={{0,4},{4,0},{8,12},{12,8},{1,5},{5,1},{9,13},{13,9},{2,6},{6,2},{1... | collective-permute-start | bytes 393224 | tf_op jit(solution)/shard_map/ppermute | solution.py:403
  20.9 5.0 %collective-permute-start.7 = (bf16[3,144,256]{2,1,0:T(8,128)(2,1)S(1)}, bf16[3,144,256]{2,1,0:T(8,128)(2,1)S(1)}, u32[]{:S(2)}, u32[]{:S(2)}) collective-permute-start(bf16[3,144,256]{2,1,0:T(8,128)(2,1)S(1)} %shard_map.129.refs_2_.b0.info_ref), channel_id=1, source_target_pairs={{0,1},{1,0},{2,3},{3,2},{4,5},{5,4},{6,7},{7,6},{8,9},{9,8},{10,11... | collective-permute-start | bytes 663560 | tf_op jit(solution)/shard_map/ppermute | solution.py:403
  21.0 4.8 %collective-permute-start.10 = (bf16[3,144,256]{2,1,0:T(8,128)(2,1)S(1)}, bf16[3,144,256]{2,1,0:T(8,128)(2,1)S(1)}, u32[]{:S(2)}, u32[]{:S(2)}) collective-permute-start(bf16[3,144,256]{2,1,0:T(8,128)(2,1)S(1)} %bitcast.8), channel_id=1, source_target_pairs={{0,1},{1,0},{2,3},{3,2},{4,5},{5,4},{6,7},{7,6},{8,9},{9,8},{10,11... | collective-permute-start | bytes 663560 | tf_op jit(solution)/shard_map/ppermute | solution.py:403
  21.6 3.8 %collective-permute-start = (bf16[144,256]{1,0:T(8,128)(2,1)S(1)}, bf16[144,256]{1,0:T(8,128)(2,1)S(1)}, u32[]{:S(2)}, u32[]{:S(2)}) collective-permute-start(bf16[144,256]{1,0:T(8,128)(2,1)S(1)} %shard_map.127.o0.own_ref), channel_id=1, source_target_pairs={{0,1},{1,0},{2,3},{3,2},{4,5},{5,4},{6,7},{7,6},{8,9},{9,8},{10,11... | collective-permute-start | bytes 221192 | tf_op jit(solution)/shard_map/ppermute | solution.py:403
  21.7 4.2 %collective-permute-start.2 = (bf16[144,256]{1,0:T(8,128)(2,1)S(1)}, bf16[144,256]{1,0:T(8,128)(2,1)S(1)}, u32[]{:S(2)}, u32[]{:S(2)}) collective-permute-start(bf16[144,256]{1,0:T(8,128)(2,1)S(1)} %collective-permute-done.1.refs_4_.o2), channel_id=1, source_target_pairs={{0,1},{1,0},{2,3},{3,2},{4,5},{5,4},{6,7},{7,6},{8,9},{9,8},{10,11... | collective-permute-start | bytes 221192 | tf_op jit(solution)/shard_map/ppermute | solution.py:403
  22.1 15.6 %collective-permute-start.11 = (bf16[2,128,256]{2,1,0:T(8,128)(2,1)S(1)}, bf16[2,128,256]{2,1,0:T(8,128)(2,1)S(1)}, u32[]{:S(2)}, u32[]{:S(2)}) collective-permute-start(bf16[2,128,256]{2,1,0:T(8,128)(2,1)S(1)} %shard_map.131.later_ref.refs_0_.a0), channel_id=1, source_target_pairs={{0,8},{4,12},{8,0},{12,4},{1,9},{5,13},{9,1},{13,5},{2,10},{6,14},... | collective-permute-start | bytes 393224 | tf_op jit(solution)/shard_map/ppermute | solution.py:403
  25.4 12.3 %collective-permute-start.12 = (bf16[2,128,256]{2,1,0:T(8,128)(2,1)S(1)}, bf16[2,128,256]{2,1,0:T(8,128)(2,1)S(1)}, u32[]{:S(2)}, u32[]{:S(2)}) collective-permute-start(bf16[2,128,256]{2,1,0:T(8,128)(2,1)S(1)} %shard_map.131.later_ref.refs_0_.a0), channel_id=1, source_target_pairs={{0,12},{4,8},{8,4},{12,0},{1,13},{5,9},{9,5},{13,1},{2,14},{6,10},... | collective-permute-start | bytes 393224 | tf_op jit(solution)/shard_map/ppermute | solution.py:403
  38.2 2.7 %collective-permute-start.13 = (bf16[4,4,128,256]{3,2,1,0:T(8,128)(2,1)S(1)}, bf16[4,4,128,256]{3,2,1,0:T(8,128)(2,1)S(1)}, u32[]{:S(2)}, u32[]{:S(2)}) collective-permute-start(bf16[4,4,128,256]{3,2,1,0:T(8,128)(2,1)S(1)} %get-tuple-element.48), channel_id=1, source_target_pairs={{0,1},{1,0},{2,3},{3,2},{4,5},{5,4},{6,7},{7,6},{8,9},{9,8},{10,11... | collective-permute-start | bytes 3145736 | tf_op jit(solution)/shard_map/ppermute | solution.py:403
  41.1 13.1 %collective-permute-start.14 = (bf16[4,128,256]{2,1,0:T(8,128)(2,1)S(1)}, bf16[4,128,256]{2,1,0:T(8,128)(2,1)S(1)}, u32[]{:S(2)}, u32[]{:S(2)}) collective-permute-start(bf16[4,128,256]{2,1,0:T(8,128)(2,1)S(1)} %get-tuple-element.50), channel_id=1, source_target_pairs={{0,2},{1,3},{2,0},{3,1},{4,6},{5,7},{6,4},{7,5},{8,10},{9,11},{10,... | collective-permute-start | bytes 786440 | tf_op jit(solution)/shard_map/ppermute | solution.py:403
  54.9 5.2 %collective-permute-start.18 = (bf16[2,4,144,256]{3,2,1,0:T(8,128)(2,1)S(1)}, bf16[2,4,144,256]{3,2,1,0:T(8,128)(2,1)S(1)}, u32[]{:S(2)}, u32[]{:S(2)}) collective-permute-start(bf16[2,4,144,256]{3,2,1,0:T(8,128)(2,1)S(1)} %get-tuple-element.62), channel_id=1, source_target_pairs={{0,1},{1,0},{2,3},{3,2},{4,5},{5,4},{6,7},{7,6},{8,9},{9,8},{10,11... | collective-permute-start | bytes 1769480 | tf_op jit(solution)/shard_map/ppermute | solution.py:403
  60.2 10.5 %collective-permute-start.19 = (bf16[4,144,256]{2,1,0:T(8,128)(2,1)S(1)}, bf16[4,144,256]{2,1,0:T(8,128)(2,1)S(1)}, u32[]{:S(2)}, u32[]{:S(2)}) collective-permute-start(bf16[4,144,256]{2,1,0:T(8,128)(2,1)S(1)} %get-tuple-element.66), channel_id=1, source_target_pairs={{0,2},{1,3},{2,0},{3,1},{4,6},{5,7},{6,4},{7,5},{8,10},{9,11},{10,... | collective-permute-start | bytes 884744 | tf_op jit(solution)/shard_map/ppermute | solution.py:403
  61.0 13.8 %collective-permute-start.15 = (bf16[128,256]{1,0:T(8,128)(2,1)S(1)}, bf16[128,256]{1,0:T(8,128)(2,1)S(1)}, u32[]{:S(2)}, u32[]{:S(2)}) collective-permute-start(bf16[128,256]{1,0:T(8,128)(2,1)S(1)} %get-tuple-element.52), channel_id=1, source_target_pairs={{0,4},{4,0},{8,12},{12,8},{1,5},{5,1},{9,13},{13,9},{2,6},{6,2},{1... | collective-permute-start | bytes 196616 | tf_op jit(solution)/shard_map/ppermute | solution.py:403
  61.9 13.4 %collective-permute-start.16 = (bf16[128,256]{1,0:T(8,128)(2,1)S(1)}, bf16[128,256]{1,0:T(8,128)(2,1)S(1)}, u32[]{:S(2)}, u32[]{:S(2)}) collective-permute-start(bf16[128,256]{1,0:T(8,128)(2,1)S(1)} %get-tuple-element.53), channel_id=1, source_target_pairs={{0,8},{4,12},{8,0},{12,4},{1,9},{5,13},{9,1},{13,5},{2,10},{6,14},... | collective-permute-start | bytes 196616 | tf_op jit(solution)/shard_map/ppermute | solution.py:403
  64.9 10.3 %collective-permute-start.17 = (bf16[128,256]{1,0:T(8,128)(2,1)S(1)}, bf16[128,256]{1,0:T(8,128)(2,1)S(1)}, u32[]{:S(2)}, u32[]{:S(2)}) collective-permute-start(bf16[128,256]{1,0:T(8,128)(2,1)S(1)} %get-tuple-element.54), channel_id=1, source_target_pairs={{0,12},{4,8},{8,4},{12,0},{1,13},{5,9},{9,5},{13,1},{2,14},{6,10},... | collective-permute-start | bytes 196616 | tf_op jit(solution)/shard_map/ppermute | solution.py:403
  70.8 10.2 %collective-permute-start.20 = (bf16[144,256]{1,0:T(8,128)(2,1)S(1)}, bf16[144,256]{1,0:T(8,128)(2,1)S(1)}, u32[]{:S(2)}, u32[]{:S(2)}) collective-permute-start(bf16[144,256]{1,0:T(8,128)(2,1)S(1)} %get-tuple-element.70), channel_id=1, source_target_pairs={{0,4},{4,0},{8,12},{12,8},{1,5},{5,1},{9,13},{13,9},{2,6},{6,2},{1... | collective-permute-start | bytes 221192 | tf_op jit(solution)/shard_map/ppermute | solution.py:403
  71.0 10.1 %collective-permute-start.21 = (bf16[144,256]{1,0:T(8,128)(2,1)S(1)}, bf16[144,256]{1,0:T(8,128)(2,1)S(1)}, u32[]{:S(2)}, u32[]{:S(2)}) collective-permute-start(bf16[144,256]{1,0:T(8,128)(2,1)S(1)} %get-tuple-element.71), channel_id=1, source_target_pairs={{0,8},{4,12},{8,0},{12,4},{1,9},{5,13},{9,1},{13,5},{2,10},{6,14},... | collective-permute-start | bytes 221192 | tf_op jit(solution)/shard_map/ppermute | solution.py:403
  74.8 6.3 %collective-permute-start.22 = (bf16[144,256]{1,0:T(8,128)(2,1)S(1)}, bf16[144,256]{1,0:T(8,128)(2,1)S(1)}, u32[]{:S(2)}, u32[]{:S(2)}) collective-permute-start(bf16[144,256]{1,0:T(8,128)(2,1)S(1)} %get-tuple-element.72), channel_id=1, source_target_pairs={{0,12},{4,8},{8,4},{12,0},{1,13},{5,9},{9,5},{13,1},{2,14},{6,10},... | collective-permute-start | bytes 221192 | tf_op jit(solution)/shard_map/ppermute | solution.py:403
  (1 other events, 15.0 us)

commit v11 on v10

--- a/solution.py
+++ b/solution.py
@@ -62,8 +62,8 @@
             home[q // 2, s, 0:tokens, :] = tn(onehot[s], rows[s, :, columns(me, q, width)]).astype(BF16)
 
 
-RING = 8
-GROUP = 4
+RING = 4
+GROUP = 2
 
 
 def ring(weight, slots, sems, columns=None):
@@ -178,19 +178,27 @@
 
 
 def home_kernel(onehot, rows, *refs):
-    grads, (keep, send) = refs[:-2], refs[-2:]
+    keep, send = refs[-2:]
     send_home(keep, send, lax.axis_index("etp"), onehot, rows, keep.shape[2], keep.shape[3])
-    for s, grad in enumerate(grads):
-        for q in range(2):
-            send[2 + q, s] = grad[q]
-
-
-def home_values_kernel(choose, onehot, rows, dots, own_ref, info_ref, *refs):
-    keep, send = refs[-2:]
+
+
+def half(me, other, size):
+    return pl.ds(pl.multiple_of(lax.bitwise_xor(me // 2, other) * size, size), size)
+
+
+def half_home(me, onehot, rows, keep, send, tokens, width):
+    for s in range(onehot.shape[0]):
+        for q, home in enumerate((keep, send)):
+            at = pl.multiple_of(lax.rem(lax.bitwise_xor(me, q), 2) * width, width)
+            home[s, 0:tokens, :] = tn(onehot[s], rows[s, :, pl.ds(at, width)]).astype(BF16)
+
+
+def values_kernel(choose, onehot, rows, dots, own_ref, info_ref, *refs):
+    keep, send, value_ref = refs[-3:]
     sources, slots, tokens = onehot.shape
     experts = slots // CAP
-    width = keep.shape[3]
-    send_home(keep, send, lax.axis_index("etp"), onehot, rows, tokens, width)
+    width = keep.shape[2]
+    half_home(lax.axis_index("etp"), onehot, rows, keep, send, tokens, width)
     expert = lax.broadcasted_iota(jnp.int32, (experts, tokens), 0)
     mine = (lax.axis_index("expert") * experts + expert).astype(F32)
     for s in range(sources):
@@ -201,13 +209,35 @@
         values = [jnp.sum(jnp.where(ids[k:k + 1, :] == mine, share, 0.0), axis=0, keepdims=True) for k in range(choose)]
         values = jnp.concatenate(values + [jnp.zeros((EXTRA - choose, tokens), F32)], axis=0)
         values = jnp.concatenate([values, jnp.zeros((EXTRA, width - tokens), F32)], axis=1).astype(BF16)
-        for home in (keep, send):
-            home[0, s, tokens:tokens + EXTRA, :] = values
-            home[1, s, tokens:tokens + EXTRA, :] = values
+        keep[s, tokens:tokens + EXTRA, :] = values
+        send[s, tokens:tokens + EXTRA, :] = values
+        value_ref[s] = values
+
+
+def own_kernel(gate_ref, up_ref, p_ref, q_ref, onehot, slot_gate, value_ref, earlier_ref, keep, send, back_rows):
+    sources, slots, tokens = onehot.shape
+    width = keep.shape[2]
+    me = lax.axis_index("etp")
+    here = half(me, 0, 2 * width)
+
+    def turn(i, _):
+        for e in [i * GROUP + j for j in range(GROUP)]:
+            back = nn(p_ref[e], gate_ref[e, :, here]) + nn(q_ref[e], up_ref[e, :, here])
+            back = (back * slot_gate[e][:, 0:1]).astype(BF16)
+            at = pl.ds(pl.multiple_of(e * CAP, CAP), CAP)
+            for s in range(sources):
+                back_rows[s, at, :] = back[s * CAP:(s + 1) * CAP]
+        return 0
+
+    lax.fori_loop(0, slots // CAP // GROUP, turn, 0)
+    half_home(me, onehot, back_rows, keep, send, tokens, width)
+    for s in range(sources):
+        keep[s, tokens:tokens + EXTRA, :] = value_ref[s]
+        send[s, tokens:tokens + EXTRA, :] = value_ref[s]
 
 
 def backward_kernel(
-    a0, a1, a2, a3, near_ref,
+    a0, a1, a2, a3, n0, n1, n2, n3,
     gate_ref, up_ref, down_hbm, act_ref, slope_ref, silu_ref, onehot, slot_gate, earlier_ref,
     back_rows, dots, rows_ref, p_ref, q_ref,
     down_ref, down_sems,
@@ -217,9 +247,10 @@
     width = a0.shape[2]
     me = lax.axis_index("etp")
     start_down, wait_down = ring(down_hbm, down_ref, down_sems)
-    for s, here in enumerate((a0, a1, a2, a3)):
+    there = half(me, 1, 2 * width)
+    for s, (here, near) in enumerate(((a0, n0), (a1, n1), (a2, n2), (a3, n3))):
         for q in range(4):
-            block = near_ref[2 + q // 2, s] if q % 2 else here[q // 2]
+            block = (near if q % 2 else here)[q // 2]
             picked = nn(onehot[s], block).astype(BF16).reshape(experts, CAP, width)
             rows_ref[:, s * CAP:(s + 1) * CAP, columns(me, q, width)] = picked
 
@@ -232,7 +263,7 @@
         q_ref[e] = (grad * silu_ref[e]).astype(BF16)
 
     def project(e):
-        back = nn(p_ref[e], gate_ref[e]) + nn(q_ref[e], up_ref[e])
+        back = nn(p_ref[e], gate_ref[e, :, there]) + nn(q_ref[e], up_ref[e, :, there])
         back = (back * slot_gate[e][:, 0:1]).astype(BF16)
         at = pl.ds(pl.multiple_of(e * CAP, CAP), CAP)
         for s in range(sources):
@@ -263,21 +294,28 @@
         near[s] = (keep[0, s].astype(F32) + came[0, s].astype(F32)).astype(BF16)
 
 
-def chips_kernel(near, came, *refs):
-    parts = refs[-near.shape[0]:]
-    for s in range(near.shape[0]):
-        parts[s][...] = (near[s].astype(F32) + came[s].astype(F32)).astype(BF16)
+def pair_kernel(keep, came, *refs):
+    refs[-1][...] = (keep[...].astype(F32) + came[...].astype(F32)).astype(BF16)
+
+
+def chips_kernel(out_near, out_came, back_keep, back_near, back_came, *refs):
+    sources, tokens = out_near.shape[:2]
+    parts = refs[-sources:]
+    for s in range(sources):
+        parts[s][0:tokens, :] = (out_near[s].astype(F32) + out_came[s].astype(F32)).astype(BF16)
+        back = back_keep[s].astype(F32) + back_near[s].astype(F32) + back_came[s].astype(F32)
+        parts[s][tokens:, :] = back.astype(BF16)
 
 
 def total_kernel(count, *refs):
+    out_ref, back_ref, value_ref = refs[count:]
+    tokens = out_ref.shape[0]
     total = refs[0][...].astype(F32)
     for ref in refs[1:count]:
         total = total + ref[...].astype(F32)
-    rows = refs[count]
-    tokens = rows.shape[0]
-    rows[...] = total[0:tokens].astype(BF16)
-    for values in refs[count + 1:]:
-        values[...] = total[tokens:tokens + values.shape[0], 0:values.shape[1]]
+    out_ref[...] = total[0:tokens].astype(BF16)
+    back_ref[...] = total[tokens:2 * tokens].astype(BF16)
+    value_ref[...] = total[2 * tokens:2 * tokens + value_ref.shape[0], 0:value_ref.shape[1]]
 
 
 BANKS = 8
@@ -409,14 +447,6 @@
     return kernel_call(add_kernel, [shape, shape], [], 0, limit=2, in_hbm=hbm)(keep, came, *earlier)
 
 
-def add_chips(near, far, *earlier):
-    sources = near.shape[0]
-    shape = jax.ShapeDtypeStruct(near.shape[1:], BF16)
-    hbm = [2] if earlier else []
-    parts = kernel_call(chips_kernel, [shape] * sources, [], 0, limit=2, in_hbm=hbm)(near, far, *earlier)
-    return parts[0], [swap(parts[s], s, "expert") for s in range(1, sources)]
-
-
 def gathered_body(
     hidden_in, out_grad, expert_ids, gate_values, capacity_blocks, gate_weight, up_weight, down_weight
 ):
@@ -464,7 +494,7 @@
         ],
         [pltpu.VMEM((RING, units, model), BF16), pltpu.SemaphoreType.DMA((RING,))],
         3 * product,
-        limit=10,
+        limit=6,
         in_hbm=(11,),
     )(
         capacity_blocks,
@@ -474,18 +504,13 @@
     )
 
     keep, send = kernel_call(
-        home_kernel,
-        [sent(2, sources, tokens, width), sent(4, sources, tokens, width)],
-        [],
-        2 * slots * sources * tokens * model,
-        limit=2,
+        home_kernel, [sent(2, sources, tokens, width)] * 2, [], 2 * slots * sources * tokens * model, limit=2,
     )(onehot, out_rows, *grads)
-    near = swap(send, 1)
-    out_near, out_far = add_cores(keep, near)
+    out_near, out_far = add_cores(keep, swap(send, 1))
     back_rows, dots, y_rows, gate_part, up_part = kernel_call(
         backward_kernel,
         [
-            held(sources, slots, model),
+            held(sources, slots, model // 2),
             held(local_experts, rows, tokens, kind=F32),
             held(local_experts, rows, model),
             held(local_experts, rows, units),
@@ -493,36 +518,48 @@
         ],
         [pltpu.VMEM((RING, units, model), BF16), pltpu.SemaphoreType.DMA((RING,))],
         3 * product,
-        limit=13,
-        in_hbm=(7,),
+        limit=8,
+        in_hbm=(10,),
     )(
-        *grads, near,
+        *grads, *[swap(x, 1) for x in grads],
         gate_t, up_t, down_weight, activ, slope, silu, onehot, slot_gate, out_near,
     )
 
-    out_own, out_parts = add_chips(out_near, swap(out_far, 2))
-    keep, send = kernel_call(
-        functools.partial(home_values_kernel, choose),
-        [sent(2, sources, tokens + EXTRA, width)] * 2,
+    out_came = swap(out_far, 2)
+    back_sum = sent(sources, tokens + EXTRA, width)
+    far_keep, far_send, values = kernel_call(
+        functools.partial(values_kernel, choose),
+        [back_sum, back_sum, held(sources, EXTRA, width)],
         [],
-        2 * slots * sources * tokens * model,
+        slots * sources * tokens * model,
         limit=2,
-    )(onehot, back_rows, dots, own, came, out_own)
-    (down_grad,) = weight_grads([(scaled, y_rows, 0, local_experts)])
-    back_near, back_far = add_cores(keep, swap(send, 1), down_grad)
-    (up_grad,) = weight_grads([(up_part, x_rows, 0, local_experts)], None, back_near)
-    (layer_out,) = kernel_call(functools.partial(total_kernel, sources), [sent(tokens, width)], [], 0, limit=2)(
-        out_own, *out_parts
-    )
-    back_own, back_parts = add_chips(back_near, swap(back_far, 2), up_grad)
-    (gate_grad,) = weight_grads([(gate_part, x_rows, 0, local_experts)], None, back_own)
-    input_grad, value_grad = kernel_call(
+    )(onehot, back_rows, dots, own, came, out_came)
+    near_keep, near_send = kernel_call(
+        own_kernel,
+        [back_sum, back_sum],
+        [pltpu.VMEM((sources, slots, model // 2), BF16)],
+        product,
+        limit=4,
+    )(gate_t, up_t, gate_part, up_part, onehot, slot_gate, values, far_keep)
+    (back_far,) = kernel_call(pair_kernel, [back_sum], [], 0, limit=2)(far_keep, swap(far_send, 1), near_keep)
+    some = local_experts // 2
+    up_grad, down_grad = weight_grads(
+        [(up_part, x_rows, 0, local_experts), (scaled, y_rows, 0, some)], None, back_far
+    )
+    height = 2 * tokens + EXTRA
+    parts = kernel_call(chips_kernel, [sent(height, width)] * sources, [], 0, limit=2, in_hbm=(5,))(
+        out_near, out_came, near_keep, swap(near_send, 1), swap(back_far, 2), up_grad
+    )
+    down_grad, gate_grad = weight_grads(
+        [(scaled, y_rows, some, local_experts), (gate_part, x_rows, 0, local_experts)], down_grad, parts[0]
+    )
+    layer_out, input_grad, value_grad = kernel_call(
         functools.partial(total_kernel, sources),
-        [sent(tokens, width), jax.ShapeDtypeStruct((choose, tokens), F32)],
+        [sent(tokens, width), sent(tokens, width), jax.ShapeDtypeStruct((choose, tokens), F32)],
         [],
         0,
         limit=2,
-    )(back_own, *back_parts)
+    )(parts[0], *[swap(parts[s], s, "expert") for s in range(1, sources)])
     return (
         layer_out,
         input_grad,

time: 81.9 us -> 82.1 us (level)
  Pallas kernels: 51.6 us -> 53.7 us
  starting transfers between devices: 25.2 us -> 24 us
    pallas_call x17 -> x15, Pallas kernels: 42.8 us -> 44.9 us  [call(): pl.pallas_call(kernel, in_specs=specs, out_specs=out_specs or [pl.BlockSp...]
    ppermute x23 -> x25, starting transfers between devices: 25.2 us -> 24 us  [swap(): return lax.ppermute(array, axis, [(i, i ^ bit) for i in range(count)])]
    ppermute x23 -> x25, waiting for transfers between devices: 3.95 us -> 3.16 us  [swap(): return lax.ppermute(array, axis, [(i, i ^ bit) for i in range(count)])]
  transfers between devices with their start and end apart: 23 -> 25, of which waited for: 2 -> 3; matrix products, arithmetic and copies ran while one was open for 0% -> 0% of each run, Pallas kernels for 59% -> 62%
where the time goes in v11:
time: 82.1 us; the launch traced here: 81.8 us
  Pallas kernels  53.7 us (65%)
  starting transfers between devices  24 us (29%)
  waiting for transfers between devices  3.16 us (4%)
  between operations  0.89 us (1%)
    pallas_call x15, Pallas kernels, call(): pl.pallas_call(kernel, in_specs=specs, out_specs=out_specs or [pl.BlockSp...  44.9 us
    ppermute x25, starting transfers between devices, swap(): return lax.ppermute(array, axis, [(i, i ^ bit) for i in range(count)])  24 us
    pallas_call x2, Pallas kernels, in_vmem(): pl.pallas_call(load_kernel, in_specs=[pl.BlockSpec(memory_space=pltpu.HBM...  8.84 us
    ppermute x25, waiting for transfers between devices, swap(): return lax.ppermute(array, axis, [(i, i ^ bit) for i in range(count)])  3.16 us
  transfers between devices with their start and end apart: 25, of which 3 were waited for; matrix products, arithmetic and copies ran while one was open for 0% of the time, Pallas kernels for 62%

profile of v11, /device:TPU:0, one launch (start us, length us, event | category | flops | bytes accessed | tf_op | source)
XLA Modules:
  0.0 81.8 jit_solution(7485477675984300422)
XLA Ops:
  0.6 0.9 %shard_map.127.o0.own_ref = bf16[144,256]{1,0:T(8,128)(2,1)S(1)} custom-call(bf16[128,256]{1,0:T(8,128)(2,1)} %hidden_hbm.1, s32[6,128]{1,0:T(8,128)} %bitcast.13, f32[6,128]{1,0:T(8,128)} %bitcast.14), custom_call_target="tpu_custom_call" | custom-call | tf_op jit(solution)/shard_map/pallas_call | solution.py:405
  1.6 5.1 %collective-permute-start.5 = (bf16[144,256]{1,0:T(8,128)(2,1)S(1)}, bf16[144,256]{1,0:T(8,128)(2,1)S(1)}, u32[]{:S(2)}, u32[]{:S(2)}) collective-permute-start(bf16[144,256]{1,0:T(8,128)(2,1)S(1)} %shard_map.127.o0.own_ref), channel_id=1, source_target_pairs={{0,12},{4,8},{8,4},{12,0},{1,13},{5,9},{9,5},{13,1},{2,14},{6,10},... | collective-permute-start | bytes 221192 | tf_op jit(solution)/shard_map/ppermute | solution.py:441
  6.7 0.6 collective-permute-start.3
  7.3 1.6 %collective-permute-start.1 = (bf16[144,256]{1,0:T(8,128)(2,1)S(1)}, bf16[144,256]{1,0:T(8,128)(2,1)S(1)}, u32[]{:S(2)}, u32[]{:S(2)}) collective-permute-start(bf16[144,256]{1,0:T(8,128)(2,1)S(1)} %shard_map.127.o0.own_ref), channel_id=1, source_target_pairs={{0,2},{1,3},{2,0},{3,1},{4,6},{5,7},{6,4},{7,5},{8,10},{9,11},{10,... | collective-permute-start | bytes 221192 | tf_op jit(solution)/shard_map/ppermute | solution.py:441
  9.3 4.4 %shard_map.128 = (bf16[16,352,1024]{2,1,0:T(8,128)(2,1)S(1)}, f32[8,128]{1,0:T(8,128)S(1)}) custom-call(bf16[16,352,1024]{2,1,0:T(8,128)(2,1)} %bitcast.10), custom_call_target="tpu_custom_call" | custom-call | bytes 11534336 | tf_op jit(solution)/shard_map/pallas_call | solution.py:370
  13.9 1.7 %collective-permute-start.8 = (bf16[3,144,256]{2,1,0:T(8,128)(2,1)S(1)}, bf16[3,144,256]{2,1,0:T(8,128)(2,1)S(1)}, u32[]{:S(2)}, u32[]{:S(2)}) collective-permute-start(bf16[3,144,256]{2,1,0:T(8,128)(2,1)S(1)} %shard_map.129.refs_2_.b0.info_ref), channel_id=1, source_target_pairs={{0,2},{1,3},{2,0},{3,1},{4,6},{5,7},{6,4},{7,5},{8,10},{9,11},{10,... | collective-permute-start | bytes 663560 | tf_op jit(solution)/shard_map/ppermute | solution.py:441
  15.6 1.3 %collective-permute-start.9 = (bf16[2,128,256]{2,1,0:T(8,128)(2,1)S(1)}, bf16[2,128,256]{2,1,0:T(8,128)(2,1)S(1)}, u32[]{:S(2)}, u32[]{:S(2)}) collective-permute-start(bf16[2,128,256]{2,1,0:T(8,128)(2,1)S(1)} %shard_map.131.later_ref.refs_0_.a0), channel_id=1, source_target_pairs={{0,4},{4,0},{8,12},{12,8},{1,5},{5,1},{9,13},{13,9},{2,6},{6,2},{1... | collective-permute-start | bytes 393224 | tf_op jit(solution)/shard_map/ppermute | solution.py:441
  16.9 4.4 %shard_map.130 = (bf16[16,352,1024]{2,1,0:T(8,128)(2,1)S(1)}, f32[8,128]{1,0:T(8,128)S(1)}) custom-call(bf16[16,352,1024]{2,1,0:T(8,128)(2,1)} %bitcast.11), custom_call_target="tpu_custom_call" | custom-call | bytes 11534336 | tf_op jit(solution)/shard_map/pallas_call | solution.py:370
  21.4 0.5 collective-permute-start.10
  22.5 2.4 %collective-permute-start.12 = (bf16[2,128,256]{2,1,0:T(8,128)(2,1)S(1)}, bf16[2,128,256]{2,1,0:T(8,128)(2,1)S(1)}, u32[]{:S(2)}, u32[]{:S(2)}) collective-permute-start(bf16[2,128,256]{2,1,0:T(8,128)(2,1)S(1)} %shard_map.131.later_ref.refs_0_.a0), channel_id=1, source_target_pairs={{0,12},{4,8},{8,4},{12,0},{1,13},{5,9},{9,5},{13,1},{2,14},{6,10},... | collective-permute-start | bytes 393224 | tf_op jit(solution)/shard_map/ppermute | solution.py:441
  24.9 1.3 %collective-permute-start.11 = (bf16[2,128,256]{2,1,0:T(8,128)(2,1)S(1)}, bf16[2,128,256]{2,1,0:T(8,128)(2,1)S(1)}, u32[]{:S(2)}, u32[]{:S(2)}) collective-permute-start(bf16[2,128,256]{2,1,0:T(8,128)(2,1)S(1)} %shard_map.131.later_ref.refs_0_.a0), channel_id=1, source_target_pairs={{0,8},{4,12},{8,0},{12,4},{1,9},{5,13},{9,1},{13,5},{2,10},{6,14},... | collective-permute-start | bytes 393224 | tf_op jit(solution)/shard_map/ppermute | solution.py:441
  26.2 12.5 %shard_map.133 = (bf16[4,256,1024]{2,1,0:T(8,128)(2,1)S(1)}, bf16[16,64,1024]{2,1,0:T(8,128)(2,1)S(1)}, bf16[16,64,352]{2,1,0:T(8,128)(2,1)S(1)}, bf16[16,64,352...) custom-call(s32[64]{0:T(128)S(1)} %copy-done.1, ...), custom_call_target="tpu_custom_call" | custom-call | flops 2214592512 | bytes 69206016 | tf_op jit(solution)/shard_map/pallas_call | solution.py:405
  40.4 0.8 collective-permute-done.13.came
  41.4 0.6 collective-permute-start.14
  42.0 11.2 %shard_map.136 = (bf16[4,256,512]{2,1,0:T(8,128)(2,1)S(1)}, f32[16,64,128]{2,1,0:T(8,128)S(1)}, bf16[16,64,1024]{2,1,0:T(8,128)(2,1)S(1)}, bf16[16,64,352]{2,1,0:T(8,128)(2,1)S(1)}, bf16[16,64,352]{2,1,0:T(8,128)(2,1)S(1)}) custom-call(bf16[2,128,256]{2,1,0:T(8,128)(2,1)S(1)} %shard_map.131.later_ref.refs_0_.a0, ...), custom_call_target="tpu_custom_call" | custom-call | flops 2214592512 | bytes 69206016 | tf_op jit(solution)/shard_map/pallas_call | solution.py:405
  53.8 3.6 %shard_map.138 = (bf16[4,144,256]{2,1,0:T(8,128)(2,1)S(1)}, bf16[4,144,256]{2,1,0:T(8,128)(2,1)S(1)}) custom-call(bf16[16,352,1024]{2,1,0:T(8,128)(2,1)S(1)} %get-tuple-element.45.gate_ref, bf16[16,352,1024]{2,1,0:T(8,128)(2,1)S(1)} %get-tuple-element.46.up_ref, bf16[16,64,352]{2,1,0:T(8,128)(2,1)S(1)} %get-tuple-element.57.p_ref.refs_1_, ...), custom_call_target="tpu_custom_call" | custom-call | flops 738197504 | bytes 23068672 | tf_op jit(solution)/shard_map/pallas_call | solution.py:405
  57.9 1.5 %collective-permute-start.21 = (bf16[4,144,256]{2,1,0:T(8,128)(2,1)S(1)}, bf16[4,144,256]{2,1,0:T(8,128)(2,1)S(1)}, u32[]{:S(2)}, u32[]{:S(2)}) collective-permute-start(bf16[4,144,256]{2,1,0:T(8,128)(2,1)S(1)} %shard_map.139.refs_4_), channel_id=1, source_target_pairs={{0,2},{1,3},{2,0},{3,1},{4,6},{5,7},{6,4},{7,5},{8,10},{9,11},{10,... | collective-permute-start | bytes 884744 | tf_op jit(solution)/shard_map/ppermute | solution.py:441
  59.4 7.3 %shard_map.140 = (bf16[16,352,1024]{2,1,0:T(8,128)(2,1)}, bf16[16,352,1024]{2,1,0:T(8,128)(2,1)}) custom-call(bf16[16,64,352]{2,1,0:T(8,128)(2,1)S(1)} %get-tuple-element.58.q_ref.refs_0_, bf16[16,64,352]{2,1,0:T(8,128)(2,1)S(1)} %get-tuple-element.66.refs_1_.refs_0_, bf16[16,64,1024]{2,1,0:T(8,128)(2,1)S(1)} %get-tuple-element.67.refs_2_.refs_3_, ...), custom_call_target="tpu_custom_call" | custom-call | flops 1107296256 | bytes 34603008 | tf_op jit(solution)/shard_map/pallas_call | solution.py:405
  67.2 0.8 collective-permute-start.22
  67.9 2.0 %collective-permute-start.23 = (bf16[272,256]{1,0:T(8,128)(2,1)S(1)}, bf16[272,256]{1,0:T(8,128)(2,1)S(1)}, u32[]{:S(2)}, u32[]{:S(2)}) collective-permute-start(bf16[272,256]{1,0:T(8,128)(2,1)S(1)} %get-tuple-element.72), channel_id=1, source_target_pairs={{0,8},{4,12},{8,0},{12,4},{1,9},{5,13},{9,1},{13,5},{2,10},{6,14},... | collective-permute-start | bytes 417800 | tf_op jit(solution)/shard_map/ppermute | solution.py:441
  69.9 1.7 %collective-permute-start.24 = (bf16[272,256]{1,0:T(8,128)(2,1)S(1)}, bf16[272,256]{1,0:T(8,128)(2,1)S(1)}, u32[]{:S(2)}, u32[]{:S(2)}) collective-permute-start(bf16[272,256]{1,0:T(8,128)(2,1)S(1)} %get-tuple-element.73), channel_id=1, source_target_pairs={{0,12},{4,8},{8,4},{12,0},{1,13},{5,9},{9,5},{13,1},{2,14},{6,10},... | collective-permute-start | bytes 417800 | tf_op jit(solution)/shard_map/ppermute | solution.py:441
  71.6 7.3 %shard_map.143 = (bf16[16,352,1024]{2,1,0:T(8,128)(2,1)}, bf16[16,352,1024]{2,1,0:T(8,128)(2,1)}) custom-call(bf16[16,64,352]{2,1,0:T(8,128)(2,1)S(1)} %get-tuple-element.66.refs_1_.refs_0_, bf16[16,64,352]{2,1,0:T(8,128)(2,1)S(1)} %get-tuple-element.57.p_ref.refs_1_, ...), custom_call_target="tpu_custom_call", output_to_operand_aliasing={{0}: (4, {})} | custom-call | flops 1107296256 | bytes 34603008 | tf_op jit(solution)/shard_map/pallas_call | solution.py:405
  79.0 2.1 %collective-permute-done.23.refs_2_ = bf16[272,256]{1,0:T(8,128)(2,1)S(1)} collective-permute-done((bf16[272,256]{1,0:T(8,128)(2,1)S(1)}, bf16[272,256]{1,0:T(8,128)(2,1)S(1)}, u32[]{:S(2)}, u32[]{:S(2)}) %collective-permute-start.23) | collective-permute-done | bytes 139296 | tf_op jit(solution)/shard_map/ppermute | solution.py:441
  81.1 0.7 shard_map.142
  (47 shorter events, 4.4 us)
Async XLA Ops:
  1.6 12.2 %collective-permute-start.5 = (bf16[144,256]{1,0:T(8,128)(2,1)S(1)}, bf16[144,256]{1,0:T(8,128)(2,1)S(1)}, u32[]{:S(2)}, u32[]{:S(2)}) collective-permute-start(bf16[144,256]{1,0:T(8,128)(2,1)S(1)} %shard_map.127.o0.own_ref), channel_id=1, source_target_pairs={{0,12},{4,8},{8,4},{12,0},{1,13},{5,9},{9,5},{13,1},{2,14},{6,10},... | collective-permute-start | bytes 221192 | tf_op jit(solution)/shard_map/ppermute | solution.py:441
  6.7 7.1 %collective-permute-start.4 = (bf16[144,256]{1,0:T(8,128)(2,1)S(1)}, bf16[144,256]{1,0:T(8,128)(2,1)S(1)}, u32[]{:S(2)}, u32[]{:S(2)}) collective-permute-start(bf16[144,256]{1,0:T(8,128)(2,1)S(1)} %shard_map.127.o0.own_ref), channel_id=1, source_target_pairs={{0,8},{4,12},{8,0},{12,4},{1,9},{5,13},{9,1},{13,5},{2,10},{6,14},... | collective-permute-start | bytes 221192 | tf_op jit(solution)/shard_map/ppermute | solution.py:441
  6.7 7.1 %collective-permute-start.3 = (bf16[144,256]{1,0:T(8,128)(2,1)S(1)}, bf16[144,256]{1,0:T(8,128)(2,1)S(1)}, u32[]{:S(2)}, u32[]{:S(2)}) collective-permute-start(bf16[144,256]{1,0:T(8,128)(2,1)S(1)} %shard_map.127.o0.own_ref), channel_id=1, source_target_pairs={{0,4},{4,0},{8,12},{12,8},{1,5},{5,1},{9,13},{13,9},{2,6},{6,2},{1... | collective-permute-start | bytes 221192 | tf_op jit(solution)/shard_map/ppermute | solution.py:441
  7.3 6.5 %collective-permute-start.1 = (bf16[144,256]{1,0:T(8,128)(2,1)S(1)}, bf16[144,256]{1,0:T(8,128)(2,1)S(1)}, u32[]{:S(2)}, u32[]{:S(2)}) collective-permute-start(bf16[144,256]{1,0:T(8,128)(2,1)S(1)} %shard_map.127.o0.own_ref), channel_id=1, source_target_pairs={{0,2},{1,3},{2,0},{3,1},{4,6},{5,7},{6,4},{7,5},{8,10},{9,11},{10,... | collective-permute-start | bytes 221192 | tf_op jit(solution)/shard_map/ppermute | solution.py:441
  9.0 4.8 %collective-permute-start.6 = (bf16[128,256]{1,0:T(8,128)(2,1)}, bf16[128,256]{1,0:T(8,128)(2,1)S(1)}, u32[]{:S(2)}, u32[]{:S(2)}) collective-permute-start(bf16[128,256]{1,0:T(8,128)(2,1)} %refs_0_.1), channel_id=1, source_target_pairs={{0,2},{1,3},{2,0},{3,1},{4,6},{5,7},{6,4},{7,5},{8,10},{9,11},{10,... | collective-permute-start | bytes 196616 | tf_op jit(solution)/shard_map/ppermute | solution.py:441
  13.9 7.5 %collective-permute-start.8 = (bf16[3,144,256]{2,1,0:T(8,128)(2,1)S(1)}, bf16[3,144,256]{2,1,0:T(8,128)(2,1)S(1)}, u32[]{:S(2)}, u32[]{:S(2)}) collective-permute-start(bf16[3,144,256]{2,1,0:T(8,128)(2,1)S(1)} %shard_map.129.refs_2_.b0.info_ref), channel_id=1, source_target_pairs={{0,2},{1,3},{2,0},{3,1},{4,6},{5,7},{6,4},{7,5},{8,10},{9,11},{10,... | collective-permute-start | bytes 663560 | tf_op jit(solution)/shard_map/ppermute | solution.py:441
  15.6 5.8 %collective-permute-start.9 = (bf16[2,128,256]{2,1,0:T(8,128)(2,1)S(1)}, bf16[2,128,256]{2,1,0:T(8,128)(2,1)S(1)}, u32[]{:S(2)}, u32[]{:S(2)}) collective-permute-start(bf16[2,128,256]{2,1,0:T(8,128)(2,1)S(1)} %shard_map.131.later_ref.refs_0_.a0), channel_id=1, source_target_pairs={{0,4},{4,0},{8,12},{12,8},{1,5},{5,1},{9,13},{13,9},{2,6},{6,2},{1... | collective-permute-start | bytes 393224 | tf_op jit(solution)/shard_map/ppermute | solution.py:441
  21.3 4.9 %collective-permute-start.7 = (bf16[3,144,256]{2,1,0:T(8,128)(2,1)S(1)}, bf16[3,144,256]{2,1,0:T(8,128)(2,1)S(1)}, u32[]{:S(2)}, u32[]{:S(2)}) collective-permute-start(bf16[3,144,256]{2,1,0:T(8,128)(2,1)S(1)} %shard_map.129.refs_2_.b0.info_ref), channel_id=1, source_target_pairs={{0,1},{1,0},{2,3},{3,2},{4,5},{5,4},{6,7},{7,6},{8,9},{9,8},{10,11... | collective-permute-start | bytes 663560 | tf_op jit(solution)/shard_map/ppermute | solution.py:441
  21.4 4.8 %collective-permute-start.10 = (bf16[3,144,256]{2,1,0:T(8,128)(2,1)S(1)}, bf16[3,144,256]{2,1,0:T(8,128)(2,1)S(1)}, u32[]{:S(2)}, u32[]{:S(2)}) collective-permute-start(bf16[3,144,256]{2,1,0:T(8,128)(2,1)S(1)} %bitcast.8), channel_id=1, source_target_pairs={{0,1},{1,0},{2,3},{3,2},{4,5},{5,4},{6,7},{7,6},{8,9},{9,8},{10,11... | collective-permute-start | bytes 663560 | tf_op jit(solution)/shard_map/ppermute | solution.py:441
  22.0 2.9 %collective-permute-start = (bf16[144,256]{1,0:T(8,128)(2,1)S(1)}, bf16[144,256]{1,0:T(8,128)(2,1)S(1)}, u32[]{:S(2)}, u32[]{:S(2)}) collective-permute-start(bf16[144,256]{1,0:T(8,128)(2,1)S(1)} %shard_map.127.o0.own_ref), channel_id=1, source_target_pairs={{0,1},{1,0},{2,3},{3,2},{4,5},{5,4},{6,7},{7,6},{8,9},{9,8},{10,11... | collective-permute-start | bytes 221192 | tf_op jit(solution)/shard_map/ppermute | solution.py:441
  22.1 4.1 %collective-permute-start.2 = (bf16[144,256]{1,0:T(8,128)(2,1)S(1)}, bf16[144,256]{1,0:T(8,128)(2,1)S(1)}, u32[]{:S(2)}, u32[]{:S(2)}) collective-permute-start(bf16[144,256]{1,0:T(8,128)(2,1)S(1)} %collective-permute-done.1.refs_4_.o2), channel_id=1, source_target_pairs={{0,1},{1,0},{2,3},{3,2},{4,5},{5,4},{6,7},{7,6},{8,9},{9,8},{10,11... | collective-permute-start | bytes 221192 | tf_op jit(solution)/shard_map/ppermute | solution.py:441
  22.5 16.3 %collective-permute-start.12 = (bf16[2,128,256]{2,1,0:T(8,128)(2,1)S(1)}, bf16[2,128,256]{2,1,0:T(8,128)(2,1)S(1)}, u32[]{:S(2)}, u32[]{:S(2)}) collective-permute-start(bf16[2,128,256]{2,1,0:T(8,128)(2,1)S(1)} %shard_map.131.later_ref.refs_0_.a0), channel_id=1, source_target_pairs={{0,12},{4,8},{8,4},{12,0},{1,13},{5,9},{9,5},{13,1},{2,14},{6,10},... | collective-permute-start | bytes 393224 | tf_op jit(solution)/shard_map/ppermute | solution.py:441
  24.9 13.9 %collective-permute-start.11 = (bf16[2,128,256]{2,1,0:T(8,128)(2,1)S(1)}, bf16[2,128,256]{2,1,0:T(8,128)(2,1)S(1)}, u32[]{:S(2)}, u32[]{:S(2)}) collective-permute-start(bf16[2,128,256]{2,1,0:T(8,128)(2,1)S(1)} %shard_map.131.later_ref.refs_0_.a0), channel_id=1, source_target_pairs={{0,8},{4,12},{8,0},{12,4},{1,9},{5,13},{9,1},{13,5},{2,10},{6,14},... | collective-permute-start | bytes 393224 | tf_op jit(solution)/shard_map/ppermute | solution.py:441
  39.3 2.0 %collective-permute-start.13 = (bf16[2,4,128,256]{3,2,1,0:T(8,128)(2,1)S(1)}, bf16[2,4,128,256]{3,2,1,0:T(8,128)(2,1)S(1)}, u32[]{:S(2)}, u32[]{:S(2)}) collective-permute-start(bf16[2,4,128,256]{3,2,1,0:T(8,128)(2,1)S(1)} %get-tuple-element.50), channel_id=1, source_target_pairs={{0,1},{1,0},{2,3},{3,2},{4,5},{5,4},{6,7},{7,6},{8,9},{9,8},{10,11... | collective-permute-start | bytes 1572872 | tf_op jit(solution)/shard_map/ppermute | solution.py:441
  39.3 2.6 %collective-permute-start.15 = (bf16[2,128,256]{2,1,0:T(8,128)(2,1)S(1)}, bf16[2,128,256]{2,1,0:T(8,128)(2,1)S(1)}, u32[]{:S(2)}, u32[]{:S(2)}) collective-permute-start(bf16[2,128,256]{2,1,0:T(8,128)(2,1)S(1)} %shard_map.131.later_ref.refs_0_.a0), channel_id=1, source_target_pairs={{0,1},{1,0},{2,3},{3,2},{4,5},{5,4},{6,7},{7,6},{8,9},{9,8},{10,11... | collective-permute-start | bytes 393224 | tf_op jit(solution)/shard_map/ppermute | solution.py:441
  39.8 2.2 %collective-permute-start.18 = (bf16[2,128,256]{2,1,0:T(8,128)(2,1)S(1)}, bf16[2,128,256]{2,1,0:T(8,128)(2,1)S(1)}, u32[]{:S(2)}, u32[]{:S(2)}) collective-permute-start(bf16[2,128,256]{2,1,0:T(8,128)(2,1)S(1)} %collective-permute-done.12.refs_3_.a3), channel_id=1, source_target_pairs={{0,1},{1,0},{2,3},{3,2},{4,5},{5,4},{6,7},{7,6},{8,9},{9,8},{10,11... | collective-permute-start | bytes 393224 | tf_op jit(solution)/shard_map/ppermute | solution.py:441
  39.9 2.1 %collective-permute-start.17 = (bf16[2,128,256]{2,1,0:T(8,128)(2,1)S(1)}, bf16[2,128,256]{2,1,0:T(8,128)(2,1)S(1)}, u32[]{:S(2)}, u32[]{:S(2)}) collective-permute-start(bf16[2,128,256]{2,1,0:T(8,128)(2,1)S(1)} %collective-permute-done.11.refs_2_.a2), channel_id=1, source_target_pairs={{0,1},{1,0},{2,3},{3,2},{4,5},{5,4},{6,7},{7,6},{8,9},{9,8},{10,11... | collective-permute-start | bytes 393224 | tf_op jit(solution)/shard_map/ppermute | solution.py:441
  41.4 11.8 %collective-permute-start.14 = (bf16[4,128,256]{2,1,0:T(8,128)(2,1)S(1)}, bf16[4,128,256]{2,1,0:T(8,128)(2,1)S(1)}, u32[]{:S(2)}, u32[]{:S(2)}) collective-permute-start(bf16[4,128,256]{2,1,0:T(8,128)(2,1)S(1)} %get-tuple-element.52), channel_id=1, source_target_pairs={{0,2},{1,3},{2,0},{3,1},{4,6},{5,7},{6,4},{7,5},{8,10},{9,11},{10,... | collective-permute-start | bytes 786440 | tf_op jit(solution)/shard_map/ppermute | solution.py:441
  53.6 4.2 %collective-permute-start.20 = (bf16[4,144,256]{2,1,0:T(8,128)(2,1)S(1)}, bf16[4,144,256]{2,1,0:T(8,128)(2,1)S(1)}, u32[]{:S(2)}, u32[]{:S(2)}) collective-permute-start(bf16[4,144,256]{2,1,0:T(8,128)(2,1)S(1)} %get-tuple-element.65), channel_id=1, source_target_pairs={{0,1},{1,0},{2,3},{3,2},{4,5},{5,4},{6,7},{7,6},{8,9},{9,8},{10,11... | collective-permute-start | bytes 884744 | tf_op jit(solution)/shard_map/ppermute | solution.py:441
  57.4 9.4 %collective-permute-start.19 = (bf16[4,144,256]{2,1,0:T(8,128)(2,1)S(1)}, bf16[4,144,256]{2,1,0:T(8,128)(2,1)S(1)}, u32[]{:S(2)}, u32[]{:S(2)}) collective-permute-start(bf16[4,144,256]{2,1,0:T(8,128)(2,1)S(1)} %get-tuple-element.64), channel_id=1, source_target_pairs={{0,1},{1,0},{2,3},{3,2},{4,5},{5,4},{6,7},{7,6},{8,9},{9,8},{10,11... | collective-permute-start | bytes 884744 | tf_op jit(solution)/shard_map/ppermute | solution.py:441
  57.9 9.1 %collective-permute-start.21 = (bf16[4,144,256]{2,1,0:T(8,128)(2,1)S(1)}, bf16[4,144,256]{2,1,0:T(8,128)(2,1)S(1)}, u32[]{:S(2)}, u32[]{:S(2)}) collective-permute-start(bf16[4,144,256]{2,1,0:T(8,128)(2,1)S(1)} %shard_map.139.refs_4_), channel_id=1, source_target_pairs={{0,2},{1,3},{2,0},{3,1},{4,6},{5,7},{6,4},{7,5},{8,10},{9,11},{10,... | collective-permute-start | bytes 884744 | tf_op jit(solution)/shard_map/ppermute | solution.py:441
  67.2 11.8 %collective-permute-start.22 = (bf16[272,256]{1,0:T(8,128)(2,1)S(1)}, bf16[272,256]{1,0:T(8,128)(2,1)S(1)}, u32[]{:S(2)}, u32[]{:S(2)}) collective-permute-start(bf16[272,256]{1,0:T(8,128)(2,1)S(1)} %get-tuple-element.71), channel_id=1, source_target_pairs={{0,4},{4,0},{8,12},{12,8},{1,5},{5,1},{9,13},{13,9},{2,6},{6,2},{1... | collective-permute-start | bytes 417800 | tf_op jit(solution)/shard_map/ppermute | solution.py:441
  67.9 13.1 %collective-permute-start.23 = (bf16[272,256]{1,0:T(8,128)(2,1)S(1)}, bf16[272,256]{1,0:T(8,128)(2,1)S(1)}, u32[]{:S(2)}, u32[]{:S(2)}) collective-permute-start(bf16[272,256]{1,0:T(8,128)(2,1)S(1)} %get-tuple-element.72), channel_id=1, source_target_pairs={{0,8},{4,12},{8,0},{12,4},{1,9},{5,13},{9,1},{13,5},{2,10},{6,14},... | collective-permute-start | bytes 417800 | tf_op jit(solution)/shard_map/ppermute | solution.py:441
  69.9 11.1 %collective-permute-start.24 = (bf16[272,256]{1,0:T(8,128)(2,1)S(1)}, bf16[272,256]{1,0:T(8,128)(2,1)S(1)}, u32[]{:S(2)}, u32[]{:S(2)}) collective-permute-start(bf16[272,256]{1,0:T(8,128)(2,1)S(1)} %get-tuple-element.73), channel_id=1, source_target_pairs={{0,12},{4,8},{8,4},{12,0},{1,13},{5,9},{9,5},{13,1},{2,14},{6,10},... | collective-permute-start | bytes 417800 | tf_op jit(solution)/shard_map/ppermute | solution.py:441
  (3 other events, 33.5 us)

commit v12 on v11

--- a/solution.py
+++ b/solution.py
@@ -62,8 +62,8 @@
             home[q // 2, s, 0:tokens, :] = tn(onehot[s], rows[s, :, columns(me, q, width)]).astype(BF16)
 
 
-RING = 4
-GROUP = 2
+RING = 8
+GROUP = 4
 
 
 def ring(weight, slots, sems, columns=None):
@@ -494,7 +494,7 @@
         ],
         [pltpu.VMEM((RING, units, model), BF16), pltpu.SemaphoreType.DMA((RING,))],
         3 * product,
-        limit=6,
+        limit=16,
         in_hbm=(11,),
     )(
         capacity_blocks,
@@ -518,7 +518,7 @@
         ],
         [pltpu.VMEM((RING, units, model), BF16), pltpu.SemaphoreType.DMA((RING,))],
         3 * product,
-        limit=8,
+        limit=16,
         in_hbm=(10,),
     )(
         *grads, *[swap(x, 1) for x in grads],
@@ -539,7 +539,7 @@
         [back_sum, back_sum],
         [pltpu.VMEM((sources, slots, model // 2), BF16)],
         product,
-        limit=4,
+        limit=16,
     )(gate_t, up_t, gate_part, up_part, onehot, slot_gate, values, far_keep)
     (back_far,) = kernel_call(pair_kernel, [back_sum], [], 0, limit=2)(far_keep, swap(far_send, 1), near_keep)
     some = local_experts // 2

time: 82.1 us -> 79.2 us (0.965)
  Pallas kernels: 53.7 us -> 50.9 us
    pallas_call x15, Pallas kernels: 44.9 us -> 42.1 us  [call(): pl.pallas_call(kernel, in_specs=specs, out_specs=out_specs or [pl.BlockSp...]
  transfers between devices with their start and end apart: 25 -> 25, of which waited for: 3 -> 3; matrix products, arithmetic and copies ran while one was open for 0% -> 0% of each run, Pallas kernels for 62% -> 61%
where the time goes in v12:
time: 79.2 us; the launch traced here: 79.1 us
  Pallas kernels  50.9 us (64%)
  starting transfers between devices  24.1 us (30%)
  waiting for transfers between devices  3.18 us (4%)
  between operations  0.89 us (1%)
    pallas_call x15, Pallas kernels, call(): pl.pallas_call(kernel, in_specs=specs, out_specs=out_specs or [pl.BlockSp...  42.1 us
    ppermute x25, starting transfers between devices, swap(): return lax.ppermute(array, axis, [(i, i ^ bit) for i in range(count)])  24.1 us
    pallas_call x2, Pallas kernels, in_vmem(): pl.pallas_call(load_kernel, in_specs=[pl.BlockSpec(memory_space=pltpu.HBM...  8.84 us
    ppermute x25, waiting for transfers between devices, swap(): return lax.ppermute(array, axis, [(i, i ^ bit) for i in range(count)])  3.18 us
  transfers between devices with their start and end apart: 25, of which 3 were waited for; matrix products, arithmetic and copies ran while one was open for 0% of the time, Pallas kernels for 61%

profile of v12, /device:TPU:0, one launch (start us, length us, event | category | flops | bytes accessed | tf_op | source)
XLA Modules:
  0.0 79.1 jit_solution(12567628275244647178)
XLA Ops:
  0.6 0.9 %shard_map.127.o0.own_ref = bf16[144,256]{1,0:T(8,128)(2,1)S(1)} custom-call(bf16[128,256]{1,0:T(8,128)(2,1)} %hidden_hbm.1, s32[6,128]{1,0:T(8,128)} %bitcast.13, f32[6,128]{1,0:T(8,128)} %bitcast.14), custom_call_target="tpu_custom_call" | custom-call | tf_op jit(solution)/shard_map/pallas_call | solution.py:405
  1.6 5.1 %collective-permute-start.5 = (bf16[144,256]{1,0:T(8,128)(2,1)S(1)}, bf16[144,256]{1,0:T(8,128)(2,1)S(1)}, u32[]{:S(2)}, u32[]{:S(2)}) collective-permute-start(bf16[144,256]{1,0:T(8,128)(2,1)S(1)} %shard_map.127.o0.own_ref), channel_id=1, source_target_pairs={{0,12},{4,8},{8,4},{12,0},{1,13},{5,9},{9,5},{13,1},{2,14},{6,10},... | collective-permute-start | bytes 221192 | tf_op jit(solution)/shard_map/ppermute | solution.py:441
  6.7 0.6 collective-permute-start.3
  7.3 1.6 %collective-permute-start.1 = (bf16[144,256]{1,0:T(8,128)(2,1)S(1)}, bf16[144,256]{1,0:T(8,128)(2,1)S(1)}, u32[]{:S(2)}, u32[]{:S(2)}) collective-permute-start(bf16[144,256]{1,0:T(8,128)(2,1)S(1)} %shard_map.127.o0.own_ref), channel_id=1, source_target_pairs={{0,2},{1,3},{2,0},{3,1},{4,6},{5,7},{6,4},{7,5},{8,10},{9,11},{10,... | collective-permute-start | bytes 221192 | tf_op jit(solution)/shard_map/ppermute | solution.py:441
  9.3 4.4 %shard_map.128 = (bf16[16,352,1024]{2,1,0:T(8,128)(2,1)S(1)}, f32[8,128]{1,0:T(8,128)S(1)}) custom-call(bf16[16,352,1024]{2,1,0:T(8,128)(2,1)} %bitcast.10), custom_call_target="tpu_custom_call" | custom-call | bytes 11534336 | tf_op jit(solution)/shard_map/pallas_call | solution.py:370
  13.9 1.7 %collective-permute-start.8 = (bf16[3,144,256]{2,1,0:T(8,128)(2,1)S(1)}, bf16[3,144,256]{2,1,0:T(8,128)(2,1)S(1)}, u32[]{:S(2)}, u32[]{:S(2)}) collective-permute-start(bf16[3,144,256]{2,1,0:T(8,128)(2,1)S(1)} %shard_map.129.refs_2_.b0.info_ref), channel_id=1, source_target_pairs={{0,2},{1,3},{2,0},{3,1},{4,6},{5,7},{6,4},{7,5},{8,10},{9,11},{10,... | collective-permute-start | bytes 663560 | tf_op jit(solution)/shard_map/ppermute | solution.py:441
  15.6 1.3 %collective-permute-start.9 = (bf16[2,128,256]{2,1,0:T(8,128)(2,1)S(1)}, bf16[2,128,256]{2,1,0:T(8,128)(2,1)S(1)}, u32[]{:S(2)}, u32[]{:S(2)}) collective-permute-start(bf16[2,128,256]{2,1,0:T(8,128)(2,1)S(1)} %shard_map.131.later_ref.refs_0_.a0), channel_id=1, source_target_pairs={{0,4},{4,0},{8,12},{12,8},{1,5},{5,1},{9,13},{13,9},{2,6},{6,2},{1... | collective-permute-start | bytes 393224 | tf_op jit(solution)/shard_map/ppermute | solution.py:441
  16.9 4.4 %shard_map.130 = (bf16[16,352,1024]{2,1,0:T(8,128)(2,1)S(1)}, f32[8,128]{1,0:T(8,128)S(1)}) custom-call(bf16[16,352,1024]{2,1,0:T(8,128)(2,1)} %bitcast.11), custom_call_target="tpu_custom_call" | custom-call | bytes 11534336 | tf_op jit(solution)/shard_map/pallas_call | solution.py:370
  21.4 0.5 collective-permute-start.10
  22.5 2.4 %collective-permute-start.12 = (bf16[2,128,256]{2,1,0:T(8,128)(2,1)S(1)}, bf16[2,128,256]{2,1,0:T(8,128)(2,1)S(1)}, u32[]{:S(2)}, u32[]{:S(2)}) collective-permute-start(bf16[2,128,256]{2,1,0:T(8,128)(2,1)S(1)} %shard_map.131.later_ref.refs_0_.a0), channel_id=1, source_target_pairs={{0,12},{4,8},{8,4},{12,0},{1,13},{5,9},{9,5},{13,1},{2,14},{6,10},... | collective-permute-start | bytes 393224 | tf_op jit(solution)/shard_map/ppermute | solution.py:441
  24.9 1.3 %collective-permute-start.11 = (bf16[2,128,256]{2,1,0:T(8,128)(2,1)S(1)}, bf16[2,128,256]{2,1,0:T(8,128)(2,1)S(1)}, u32[]{:S(2)}, u32[]{:S(2)}) collective-permute-start(bf16[2,128,256]{2,1,0:T(8,128)(2,1)S(1)} %shard_map.131.later_ref.refs_0_.a0), channel_id=1, source_target_pairs={{0,8},{4,12},{8,0},{12,4},{1,9},{5,13},{9,1},{13,5},{2,10},{6,14},... | collective-permute-start | bytes 393224 | tf_op jit(solution)/shard_map/ppermute | solution.py:441
  26.2 11.8 %shard_map.133 = (bf16[4,256,1024]{2,1,0:T(8,128)(2,1)S(1)}, bf16[16,64,1024]{2,1,0:T(8,128)(2,1)S(1)}, bf16[16,64,352]{2,1,0:T(8,128)(2,1)S(1)}, bf16[16,64,352...) custom-call(s32[64]{0:T(128)S(1)} %copy-done.1, ...), custom_call_target="tpu_custom_call" | custom-call | flops 2214592512 | bytes 69206016 | tf_op jit(solution)/shard_map/pallas_call | solution.py:405
  39.7 0.8 %collective-permute-done.13.came = bf16[2,4,128,256]{3,2,1,0:T(8,128)(2,1)S(1)} collective-permute-done((bf16[2,4,128,256]{3,2,1,0:T(8,128)(2,1)S(1)}, bf16[2,4,128,256]{3,2,1,0:T(8,128)(2,1)S(1)}, u32[]{:S(2)}, u32[]{:S(2)}) %collective-permute-start.13) | collective-permute-done | bytes 524320 | tf_op jit(solution)/shard_map/ppermute | solution.py:441
  40.6 0.6 collective-permute-start.14
  41.2 9.7 %shard_map.136 = (bf16[4,256,512]{2,1,0:T(8,128)(2,1)S(1)}, f32[16,64,128]{2,1,0:T(8,128)S(1)}, bf16[16,64,1024]{2,1,0:T(8,128)(2,1)S(1)}, bf16[16,64,352]{2,1,0:T(8,128)(2,1)S(1)}, bf16[16,64,352]{2,1,0:T(8,128)(2,1)S(1)}) custom-call(bf16[2,128,256]{2,1,0:T(8,128)(2,1)S(1)} %shard_map.131.later_ref.refs_0_.a0, ...), custom_call_target="tpu_custom_call" | custom-call | flops 2214592512 | bytes 69206016 | tf_op jit(solution)/shard_map/pallas_call | solution.py:405
  51.5 3.1 %shard_map.138 = (bf16[4,144,256]{2,1,0:T(8,128)(2,1)S(1)}, bf16[4,144,256]{2,1,0:T(8,128)(2,1)S(1)}) custom-call(bf16[16,352,1024]{2,1,0:T(8,128)(2,1)S(1)} %get-tuple-element.45.gate_ref, bf16[16,352,1024]{2,1,0:T(8,128)(2,1)S(1)} %get-tuple-element.46.up_ref, bf16[16,64,352]{2,1,0:T(8,128)(2,1)S(1)} %get-tuple-element.57.p_ref.refs_1_, ...), custom_call_target="tpu_custom_call" | custom-call | flops 738197504 | bytes 23068672 | tf_op jit(solution)/shard_map/pallas_call | solution.py:405
  55.1 1.6 %collective-permute-start.21 = (bf16[4,144,256]{2,1,0:T(8,128)(2,1)S(1)}, bf16[4,144,256]{2,1,0:T(8,128)(2,1)S(1)}, u32[]{:S(2)}, u32[]{:S(2)}) collective-permute-start(bf16[4,144,256]{2,1,0:T(8,128)(2,1)S(1)} %shard_map.139.refs_4_), channel_id=1, source_target_pairs={{0,2},{1,3},{2,0},{3,1},{4,6},{5,7},{6,4},{7,5},{8,10},{9,11},{10,... | collective-permute-start | bytes 884744 | tf_op jit(solution)/shard_map/ppermute | solution.py:441
  56.7 7.3 %shard_map.140 = (bf16[16,352,1024]{2,1,0:T(8,128)(2,1)}, bf16[16,352,1024]{2,1,0:T(8,128)(2,1)}) custom-call(bf16[16,64,352]{2,1,0:T(8,128)(2,1)S(1)} %get-tuple-element.58.q_ref.refs_0_, bf16[16,64,352]{2,1,0:T(8,128)(2,1)S(1)} %get-tuple-element.66.refs_1_.refs_0_, bf16[16,64,1024]{2,1,0:T(8,128)(2,1)S(1)} %get-tuple-element.67.refs_2_.refs_3_, ...), custom_call_target="tpu_custom_call" | custom-call | flops 1107296256 | bytes 34603008 | tf_op jit(solution)/shard_map/pallas_call | solution.py:405
  64.4 0.7 collective-permute-start.22
  65.1 2.1 %collective-permute-start.23 = (bf16[272,256]{1,0:T(8,128)(2,1)S(1)}, bf16[272,256]{1,0:T(8,128)(2,1)S(1)}, u32[]{:S(2)}, u32[]{:S(2)}) collective-permute-start(bf16[272,256]{1,0:T(8,128)(2,1)S(1)} %get-tuple-element.72), channel_id=1, source_target_pairs={{0,8},{4,12},{8,0},{12,4},{1,9},{5,13},{9,1},{13,5},{2,10},{6,14},... | collective-permute-start | bytes 417800 | tf_op jit(solution)/shard_map/ppermute | solution.py:441
  67.2 1.6 %collective-permute-start.24 = (bf16[272,256]{1,0:T(8,128)(2,1)S(1)}, bf16[272,256]{1,0:T(8,128)(2,1)S(1)}, u32[]{:S(2)}, u32[]{:S(2)}) collective-permute-start(bf16[272,256]{1,0:T(8,128)(2,1)S(1)} %get-tuple-element.73), channel_id=1, source_target_pairs={{0,12},{4,8},{8,4},{12,0},{1,13},{5,9},{9,5},{13,1},{2,14},{6,10},... | collective-permute-start | bytes 417800 | tf_op jit(solution)/shard_map/ppermute | solution.py:441
  68.8 7.3 %shard_map.143 = (bf16[16,352,1024]{2,1,0:T(8,128)(2,1)}, bf16[16,352,1024]{2,1,0:T(8,128)(2,1)}) custom-call(bf16[16,64,352]{2,1,0:T(8,128)(2,1)S(1)} %get-tuple-element.66.refs_1_.refs_0_, bf16[16,64,352]{2,1,0:T(8,128)(2,1)S(1)} %get-tuple-element.57.p_ref.refs_1_, ...), custom_call_target="tpu_custom_call", output_to_operand_aliasing={{0}: (4, {})} | custom-call | flops 1107296256 | bytes 34603008 | tf_op jit(solution)/shard_map/pallas_call | solution.py:405
  76.2 2.2 %collective-permute-done.23.refs_2_ = bf16[272,256]{1,0:T(8,128)(2,1)S(1)} collective-permute-done((bf16[272,256]{1,0:T(8,128)(2,1)S(1)}, bf16[272,256]{1,0:T(8,128)(2,1)S(1)}, u32[]{:S(2)}, u32[]{:S(2)}) %collective-permute-start.23) | collective-permute-done | bytes 139296 | tf_op jit(solution)/shard_map/ppermute | solution.py:441
  78.4 0.7 shard_map.142
  (47 shorter events, 4.3 us)
Async XLA Ops:
  1.6 12.2 %collective-permute-start.5 = (bf16[144,256]{1,0:T(8,128)(2,1)S(1)}, bf16[144,256]{1,0:T(8,128)(2,1)S(1)}, u32[]{:S(2)}, u32[]{:S(2)}) collective-permute-start(bf16[144,256]{1,0:T(8,128)(2,1)S(1)} %shard_map.127.o0.own_ref), channel_id=1, source_target_pairs={{0,12},{4,8},{8,4},{12,0},{1,13},{5,9},{9,5},{13,1},{2,14},{6,10},... | collective-permute-start | bytes 221192 | tf_op jit(solution)/shard_map/ppermute | solution.py:441
  6.7 7.1 %collective-permute-start.4 = (bf16[144,256]{1,0:T(8,128)(2,1)S(1)}, bf16[144,256]{1,0:T(8,128)(2,1)S(1)}, u32[]{:S(2)}, u32[]{:S(2)}) collective-permute-start(bf16[144,256]{1,0:T(8,128)(2,1)S(1)} %shard_map.127.o0.own_ref), channel_id=1, source_target_pairs={{0,8},{4,12},{8,0},{12,4},{1,9},{5,13},{9,1},{13,5},{2,10},{6,14},... | collective-permute-start | bytes 221192 | tf_op jit(solution)/shard_map/ppermute | solution.py:441
  6.7 7.1 %collective-permute-start.3 = (bf16[144,256]{1,0:T(8,128)(2,1)S(1)}, bf16[144,256]{1,0:T(8,128)(2,1)S(1)}, u32[]{:S(2)}, u32[]{:S(2)}) collective-permute-start(bf16[144,256]{1,0:T(8,128)(2,1)S(1)} %shard_map.127.o0.own_ref), channel_id=1, source_target_pairs={{0,4},{4,0},{8,12},{12,8},{1,5},{5,1},{9,13},{13,9},{2,6},{6,2},{1... | collective-permute-start | bytes 221192 | tf_op jit(solution)/shard_map/ppermute | solution.py:441
  7.3 6.5 %collective-permute-start.1 = (bf16[144,256]{1,0:T(8,128)(2,1)S(1)}, bf16[144,256]{1,0:T(8,128)(2,1)S(1)}, u32[]{:S(2)}, u32[]{:S(2)}) collective-permute-start(bf16[144,256]{1,0:T(8,128)(2,1)S(1)} %shard_map.127.o0.own_ref), channel_id=1, source_target_pairs={{0,2},{1,3},{2,0},{3,1},{4,6},{5,7},{6,4},{7,5},{8,10},{9,11},{10,... | collective-permute-start | bytes 221192 | tf_op jit(solution)/shard_map/ppermute | solution.py:441
  9.0 4.8 %collective-permute-start.6 = (bf16[128,256]{1,0:T(8,128)(2,1)}, bf16[128,256]{1,0:T(8,128)(2,1)S(1)}, u32[]{:S(2)}, u32[]{:S(2)}) collective-permute-start(bf16[128,256]{1,0:T(8,128)(2,1)} %refs_0_.1), channel_id=1, source_target_pairs={{0,2},{1,3},{2,0},{3,1},{4,6},{5,7},{6,4},{7,5},{8,10},{9,11},{10,... | collective-permute-start | bytes 196616 | tf_op jit(solution)/shard_map/ppermute | solution.py:441
  13.9 7.5 %collective-permute-start.8 = (bf16[3,144,256]{2,1,0:T(8,128)(2,1)S(1)}, bf16[3,144,256]{2,1,0:T(8,128)(2,1)S(1)}, u32[]{:S(2)}, u32[]{:S(2)}) collective-permute-start(bf16[3,144,256]{2,1,0:T(8,128)(2,1)S(1)} %shard_map.129.refs_2_.b0.info_ref), channel_id=1, source_target_pairs={{0,2},{1,3},{2,0},{3,1},{4,6},{5,7},{6,4},{7,5},{8,10},{9,11},{10,... | collective-permute-start | bytes 663560 | tf_op jit(solution)/shard_map/ppermute | solution.py:441
  15.6 5.8 %collective-permute-start.9 = (bf16[2,128,256]{2,1,0:T(8,128)(2,1)S(1)}, bf16[2,128,256]{2,1,0:T(8,128)(2,1)S(1)}, u32[]{:S(2)}, u32[]{:S(2)}) collective-permute-start(bf16[2,128,256]{2,1,0:T(8,128)(2,1)S(1)} %shard_map.131.later_ref.refs_0_.a0), channel_id=1, source_target_pairs={{0,4},{4,0},{8,12},{12,8},{1,5},{5,1},{9,13},{13,9},{2,6},{6,2},{1... | collective-permute-start | bytes 393224 | tf_op jit(solution)/shard_map/ppermute | solution.py:441
  21.3 4.9 %collective-permute-start.7 = (bf16[3,144,256]{2,1,0:T(8,128)(2,1)S(1)}, bf16[3,144,256]{2,1,0:T(8,128)(2,1)S(1)}, u32[]{:S(2)}, u32[]{:S(2)}) collective-permute-start(bf16[3,144,256]{2,1,0:T(8,128)(2,1)S(1)} %shard_map.129.refs_2_.b0.info_ref), channel_id=1, source_target_pairs={{0,1},{1,0},{2,3},{3,2},{4,5},{5,4},{6,7},{7,6},{8,9},{9,8},{10,11... | collective-permute-start | bytes 663560 | tf_op jit(solution)/shard_map/ppermute | solution.py:441
  21.4 4.8 %collective-permute-start.10 = (bf16[3,144,256]{2,1,0:T(8,128)(2,1)S(1)}, bf16[3,144,256]{2,1,0:T(8,128)(2,1)S(1)}, u32[]{:S(2)}, u32[]{:S(2)}) collective-permute-start(bf16[3,144,256]{2,1,0:T(8,128)(2,1)S(1)} %bitcast.8), channel_id=1, source_target_pairs={{0,1},{1,0},{2,3},{3,2},{4,5},{5,4},{6,7},{7,6},{8,9},{9,8},{10,11... | collective-permute-start | bytes 663560 | tf_op jit(solution)/shard_map/ppermute | solution.py:441
  22.0 2.9 %collective-permute-start = (bf16[144,256]{1,0:T(8,128)(2,1)S(1)}, bf16[144,256]{1,0:T(8,128)(2,1)S(1)}, u32[]{:S(2)}, u32[]{:S(2)}) collective-permute-start(bf16[144,256]{1,0:T(8,128)(2,1)S(1)} %shard_map.127.o0.own_ref), channel_id=1, source_target_pairs={{0,1},{1,0},{2,3},{3,2},{4,5},{5,4},{6,7},{7,6},{8,9},{9,8},{10,11... | collective-permute-start | bytes 221192 | tf_op jit(solution)/shard_map/ppermute | solution.py:441
  22.1 4.1 %collective-permute-start.2 = (bf16[144,256]{1,0:T(8,128)(2,1)S(1)}, bf16[144,256]{1,0:T(8,128)(2,1)S(1)}, u32[]{:S(2)}, u32[]{:S(2)}) collective-permute-start(bf16[144,256]{1,0:T(8,128)(2,1)S(1)} %collective-permute-done.1.refs_4_.o2), channel_id=1, source_target_pairs={{0,1},{1,0},{2,3},{3,2},{4,5},{5,4},{6,7},{7,6},{8,9},{9,8},{10,11... | collective-permute-start | bytes 221192 | tf_op jit(solution)/shard_map/ppermute | solution.py:441
  22.5 15.5 %collective-permute-start.12 = (bf16[2,128,256]{2,1,0:T(8,128)(2,1)S(1)}, bf16[2,128,256]{2,1,0:T(8,128)(2,1)S(1)}, u32[]{:S(2)}, u32[]{:S(2)}) collective-permute-start(bf16[2,128,256]{2,1,0:T(8,128)(2,1)S(1)} %shard_map.131.later_ref.refs_0_.a0), channel_id=1, source_target_pairs={{0,12},{4,8},{8,4},{12,0},{1,13},{5,9},{9,5},{13,1},{2,14},{6,10},... | collective-permute-start | bytes 393224 | tf_op jit(solution)/shard_map/ppermute | solution.py:441
  24.9 13.1 %collective-permute-start.11 = (bf16[2,128,256]{2,1,0:T(8,128)(2,1)S(1)}, bf16[2,128,256]{2,1,0:T(8,128)(2,1)S(1)}, u32[]{:S(2)}, u32[]{:S(2)}) collective-permute-start(bf16[2,128,256]{2,1,0:T(8,128)(2,1)S(1)} %shard_map.131.later_ref.refs_0_.a0), channel_id=1, source_target_pairs={{0,8},{4,12},{8,0},{12,4},{1,9},{5,13},{9,1},{13,5},{2,10},{6,14},... | collective-permute-start | bytes 393224 | tf_op jit(solution)/shard_map/ppermute | solution.py:441
  38.5 2.0 %collective-permute-start.13 = (bf16[2,4,128,256]{3,2,1,0:T(8,128)(2,1)S(1)}, bf16[2,4,128,256]{3,2,1,0:T(8,128)(2,1)S(1)}, u32[]{:S(2)}, u32[]{:S(2)}) collective-permute-start(bf16[2,4,128,256]{3,2,1,0:T(8,128)(2,1)S(1)} %get-tuple-element.50), channel_id=1, source_target_pairs={{0,1},{1,0},{2,3},{3,2},{4,5},{5,4},{6,7},{7,6},{8,9},{9,8},{10,11... | collective-permute-start | bytes 1572872 | tf_op jit(solution)/shard_map/ppermute | solution.py:441
  38.6 2.6 %collective-permute-start.15 = (bf16[2,128,256]{2,1,0:T(8,128)(2,1)S(1)}, bf16[2,128,256]{2,1,0:T(8,128)(2,1)S(1)}, u32[]{:S(2)}, u32[]{:S(2)}) collective-permute-start(bf16[2,128,256]{2,1,0:T(8,128)(2,1)S(1)} %shard_map.131.later_ref.refs_0_.a0), channel_id=1, source_target_pairs={{0,1},{1,0},{2,3},{3,2},{4,5},{5,4},{6,7},{7,6},{8,9},{9,8},{10,11... | collective-permute-start | bytes 393224 | tf_op jit(solution)/shard_map/ppermute | solution.py:441
  39.1 2.1 %collective-permute-start.18 = (bf16[2,128,256]{2,1,0:T(8,128)(2,1)S(1)}, bf16[2,128,256]{2,1,0:T(8,128)(2,1)S(1)}, u32[]{:S(2)}, u32[]{:S(2)}) collective-permute-start(bf16[2,128,256]{2,1,0:T(8,128)(2,1)S(1)} %collective-permute-done.12.refs_3_.a3), channel_id=1, source_target_pairs={{0,1},{1,0},{2,3},{3,2},{4,5},{5,4},{6,7},{7,6},{8,9},{9,8},{10,11... | collective-permute-start | bytes 393224 | tf_op jit(solution)/shard_map/ppermute | solution.py:441
  39.2 2.0 %collective-permute-start.17 = (bf16[2,128,256]{2,1,0:T(8,128)(2,1)S(1)}, bf16[2,128,256]{2,1,0:T(8,128)(2,1)S(1)}, u32[]{:S(2)}, u32[]{:S(2)}) collective-permute-start(bf16[2,128,256]{2,1,0:T(8,128)(2,1)S(1)} %collective-permute-done.11.refs_2_.a2), channel_id=1, source_target_pairs={{0,1},{1,0},{2,3},{3,2},{4,5},{5,4},{6,7},{7,6},{8,9},{9,8},{10,11... | collective-permute-start | bytes 393224 | tf_op jit(solution)/shard_map/ppermute | solution.py:441
  40.6 10.3 %collective-permute-start.14 = (bf16[4,128,256]{2,1,0:T(8,128)(2,1)S(1)}, bf16[4,128,256]{2,1,0:T(8,128)(2,1)S(1)}, u32[]{:S(2)}, u32[]{:S(2)}) collective-permute-start(bf16[4,128,256]{2,1,0:T(8,128)(2,1)S(1)} %get-tuple-element.52), channel_id=1, source_target_pairs={{0,2},{1,3},{2,0},{3,1},{4,6},{5,7},{6,4},{7,5},{8,10},{9,11},{10,... | collective-permute-start | bytes 786440 | tf_op jit(solution)/shard_map/ppermute | solution.py:441
  51.3 3.7 %collective-permute-start.20 = (bf16[4,144,256]{2,1,0:T(8,128)(2,1)S(1)}, bf16[4,144,256]{2,1,0:T(8,128)(2,1)S(1)}, u32[]{:S(2)}, u32[]{:S(2)}) collective-permute-start(bf16[4,144,256]{2,1,0:T(8,128)(2,1)S(1)} %get-tuple-element.65), channel_id=1, source_target_pairs={{0,1},{1,0},{2,3},{3,2},{4,5},{5,4},{6,7},{7,6},{8,9},{9,8},{10,11... | collective-permute-start | bytes 884744 | tf_op jit(solution)/shard_map/ppermute | solution.py:441
  54.6 9.5 %collective-permute-start.19 = (bf16[4,144,256]{2,1,0:T(8,128)(2,1)S(1)}, bf16[4,144,256]{2,1,0:T(8,128)(2,1)S(1)}, u32[]{:S(2)}, u32[]{:S(2)}) collective-permute-start(bf16[4,144,256]{2,1,0:T(8,128)(2,1)S(1)} %get-tuple-element.64), channel_id=1, source_target_pairs={{0,1},{1,0},{2,3},{3,2},{4,5},{5,4},{6,7},{7,6},{8,9},{9,8},{10,11... | collective-permute-start | bytes 884744 | tf_op jit(solution)/shard_map/ppermute | solution.py:441
  55.1 9.1 %collective-permute-start.21 = (bf16[4,144,256]{2,1,0:T(8,128)(2,1)S(1)}, bf16[4,144,256]{2,1,0:T(8,128)(2,1)S(1)}, u32[]{:S(2)}, u32[]{:S(2)}) collective-permute-start(bf16[4,144,256]{2,1,0:T(8,128)(2,1)S(1)} %shard_map.139.refs_4_), channel_id=1, source_target_pairs={{0,2},{1,3},{2,0},{3,1},{4,6},{5,7},{6,4},{7,5},{8,10},{9,11},{10,... | collective-permute-start | bytes 884744 | tf_op jit(solution)/shard_map/ppermute | solution.py:441
  64.4 11.8 %collective-permute-start.22 = (bf16[272,256]{1,0:T(8,128)(2,1)S(1)}, bf16[272,256]{1,0:T(8,128)(2,1)S(1)}, u32[]{:S(2)}, u32[]{:S(2)}) collective-permute-start(bf16[272,256]{1,0:T(8,128)(2,1)S(1)} %get-tuple-element.71), channel_id=1, source_target_pairs={{0,4},{4,0},{8,12},{12,8},{1,5},{5,1},{9,13},{13,9},{2,6},{6,2},{1... | collective-permute-start | bytes 417800 | tf_op jit(solution)/shard_map/ppermute | solution.py:441
  65.1 13.2 %collective-permute-start.23 = (bf16[272,256]{1,0:T(8,128)(2,1)S(1)}, bf16[272,256]{1,0:T(8,128)(2,1)S(1)}, u32[]{:S(2)}, u32[]{:S(2)}) collective-permute-start(bf16[272,256]{1,0:T(8,128)(2,1)S(1)} %get-tuple-element.72), channel_id=1, source_target_pairs={{0,8},{4,12},{8,0},{12,4},{1,9},{5,13},{9,1},{13,5},{2,10},{6,14},... | collective-permute-start | bytes 417800 | tf_op jit(solution)/shard_map/ppermute | solution.py:441
  67.2 11.2 %collective-permute-start.24 = (bf16[272,256]{1,0:T(8,128)(2,1)S(1)}, bf16[272,256]{1,0:T(8,128)(2,1)S(1)}, u32[]{:S(2)}, u32[]{:S(2)}) collective-permute-start(bf16[272,256]{1,0:T(8,128)(2,1)S(1)} %get-tuple-element.73), channel_id=1, source_target_pairs={{0,12},{4,8},{8,4},{12,0},{1,13},{5,9},{9,5},{13,1},{2,14},{6,10},... | collective-permute-start | bytes 417800 | tf_op jit(solution)/shard_map/ppermute | solution.py:441
  (3 other events, 33.4 us)

commit v13 on v12

--- a/solution.py
+++ b/solution.py
@@ -237,20 +237,21 @@
 
 
 def backward_kernel(
-    a0, a1, a2, a3, n0, n1, n2, n3,
+    a01, a23, n01, n23,
     gate_ref, up_ref, down_hbm, act_ref, slope_ref, silu_ref, onehot, slot_gate, earlier_ref,
     back_rows, dots, rows_ref, p_ref, q_ref,
     down_ref, down_sems,
 ):
     sources, slots, tokens = onehot.shape
     experts = slots // CAP
-    width = a0.shape[2]
+    width = a01.shape[3]
     me = lax.axis_index("etp")
     start_down, wait_down = ring(down_hbm, down_ref, down_sems)
     there = half(me, 1, 2 * width)
-    for s, (here, near) in enumerate(((a0, n0), (a1, n1), (a2, n2), (a3, n3))):
+    for s in range(sources):
+        here, near = ((a01, n01), (a23, n23))[s // 2]
         for q in range(4):
-            block = (near if q % 2 else here)[q // 2]
+            block = (near if q % 2 else here)[s % 2, q // 2]
             picked = nn(onehot[s], block).astype(BF16).reshape(experts, CAP, width)
             rows_ref[:, s * CAP:(s + 1) * CAP, columns(me, q, width)] = picked
 
@@ -477,9 +478,10 @@
     came_across_there = swap(came, 2)
     across_near = swap(own_across, 1)
     grads = join([out_grad, grad_across], came)
-    grads = [grads] + [swap(grads, s, "expert") for s in range(1, sources)]
-
-    came_across = join([came_across_there], up_there, grads[1])[0]
+    near_grads = join([grads, swap(grads, 1, "expert")])
+    far_grads = swap(near_grads, 2, "expert")
+
+    came_across = join([came_across_there], up_there, near_grads)[0]
     out_rows, x_rows, activ, scaled, slope, silu, onehot, slot_gate = kernel_call(
         functools.partial(forward_kernel, choose),
         [
@@ -500,12 +502,12 @@
         capacity_blocks,
         own, swap(own, 1), own_across, across_near,
         came, swap(came, 1), came_across, swap(came_across, 1),
-        gate_t, up_t, down_weight, grads[0],
+        gate_t, up_t, down_weight, near_grads,
     )
 
     keep, send = kernel_call(
         home_kernel, [sent(2, sources, tokens, width)] * 2, [], 2 * slots * sources * tokens * model, limit=2,
-    )(onehot, out_rows, *grads)
+    )(onehot, out_rows, far_grads)
     out_near, out_far = add_cores(keep, swap(send, 1))
     back_rows, dots, y_rows, gate_part, up_part = kernel_call(
         backward_kernel,
@@ -519,9 +521,9 @@
         [pltpu.VMEM((RING, units, model), BF16), pltpu.SemaphoreType.DMA((RING,))],
         3 * product,
         limit=16,
-        in_hbm=(10,),
+        in_hbm=(6,),
     )(
-        *grads, *[swap(x, 1) for x in grads],
+        near_grads, far_grads, swap(near_grads, 1), swap(far_grads, 1),
         gate_t, up_t, down_weight, activ, slope, silu, onehot, slot_gate, out_near,
     )
 

time: 79.2 us -> 78.5 us (level)
  starting transfers between devices: 24.1 us -> 22.6 us
    ppermute x25 -> x22, starting transfers between devices: 24.1 us -> 22.6 us  [swap(): return lax.ppermute(array, axis, [(i, i ^ bit) for i in range(count)])]
    ppermute x25 -> x22, waiting for transfers between devices: 3.18 us -> 3.9 us  [swap(): return lax.ppermute(array, axis, [(i, i ^ bit) for i in range(count)])]
    pallas_call x15 -> x16, Pallas kernels: 42.1 us -> 42.1 us  [call(): pl.pallas_call(kernel, in_specs=specs, out_specs=out_specs or [pl.BlockSp...]
  transfers between devices with their start and end apart: 25 -> 22, of which waited for: 3 -> 4; matrix products, arithmetic and copies ran while one was open for 0% -> 0% of each run, Pallas kernels for 61% -> 62%
where the time goes in v13:
time: 78.5 us; the launch traced here: 78.3 us
  Pallas kernels  50.9 us (65%)
  starting transfers between devices  22.6 us (29%)
  waiting for transfers between devices  3.9 us (5%)
  between operations  0.89 us (1%)
    pallas_call x16, Pallas kernels, call(): pl.pallas_call(kernel, in_specs=specs, out_specs=out_specs or [pl.BlockSp...  42.1 us
    ppermute x22, starting transfers between devices, swap(): return lax.ppermute(array, axis, [(i, i ^ bit) for i in range(count)])  22.6 us
    pallas_call x2, Pallas kernels, in_vmem(): pl.pallas_call(load_kernel, in_specs=[pl.BlockSpec(memory_space=pltpu.HBM...  8.84 us
    ppermute x22, waiting for transfers between devices, swap(): return lax.ppermute(array, axis, [(i, i ^ bit) for i in range(count)])  3.9 us
  transfers between devices with their start and end apart: 22, of which 4 were waited for; matrix products, arithmetic and copies ran while one was open for 0% of the time, Pallas kernels for 62%

profile of v13, /device:TPU:0, one launch (start us, length us, event | category | flops | bytes accessed | tf_op | source)
XLA Modules:
  0.0 78.3 jit_solution(10018512348437076407)
XLA Ops:
  0.6 0.9 %shard_map.127.o0.own_ref = bf16[144,256]{1,0:T(8,128)(2,1)S(1)} custom-call(bf16[128,256]{1,0:T(8,128)(2,1)} %hidden_hbm.1, s32[6,128]{1,0:T(8,128)} %bitcast.13, f32[6,128]{1,0:T(8,128)} %bitcast.14), custom_call_target="tpu_custom_call" | custom-call | tf_op jit(solution)/shard_map/pallas_call | solution.py:406
  1.6 5.1 %collective-permute-start.5 = (bf16[144,256]{1,0:T(8,128)(2,1)S(1)}, bf16[144,256]{1,0:T(8,128)(2,1)S(1)}, u32[]{:S(2)}, u32[]{:S(2)}) collective-permute-start(bf16[144,256]{1,0:T(8,128)(2,1)S(1)} %shard_map.127.o0.own_ref), channel_id=1, source_target_pairs={{0,12},{4,8},{8,4},{12,0},{1,13},{5,9},{9,5},{13,1},{2,14},{6,10},... | collective-permute-start | bytes 221192 | tf_op jit(solution)/shard_map/ppermute | solution.py:442
  6.7 0.6 collective-permute-start.3
  7.3 1.6 %collective-permute-start.1 = (bf16[144,256]{1,0:T(8,128)(2,1)S(1)}, bf16[144,256]{1,0:T(8,128)(2,1)S(1)}, u32[]{:S(2)}, u32[]{:S(2)}) collective-permute-start(bf16[144,256]{1,0:T(8,128)(2,1)S(1)} %shard_map.127.o0.own_ref), channel_id=1, source_target_pairs={{0,2},{1,3},{2,0},{3,1},{4,6},{5,7},{6,4},{7,5},{8,10},{9,11},{10,... | collective-permute-start | bytes 221192 | tf_op jit(solution)/shard_map/ppermute | solution.py:442
  9.3 4.4 %shard_map.128 = (bf16[16,352,1024]{2,1,0:T(8,128)(2,1)S(1)}, f32[8,128]{1,0:T(8,128)S(1)}) custom-call(bf16[16,352,1024]{2,1,0:T(8,128)(2,1)} %bitcast.10), custom_call_target="tpu_custom_call" | custom-call | bytes 11534336 | tf_op jit(solution)/shard_map/pallas_call | solution.py:371
  13.9 1.7 %collective-permute-start.8 = (bf16[3,144,256]{2,1,0:T(8,128)(2,1)S(1)}, bf16[3,144,256]{2,1,0:T(8,128)(2,1)S(1)}, u32[]{:S(2)}, u32[]{:S(2)}) collective-permute-start(bf16[3,144,256]{2,1,0:T(8,128)(2,1)S(1)} %shard_map.129.refs_2_.b0.info_ref), channel_id=1, source_target_pairs={{0,2},{1,3},{2,0},{3,1},{4,6},{5,7},{6,4},{7,5},{8,10},{9,11},{10,... | collective-permute-start | bytes 663560 | tf_op jit(solution)/shard_map/ppermute | solution.py:442
  15.6 1.3 %collective-permute-start.9 = (bf16[2,128,256]{2,1,0:T(8,128)(2,1)S(1)}, bf16[2,128,256]{2,1,0:T(8,128)(2,1)S(1)}, u32[]{:S(2)}, u32[]{:S(2)}) collective-permute-start(bf16[2,128,256]{2,1,0:T(8,128)(2,1)S(1)} %shard_map.131.refs_0_), channel_id=1, source_target_pairs={{0,4},{4,0},{8,12},{12,8},{1,5},{5,1},{9,13},{13,9},{2,6},{6,2},{1... | collective-permute-start | bytes 393224 | tf_op jit(solution)/shard_map/ppermute | solution.py:442
  16.9 4.4 %shard_map.130 = (bf16[16,352,1024]{2,1,0:T(8,128)(2,1)S(1)}, f32[8,128]{1,0:T(8,128)S(1)}) custom-call(bf16[16,352,1024]{2,1,0:T(8,128)(2,1)} %bitcast.11), custom_call_target="tpu_custom_call" | custom-call | bytes 11534336 | tf_op jit(solution)/shard_map/pallas_call | solution.py:371
  21.5 0.5 collective-permute-start.10
  22.5 2.9 %collective-permute-start.11 = (bf16[2,2,128,256]{3,2,1,0:T(8,128)(2,1)S(1)}, bf16[2,2,128,256]{3,2,1,0:T(8,128)(2,1)S(1)}, u32[]{:S(2)}, u32[]{:S(2)}) collective-permute-start(bf16[2,2,128,256]{3,2,1,0:T(8,128)(2,1)S(1)} %shard_map.132.refs_2_.later_ref.a01), channel_id=1, source_target_pairs={{0,8},{4,12},{8,0},{12,4},{1,9},{5,13},{9,1},{13,5},{2,10},{6,14},... | collective-permute-start | bytes 786440 | tf_op jit(solution)/shard_map/ppermute | solution.py:442
  25.5 11.7 %shard_map.134 = (bf16[4,256,1024]{2,1,0:T(8,128)(2,1)S(1)}, bf16[16,64,1024]{2,1,0:T(8,128)(2,1)S(1)}, bf16[16,64,352]{2,1,0:T(8,128)(2,1)S(1)}, bf16[16,64,352...) custom-call(s32[64]{0:T(128)S(1)} %copy-done.1, ...), custom_call_target="tpu_custom_call" | custom-call | flops 2214592512 | bytes 69206016 | tf_op jit(solution)/shard_map/pallas_call | solution.py:406
  37.5 0.5 shard_map.135
  38.7 1.3 %collective-permute-done.12.came = bf16[2,4,128,256]{3,2,1,0:T(8,128)(2,1)S(1)} collective-permute-done((bf16[2,4,128,256]{3,2,1,0:T(8,128)(2,1)S(1)}, bf16[2,4,128,256]{3,2,1,0:T(8,128)(2,1)S(1)}, u32[]{:S(2)}, u32[]{:S(2)}) %collective-permute-start.12) | collective-permute-done | bytes 524320 | tf_op jit(solution)/shard_map/ppermute | solution.py:442
  40.1 0.7 collective-permute-start.13
  40.8 9.7 %shard_map.137 = (bf16[4,256,512]{2,1,0:T(8,128)(2,1)S(1)}, f32[16,64,128]{2,1,0:T(8,128)S(1)}, bf16[16,64,1024]{2,1,0:T(8,128)(2,1)S(1)}, bf16[16,64,352]{2,1,0:T(8,128)(2,1)S(1)}, bf16[16,64,352]{2,1,0:T(8,128)(2,1)S(1)}) custom-call(bf16[2,2,128,256]{3,2,1,0:T(8,128)(2,1)S(1)} %shard_map.132.refs_2_.later_ref.a01, ...), custom_call_target="tpu_custom_call" | custom-call | flops 2214592512 | bytes 69206016 | tf_op jit(solution)/shard_map/pallas_call | solution.py:406
  51.0 3.1 %shard_map.139 = (bf16[4,144,256]{2,1,0:T(8,128)(2,1)S(1)}, bf16[4,144,256]{2,1,0:T(8,128)(2,1)S(1)}) custom-call(bf16[16,352,1024]{2,1,0:T(8,128)(2,1)S(1)} %get-tuple-element.45.gate_ref, bf16[16,352,1024]{2,1,0:T(8,128)(2,1)S(1)} %get-tuple-element.46.up_ref, bf16[16,64,352]{2,1,0:T(8,128)(2,1)S(1)} %get-tuple-element.57.p_ref.refs_1_, ...), custom_call_target="tpu_custom_call" | custom-call | flops 738197504 | bytes 23068672 | tf_op jit(solution)/shard_map/pallas_call | solution.py:406
  54.2 0.5 collective-permute-start.16
  54.7 1.4 %collective-permute-start.18 = (bf16[4,144,256]{2,1,0:T(8,128)(2,1)S(1)}, bf16[4,144,256]{2,1,0:T(8,128)(2,1)S(1)}, u32[]{:S(2)}, u32[]{:S(2)}) collective-permute-start(bf16[4,144,256]{2,1,0:T(8,128)(2,1)S(1)} %shard_map.140.refs_4_), channel_id=1, source_target_pairs={{0,2},{1,3},{2,0},{3,1},{4,6},{5,7},{6,4},{7,5},{8,10},{9,11},{10,... | collective-permute-start | bytes 884744 | tf_op jit(solution)/shard_map/ppermute | solution.py:442
  56.1 7.3 %shard_map.141 = (bf16[16,352,1024]{2,1,0:T(8,128)(2,1)}, bf16[16,352,1024]{2,1,0:T(8,128)(2,1)}) custom-call(bf16[16,64,352]{2,1,0:T(8,128)(2,1)S(1)} %get-tuple-element.58.q_ref.refs_0_, bf16[16,64,352]{2,1,0:T(8,128)(2,1)S(1)} %get-tuple-element.66.refs_1_.refs_0_, bf16[16,64,1024]{2,1,0:T(8,128)(2,1)S(1)} %get-tuple-element.67.refs_2_.refs_3_, ...), custom_call_target="tpu_custom_call" | custom-call | flops 1107296256 | bytes 34603008 | tf_op jit(solution)/shard_map/pallas_call | solution.py:406
  64.0 3.3 %collective-permute-start.20 = (bf16[272,256]{1,0:T(8,128)(2,1)S(1)}, bf16[272,256]{1,0:T(8,128)(2,1)S(1)}, u32[]{:S(2)}, u32[]{:S(2)}) collective-permute-start(bf16[272,256]{1,0:T(8,128)(2,1)S(1)} %get-tuple-element.72), channel_id=1, source_target_pairs={{0,8},{4,12},{8,0},{12,4},{1,9},{5,13},{9,1},{13,5},{2,10},{6,14},... | collective-permute-start | bytes 417800 | tf_op jit(solution)/shard_map/ppermute | solution.py:442
  67.3 1.1 %collective-permute-start.21 = (bf16[272,256]{1,0:T(8,128)(2,1)S(1)}, bf16[272,256]{1,0:T(8,128)(2,1)S(1)}, u32[]{:S(2)}, u32[]{:S(2)}) collective-permute-start(bf16[272,256]{1,0:T(8,128)(2,1)S(1)} %get-tuple-element.73), channel_id=1, source_target_pairs={{0,12},{4,8},{8,4},{12,0},{1,13},{5,9},{9,5},{13,1},{2,14},{6,10},... | collective-permute-start | bytes 417800 | tf_op jit(solution)/shard_map/ppermute | solution.py:442
  68.4 7.3 %shard_map.144 = (bf16[16,352,1024]{2,1,0:T(8,128)(2,1)}, bf16[16,352,1024]{2,1,0:T(8,128)(2,1)}) custom-call(bf16[16,64,352]{2,1,0:T(8,128)(2,1)S(1)} %get-tuple-element.66.refs_1_.refs_0_, bf16[16,64,352]{2,1,0:T(8,128)(2,1)S(1)} %get-tuple-element.57.p_ref.refs_1_, ...), custom_call_target="tpu_custom_call", output_to_operand_aliasing={{0}: (4, {})} | custom-call | flops 1107296256 | bytes 34603008 | tf_op jit(solution)/shard_map/pallas_call | solution.py:406
  75.8 1.8 %collective-permute-done.20.refs_2_ = bf16[272,256]{1,0:T(8,128)(2,1)S(1)} collective-permute-done((bf16[272,256]{1,0:T(8,128)(2,1)S(1)}, bf16[272,256]{1,0:T(8,128)(2,1)S(1)}, u32[]{:S(2)}, u32[]{:S(2)}) %collective-permute-start.20) | collective-permute-done | bytes 139296 | tf_op jit(solution)/shard_map/ppermute | solution.py:442
  77.6 0.7 shard_map.143
  (42 shorter events, 3.4 us)
Async XLA Ops:
  0.6 14.9 %copy-start = (bf16[128,256]{1,0:T(8,128)(2,1)S(1)}, bf16[128,256]{1,0:T(8,128)(2,1)}, u32[]{:S(2)}) copy-start(bf16[128,256]{1,0:T(8,128)(2,1)} %refs_0_.1) | copy-start | bytes 196612
  1.6 12.2 %collective-permute-start.5 = (bf16[144,256]{1,0:T(8,128)(2,1)S(1)}, bf16[144,256]{1,0:T(8,128)(2,1)S(1)}, u32[]{:S(2)}, u32[]{:S(2)}) collective-permute-start(bf16[144,256]{1,0:T(8,128)(2,1)S(1)} %shard_map.127.o0.own_ref), channel_id=1, source_target_pairs={{0,12},{4,8},{8,4},{12,0},{1,13},{5,9},{9,5},{13,1},{2,14},{6,10},... | collective-permute-start | bytes 221192 | tf_op jit(solution)/shard_map/ppermute | solution.py:442
  6.7 7.1 %collective-permute-start.4 = (bf16[144,256]{1,0:T(8,128)(2,1)S(1)}, bf16[144,256]{1,0:T(8,128)(2,1)S(1)}, u32[]{:S(2)}, u32[]{:S(2)}) collective-permute-start(bf16[144,256]{1,0:T(8,128)(2,1)S(1)} %shard_map.127.o0.own_ref), channel_id=1, source_target_pairs={{0,8},{4,12},{8,0},{12,4},{1,9},{5,13},{9,1},{13,5},{2,10},{6,14},... | collective-permute-start | bytes 221192 | tf_op jit(solution)/shard_map/ppermute | solution.py:442
  6.7 7.1 %collective-permute-start.3 = (bf16[144,256]{1,0:T(8,128)(2,1)S(1)}, bf16[144,256]{1,0:T(8,128)(2,1)S(1)}, u32[]{:S(2)}, u32[]{:S(2)}) collective-permute-start(bf16[144,256]{1,0:T(8,128)(2,1)S(1)} %shard_map.127.o0.own_ref), channel_id=1, source_target_pairs={{0,4},{4,0},{8,12},{12,8},{1,5},{5,1},{9,13},{13,9},{2,6},{6,2},{1... | collective-permute-start | bytes 221192 | tf_op jit(solution)/shard_map/ppermute | solution.py:442
  7.3 6.5 %collective-permute-start.1 = (bf16[144,256]{1,0:T(8,128)(2,1)S(1)}, bf16[144,256]{1,0:T(8,128)(2,1)S(1)}, u32[]{:S(2)}, u32[]{:S(2)}) collective-permute-start(bf16[144,256]{1,0:T(8,128)(2,1)S(1)} %shard_map.127.o0.own_ref), channel_id=1, source_target_pairs={{0,2},{1,3},{2,0},{3,1},{4,6},{5,7},{6,4},{7,5},{8,10},{9,11},{10,... | collective-permute-start | bytes 221192 | tf_op jit(solution)/shard_map/ppermute | solution.py:442
  9.0 4.8 %collective-permute-start.6 = (bf16[128,256]{1,0:T(8,128)(2,1)}, bf16[128,256]{1,0:T(8,128)(2,1)S(1)}, u32[]{:S(2)}, u32[]{:S(2)}) collective-permute-start(bf16[128,256]{1,0:T(8,128)(2,1)} %refs_0_.1), channel_id=1, source_target_pairs={{0,2},{1,3},{2,0},{3,1},{4,6},{5,7},{6,4},{7,5},{8,10},{9,11},{10,... | collective-permute-start | bytes 196616 | tf_op jit(solution)/shard_map/ppermute | solution.py:442
  9.3 16.1 %copy-start.1 = (s32[64]{0:T(128)S(1)}, s32[64]{0:T(128)}, u32[]{:S(2)}) copy-start(s32[64]{0:T(128)} %capacity_ref.1) | copy-start | bytes 772
  13.9 7.6 %collective-permute-start.8 = (bf16[3,144,256]{2,1,0:T(8,128)(2,1)S(1)}, bf16[3,144,256]{2,1,0:T(8,128)(2,1)S(1)}, u32[]{:S(2)}, u32[]{:S(2)}) collective-permute-start(bf16[3,144,256]{2,1,0:T(8,128)(2,1)S(1)} %shard_map.129.refs_2_.b0.info_ref), channel_id=1, source_target_pairs={{0,2},{1,3},{2,0},{3,1},{4,6},{5,7},{6,4},{7,5},{8,10},{9,11},{10,... | collective-permute-start | bytes 663560 | tf_op jit(solution)/shard_map/ppermute | solution.py:442
  15.6 5.8 %collective-permute-start.9 = (bf16[2,128,256]{2,1,0:T(8,128)(2,1)S(1)}, bf16[2,128,256]{2,1,0:T(8,128)(2,1)S(1)}, u32[]{:S(2)}, u32[]{:S(2)}) collective-permute-start(bf16[2,128,256]{2,1,0:T(8,128)(2,1)S(1)} %shard_map.131.refs_0_), channel_id=1, source_target_pairs={{0,4},{4,0},{8,12},{12,8},{1,5},{5,1},{9,13},{13,9},{2,6},{6,2},{1... | collective-permute-start | bytes 393224 | tf_op jit(solution)/shard_map/ppermute | solution.py:442
  21.3 4.1 %collective-permute-start.7 = (bf16[3,144,256]{2,1,0:T(8,128)(2,1)S(1)}, bf16[3,144,256]{2,1,0:T(8,128)(2,1)S(1)}, u32[]{:S(2)}, u32[]{:S(2)}) collective-permute-start(bf16[3,144,256]{2,1,0:T(8,128)(2,1)S(1)} %shard_map.129.refs_2_.b0.info_ref), channel_id=1, source_target_pairs={{0,1},{1,0},{2,3},{3,2},{4,5},{5,4},{6,7},{7,6},{8,9},{9,8},{10,11... | collective-permute-start | bytes 663560 | tf_op jit(solution)/shard_map/ppermute | solution.py:442
  21.5 4.0 %collective-permute-start.10 = (bf16[3,144,256]{2,1,0:T(8,128)(2,1)S(1)}, bf16[3,144,256]{2,1,0:T(8,128)(2,1)S(1)}, u32[]{:S(2)}, u32[]{:S(2)}) collective-permute-start(bf16[3,144,256]{2,1,0:T(8,128)(2,1)S(1)} %bitcast.8), channel_id=1, source_target_pairs={{0,1},{1,0},{2,3},{3,2},{4,5},{5,4},{6,7},{7,6},{8,9},{9,8},{10,11... | collective-permute-start | bytes 663560 | tf_op jit(solution)/shard_map/ppermute | solution.py:442
  22.0 3.4 %collective-permute-start = (bf16[144,256]{1,0:T(8,128)(2,1)S(1)}, bf16[144,256]{1,0:T(8,128)(2,1)S(1)}, u32[]{:S(2)}, u32[]{:S(2)}) collective-permute-start(bf16[144,256]{1,0:T(8,128)(2,1)S(1)} %shard_map.127.o0.own_ref), channel_id=1, source_target_pairs={{0,1},{1,0},{2,3},{3,2},{4,5},{5,4},{6,7},{7,6},{8,9},{9,8},{10,11... | collective-permute-start | bytes 221192 | tf_op jit(solution)/shard_map/ppermute | solution.py:442
  22.1 3.4 %collective-permute-start.2 = (bf16[144,256]{1,0:T(8,128)(2,1)S(1)}, bf16[144,256]{1,0:T(8,128)(2,1)S(1)}, u32[]{:S(2)}, u32[]{:S(2)}) collective-permute-start(bf16[144,256]{1,0:T(8,128)(2,1)S(1)} %collective-permute-done.1.refs_4_.o2), channel_id=1, source_target_pairs={{0,1},{1,0},{2,3},{3,2},{4,5},{5,4},{6,7},{7,6},{8,9},{9,8},{10,11... | collective-permute-start | bytes 221192 | tf_op jit(solution)/shard_map/ppermute | solution.py:442
  22.5 15.0 %collective-permute-start.11 = (bf16[2,2,128,256]{3,2,1,0:T(8,128)(2,1)S(1)}, bf16[2,2,128,256]{3,2,1,0:T(8,128)(2,1)S(1)}, u32[]{:S(2)}, u32[]{:S(2)}) collective-permute-start(bf16[2,2,128,256]{3,2,1,0:T(8,128)(2,1)S(1)} %shard_map.132.refs_2_.later_ref.a01), channel_id=1, source_target_pairs={{0,8},{4,12},{8,0},{12,4},{1,9},{5,13},{9,1},{13,5},{2,10},{6,14},... | collective-permute-start | bytes 786440 | tf_op jit(solution)/shard_map/ppermute | solution.py:442
  38.0 2.0 %collective-permute-start.12 = (bf16[2,4,128,256]{3,2,1,0:T(8,128)(2,1)S(1)}, bf16[2,4,128,256]{3,2,1,0:T(8,128)(2,1)S(1)}, u32[]{:S(2)}, u32[]{:S(2)}) collective-permute-start(bf16[2,4,128,256]{3,2,1,0:T(8,128)(2,1)S(1)} %get-tuple-element.50), channel_id=1, source_target_pairs={{0,1},{1,0},{2,3},{3,2},{4,5},{5,4},{6,7},{7,6},{8,9},{9,8},{10,11... | collective-permute-start | bytes 1572872 | tf_op jit(solution)/shard_map/ppermute | solution.py:442
  38.2 2.6 %collective-permute-start.14 = (bf16[2,2,128,256]{3,2,1,0:T(8,128)(2,1)S(1)}, bf16[2,2,128,256]{3,2,1,0:T(8,128)(2,1)S(1)}, u32[]{:S(2)}, u32[]{:S(2)}) collective-permute-start(bf16[2,2,128,256]{3,2,1,0:T(8,128)(2,1)S(1)} %shard_map.132.refs_2_.later_ref.a01), channel_id=1, source_target_pairs={{0,1},{1,0},{2,3},{3,2},{4,5},{5,4},{6,7},{7,6},{8,9},{9,8},{10,11... | collective-permute-start | bytes 786440 | tf_op jit(solution)/shard_map/ppermute | solution.py:442
  38.6 2.2 %collective-permute-start.15 = (bf16[2,2,128,256]{3,2,1,0:T(8,128)(2,1)S(1)}, bf16[2,2,128,256]{3,2,1,0:T(8,128)(2,1)S(1)}, u32[]{:S(2)}, u32[]{:S(2)}) collective-permute-start(bf16[2,2,128,256]{3,2,1,0:T(8,128)(2,1)S(1)} %collective-permute-done.11.refs_0_.a23), channel_id=1, source_target_pairs={{0,1},{1,0},{2,3},{3,2},{4,5},{5,4},{6,7},{7,6},{8,9},{9,8},{10,11... | collective-permute-start | bytes 786440 | tf_op jit(solution)/shard_map/ppermute | solution.py:442
  40.1 10.3 %collective-permute-start.13 = (bf16[4,128,256]{2,1,0:T(8,128)(2,1)S(1)}, bf16[4,128,256]{2,1,0:T(8,128)(2,1)S(1)}, u32[]{:S(2)}, u32[]{:S(2)}) collective-permute-start(bf16[4,128,256]{2,1,0:T(8,128)(2,1)S(1)} %get-tuple-element.52), channel_id=1, source_target_pairs={{0,2},{1,3},{2,0},{3,1},{4,6},{5,7},{6,4},{7,5},{8,10},{9,11},{10,... | collective-permute-start | bytes 786440 | tf_op jit(solution)/shard_map/ppermute | solution.py:442
  50.9 3.7 %collective-permute-start.17 = (bf16[4,144,256]{2,1,0:T(8,128)(2,1)S(1)}, bf16[4,144,256]{2,1,0:T(8,128)(2,1)S(1)}, u32[]{:S(2)}, u32[]{:S(2)}) collective-permute-start(bf16[4,144,256]{2,1,0:T(8,128)(2,1)S(1)} %get-tuple-element.65), channel_id=1, source_target_pairs={{0,1},{1,0},{2,3},{3,2},{4,5},{5,4},{6,7},{7,6},{8,9},{9,8},{10,11... | collective-permute-start | bytes 884744 | tf_op jit(solution)/shard_map/ppermute | solution.py:442
  54.2 9.3 %collective-permute-start.16 = (bf16[4,144,256]{2,1,0:T(8,128)(2,1)S(1)}, bf16[4,144,256]{2,1,0:T(8,128)(2,1)S(1)}, u32[]{:S(2)}, u32[]{:S(2)}) collective-permute-start(bf16[4,144,256]{2,1,0:T(8,128)(2,1)S(1)} %get-tuple-element.64), channel_id=1, source_target_pairs={{0,1},{1,0},{2,3},{3,2},{4,5},{5,4},{6,7},{7,6},{8,9},{9,8},{10,11... | collective-permute-start | bytes 884744 | tf_op jit(solution)/shard_map/ppermute | solution.py:442
  54.7 9.1 %collective-permute-start.18 = (bf16[4,144,256]{2,1,0:T(8,128)(2,1)S(1)}, bf16[4,144,256]{2,1,0:T(8,128)(2,1)S(1)}, u32[]{:S(2)}, u32[]{:S(2)}) collective-permute-start(bf16[4,144,256]{2,1,0:T(8,128)(2,1)S(1)} %shard_map.140.refs_4_), channel_id=1, source_target_pairs={{0,2},{1,3},{2,0},{3,1},{4,6},{5,7},{6,4},{7,5},{8,10},{9,11},{10,... | collective-permute-start | bytes 884744 | tf_op jit(solution)/shard_map/ppermute | solution.py:442
  64.0 11.8 %collective-permute-start.19 = (bf16[272,256]{1,0:T(8,128)(2,1)S(1)}, bf16[272,256]{1,0:T(8,128)(2,1)S(1)}, u32[]{:S(2)}, u32[]{:S(2)}) collective-permute-start(bf16[272,256]{1,0:T(8,128)(2,1)S(1)} %get-tuple-element.71), channel_id=1, source_target_pairs={{0,4},{4,0},{8,12},{12,8},{1,5},{5,1},{9,13},{13,9},{2,6},{6,2},{1... | collective-permute-start | bytes 417800 | tf_op jit(solution)/shard_map/ppermute | solution.py:442
  64.0 13.6 %collective-permute-start.20 = (bf16[272,256]{1,0:T(8,128)(2,1)S(1)}, bf16[272,256]{1,0:T(8,128)(2,1)S(1)}, u32[]{:S(2)}, u32[]{:S(2)}) collective-permute-start(bf16[272,256]{1,0:T(8,128)(2,1)S(1)} %get-tuple-element.72), channel_id=1, source_target_pairs={{0,8},{4,12},{8,0},{12,4},{1,9},{5,13},{9,1},{13,5},{2,10},{6,14},... | collective-permute-start | bytes 417800 | tf_op jit(solution)/shard_map/ppermute | solution.py:442
  67.3 10.3 %collective-permute-start.21 = (bf16[272,256]{1,0:T(8,128)(2,1)S(1)}, bf16[272,256]{1,0:T(8,128)(2,1)S(1)}, u32[]{:S(2)}, u32[]{:S(2)}) collective-permute-start(bf16[272,256]{1,0:T(8,128)(2,1)S(1)} %get-tuple-element.73), channel_id=1, source_target_pairs={{0,12},{4,8},{8,4},{12,0},{1,13},{5,9},{9,5},{13,1},{2,14},{6,10},... | collective-permute-start | bytes 417800 | tf_op jit(solution)/shard_map/ppermute | solution.py:442

commit v14 on v13

--- a/solution.py
+++ b/solution.py
@@ -299,24 +299,30 @@
     refs[-1][...] = (keep[...].astype(F32) + came[...].astype(F32)).astype(BF16)
 
 
-def chips_kernel(out_near, out_came, back_keep, back_near, back_came, *refs):
-    sources, tokens = out_near.shape[:2]
+def pairs_kernel(near, came, *refs):
+    for s in range(near.shape[0]):
+        refs[-2 + s % 2][s // 2] = (near[s].astype(F32) + came[s].astype(F32)).astype(BF16)
+
+
+def chips_kernel(out_even, out_came, back_keep, back_near, back_came, *refs):
+    sources, tokens = back_keep.shape[0], out_even.shape[1]
     parts = refs[-sources:]
     for s in range(sources):
-        parts[s][0:tokens, :] = (out_near[s].astype(F32) + out_came[s].astype(F32)).astype(BF16)
         back = back_keep[s].astype(F32) + back_near[s].astype(F32) + back_came[s].astype(F32)
-        parts[s][tokens:, :] = back.astype(BF16)
-
-
-def total_kernel(count, *refs):
-    out_ref, back_ref, value_ref = refs[count:]
+        start = 0
+        if s % 2 == 0:
+            parts[s][0:tokens, :] = (out_even[s // 2].astype(F32) + out_came[s // 2].astype(F32)).astype(BF16)
+            start = tokens
+        parts[s][start:, :] = back.astype(BF16)
+
+
+def total_kernel(p0, p1, p2, p3, out_ref, back_ref, value_ref):
     tokens = out_ref.shape[0]
-    total = refs[0][...].astype(F32)
-    for ref in refs[1:count]:
-        total = total + ref[...].astype(F32)
-    out_ref[...] = total[0:tokens].astype(BF16)
-    back_ref[...] = total[tokens:2 * tokens].astype(BF16)
-    value_ref[...] = total[2 * tokens:2 * tokens + value_ref.shape[0], 0:value_ref.shape[1]]
+    both = p0[...].astype(F32) + p2[...].astype(F32)
+    out_ref[...] = both[0:tokens].astype(BF16)
+    back = both[tokens:] + p1[...].astype(F32) + p3[...].astype(F32)
+    back_ref[...] = back[0:tokens].astype(BF16)
+    value_ref[...] = back[tokens:tokens + value_ref.shape[0], 0:value_ref.shape[1]]
 
 
 BANKS = 8
@@ -527,7 +533,9 @@
         gate_t, up_t, down_weight, activ, slope, silu, onehot, slot_gate, out_near,
     )
 
-    out_came = swap(out_far, 2)
+    pair = sent(2, tokens, width)
+    out_even, out_odd = kernel_call(pairs_kernel, [pair, pair], [], 0, limit=2)(out_near, swap(out_far, 2))
+    out_came = swap(out_odd, 1, "expert")
     back_sum = sent(sources, tokens + EXTRA, width)
     far_keep, far_send, values = kernel_call(
         functools.partial(values_kernel, choose),
@@ -535,7 +543,7 @@
         [],
         slots * sources * tokens * model,
         limit=2,
-    )(onehot, back_rows, dots, own, came, out_came)
+    )(onehot, back_rows, dots, own, came, out_even)
     near_keep, near_send = kernel_call(
         own_kernel,
         [back_sum, back_sum],
@@ -549,14 +557,15 @@
         [(up_part, x_rows, 0, local_experts), (scaled, y_rows, 0, some)], None, back_far
     )
     height = 2 * tokens + EXTRA
-    parts = kernel_call(chips_kernel, [sent(height, width)] * sources, [], 0, limit=2, in_hbm=(5,))(
-        out_near, out_came, near_keep, swap(near_send, 1), swap(back_far, 2), up_grad
+    heights = [sent(height - tokens * (s % 2), width) for s in range(sources)]
+    parts = kernel_call(chips_kernel, heights, [], 0, limit=2, in_hbm=(5,))(
+        out_even, out_came, near_keep, swap(near_send, 1), swap(back_far, 2), up_grad
     )
     down_grad, gate_grad = weight_grads(
         [(scaled, y_rows, some, local_experts), (gate_part, x_rows, 0, local_experts)], down_grad, parts[0]
     )
     layer_out, input_grad, value_grad = kernel_call(
-        functools.partial(total_kernel, sources),
+        total_kernel,
         [sent(tokens, width), sent(tokens, width), jax.ShapeDtypeStruct((choose, tokens), F32)],
         [],
         0,

time: 78.5 us -> 76.8 us (0.978)
  waiting for transfers between devices: 3.9 us -> 1.94 us
    ppermute x22 -> x23, waiting for transfers between devices: 3.9 us -> 1.94 us  [swap(): return lax.ppermute(array, axis, [(i, i ^ bit) for i in range(count)])]
    ppermute x22 -> x23, starting transfers between devices: 22.6 us -> 22.8 us  [swap(): return lax.ppermute(array, axis, [(i, i ^ bit) for i in range(count)])]
    pallas_call x16 -> x17, Pallas kernels: 42.1 us -> 42.1 us  [call(): pl.pallas_call(kernel, in_specs=specs, out_specs=out_specs or [pl.BlockSp...]
  transfers between devices with their start and end apart: 22 -> 23, of which waited for: 4 -> 3; matrix products, arithmetic and copies ran while one was open for 0% -> 0% of each run, Pallas kernels for 62% -> 63%
where the time goes in v14:
time: 76.8 us; the launch traced here: 76.6 us
  Pallas kernels  51 us (66%)
  starting transfers between devices  22.8 us (30%)
  waiting for transfers between devices  1.94 us (3%)
  between operations  0.91 us (1%)
    pallas_call x17, Pallas kernels, call(): pl.pallas_call(kernel, in_specs=specs, out_specs=out_specs or [pl.BlockSp...  42.1 us
    ppermute x23, starting transfers between devices, swap(): return lax.ppermute(array, axis, [(i, i ^ bit) for i in range(count)])  22.8 us
    pallas_call x2, Pallas kernels, in_vmem(): pl.pallas_call(load_kernel, in_specs=[pl.BlockSpec(memory_space=pltpu.HBM...  8.84 us
    ppermute x23, waiting for transfers between devices, swap(): return lax.ppermute(array, axis, [(i, i ^ bit) for i in range(count)])  1.94 us
  transfers between devices with their start and end apart: 23, of which 3 were waited for; matrix products, arithmetic and copies ran while one was open for 0% of the time, Pallas kernels for 63%

profile of v14, /device:TPU:0, one launch (start us, length us, event | category | flops | bytes accessed | tf_op | source)
XLA Modules:
  0.0 76.6 jit_solution(1404073218352773441)
XLA Ops:
  0.6 0.9 %shard_map.127.o0.own_ref = bf16[144,256]{1,0:T(8,128)(2,1)S(1)} custom-call(bf16[128,256]{1,0:T(8,128)(2,1)} %hidden_hbm.1, s32[6,128]{1,0:T(8,128)} %bitcast.13, f32[6,128]{1,0:T(8,128)} %bitcast.14), custom_call_target="tpu_custom_call" | custom-call | tf_op jit(solution)/shard_map/pallas_call | solution.py:412
  1.6 5.1 %collective-permute-start.5 = (bf16[144,256]{1,0:T(8,128)(2,1)S(1)}, bf16[144,256]{1,0:T(8,128)(2,1)S(1)}, u32[]{:S(2)}, u32[]{:S(2)}) collective-permute-start(bf16[144,256]{1,0:T(8,128)(2,1)S(1)} %shard_map.127.o0.own_ref), channel_id=1, source_target_pairs={{0,12},{4,8},{8,4},{12,0},{1,13},{5,9},{9,5},{13,1},{2,14},{6,10},... | collective-permute-start | bytes 221192 | tf_op jit(solution)/shard_map/ppermute | solution.py:448
  6.7 0.6 collective-permute-start.3
  7.3 1.6 %collective-permute-start.1 = (bf16[144,256]{1,0:T(8,128)(2,1)S(1)}, bf16[144,256]{1,0:T(8,128)(2,1)S(1)}, u32[]{:S(2)}, u32[]{:S(2)}) collective-permute-start(bf16[144,256]{1,0:T(8,128)(2,1)S(1)} %shard_map.127.o0.own_ref), channel_id=1, source_target_pairs={{0,2},{1,3},{2,0},{3,1},{4,6},{5,7},{6,4},{7,5},{8,10},{9,11},{10,... | collective-permute-start | bytes 221192 | tf_op jit(solution)/shard_map/ppermute | solution.py:448
  9.3 4.4 %shard_map.128 = (bf16[16,352,1024]{2,1,0:T(8,128)(2,1)S(1)}, f32[8,128]{1,0:T(8,128)S(1)}) custom-call(bf16[16,352,1024]{2,1,0:T(8,128)(2,1)} %bitcast.10), custom_call_target="tpu_custom_call" | custom-call | bytes 11534336 | tf_op jit(solution)/shard_map/pallas_call | solution.py:377
  13.9 1.7 %collective-permute-start.8 = (bf16[3,144,256]{2,1,0:T(8,128)(2,1)S(1)}, bf16[3,144,256]{2,1,0:T(8,128)(2,1)S(1)}, u32[]{:S(2)}, u32[]{:S(2)}) collective-permute-start(bf16[3,144,256]{2,1,0:T(8,128)(2,1)S(1)} %shard_map.129.refs_2_.b0.info_ref), channel_id=1, source_target_pairs={{0,2},{1,3},{2,0},{3,1},{4,6},{5,7},{6,4},{7,5},{8,10},{9,11},{10,... | collective-permute-start | bytes 663560 | tf_op jit(solution)/shard_map/ppermute | solution.py:448
  15.6 1.3 %collective-permute-start.9 = (bf16[2,128,256]{2,1,0:T(8,128)(2,1)S(1)}, bf16[2,128,256]{2,1,0:T(8,128)(2,1)S(1)}, u32[]{:S(2)}, u32[]{:S(2)}) collective-permute-start(bf16[2,128,256]{2,1,0:T(8,128)(2,1)S(1)} %shard_map.131.refs_0_), channel_id=1, source_target_pairs={{0,4},{4,0},{8,12},{12,8},{1,5},{5,1},{9,13},{13,9},{2,6},{6,2},{1... | collective-permute-start | bytes 393224 | tf_op jit(solution)/shard_map/ppermute | solution.py:448
  16.9 4.4 %shard_map.130 = (bf16[16,352,1024]{2,1,0:T(8,128)(2,1)S(1)}, f32[8,128]{1,0:T(8,128)S(1)}) custom-call(bf16[16,352,1024]{2,1,0:T(8,128)(2,1)} %bitcast.11), custom_call_target="tpu_custom_call" | custom-call | bytes 11534336 | tf_op jit(solution)/shard_map/pallas_call | solution.py:377
  21.5 0.5 collective-permute-start.10
  22.5 2.9 %collective-permute-start.11 = (bf16[2,2,128,256]{3,2,1,0:T(8,128)(2,1)S(1)}, bf16[2,2,128,256]{3,2,1,0:T(8,128)(2,1)S(1)}, u32[]{:S(2)}, u32[]{:S(2)}) collective-permute-start(bf16[2,2,128,256]{3,2,1,0:T(8,128)(2,1)S(1)} %shard_map.132.refs_2_.later_ref.a01), channel_id=1, source_target_pairs={{0,8},{4,12},{8,0},{12,4},{1,9},{5,13},{9,1},{13,5},{2,10},{6,14},... | collective-permute-start | bytes 786440 | tf_op jit(solution)/shard_map/ppermute | solution.py:448
  25.5 11.7 %shard_map.134 = (bf16[4,256,1024]{2,1,0:T(8,128)(2,1)S(1)}, bf16[16,64,1024]{2,1,0:T(8,128)(2,1)S(1)}, bf16[16,64,352]{2,1,0:T(8,128)(2,1)S(1)}, bf16[16,64,352...) custom-call(s32[64]{0:T(128)S(1)} %copy-done.1, ...), custom_call_target="tpu_custom_call" | custom-call | flops 2214592512 | bytes 69206016 | tf_op jit(solution)/shard_map/pallas_call | solution.py:412
  37.5 0.5 shard_map.135
  38.2 0.5 collective-permute-start.15
  38.7 1.3 %collective-permute-done.12.came = bf16[2,4,128,256]{3,2,1,0:T(8,128)(2,1)S(1)} collective-permute-done((bf16[2,4,128,256]{3,2,1,0:T(8,128)(2,1)S(1)}, bf16[2,4,128,256]{3,2,1,0:T(8,128)(2,1)S(1)}, u32[]{:S(2)}, u32[]{:S(2)}) %collective-permute-start.12) | collective-permute-done | bytes 524320 | tf_op jit(solution)/shard_map/ppermute | solution.py:448
  40.1 0.7 collective-permute-start.13
  40.8 9.7 %shard_map.138 = (bf16[4,256,512]{2,1,0:T(8,128)(2,1)S(1)}, f32[16,64,128]{2,1,0:T(8,128)S(1)}, bf16[16,64,1024]{2,1,0:T(8,128)(2,1)S(1)}, bf16[16,64,352]{2,1,0:T(8,128)(2,1)S(1)}, bf16[16,64,352]{2,1,0:T(8,128)(2,1)S(1)}) custom-call(bf16[2,2,128,256]{3,2,1,0:T(8,128)(2,1)S(1)} %shard_map.132.refs_2_.later_ref.a01, ...), custom_call_target="tpu_custom_call" | custom-call | flops 2214592512 | bytes 69206016 | tf_op jit(solution)/shard_map/pallas_call | solution.py:412
  51.1 3.1 %shard_map.140 = (bf16[4,144,256]{2,1,0:T(8,128)(2,1)S(1)}, bf16[4,144,256]{2,1,0:T(8,128)(2,1)S(1)}) custom-call(bf16[16,352,1024]{2,1,0:T(8,128)(2,1)S(1)} %get-tuple-element.47.gate_ref, bf16[16,352,1024]{2,1,0:T(8,128)(2,1)S(1)} %get-tuple-element.48.up_ref, bf16[16,64,352]{2,1,0:T(8,128)(2,1)S(1)} %get-tuple-element.61.p_ref.refs_1_, ...), custom_call_target="tpu_custom_call" | custom-call | flops 738197504 | bytes 23068672 | tf_op jit(solution)/shard_map/pallas_call | solution.py:412
  54.2 0.5 collective-permute-start.17
  54.8 1.5 %collective-permute-start.19 = (bf16[4,144,256]{2,1,0:T(8,128)(2,1)S(1)}, bf16[4,144,256]{2,1,0:T(8,128)(2,1)S(1)}, u32[]{:S(2)}, u32[]{:S(2)}) collective-permute-start(bf16[4,144,256]{2,1,0:T(8,128)(2,1)S(1)} %shard_map.141.refs_4_), channel_id=1, source_target_pairs={{0,2},{1,3},{2,0},{3,1},{4,6},{5,7},{6,4},{7,5},{8,10},{9,11},{10,... | collective-permute-start | bytes 884744 | tf_op jit(solution)/shard_map/ppermute | solution.py:448
  56.3 7.3 %shard_map.142 = (bf16[16,352,1024]{2,1,0:T(8,128)(2,1)}, bf16[16,352,1024]{2,1,0:T(8,128)(2,1)}) custom-call(bf16[16,64,352]{2,1,0:T(8,128)(2,1)S(1)} %get-tuple-element.62.q_ref.refs_0_, bf16[16,64,352]{2,1,0:T(8,128)(2,1)S(1)} %get-tuple-element.70.refs_1_.refs_0_, bf16[16,64,1024]{2,1,0:T(8,128)(2,1)S(1)} %get-tuple-element.71.refs_2_.refs_3_, ...), custom_call_target="tpu_custom_call" | custom-call | flops 1107296256 | bytes 34603008 | tf_op jit(solution)/shard_map/pallas_call | solution.py:412
  64.0 3.0 %collective-permute-start.21 = (bf16[272,256]{1,0:T(8,128)(2,1)S(1)}, bf16[272,256]{1,0:T(8,128)(2,1)S(1)}, u32[]{:S(2)}, u32[]{:S(2)}) collective-permute-start(bf16[272,256]{1,0:T(8,128)(2,1)S(1)} %get-tuple-element.76), channel_id=1, source_target_pairs={{0,8},{4,12},{8,0},{12,4},{1,9},{5,13},{9,1},{13,5},{2,10},{6,14},... | collective-permute-start | bytes 417800 | tf_op jit(solution)/shard_map/ppermute | solution.py:448
  67.4 1.1 %collective-permute-start.22 = (bf16[144,256]{1,0:T(8,128)(2,1)S(1)}, bf16[144,256]{1,0:T(8,128)(2,1)S(1)}, u32[]{:S(2)}, u32[]{:S(2)}) collective-permute-start(bf16[144,256]{1,0:T(8,128)(2,1)S(1)} %get-tuple-element.77), channel_id=1, source_target_pairs={{0,12},{4,8},{8,4},{12,0},{1,13},{5,9},{9,5},{13,1},{2,14},{6,10},... | collective-permute-start | bytes 221192 | tf_op jit(solution)/shard_map/ppermute | solution.py:448
  68.5 7.3 %shard_map.145 = (bf16[16,352,1024]{2,1,0:T(8,128)(2,1)}, bf16[16,352,1024]{2,1,0:T(8,128)(2,1)}) custom-call(bf16[16,64,352]{2,1,0:T(8,128)(2,1)S(1)} %get-tuple-element.70.refs_1_.refs_0_, bf16[16,64,352]{2,1,0:T(8,128)(2,1)S(1)} %get-tuple-element.61.p_ref.refs_1_, ...), custom_call_target="tpu_custom_call", output_to_operand_aliasing={{0}: (4, {})} | custom-call | flops 1107296256 | bytes 34603008 | tf_op jit(solution)/shard_map/pallas_call | solution.py:412
  75.9 0.7 shard_map.144
  (45 shorter events, 3.2 us)
Async XLA Ops:
  1.6 12.2 %collective-permute-start.5 = (bf16[144,256]{1,0:T(8,128)(2,1)S(1)}, bf16[144,256]{1,0:T(8,128)(2,1)S(1)}, u32[]{:S(2)}, u32[]{:S(2)}) collective-permute-start(bf16[144,256]{1,0:T(8,128)(2,1)S(1)} %shard_map.127.o0.own_ref), channel_id=1, source_target_pairs={{0,12},{4,8},{8,4},{12,0},{1,13},{5,9},{9,5},{13,1},{2,14},{6,10},... | collective-permute-start | bytes 221192 | tf_op jit(solution)/shard_map/ppermute | solution.py:448
  6.7 7.1 %collective-permute-start.4 = (bf16[144,256]{1,0:T(8,128)(2,1)S(1)}, bf16[144,256]{1,0:T(8,128)(2,1)S(1)}, u32[]{:S(2)}, u32[]{:S(2)}) collective-permute-start(bf16[144,256]{1,0:T(8,128)(2,1)S(1)} %shard_map.127.o0.own_ref), channel_id=1, source_target_pairs={{0,8},{4,12},{8,0},{12,4},{1,9},{5,13},{9,1},{13,5},{2,10},{6,14},... | collective-permute-start | bytes 221192 | tf_op jit(solution)/shard_map/ppermute | solution.py:448
  6.7 7.1 %collective-permute-start.3 = (bf16[144,256]{1,0:T(8,128)(2,1)S(1)}, bf16[144,256]{1,0:T(8,128)(2,1)S(1)}, u32[]{:S(2)}, u32[]{:S(2)}) collective-permute-start(bf16[144,256]{1,0:T(8,128)(2,1)S(1)} %shard_map.127.o0.own_ref), channel_id=1, source_target_pairs={{0,4},{4,0},{8,12},{12,8},{1,5},{5,1},{9,13},{13,9},{2,6},{6,2},{1... | collective-permute-start | bytes 221192 | tf_op jit(solution)/shard_map/ppermute | solution.py:448
  7.3 6.5 %collective-permute-start.1 = (bf16[144,256]{1,0:T(8,128)(2,1)S(1)}, bf16[144,256]{1,0:T(8,128)(2,1)S(1)}, u32[]{:S(2)}, u32[]{:S(2)}) collective-permute-start(bf16[144,256]{1,0:T(8,128)(2,1)S(1)} %shard_map.127.o0.own_ref), channel_id=1, source_target_pairs={{0,2},{1,3},{2,0},{3,1},{4,6},{5,7},{6,4},{7,5},{8,10},{9,11},{10,... | collective-permute-start | bytes 221192 | tf_op jit(solution)/shard_map/ppermute | solution.py:448
  9.0 4.8 %collective-permute-start.6 = (bf16[128,256]{1,0:T(8,128)(2,1)}, bf16[128,256]{1,0:T(8,128)(2,1)S(1)}, u32[]{:S(2)}, u32[]{:S(2)}) collective-permute-start(bf16[128,256]{1,0:T(8,128)(2,1)} %refs_0_.1), channel_id=1, source_target_pairs={{0,2},{1,3},{2,0},{3,1},{4,6},{5,7},{6,4},{7,5},{8,10},{9,11},{10,... | collective-permute-start | bytes 196616 | tf_op jit(solution)/shard_map/ppermute | solution.py:448
  9.3 16.1 %copy-start.1 = (s32[64]{0:T(128)S(1)}, s32[64]{0:T(128)}, u32[]{:S(2)}) copy-start(s32[64]{0:T(128)} %capacity_ref.1) | copy-start | bytes 772
  13.9 7.6 %collective-permute-start.8 = (bf16[3,144,256]{2,1,0:T(8,128)(2,1)S(1)}, bf16[3,144,256]{2,1,0:T(8,128)(2,1)S(1)}, u32[]{:S(2)}, u32[]{:S(2)}) collective-permute-start(bf16[3,144,256]{2,1,0:T(8,128)(2,1)S(1)} %shard_map.129.refs_2_.b0.info_ref), channel_id=1, source_target_pairs={{0,2},{1,3},{2,0},{3,1},{4,6},{5,7},{6,4},{7,5},{8,10},{9,11},{10,... | collective-permute-start | bytes 663560 | tf_op jit(solution)/shard_map/ppermute | solution.py:448
  15.6 5.8 %collective-permute-start.9 = (bf16[2,128,256]{2,1,0:T(8,128)(2,1)S(1)}, bf16[2,128,256]{2,1,0:T(8,128)(2,1)S(1)}, u32[]{:S(2)}, u32[]{:S(2)}) collective-permute-start(bf16[2,128,256]{2,1,0:T(8,128)(2,1)S(1)} %shard_map.131.refs_0_), channel_id=1, source_target_pairs={{0,4},{4,0},{8,12},{12,8},{1,5},{5,1},{9,13},{13,9},{2,6},{6,2},{1... | collective-permute-start | bytes 393224 | tf_op jit(solution)/shard_map/ppermute | solution.py:448
  21.3 4.1 %collective-permute-start.7 = (bf16[3,144,256]{2,1,0:T(8,128)(2,1)S(1)}, bf16[3,144,256]{2,1,0:T(8,128)(2,1)S(1)}, u32[]{:S(2)}, u32[]{:S(2)}) collective-permute-start(bf16[3,144,256]{2,1,0:T(8,128)(2,1)S(1)} %shard_map.129.refs_2_.b0.info_ref), channel_id=1, source_target_pairs={{0,1},{1,0},{2,3},{3,2},{4,5},{5,4},{6,7},{7,6},{8,9},{9,8},{10,11... | collective-permute-start | bytes 663560 | tf_op jit(solution)/shard_map/ppermute | solution.py:448
  21.5 4.0 %collective-permute-start.10 = (bf16[3,144,256]{2,1,0:T(8,128)(2,1)S(1)}, bf16[3,144,256]{2,1,0:T(8,128)(2,1)S(1)}, u32[]{:S(2)}, u32[]{:S(2)}) collective-permute-start(bf16[3,144,256]{2,1,0:T(8,128)(2,1)S(1)} %bitcast.8), channel_id=1, source_target_pairs={{0,1},{1,0},{2,3},{3,2},{4,5},{5,4},{6,7},{7,6},{8,9},{9,8},{10,11... | collective-permute-start | bytes 663560 | tf_op jit(solution)/shard_map/ppermute | solution.py:448
  22.0 3.4 %collective-permute-start = (bf16[144,256]{1,0:T(8,128)(2,1)S(1)}, bf16[144,256]{1,0:T(8,128)(2,1)S(1)}, u32[]{:S(2)}, u32[]{:S(2)}) collective-permute-start(bf16[144,256]{1,0:T(8,128)(2,1)S(1)} %shard_map.127.o0.own_ref), channel_id=1, source_target_pairs={{0,1},{1,0},{2,3},{3,2},{4,5},{5,4},{6,7},{7,6},{8,9},{9,8},{10,11... | collective-permute-start | bytes 221192 | tf_op jit(solution)/shard_map/ppermute | solution.py:448
  22.1 3.4 %collective-permute-start.2 = (bf16[144,256]{1,0:T(8,128)(2,1)S(1)}, bf16[144,256]{1,0:T(8,128)(2,1)S(1)}, u32[]{:S(2)}, u32[]{:S(2)}) collective-permute-start(bf16[144,256]{1,0:T(8,128)(2,1)S(1)} %collective-permute-done.1.refs_4_.o2), channel_id=1, source_target_pairs={{0,1},{1,0},{2,3},{3,2},{4,5},{5,4},{6,7},{7,6},{8,9},{9,8},{10,11... | collective-permute-start | bytes 221192 | tf_op jit(solution)/shard_map/ppermute | solution.py:448
  22.5 15.0 %collective-permute-start.11 = (bf16[2,2,128,256]{3,2,1,0:T(8,128)(2,1)S(1)}, bf16[2,2,128,256]{3,2,1,0:T(8,128)(2,1)S(1)}, u32[]{:S(2)}, u32[]{:S(2)}) collective-permute-start(bf16[2,2,128,256]{3,2,1,0:T(8,128)(2,1)S(1)} %shard_map.132.refs_2_.later_ref.a01), channel_id=1, source_target_pairs={{0,8},{4,12},{8,0},{12,4},{1,9},{5,13},{9,1},{13,5},{2,10},{6,14},... | collective-permute-start | bytes 786440 | tf_op jit(solution)/shard_map/ppermute | solution.py:448
  38.0 2.0 %collective-permute-start.12 = (bf16[2,4,128,256]{3,2,1,0:T(8,128)(2,1)S(1)}, bf16[2,4,128,256]{3,2,1,0:T(8,128)(2,1)S(1)}, u32[]{:S(2)}, u32[]{:S(2)}) collective-permute-start(bf16[2,4,128,256]{3,2,1,0:T(8,128)(2,1)S(1)} %get-tuple-element.52), channel_id=1, source_target_pairs={{0,1},{1,0},{2,3},{3,2},{4,5},{5,4},{6,7},{7,6},{8,9},{9,8},{10,11... | collective-permute-start | bytes 1572872 | tf_op jit(solution)/shard_map/ppermute | solution.py:448
  38.2 2.6 %collective-permute-start.15 = (bf16[2,2,128,256]{3,2,1,0:T(8,128)(2,1)S(1)}, bf16[2,2,128,256]{3,2,1,0:T(8,128)(2,1)S(1)}, u32[]{:S(2)}, u32[]{:S(2)}) collective-permute-start(bf16[2,2,128,256]{3,2,1,0:T(8,128)(2,1)S(1)} %shard_map.132.refs_2_.later_ref.a01), channel_id=1, source_target_pairs={{0,1},{1,0},{2,3},{3,2},{4,5},{5,4},{6,7},{7,6},{8,9},{9,8},{10,11... | collective-permute-start | bytes 786440 | tf_op jit(solution)/shard_map/ppermute | solution.py:448
  38.6 2.2 %collective-permute-start.16 = (bf16[2,2,128,256]{3,2,1,0:T(8,128)(2,1)S(1)}, bf16[2,2,128,256]{3,2,1,0:T(8,128)(2,1)S(1)}, u32[]{:S(2)}, u32[]{:S(2)}) collective-permute-start(bf16[2,2,128,256]{3,2,1,0:T(8,128)(2,1)S(1)} %collective-permute-done.11.refs_0_.a23), channel_id=1, source_target_pairs={{0,1},{1,0},{2,3},{3,2},{4,5},{5,4},{6,7},{7,6},{8,9},{9,8},{10,11... | collective-permute-start | bytes 786440 | tf_op jit(solution)/shard_map/ppermute | solution.py:448
  40.1 10.3 %collective-permute-start.13 = (bf16[4,128,256]{2,1,0:T(8,128)(2,1)S(1)}, bf16[4,128,256]{2,1,0:T(8,128)(2,1)S(1)}, u32[]{:S(2)}, u32[]{:S(2)}) collective-permute-start(bf16[4,128,256]{2,1,0:T(8,128)(2,1)S(1)} %get-tuple-element.54), channel_id=1, source_target_pairs={{0,2},{1,3},{2,0},{3,1},{4,6},{5,7},{6,4},{7,5},{8,10},{9,11},{10,... | collective-permute-start | bytes 786440 | tf_op jit(solution)/shard_map/ppermute | solution.py:448
  51.0 3.7 %collective-permute-start.18 = (bf16[4,144,256]{2,1,0:T(8,128)(2,1)S(1)}, bf16[4,144,256]{2,1,0:T(8,128)(2,1)S(1)}, u32[]{:S(2)}, u32[]{:S(2)}) collective-permute-start(bf16[4,144,256]{2,1,0:T(8,128)(2,1)S(1)} %get-tuple-element.69), channel_id=1, source_target_pairs={{0,1},{1,0},{2,3},{3,2},{4,5},{5,4},{6,7},{7,6},{8,9},{9,8},{10,11... | collective-permute-start | bytes 884744 | tf_op jit(solution)/shard_map/ppermute | solution.py:448
  54.2 9.4 %collective-permute-start.17 = (bf16[4,144,256]{2,1,0:T(8,128)(2,1)S(1)}, bf16[4,144,256]{2,1,0:T(8,128)(2,1)S(1)}, u32[]{:S(2)}, u32[]{:S(2)}) collective-permute-start(bf16[4,144,256]{2,1,0:T(8,128)(2,1)S(1)} %get-tuple-element.68), channel_id=1, source_target_pairs={{0,1},{1,0},{2,3},{3,2},{4,5},{5,4},{6,7},{7,6},{8,9},{9,8},{10,11... | collective-permute-start | bytes 884744 | tf_op jit(solution)/shard_map/ppermute | solution.py:448
  54.8 9.1 %collective-permute-start.19 = (bf16[4,144,256]{2,1,0:T(8,128)(2,1)S(1)}, bf16[4,144,256]{2,1,0:T(8,128)(2,1)S(1)}, u32[]{:S(2)}, u32[]{:S(2)}) collective-permute-start(bf16[4,144,256]{2,1,0:T(8,128)(2,1)S(1)} %shard_map.141.refs_4_), channel_id=1, source_target_pairs={{0,2},{1,3},{2,0},{3,1},{4,6},{5,7},{6,4},{7,5},{8,10},{9,11},{10,... | collective-permute-start | bytes 884744 | tf_op jit(solution)/shard_map/ppermute | solution.py:448
  56.3 7.4 %collective-permute-start.14 = (bf16[2,128,256]{2,1,0:T(8,128)(2,1)S(1)}, bf16[2,128,256]{2,1,0:T(8,128)(2,1)S(1)}, u32[]{:S(2)}, u32[]{:S(2)}) collective-permute-start(bf16[2,128,256]{2,1,0:T(8,128)(2,1)S(1)} %get-tuple-element.56), channel_id=1, source_target_pairs={{0,4},{4,0},{8,12},{12,8},{1,5},{5,1},{9,13},{13,9},{2,6},{6,2},{1... | collective-permute-start | bytes 393224 | tf_op jit(solution)/shard_map/ppermute | solution.py:448
  64.0 11.9 %collective-permute-start.21 = (bf16[272,256]{1,0:T(8,128)(2,1)S(1)}, bf16[272,256]{1,0:T(8,128)(2,1)S(1)}, u32[]{:S(2)}, u32[]{:S(2)}) collective-permute-start(bf16[272,256]{1,0:T(8,128)(2,1)S(1)} %get-tuple-element.76), channel_id=1, source_target_pairs={{0,8},{4,12},{8,0},{12,4},{1,9},{5,13},{9,1},{13,5},{2,10},{6,14},... | collective-permute-start | bytes 417800 | tf_op jit(solution)/shard_map/ppermute | solution.py:448
  67.0 8.9 %collective-permute-start.20 = (bf16[144,256]{1,0:T(8,128)(2,1)S(1)}, bf16[144,256]{1,0:T(8,128)(2,1)S(1)}, u32[]{:S(2)}, u32[]{:S(2)}) collective-permute-start(bf16[144,256]{1,0:T(8,128)(2,1)S(1)} %get-tuple-element.75), channel_id=1, source_target_pairs={{0,4},{4,0},{8,12},{12,8},{1,5},{5,1},{9,13},{13,9},{2,6},{6,2},{1... | collective-permute-start | bytes 221192 | tf_op jit(solution)/shard_map/ppermute | solution.py:448
  67.4 8.5 %collective-permute-start.22 = (bf16[144,256]{1,0:T(8,128)(2,1)S(1)}, bf16[144,256]{1,0:T(8,128)(2,1)S(1)}, u32[]{:S(2)}, u32[]{:S(2)}) collective-permute-start(bf16[144,256]{1,0:T(8,128)(2,1)S(1)} %get-tuple-element.77), channel_id=1, source_target_pairs={{0,12},{4,8},{8,4},{12,0},{1,13},{5,9},{9,5},{13,1},{2,14},{6,10},... | collective-permute-start | bytes 221192 | tf_op jit(solution)/shard_map/ppermute | solution.py:448
  (1 other events, 14.9 us)
